TPU v7x, 512 devices: a whole 4x4x16 slice. The times are simulated.
512 devices in a mesh: clip: 16 (over x, y), seq: 32 (over z, core).
Axes of the slice: x: 4, y: 4, z: 16, core: 2. Of those that a mesh axis runs over, the one named last changes fastest.
Arguments:
- clip_in: bfloat16 [16, 64, 64, 8, 128], P('clip', 'seq'), may hold values from -6 to 6
- first_plane: bfloat16 [3, 3, 128, 128], replicated, may hold values from -0.1875 to 0.1875
- first_time: bfloat16 [3, 128, 128], replicated, may hold values from -0.3125 to 0.3125
- down_plane: bfloat16 [3, 3, 128, 256], replicated, may hold values from -0.1875 to 0.1875
- down_time: bfloat16 [3, 256, 256], replicated, may hold values from -0.21875 to 0.21875
- last_time: bfloat16 [3, 256, 256], replicated, may hold values from -0.21875 to 0.21875
- cotan_out: bfloat16 [16, 32, 32, 4, 256], P('clip', None, 'seq'), may hold values from -6 to 6
Outputs:
- output: bfloat16 [16, 32, 32, 4, 256], P('clip', None, 'seq')
- grad_first_plane: bfloat16 [3, 3, 128, 128], replicated
- grad_first_time: bfloat16 [3, 128, 128], replicated
- grad_down_plane: bfloat16 [3, 3, 128, 256], replicated
- grad_down_time: bfloat16 [3, 256, 256], replicated
- grad_last_time: bfloat16 [3, 256, 256], replicated
All inputs are finite; a program needn't handle non-finite values.
Results may differ from a plain program's by a relative error of at most 0.014.
Values may be sent and summed in bfloat16 or wider, within the bound.
No kernel may reach another device: no remote copies, remote signals or barrier semaphores. Data moves between devices by JAX's collectives and lax.ppermute only.
A program may use at most 64 MiB of HBM per device.

v0:
```python
import jax
import jax.numpy as jnp
from jax import lax
from jax.sharding import PartitionSpec as P


def from_behind(block, axis, distance):
    devices = range(lax.axis_size(axis))
    route = [(i - distance, i) for i in devices if i - distance in devices]
    return lax.ppermute(block, axis, route)


def plane_conv(source, kernel, stride):
    num_frames, num_rows, num_cols, num_chans = source.shape
    padded = jnp.pad(source, ((0, 0), (1, 1), (1, 1), (0, 0)))
    out_rows = num_rows // stride
    out_cols = num_cols // stride
    summed = jnp.zeros((num_frames * out_rows * out_cols, kernel.shape[3]), jnp.float32)
    for row_tap in range(3):
        for col_tap in range(3):
            window = padded[
                :, row_tap : row_tap + num_rows : stride, col_tap : col_tap + num_cols : stride, :
            ]
            summed = summed + jnp.dot(
                window.reshape(-1, num_chans),
                kernel[row_tap, col_tap],
                preferred_element_type=jnp.float32,
            )
    return summed.reshape(num_frames, out_rows, out_cols, kernel.shape[3])


def plane_conv_grad(source, cotan, stride):
    num_frames, num_rows, num_cols, num_chans = source.shape
    padded = jnp.pad(source, ((0, 0), (1, 1), (1, 1), (0, 0)))
    flat_cotan = cotan.reshape(-1, cotan.shape[3])
    result = []
    for row_tap in range(3):
        row_list = []
        for col_tap in range(3):
            window = padded[
                :, row_tap : row_tap + num_rows : stride, col_tap : col_tap + num_cols : stride, :
            ]
            row_list.append(
                jnp.dot(
                    window.reshape(-1, num_chans).T, flat_cotan, preferred_element_type=jnp.float32
                )
            )
        result.append(jnp.stack(row_list, axis=0))
    return jnp.stack(result, axis=0)


def plane_back_strided(cotan, kernel):
    num_frames, half_rows, half_cols, num_chans = cotan.shape
    padded = jnp.pad(cotan, ((0, 0), (0, 1), (0, 1), (0, 0)))
    taps_by_parity = (((1, 0),), ((0, 1), (2, 0)))
    blocks = []
    for row_par in range(2):
        row_blocks = []
        for col_par in range(2):
            summed = jnp.zeros((num_frames * half_rows * half_cols, kernel.shape[2]), jnp.float32)
            for row_tap, row_off in taps_by_parity[row_par]:
                for col_tap, col_off in taps_by_parity[col_par]:
                    window = padded[
                        :, row_off : row_off + half_rows, col_off : col_off + half_cols, :
                    ]
                    summed = summed + jnp.dot(
                        window.reshape(-1, num_chans),
                        kernel[row_tap, col_tap].T,
                        preferred_element_type=jnp.float32,
                    )
            row_blocks.append(summed.reshape(num_frames, half_rows, half_cols, kernel.shape[2]))
        blocks.append(jnp.stack(row_blocks, axis=3))
    stacked = jnp.stack(blocks, axis=2)
    return stacked.reshape(num_frames, 2 * half_rows, 2 * half_cols, kernel.shape[2])


def time_conv(extended, kernel, stride):
    num_out = (extended.shape[0] - 2) // stride
    num_chans = extended.shape[-1]
    summed = jnp.zeros(
        (num_out * extended.shape[1] * extended.shape[2], kernel.shape[2]), jnp.float32
    )
    for tap_index in range(3):
        taps = extended[tap_index : tap_index + stride * num_out : stride]
        summed = summed + jnp.dot(
            taps.reshape(-1, num_chans), kernel[tap_index], preferred_element_type=jnp.float32
        )
    return summed.reshape(num_out, extended.shape[1], extended.shape[2], kernel.shape[2])


def time_conv_grad(extended, cotan, stride):
    num_out = cotan.shape[0]
    flat_cotan = cotan.reshape(-1, cotan.shape[3])
    result = []
    for tap_index in range(3):
        taps = extended[tap_index : tap_index + stride * num_out : stride]
        result.append(
            jnp.dot(
                taps.reshape(-1, extended.shape[3]).T,
                flat_cotan,
                preferred_element_type=jnp.float32,
            )
        )
    return jnp.stack(result, axis=0)


def time_back_one(ahead, kernel):
    num_frames = ahead.shape[0] - 2
    summed = jnp.zeros((num_frames * ahead.shape[1] * ahead.shape[2], kernel.shape[1]), jnp.float32)
    for tap_index in range(3):
        taps = ahead[2 - tap_index : 2 - tap_index + num_frames]
        summed = summed + jnp.dot(
            taps.reshape(-1, ahead.shape[3]),
            kernel[tap_index].T,
            preferred_element_type=jnp.float32,
        )
    return summed.reshape(num_frames, ahead.shape[1], ahead.shape[2], kernel.shape[1])


def time_back_two(ahead, kernel):
    num_frames = ahead.shape[0] - 1
    num_chans = ahead.shape[3]
    current = ahead[:num_frames].reshape(-1, num_chans)
    following = ahead[1:].reshape(-1, num_chans)
    even_part = jnp.dot(current, kernel[2].T, preferred_element_type=jnp.float32) + jnp.dot(
        following, kernel[0].T, preferred_element_type=jnp.float32
    )
    odd_part = jnp.dot(following, kernel[1].T, preferred_element_type=jnp.float32)
    shape_one = (num_frames, ahead.shape[1], ahead.shape[2], kernel.shape[1])
    stacked = jnp.stack([even_part.reshape(shape_one), odd_part.reshape(shape_one)], axis=1)
    return stacked.reshape(2 * num_frames, ahead.shape[1], ahead.shape[2], kernel.shape[1])


def silu_slope(preact):
    sigma = jax.nn.sigmoid(preact)
    return sigma * (1.0 + preact * (1.0 - sigma))


def zero_frames(count, like):
    return jnp.zeros((count,) + like.shape[1:], like.dtype)


def last_section(lowered, cotan, last_time):
    lowered_ext = jnp.concatenate([zero_frames(2, lowered), lowered], axis=0)
    output = (lowered.astype(jnp.float32) + time_conv(lowered_ext, last_time, 1)).astype(
        jnp.bfloat16
    )
    grad_last = time_conv_grad(lowered_ext, cotan, 1)
    cotan_ext = jnp.concatenate([cotan, zero_frames(2, cotan)], axis=0)
    grad_lowered = (cotan.astype(jnp.float32) + time_back_one(cotan_ext, last_time)).astype(
        jnp.bfloat16
    )
    return (output, grad_last, grad_lowered)


def local(clip_in, first_plane, first_time, down_plane, down_time, last_time, cotan_out):
    source = clip_in[0]
    cotan = cotan_out[0]
    pre_first = plane_conv(source, first_plane, 1)
    hidden = jax.nn.silu(pre_first).astype(jnp.bfloat16)
    hidden_prior = from_behind(hidden, "seq", 1)
    hidden_ext = jnp.concatenate([hidden_prior, hidden], axis=0)
    mixed = (source.astype(jnp.float32) + time_conv(hidden_ext, first_time, 1)).astype(jnp.bfloat16)
    strided = plane_conv(mixed, down_plane, 2).astype(jnp.bfloat16)
    strided_prior = from_behind(strided, "seq", 1)
    strided_ext = jnp.concatenate([strided_prior, strided], axis=0)
    pre_down = time_conv(strided_ext, down_time, 2)
    lowered = jax.nn.silu(pre_down).astype(jnp.bfloat16)
    lowered_rows = lax.all_to_all(lowered, "seq", split_axis=1, concat_axis=0, tiled=True)
    output, grad_last, grad_rows = last_section(lowered_rows, cotan, last_time)
    grad_lowered = lax.all_to_all(grad_rows, "seq", split_axis=0, concat_axis=1, tiled=True)
    grad_pre = (grad_lowered.astype(jnp.float32) * silu_slope(pre_down)).astype(jnp.bfloat16)
    grad_down_time = time_conv_grad(strided_ext, grad_pre, 2)
    pre_next = from_behind(grad_pre, "seq", -1)
    pre_ext = jnp.concatenate([grad_pre, pre_next], axis=0)
    grad_strided = time_back_two(pre_ext, down_time).astype(jnp.bfloat16)
    grad_down_plane = plane_conv_grad(mixed, grad_strided, 2)
    grad_mixed = plane_back_strided(grad_strided, down_plane).astype(jnp.bfloat16)
    grad_first_time = time_conv_grad(hidden_ext, grad_mixed, 1)
    mixed_next = from_behind(grad_mixed, "seq", -1)
    mixed_ext = jnp.concatenate([grad_mixed, mixed_next], axis=0)
    grad_hidden = time_back_one(mixed_ext, first_time)
    grad_first_pre = (grad_hidden * silu_slope(pre_first)).astype(jnp.bfloat16)
    grad_first_plane = plane_conv_grad(source, grad_first_pre, 1)
    grad_first_plane, grad_first_time, grad_down_plane, grad_down_time, grad_last = lax.psum(
        (grad_first_plane, grad_first_time, grad_down_plane, grad_down_time, grad_last),
        ("clip", "seq"),
    )
    return (
        output[None],
        grad_first_plane.astype(jnp.bfloat16),
        grad_first_time.astype(jnp.bfloat16),
        grad_down_plane.astype(jnp.bfloat16),
        grad_down_time.astype(jnp.bfloat16),
        grad_last.astype(jnp.bfloat16),
    )


def solution(mesh):
    placed = (
        P("clip", "seq", None, None, None),
        P(),
        P(),
        P(),
        P(),
        P(),
        P("clip", None, "seq", None, None),
    )
    return jax.shard_map(
        local,
        mesh=mesh,
        in_specs=placed,
        out_specs=(P("clip", None, "seq", None, None), P(), P(), P(), P(), P()),
        check_vma=False,
    )
```

profile of v0, /device:TPU:1, one launch (start us, length us, event | category | flops | bytes accessed | tf_op | source)
XLA Modules:
  0.0 287.7 jit_solution(3332292793909359838)
XLA Ops:
  0.7 0.9 reshape_squeeze.4
  1.6 1.0 pad_slice_fusion.11
  2.6 1.1 fusion.23
  3.7 1.1 convolution_add_fusion.25
  5.7 16.7 %all-to-all-start.1 = ((bf16[32,1,4,256]{3,2,1,0:T(4,128)(2,1)}), bf16[32,1,4,256]{3,2,1,0:T(4,128)(2,1)S(1)}, u32[]{:S(2)}, u32[]{:S(2)}) async-start(bf16[32,1,4,256]{3,2,1,0:T(4,128)(2,1)} %fusion.18), calls=%async_computation.1 | async-start | bytes 131072 | tf_op jit(solution)/shard_map/all_to_all | solution.py:171
  27.2 3.6 %collective-permute-start = (bf16[2,64,8,128]{3,1,2,0:T(8,128)(2,1)S(1)}, bf16[2,64,8,128]{3,1,2,0:T(8,128)(2,1)S(1)}, u32[]{:S(2)}, u32[]{:S(2)}) collective-permute-start(bf16[2,64,8,128]{3,1,2,0:T(8,128)(2,1)S(1)} %multiply_convert_fusion.2), channel_id=1, source_target_pairs={{0,1},{1,2},{2,3},{3,4},{4,5},{5,6},{6,7},{7,8},{8,9},{9,10},{10,1... | collective-permute-start | bytes 786440 | tf_op jit(solution)/shard_map/ppermute | solution.py:10
  31.0 4.6 %all-to-all-done.1 = bf16[32,1,4,256]{3,2,1,0:T(4,128)(2,1)S(1)} async-done(((bf16[32,1,4,256]{3,2,1,0:T(4,128)(2,1)}), bf16[32,1,4,256]{3,2,1,0:T(4,128)(2,1)S(1)}, u32[]{:S(2)}, u32[]{:S(2)}) %all-to-all-start.1) | async-done | bytes 65568 | tf_op jit(solution)/shard_map/all_to_all | solution.py:171
  42.7 3.6 %collective-permute-start.1 = (bf16[2,32,4,256]{3,1,2,0:T(8,128)(2,1)S(1)}, bf16[2,32,4,256]{3,1,2,0:T(8,128)(2,1)S(1)}, u32[]{:S(2)}, u32[]{:S(2)}) collective-permute-start(bf16[2,32,4,256]{3,1,2,0:T(8,128)(2,1)S(1)} %copy.119), channel_id=1, source_target_pairs={{0,1},{1,2},{2,3},{3,4},{4,5},{5,6},{6,7},{7,8},{8,9},{9,10},{10,1... | collective-permute-start | bytes 393224 | tf_op jit(solution)/shard_map/ppermute | solution.py:10
  46.5 1.8 collective-permute-done.1
  48.9 1.1 fusion.27
  50.7 13.8 %all-to-all-start = ((bf16[1,32,4,256]{3,2,0,1:T(4,128)(2,1)}), bf16[1,32,4,256]{3,2,0,1:T(4,128)(2,1)S(1)}, u32[]{:S(2)}, u32[]{:S(2)}) async-start(bf16[1,32,4,256]{3,2,0,1:T(4,128)(2,1)} %copy.124), calls=%async_computation | async-start | bytes 131072 | tf_op jit(solution)/shard_map/all_to_all | solution.py:169
  64.5 2.1 collective-permute-start.2
  66.8 0.9 convolution_bitcast_fusion.3
  67.7 0.9 convolution_bitcast_fusion.4
  68.6 0.9 convolution_bitcast_fusion.5
  69.5 1.0 collective-permute-done.2
  71.1 0.9 convolution_bitcast_fusion.6
  72.0 0.9 convolution_bitcast_fusion.7
  72.8 0.9 convolution_bitcast_fusion.8
  73.7 0.9 convolution_bitcast_fusion.9
  74.6 0.8 convolution_bitcast_fusion.10
  75.4 0.9 convolution_bitcast_fusion.11
  81.6 2.1 collective-permute-start.3
  87.4 1.8 fusion.96
  89.4 0.9 convolution_bitcast_fusion.2
  90.3 0.9 convolution_bitcast_fusion.1
  92.5 1.4 pad_maximum_fusion.1
  93.8 1.6 reshape.499
  95.4 1.6 fusion.47
  97.1 1.0 fusion.100
  98.2 1.0 fusion.1
  103.7 184.1 %all-reduce.7 = (bf16[3,3,128,128]{3,2,1,0:T(8,128)(2,1)}, bf16[3,128,128]{2,1,0:T(8,128)(2,1)}, bf16[3,3,128,256]{3,2,1,0:T(8,128)(2,1)}, bf16[3,256,256]{2,1,0:T(8,128)(2,1)}, bf16[3,256,256]{2,1,0:T(8,128)(2,1)}) all-reduce(f32[3,3,128,128]{3,2,1,0:T(8,128)S(1)} %pad_maximum_fusion.3, ...), channel_id=1, replica_groups=mesh['clip'=16,'seq'=32] {'clip','seq'}, use_global_device_ids=true, to_apply=%region_0.1 | all-reduce | flops 884736 | bytes 5308416 | tf_op jit(solution)/shard_map/psum | solution.py:185
  (206 shorter events, 29.0 us)
Async XLA Ops:
  0.6 4.4 %copy-start.13 = (bf16[1,32,1,4,256]{4,3,2,1,0:T(4,128)(2,1)S(1)}, bf16[1,32,1,4,256]{4,3,2,1,0:T(4,128)(2,1)}, u32[]{:S(2)}) copy-start(bf16[1,32,1,4,256]{4,3,2,1,0:T(4,128)(2,1)} %param.13) | copy-start | bytes 196612
  0.6 4.2 %copy-start.5 = (bf16[3,256,256]{2,1,0:T(8,128)(2,1)S(1)}, bf16[3,256,256]{2,1,0:T(8,128)(2,1)}, u32[]{:S(2)}) copy-start(bf16[3,256,256]{2,1,0:T(8,128)(2,1)} %param.12) | copy-start | bytes 1179652
  1.6 20.9 %copy-start = (bf16[1,2,64,8,128]{4,3,2,1,0:T(8,128)(2,1)S(1)}, bf16[1,2,64,8,128]{4,3,2,1,0:T(8,128)(2,1)}, u32[]{:S(2)}) copy-start(bf16[1,2,64,8,128]{4,3,2,1,0:T(8,128)(2,1)} %param.7) | copy-start | bytes 786436
  5.7 29.8 %all-to-all-start.1 = ((bf16[32,1,4,256]{3,2,1,0:T(4,128)(2,1)}), bf16[32,1,4,256]{3,2,1,0:T(4,128)(2,1)S(1)}, u32[]{:S(2)}, u32[]{:S(2)}) async-start(bf16[32,1,4,256]{3,2,1,0:T(4,128)(2,1)} %fusion.18), calls=%async_computation.1 | async-start | bytes 131072 | tf_op jit(solution)/shard_map/all_to_all | solution.py:171
  24.0 1.0 copy-start.27
  26.7 4.1 %copy-start.23 = (bf16[3,128,128]{2,1,0:T(8,128)(2,1)S(1)}, bf16[3,128,128]{2,1,0:T(8,128)(2,1)}, u32[]{:S(2)}) copy-start(bf16[3,128,128]{2,1,0:T(8,128)(2,1)} %param.9) | copy-start | bytes 294916
  27.0 3.8 %copy-start.3 = (f32[1024,128]{1,0:T(8,128)}, f32[1024,128]{1,0:T(8,128)S(1)}, u32[]{:S(2)}) copy-start(f32[1024,128]{1,0:T(8,128)S(1)} %get-tuple-element.49) | copy-start | bytes 1572868
  27.0 9.4 %copy-start.24 = (bf16[1024,128]{1,0:T(8,128)(2,1)}, bf16[1024,128]{1,0:T(8,128)(2,1)S(1)}, u32[]{:S(2)}) copy-start(bf16[1024,128]{1,0:T(8,128)(2,1)S(1)} %get-tuple-element.48) | copy-start | bytes 786436
  27.2 9.2 %collective-permute-start = (bf16[2,64,8,128]{3,1,2,0:T(8,128)(2,1)S(1)}, bf16[2,64,8,128]{3,1,2,0:T(8,128)(2,1)S(1)}, u32[]{:S(2)}, u32[]{:S(2)}) collective-permute-start(bf16[2,64,8,128]{3,1,2,0:T(8,128)(2,1)S(1)} %multiply_convert_fusion.2), channel_id=1, source_target_pairs={{0,1},{1,2},{2,3},{3,4},{4,5},{5,6},{6,7},{7,8},{8,9},{9,10},{10,1... | collective-permute-start | bytes 786440 | tf_op jit(solution)/shard_map/ppermute | solution.py:10
  37.5 2.8 copy-start.1
  41.4 4.9 %copy-start.6 = (bf16[3,256,256]{2,1,0:T(8,128)(2,1)S(1)}, bf16[3,256,256]{2,1,0:T(8,128)(2,1)}, u32[]{:S(2)}) copy-start(bf16[3,256,256]{2,1,0:T(8,128)(2,1)} %param.11) | copy-start | bytes 1179652
  42.7 5.6 %collective-permute-start.1 = (bf16[2,32,4,256]{3,1,2,0:T(8,128)(2,1)S(1)}, bf16[2,32,4,256]{3,1,2,0:T(8,128)(2,1)S(1)}, u32[]{:S(2)}, u32[]{:S(2)}) collective-permute-start(bf16[2,32,4,256]{3,1,2,0:T(8,128)(2,1)S(1)} %copy.119), channel_id=1, source_target_pairs={{0,1},{1,2},{2,3},{3,4},{4,5},{5,6},{6,7},{7,8},{8,9},{9,10},{10,1... | collective-permute-start | bytes 393224 | tf_op jit(solution)/shard_map/ppermute | solution.py:10
  48.8 18.0 %copy-start.26 = (bf16[32,4,256]{2,1,0:T(4,128)(2,1)S(1)}, bf16[32,4,256]{2,1,0:T(4,128)(2,1)}, u32[]{:S(2)}) copy-start(bf16[32,4,256]{2,1,0:T(4,128)(2,1)} %reshape.514) | copy-start | bytes 196612
  50.7 38.4 %all-to-all-start = ((bf16[1,32,4,256]{3,2,0,1:T(4,128)(2,1)}), bf16[1,32,4,256]{3,2,0,1:T(4,128)(2,1)S(1)}, u32[]{:S(2)}, u32[]{:S(2)}) async-start(bf16[1,32,4,256]{3,2,0,1:T(4,128)(2,1)} %copy.124), calls=%async_computation | async-start | bytes 131072 | tf_op jit(solution)/shard_map/all_to_all | solution.py:169
  64.5 6.1 %collective-permute-start.2 = (bf16[1,32,4,256]{3,1,2,0:T(8,128)(2,1)S(1)}, bf16[1,32,4,256]{3,1,2,0:T(8,128)(2,1)S(1)}, u32[]{:S(2)}, u32[]{:S(2)}) collective-permute-start(bf16[1,32,4,256]{3,1,2,0:T(8,128)(2,1)S(1)} %get-tuple-element.40), channel_id=1, source_target_pairs={{1,0},{2,1},{3,2},{4,3},{5,4},{6,5},{7,6},{8,7},{9,8},{10,9},{11,1... | collective-permute-start | bytes 196616 | tf_op jit(solution)/shard_map/ppermute | solution.py:10
  80.9 2.9 copy-start.25
  81.6 15.4 %collective-permute-start.3 = (bf16[2,64,8,128]{3,2,1,0:T(8,128)(2,1)S(1)}, bf16[2,64,8,128]{3,2,1,0:T(8,128)(2,1)S(1)}, u32[]{:S(2)}, u32[]{:S(2)}) collective-permute-start(bf16[2,64,8,128]{3,2,1,0:T(8,128)(2,1)S(1)} %bitcast.461), channel_id=1, source_target_pairs={{1,0},{2,1},{3,2},{4,3},{5,4},{6,5},{7,6},{8,7},{9,8},{10,9},{11,1... | collective-permute-start | bytes 786440 | tf_op jit(solution)/shard_map/ppermute | solution.py:10
  83.8 0.9 copy-start.20
  83.8 1.0 copy-start.21
  83.8 1.0 copy-start.22
  83.8 1.1 copy-start.14
  83.8 1.1 copy-start.15
  83.8 1.2 copy-start.16
  83.8 1.2 copy-start.17
  83.8 1.2 copy-start.18
  83.8 1.3 copy-start.19
  85.2 1.0 copy-start.10
  89.1 2.5 copy-start.11
  95.4 2.7 copy-start.2
  97.1 2.1 copy-start.4
  99.6 1.0 copy-start.8
  102.7 0.9 copy-start.12
  (2 other events, 1.4 us)
where the time goes:
time: 290 us; the launch traced here: 288 us
  blocking collectives  184 us (63%)
  starting transfers between devices  42 us (14%)
  matrix products  30.8 us (11%)
  local copies, waits for them, and re-layouts  16 us (6%)
  waiting for transfers between devices  7.43 us (3%)
  other arithmetic  5.45 us (2%)
    psum x1, blocking collectives, local(): lax.psum((grad_first_plane, grad_first_time, grad_down_plane, grad_down_t...  184 us
    all_to_all x1, starting transfers between devices, local(): lax.all_to_all(grad_rows, 'seq', split_axis=0, concat_axis=1, tiled=True)  16.7 us
    all_to_all x1, starting transfers between devices, local(): lax.all_to_all(lowered, 'seq', split_axis=1, concat_axis=0, tiled=True)  13.8 us
    ppermute x4, starting transfers between devices, from_behind(): return lax.ppermute(block, axis, route)  11.5 us
    dot_general x18, matrix products, plane_conv_grad(): jnp.dot(window.reshape(-1, num_chans).T, flat_cotan, preferred_element_ty...  10.2 us
    dot_general x6, matrix products, time_back_one(): jnp.dot(taps.reshape(-1, ahead.shape[3]), kernel[tap_index].T, preferred_...  6.2 us
  transfers between devices with their start and end apart: 6, of which 3 were waited for; matrix products, arithmetic and copies ran while one was open for 10% of the time, Pallas kernels for 0%

commit v1 on v0

--- a/solution.py
+++ b/solution.py
@@ -151,6 +151,60 @@
         jnp.bfloat16
     )
     return (output, grad_last, grad_lowered)
+
+
+def swap_cores(block):
+    count = lax.axis_size("seq")
+    return lax.ppermute(block, "seq", [(i, i ^ 1) for i in range(count)])
+
+
+def exchange_clip(blocks):
+    return lax.all_to_all(blocks, "clip", split_axis=0, concat_axis=0, tiled=True)
+
+
+def exchange_depth(blocks):
+    count = lax.axis_size("seq")
+    groups = [list(range(core, count, 2)) for core in range(2)]
+    return lax.all_to_all(
+        blocks, "seq", split_axis=0, concat_axis=0, axis_index_groups=groups, tiled=True
+    )
+
+
+def sum_blocks(blocks):
+    return jnp.sum(blocks.astype(jnp.float32), axis=0)
+
+
+def sum_everywhere(grads):
+    clips = lax.axis_size("clip")
+    chips = lax.axis_size("seq") // 2
+    core = lax.axis_index("seq") % 2
+    flat = jnp.concatenate([grad.reshape(-1, 128) for grad in grads], axis=0)
+    num_rows = flat.shape[0]
+    halves = flat.reshape(2, num_rows // 2, 128)
+    mine = lax.dynamic_index_in_dim(halves, core, 0, keepdims=False)
+    other = lax.dynamic_index_in_dim(halves, 1 - core, 0, keepdims=False)
+    other = swap_cores(other.astype(jnp.bfloat16))
+    half = (mine + other.astype(jnp.float32)).astype(jnp.bfloat16)
+    part = sum_blocks(exchange_clip(half.reshape(clips, -1, 128)))
+    part_rows = part.shape[0]
+    chunk = 16 * (-(-part_rows // (16 * chips)))
+    part = jnp.pad(part, ((0, chunk * chips - part_rows), (0, 0))).astype(jnp.bfloat16)
+    piece = sum_blocks(exchange_depth(part.reshape(chips, chunk, 128))).astype(jnp.bfloat16)
+    part = exchange_depth(jnp.broadcast_to(piece[None], (chips, chunk, 128)))
+    part = part.reshape(-1, 128)[:part_rows]
+    half = exchange_clip(jnp.broadcast_to(part[None], (clips, part_rows, 128)))
+    half = half.reshape(-1, 128)
+    other = swap_cores(half)
+    first = jnp.where(core == 0, half, other)
+    second = jnp.where(core == 0, other, half)
+    whole = jnp.concatenate([first, second], axis=0)
+    result = []
+    start = 0
+    for grad in grads:
+        rows = grad.size // 128
+        result.append(whole[start : start + rows].reshape(grad.shape))
+        start += rows
+    return tuple(result)
 
 
 def local(clip_in, first_plane, first_time, down_plane, down_time, last_time, cotan_out):
@@ -182,18 +236,10 @@
     grad_hidden = time_back_one(mixed_ext, first_time)
     grad_first_pre = (grad_hidden * silu_slope(pre_first)).astype(jnp.bfloat16)
     grad_first_plane = plane_conv_grad(source, grad_first_pre, 1)
-    grad_first_plane, grad_first_time, grad_down_plane, grad_down_time, grad_last = lax.psum(
-        (grad_first_plane, grad_first_time, grad_down_plane, grad_down_time, grad_last),
-        ("clip", "seq"),
-    )
-    return (
-        output[None],
-        grad_first_plane.astype(jnp.bfloat16),
-        grad_first_time.astype(jnp.bfloat16),
-        grad_down_plane.astype(jnp.bfloat16),
-        grad_down_time.astype(jnp.bfloat16),
-        grad_last.astype(jnp.bfloat16),
-    )
+    sums = sum_everywhere(
+        (grad_first_plane, grad_first_time, grad_down_plane, grad_down_time, grad_last)
+    )
+    return (output[None],) + sums
 
 
 def solution(mesh):

time: 290 us -> 205 us (0.71)
  blocking collectives: 184 us -> 59 us
  waiting for transfers between devices: 7.43 us -> 22.1 us
  starting transfers between devices: 42 us -> 56.1 us
  local copies, waits for them, and re-layouts: 16 us -> 23.8 us
    psum x1 -> x0, blocking collectives: 184 us -> none  [local(): lax.psum((grad_first_plane, grad_first_time, grad_down_plane, grad_down_t...]
    all_to_all x0 -> x3, blocking collectives: none -> 59 us  [the longest x2 38.3 us: exchange_depth(): lax.all_to_all(blocks, 'seq', split_axis=0, concat_axis=0, axis_index_gro...]
    all_to_all x0 -> x1, waiting for transfers between devices: none -> 11 us  [exchange_clip(): lax.all_to_all(blocks, 'clip', split_axis=0, concat_axis=0, tiled=True)]
    ppermute x0 -> x2, starting transfers between devices: none -> 9.4 us  [swap_cores(): return lax.ppermute(block, 'seq', [(i, i ^ 1) for i in range(count)])]
    all_to_all x0 -> x1, starting transfers between devices: none -> 4.23 us  [exchange_clip(): lax.all_to_all(blocks, 'clip', split_axis=0, concat_axis=0, tiled=True)]
    ppermute x0 -> x2, waiting for transfers between devices: none -> 3.15 us  [swap_cores(): return lax.ppermute(block, 'seq', [(i, i ^ 1) for i in range(count)])]
    reshape x0 -> x6, local copies, waits for them, and re-layouts: none -> 2.94 us  [the longest x3 2.76 us: sum_everywhere(): result.append(whole[start:start + rows].reshape(grad.shape))]
  transfers between devices with their start and end apart: 6 -> 9, of which waited for: 3 -> 6; matrix products, arithmetic and copies ran while one was open for 10% -> 17% of each run, Pallas kernels for 0% -> 0%
where the time goes in v1:
time: 205 us; the launch traced here: 204 us
  blocking collectives  59 us (29%)
  starting transfers between devices  56.1 us (27%)
  matrix products  32.8 us (16%)
  local copies, waits for them, and re-layouts  23.8 us (12%)
  waiting for transfers between devices  22.1 us (11%)
  other arithmetic  7.73 us (4%)
  between operations  2.35 us (1%)
    all_to_all x2, blocking collectives, exchange_depth(): lax.all_to_all(blocks, 'seq', split_axis=0, concat_axis=0, axis_index_gro...  38.3 us
    all_to_all x1, blocking collectives, exchange_clip(): lax.all_to_all(blocks, 'clip', split_axis=0, concat_axis=0, tiled=True)  20.8 us
    all_to_all x1, starting transfers between devices, local(): lax.all_to_all(grad_rows, 'seq', split_axis=0, concat_axis=1, tiled=True)  16.8 us
    all_to_all x1, starting transfers between devices, local(): lax.all_to_all(lowered, 'seq', split_axis=1, concat_axis=0, tiled=True)  14.3 us
    ppermute x4, starting transfers between devices, from_behind(): return lax.ppermute(block, axis, route)  11.4 us
    all_to_all x1, waiting for transfers between devices, exchange_clip(): lax.all_to_all(blocks, 'clip', split_axis=0, concat_axis=0, tiled=True)  11 us
    dot_general x18, matrix products, plane_conv_grad(): jnp.dot(window.reshape(-1, num_chans).T, flat_cotan, preferred_element_ty...  9.6 us
    ppermute x2, starting transfers between devices, swap_cores(): return lax.ppermute(block, 'seq', [(i, i ^ 1) for i in range(count)])  9.4 us
  transfers between devices with their start and end apart: 9, of which 6 were waited for; matrix products, arithmetic and copies ran while one was open for 17% of the time, Pallas kernels for 0%

profile of v1, /device:TPU:1, one launch (start us, length us, event | category | flops | bytes accessed | tf_op | source)
XLA Modules:
  0.0 203.9 jit_solution(15522905456718875701)
XLA Ops:
  2.5 1.1 fusion.25
  3.6 1.1 convolution_add_fusion.25
  4.7 1.1 convolution_add_fusion.24
  5.9 1.5 fusion.20
  7.4 16.8 %all-to-all-start.1 = ((bf16[32,1,4,256]{3,2,1,0:T(4,128)(2,1)}), bf16[32,1,4,256]{3,2,1,0:T(4,128)(2,1)S(1)}, u32[]{:S(2)}, u32[]{:S(2)}) async-start(bf16[32,1,4,256]{3,2,1,0:T(4,128)(2,1)} %fusion.20), calls=%async_computation.1 | async-start | bytes 131072 | tf_op jit(solution)/shard_map/all_to_all | solution.py:225
  29.4 3.5 %collective-permute-start = (bf16[2,64,8,128]{3,1,2,0:T(8,128)(2,1)S(1)}, bf16[2,64,8,128]{3,1,2,0:T(8,128)(2,1)S(1)}, u32[]{:S(2)}, u32[]{:S(2)}) collective-permute-start(bf16[2,64,8,128]{3,1,2,0:T(8,128)(2,1)S(1)} %multiply_convert_fusion.2), channel_id=1, source_target_pairs={{0,1},{1,2},{2,3},{3,4},{4,5},{5,6},{6,7},{7,8},{8,9},{9,10},{10,1... | collective-permute-start | bytes 786440 | tf_op jit(solution)/shard_map/ppermute | solution.py:10
  33.2 4.0 %all-to-all-done.1 = bf16[32,1,4,256]{3,2,1,0:T(4,128)(2,1)S(1)} async-done(((bf16[32,1,4,256]{3,2,1,0:T(4,128)(2,1)}), bf16[32,1,4,256]{3,2,1,0:T(4,128)(2,1)S(1)}, u32[]{:S(2)}, u32[]{:S(2)}) %all-to-all-start.1) | async-done | bytes 65568 | tf_op jit(solution)/shard_map/all_to_all | solution.py:225
  43.7 3.7 %collective-permute-start.1 = (bf16[2,32,4,256]{3,1,2,0:T(8,128)(2,1)S(1)}, bf16[2,32,4,256]{3,1,2,0:T(8,128)(2,1)S(1)}, u32[]{:S(2)}, u32[]{:S(2)}) collective-permute-start(bf16[2,32,4,256]{3,1,2,0:T(8,128)(2,1)S(1)} %copy.170), channel_id=1, source_target_pairs={{0,1},{1,2},{2,3},{3,4},{4,5},{5,6},{6,7},{7,8},{8,9},{9,10},{10,1... | collective-permute-start | bytes 393224 | tf_op jit(solution)/shard_map/ppermute | solution.py:10
  47.6 1.7 collective-permute-done.1
  51.3 14.3 %all-to-all-start = ((bf16[1,32,4,256]{3,2,0,1:T(4,128)(2,1)}), bf16[1,32,4,256]{3,2,0,1:T(4,128)(2,1)S(1)}, u32[]{:S(2)}, u32[]{:S(2)}) async-start(bf16[1,32,4,256]{3,2,0,1:T(4,128)(2,1)} %copy.175), calls=%async_computation | async-start | bytes 131072 | tf_op jit(solution)/shard_map/all_to_all | solution.py:223
  65.6 2.1 %collective-permute-start.2 = (bf16[1,32,4,256]{3,1,2,0:T(8,128)(2,1)}, bf16[1,32,4,256]{3,1,2,0:T(8,128)(2,1)}, u32[]{:S(2)}, u32[]{:S(2)}) collective-permute-start(bf16[1,32,4,256]{3,1,2,0:T(8,128)(2,1)} %get-tuple-element.45), channel_id=1, source_target_pairs={{1,0},{2,1},{3,2},{4,3},{5,4},{6,5},{7,6},{8,7},{9,8},{10,9},{11,1... | collective-permute-start | bytes 196616 | tf_op jit(solution)/shard_map/ppermute | solution.py:10
  69.5 2.2 %collective-permute-done.2 = bf16[1,32,4,256]{3,1,2,0:T(8,128)(2,1)} collective-permute-done((bf16[1,32,4,256]{3,1,2,0:T(8,128)(2,1)}, bf16[1,32,4,256]{3,1,2,0:T(8,128)(2,1)}, u32[]{:S(2)}, u32[]{:S(2)}) %collective-permute-start.2) | collective-permute-done | bytes 65568 | tf_op jit(solution)/shard_map/ppermute | solution.py:10
  72.7 1.1 convolution_add_fusion.23
  74.9 1.7 convolution_bitcast_fusion.6
  76.6 1.7 convolution_bitcast_fusion.7
  78.3 1.7 convolution_bitcast_fusion.8
  89.2 2.1 %collective-permute-start.3 = (bf16[2,64,8,128]{3,2,1,0:T(8,128)(2,1)}, bf16[2,64,8,128]{3,2,1,0:T(8,128)(2,1)}, u32[]{:S(2)}, u32[]{:S(2)}) collective-permute-start(bf16[2,64,8,128]{3,2,1,0:T(8,128)(2,1)} %bitcast.69), channel_id=1, source_target_pairs={{1,0},{2,1},{3,2},{4,3},{5,4},{6,5},{7,6},{8,7},{9,8},{10,9},{11,1... | collective-permute-start | bytes 786440 | tf_op jit(solution)/shard_map/ppermute | solution.py:10
  91.3 1.3 convolution_bitcast_fusion.17
  92.9 1.2 convolution_bitcast_fusion.16
  94.1 1.2 convolution_bitcast_fusion.18
  96.1 2.0 fusion.98
  101.9 1.4 fusion.2
  106.6 1.8 copy-done
  108.5 1.9 collective-permute-start.4
  110.4 2.4 %collective-permute-done.4 = bf16[3456,128]{1,0:T(8,128)(2,1)S(1)} collective-permute-done((bf16[3456,128]{1,0:T(8,128)(2,1)S(1)}, bf16[3456,128]{1,0:T(8,128)(2,1)S(1)}, u32[]{:S(2)}, u32[]{:S(2)}) %collective-permute-start.4) | collective-permute-done | bytes 884768 | tf_op jit(solution)/shard_map/ppermute | solution.py:158
  112.8 1.6 fusion
  114.5 20.8 %all_to_all.41 = bf16[16,216,128]{2,1,0:T(8,128)(2,1)S(1)} all-to-all(bf16[16,216,128]{2,1,0:T(8,128)(2,1)S(1)} %bitcast.481), channel_id=1, replica_groups=mesh['clip'=16,'seq'=32] {'clip'}, dimensions={0} | all-to-all | bytes 1769472 | tf_op jit(solution)/shard_map/all_to_all | solution.py:162
  135.4 23.9 %all_to_all.42 = bf16[16,16,128]{2,1,0:T(8,128)(2,1)S(1)} all-to-all(bf16[16,16,128]{2,1,0:T(8,128)(2,1)S(1)} %bitcast.523), channel_id=1, replica_groups={{0,2,4,6,8,10,12,14,16,18,20,22,24,26,28,30},{1,3,5,7,9,11,13,15,17,19,..., dimensions={0} | all-to-all | bytes 131072 | tf_op jit(solution)/shard_map/all_to_all | solution.py:168
  159.3 14.4 %all_to_all.43 = bf16[16,16,128]{2,1,0:T(8,128)(2,1)S(1)} all-to-all(bf16[16,16,128]{2,1,0:T(8,128)(2,1)S(1)} %broadcast_in_dim.4), channel_id=1, replica_groups={{0,2,4,6,8,10,12,14,16,18,20,22,24,26,28,30},{1,3,5,7,9,11,13,15,17,19,..., dimensions={0} | all-to-all | bytes 131072 | tf_op jit(solution)/shard_map/all_to_all | solution.py:168
  174.8 4.2 %all-to-all-start.5 = ((bf16[16,216,128]{2,1,0:T(8,128)(2,1)}), bf16[16,216,128]{2,1,0:T(8,128)(2,1)S(1)}, u32[]{:S(2)}, u32[]{:S(2)}) async-start(bf16[16,216,128]{2,1,0:T(8,128)(2,1)} %broadcast_in_dim.5), calls=%async_computation.5 | async-start | bytes 1769472 | tf_op jit(solution)/shard_map/all_to_all | solution.py:162
  179.0 11.0 %all-to-all-done.5 = bf16[16,216,128]{2,1,0:T(8,128)(2,1)S(1)} async-done(((bf16[16,216,128]{2,1,0:T(8,128)(2,1)}), bf16[16,216,128]{2,1,0:T(8,128)(2,1)S(1)}, u32[]{:S(2)}, u32[]{:S(2)}) %all-to-all-start.5) | async-done | bytes 884768 | tf_op jit(solution)/shard_map/all_to_all | solution.py:162
  190.0 7.5 %collective-permute-start.5 = (bf16[3456,128]{1,0:T(8,128)(2,1)S(1)}, bf16[3456,128]{1,0:T(8,128)(2,1)S(1)}, u32[]{:S(2)}, u32[]{:S(2)}) collective-permute-start(bf16[3456,128]{1,0:T(8,128)(2,1)S(1)} %bitcast.480), channel_id=1, source_target_pairs={{0,1},{1,0},{2,3},{3,2},{4,5},{5,4},{6,7},{7,6},{8,9},{9,8},{10,11... | collective-permute-start | bytes 2654216 | tf_op jit(solution)/shard_map/ppermute | solution.py:158
  (261 shorter events, 43.5 us)
Async XLA Ops:
  7.4 29.8 %all-to-all-start.1 = ((bf16[32,1,4,256]{3,2,1,0:T(4,128)(2,1)}), bf16[32,1,4,256]{3,2,1,0:T(4,128)(2,1)S(1)}, u32[]{:S(2)}, u32[]{:S(2)}) async-start(bf16[32,1,4,256]{3,2,1,0:T(4,128)(2,1)} %fusion.20), calls=%async_computation.1 | async-start | bytes 131072 | tf_op jit(solution)/shard_map/all_to_all | solution.py:225
  24.1 3.0 %copy-start.37 = (bf16[3,3,128,128]{3,2,1,0:T(8,128)(2,1)S(1)}, bf16[3,3,128,128]{3,2,1,0:T(8,128)(2,1)}, u32[]{:S(2)}) copy-start(bf16[3,3,128,128]{3,2,1,0:T(8,128)(2,1)} %param.8) | copy-start | bytes 884740
  28.2 4.7 %copy-start.34 = (bf16[3,128,128]{2,1,0:T(8,128)(2,1)S(1)}, bf16[3,128,128]{2,1,0:T(8,128)(2,1)}, u32[]{:S(2)}) copy-start(bf16[3,128,128]{2,1,0:T(8,128)(2,1)} %param.9) | copy-start | bytes 294916
  29.2 3.7 %copy-start.4 = (f32[1024,128]{1,0:T(8,128)}, f32[1024,128]{1,0:T(8,128)S(1)}, u32[]{:S(2)}) copy-start(f32[1024,128]{1,0:T(8,128)S(1)} %get-tuple-element.54) | copy-start | bytes 1572868
  29.2 4.0 %copy-start.35 = (bf16[1024,128]{1,0:T(8,128)(2,1)}, bf16[1024,128]{1,0:T(8,128)(2,1)S(1)}, u32[]{:S(2)}) copy-start(bf16[1024,128]{1,0:T(8,128)(2,1)S(1)} %get-tuple-element.53) | copy-start | bytes 786436
  29.4 8.6 %collective-permute-start = (bf16[2,64,8,128]{3,1,2,0:T(8,128)(2,1)S(1)}, bf16[2,64,8,128]{3,1,2,0:T(8,128)(2,1)S(1)}, u32[]{:S(2)}, u32[]{:S(2)}) collective-permute-start(bf16[2,64,8,128]{3,1,2,0:T(8,128)(2,1)S(1)} %multiply_convert_fusion.2), channel_id=1, source_target_pairs={{0,1},{1,2},{2,3},{3,4},{4,5},{5,6},{6,7},{7,8},{8,9},{9,10},{10,1... | collective-permute-start | bytes 786440 | tf_op jit(solution)/shard_map/ppermute | solution.py:10
  38.2 3.7 %copy-start.3 = (bf16[3,3,128,256]{3,2,1,0:T(8,128)(2,1)S(1)}, bf16[3,3,128,256]{3,2,1,0:T(8,128)(2,1)}, u32[]{:S(2)}) copy-start(bf16[3,3,128,256]{3,2,1,0:T(8,128)(2,1)} %param.10) | copy-start | bytes 1769476
  40.4 3.0 %copy-start.15 = (bf16[2,32,4,128]{3,1,2,0:T(8,128)(2,1)}, bf16[2,32,4,128]{3,1,2,0:T(8,128)(2,1)S(1)}, u32[]{:S(2)}) copy-start(bf16[2,32,4,128]{3,1,2,0:T(8,128)(2,1)S(1)} %slice.269) | copy-start | bytes 196612
  41.7 5.7 %copy-start.7 = (bf16[3,256,256]{2,1,0:T(8,128)(2,1)S(1)}, bf16[3,256,256]{2,1,0:T(8,128)(2,1)}, u32[]{:S(2)}) copy-start(bf16[3,256,256]{2,1,0:T(8,128)(2,1)} %param.11) | copy-start | bytes 1179652
  42.7 25.1 %copy-start.38 = (f32[128,256]{1,0:T(8,128)S(1)}, f32[128,256]{1,0:T(8,128)}, u32[]{:S(2)}) copy-start(f32[128,256]{1,0:T(8,128)} %reshape.579) | copy-start | bytes 393220
  43.7 5.6 %collective-permute-start.1 = (bf16[2,32,4,256]{3,1,2,0:T(8,128)(2,1)S(1)}, bf16[2,32,4,256]{3,1,2,0:T(8,128)(2,1)S(1)}, u32[]{:S(2)}, u32[]{:S(2)}) collective-permute-start(bf16[2,32,4,256]{3,1,2,0:T(8,128)(2,1)S(1)} %copy.170), channel_id=1, source_target_pairs={{0,1},{1,2},{2,3},{3,4},{4,5},{5,6},{6,7},{7,8},{8,9},{9,10},{10,1... | collective-permute-start | bytes 393224 | tf_op jit(solution)/shard_map/ppermute | solution.py:10
  51.3 46.8 %all-to-all-start = ((bf16[1,32,4,256]{3,2,0,1:T(4,128)(2,1)}), bf16[1,32,4,256]{3,2,0,1:T(4,128)(2,1)S(1)}, u32[]{:S(2)}, u32[]{:S(2)}) async-start(bf16[1,32,4,256]{3,2,0,1:T(4,128)(2,1)} %copy.175), calls=%async_computation | async-start | bytes 131072 | tf_op jit(solution)/shard_map/all_to_all | solution.py:223
  65.6 6.1 %collective-permute-start.2 = (bf16[1,32,4,256]{3,1,2,0:T(8,128)(2,1)}, bf16[1,32,4,256]{3,1,2,0:T(8,128)(2,1)}, u32[]{:S(2)}, u32[]{:S(2)}) collective-permute-start(bf16[1,32,4,256]{3,1,2,0:T(8,128)(2,1)} %get-tuple-element.45), channel_id=1, source_target_pairs={{1,0},{2,1},{3,2},{4,3},{5,4},{6,5},{7,6},{8,7},{9,8},{10,9},{11,1... | collective-permute-start | bytes 196616 | tf_op jit(solution)/shard_map/ppermute | solution.py:10
  68.9 12.1 %copy-start.18 = (bf16[2,32,4,128]{3,1,2,0:T(8,128)(2,1)S(1)}, bf16[2,32,4,128]{3,1,2,0:T(8,128)(2,1)}, u32[]{:S(2)}) copy-start(bf16[2,32,4,128]{3,1,2,0:T(8,128)(2,1)} %copy-done.17) | copy-start | bytes 196612
  69.4 12.1 %copy-start.20 = (bf16[2,32,4,128]{3,1,2,0:T(8,128)(2,1)S(1)}, bf16[2,32,4,128]{3,1,2,0:T(8,128)(2,1)}, u32[]{:S(2)}) copy-start(bf16[2,32,4,128]{3,1,2,0:T(8,128)(2,1)} %copy-done.19) | copy-start | bytes 196612
  69.4 12.3 %copy-start.16 = (bf16[2,32,4,128]{3,1,2,0:T(8,128)(2,1)S(1)}, bf16[2,32,4,128]{3,1,2,0:T(8,128)(2,1)}, u32[]{:S(2)}) copy-start(bf16[2,32,4,128]{3,1,2,0:T(8,128)(2,1)} %copy-done.15) | copy-start | bytes 196612
  84.1 4.1 %copy-start.36 = (bf16[2,32,4,1,128]{4,1,2,0,3:T(8,128)(2,1)S(1)}, bf16[2,32,4,1,128]{4,1,2,0,3:T(8,128)(2,1)}, u32[]{:S(2)}) copy-start(bf16[2,32,4,1,128]{4,1,2,0,3:T(8,128)(2,1)} %copy.185) | copy-start | bytes 196612
  86.7 6.0 %copy-start.31 = (f32[1,128,256]{2,1,0:T(8,128)S(1)}, f32[1,128,256]{2,1,0:T(8,128)}, u32[]{:S(2)}) copy-start(f32[1,128,256]{2,1,0:T(8,128)} %convolution_bitcast_fusion.6) | copy-start | bytes 393220
  86.7 6.0 %copy-start.32 = (f32[1,128,256]{2,1,0:T(8,128)S(1)}, f32[1,128,256]{2,1,0:T(8,128)}, u32[]{:S(2)}) copy-start(f32[1,128,256]{2,1,0:T(8,128)} %convolution_bitcast_fusion.7) | copy-start | bytes 393220
  86.7 6.0 %copy-start.33 = (f32[1,128,256]{2,1,0:T(8,128)S(1)}, f32[1,128,256]{2,1,0:T(8,128)}, u32[]{:S(2)}) copy-start(f32[1,128,256]{2,1,0:T(8,128)} %convolution_bitcast_fusion.8) | copy-start | bytes 393220
  89.2 10.6 %collective-permute-start.3 = (bf16[2,64,8,128]{3,2,1,0:T(8,128)(2,1)}, bf16[2,64,8,128]{3,2,1,0:T(8,128)(2,1)}, u32[]{:S(2)}, u32[]{:S(2)}) collective-permute-start(bf16[2,64,8,128]{3,2,1,0:T(8,128)(2,1)} %bitcast.69), channel_id=1, source_target_pairs={{1,0},{2,1},{3,2},{4,3},{5,4},{6,5},{7,6},{8,7},{9,8},{10,9},{11,1... | collective-permute-start | bytes 786440 | tf_op jit(solution)/shard_map/ppermute | solution.py:10
  99.8 3.5 %copy-start.5 = (f32[1024,128]{1,0:T(8,128)S(1)}, f32[1024,128]{1,0:T(8,128)}, u32[]{:S(2)}) copy-start(f32[1024,128]{1,0:T(8,128)} %copy-done.4) | copy-start | bytes 1572868
  99.8 3.8 %copy-start.9 = (bf16[1,2,64,8,128]{4,2,3,1,0:T(8,128)(2,1)S(1)}, bf16[1,2,64,8,128]{4,2,3,1,0:T(8,128)(2,1)}, u32[]{:S(2)}) copy-start(bf16[1,2,64,8,128]{4,2,3,1,0:T(8,128)(2,1)} %copy-done.8) | copy-start | bytes 786436
  99.8 4.9 %copy-start.2 = (bf16[1,2,64,8,128]{4,3,2,1,0:T(8,128)(2,1)S(1)}, bf16[1,2,64,8,128]{4,3,2,1,0:T(8,128)(2,1)}, u32[]{:S(2)}) copy-start(bf16[1,2,64,8,128]{4,3,2,1,0:T(8,128)(2,1)} %param.7) | copy-start | bytes 786436
  108.5 4.3 %collective-permute-start.4 = (bf16[3456,128]{1,0:T(8,128)(2,1)S(1)}, bf16[3456,128]{1,0:T(8,128)(2,1)S(1)}, u32[]{:S(2)}, u32[]{:S(2)}) collective-permute-start(bf16[3456,128]{1,0:T(8,128)(2,1)S(1)} %fusion.5), channel_id=1, source_target_pairs={{0,1},{1,0},{2,3},{3,2},{4,5},{5,4},{6,7},{7,6},{8,9},{9,8},{10,11... | collective-permute-start | bytes 2654216 | tf_op jit(solution)/shard_map/ppermute | solution.py:158
  114.4 83.1 %copy-start.6 = (bf16[3,256,256]{2,1,0:T(8,128)(2,1)S(1)}, bf16[3,256,256]{2,1,0:T(8,128)(2,1)}, u32[]{:S(2)}) copy-start(bf16[3,256,256]{2,1,0:T(8,128)(2,1)} %param.12) | copy-start | bytes 1179652
  114.5 83.0 %copy-start.30 = (bf16[128,256]{1,0:T(8,128)(2,1)S(1)}, bf16[128,256]{1,0:T(8,128)(2,1)}, u32[]{:S(2)}) copy-start(bf16[128,256]{1,0:T(8,128)(2,1)} %copy-done.29) | copy-start | bytes 196612
  114.5 83.2 %copy-start.28 = (bf16[128,256]{1,0:T(8,128)(2,1)S(1)}, bf16[128,256]{1,0:T(8,128)(2,1)}, u32[]{:S(2)}) copy-start(bf16[128,256]{1,0:T(8,128)(2,1)} %copy-done.27) | copy-start | bytes 196612
  114.5 83.4 %copy-start.26 = (bf16[128,256]{1,0:T(8,128)(2,1)S(1)}, bf16[128,256]{1,0:T(8,128)(2,1)}, u32[]{:S(2)}) copy-start(bf16[128,256]{1,0:T(8,128)(2,1)} %copy-done.25) | copy-start | bytes 196612
  114.5 83.6 %copy-start.13 = (bf16[1,32,4,256]{3,2,0,1:T(4,128)(2,1)S(1)}, bf16[1,32,4,256]{3,2,0,1:T(4,128)(2,1)}, u32[]{:S(2)}) copy-start(bf16[1,32,4,256]{3,2,0,1:T(4,128)(2,1)} %copy-done.12) | copy-start | bytes 196612
  174.8 15.2 %all-to-all-start.5 = ((bf16[16,216,128]{2,1,0:T(8,128)(2,1)}), bf16[16,216,128]{2,1,0:T(8,128)(2,1)S(1)}, u32[]{:S(2)}, u32[]{:S(2)}) async-start(bf16[16,216,128]{2,1,0:T(8,128)(2,1)} %broadcast_in_dim.5), calls=%async_computation.5 | async-start | bytes 1769472 | tf_op jit(solution)/shard_map/all_to_all | solution.py:162
  190.0 9.5 %collective-permute-start.5 = (bf16[3456,128]{1,0:T(8,128)(2,1)S(1)}, bf16[3456,128]{1,0:T(8,128)(2,1)S(1)}, u32[]{:S(2)}, u32[]{:S(2)}) collective-permute-start(bf16[3456,128]{1,0:T(8,128)(2,1)S(1)} %bitcast.480), channel_id=1, source_target_pairs={{0,1},{1,0},{2,3},{3,2},{4,5},{5,4},{6,7},{7,6},{8,9},{9,8},{10,11... | collective-permute-start | bytes 2654216 | tf_op jit(solution)/shard_map/ppermute | solution.py:158
  (16 other events, 25.6 us)

commit v2 on v1

v2 whole, which is shorter than its diff:
```python
import functools

import jax
import jax.numpy as jnp
from jax import lax
from jax.experimental import pallas as pl
from jax.experimental.pallas import tpu as pltpu
from jax.sharding import PartitionSpec as P


F32 = jnp.float32
BF16 = jnp.bfloat16
COLS = 8
HALF = 32
CELLS = COLS * HALF
DOWN = CELLS // 2
CH = 128
WIDE = 256


def dot(left, right):
    return lax.dot_general(left, right, (((1,), (0,)), ((), ())), preferred_element_type=F32)


def dot_nt(left, right):
    return lax.dot_general(left, right, (((1,), (1,)), ((), ())), preferred_element_type=F32)


def dot_tn(left, right):
    return lax.dot_general(left, right, (((0,), (0,)), ((), ())), preferred_element_type=F32)


def call(body, outs, scratch, *args, smem=0, flops=0):
    spaces = [pltpu.SMEM] * smem + [pltpu.VMEM] * (len(args) - smem)
    return pl.pallas_call(
        body,
        out_shape=[jax.ShapeDtypeStruct(shape, kind) for shape, kind in outs],
        in_specs=[pl.BlockSpec(memory_space=space) for space in spaces],
        out_specs=[pl.BlockSpec(memory_space=pltpu.VMEM) for _ in outs],
        scratch_shapes=[pltpu.VMEM(shape, kind) for shape, kind in scratch],
        compiler_params=pltpu.CompilerParams(vmem_limit_bytes=40 * 1024 * 1024),
        cost_estimate=pl.CostEstimate(flops=flops, bytes_accessed=4000000, transcendentals=0),
    )(*args)


def row_before(planes):
    wide = planes.astype(F32)
    rolled = pltpu.roll(wide, 1, 1)
    at = lax.broadcasted_iota(jnp.int32, wide.shape, 1)
    return jnp.where(at == 0, 0.0, rolled).astype(BF16)


def row_after(planes):
    wide = planes.astype(F32)
    rolled = pltpu.roll(wide, HALF - 1, 1)
    at = lax.broadcasted_iota(jnp.int32, wide.shape, 1)
    return jnp.where(at == HALF - 1, 0.0, rolled).astype(BF16)


def fill_windows(windows, at, even, odd):
    by_row = (row_before(odd), even, odd, row_after(even))
    edge = jnp.zeros((HALF, CH), BF16)
    for row, planes in enumerate(by_row):
        flat = planes.reshape(CELLS, CH)
        for tap in range(3):
            lanes = pl.ds((tap * 4 + row) * CH, CH)
            if tap == 0:
                windows[pl.ds(at, HALF), lanes] = edge
                windows[pl.ds(at + HALF, CELLS - HALF), lanes] = flat[: CELLS - HALF]
            elif tap == 1:
                windows[pl.ds(at, CELLS), lanes] = flat
            else:
                windows[pl.ds(at, CELLS - HALF), lanes] = flat[HALF:]
                windows[pl.ds(at + CELLS - HALF, HALF), lanes] = edge


def silu_slope(preact):
    sigma = jax.nn.sigmoid(preact)
    return sigma * (1.0 + preact * (1.0 - sigma))


def first_body(
    prior, own, first_plane, first_time, down_plane,
    pre_out, hidden_out, cells_out, strided_out,
    windows, both,
):
    both[...] = jnp.zeros_like(both)
    for tap in range(3):
        for row in range(4):
            rows = pl.ds((tap * 4 + row) * CH, CH)
            if row < 3:
                both[rows, pl.ds(0, CH)] = first_plane[row, tap]
            if row > 0:
                both[rows, pl.ds(CH, CH)] = first_plane[row - 1, tap]
    for frame in range(4):
        source = prior if frame < 2 else own
        fill_windows(windows, frame * CELLS, source[frame % 2, 0], source[frame % 2, 1])
    for frame in range(4):
        pre = dot(windows[pl.ds(frame * CELLS, CELLS), :], both[...])
        hid = (pre * jax.nn.sigmoid(pre)).astype(BF16)
        for par in range(2):
            hidden_out[frame, par] = hid[:, par * CH : (par + 1) * CH]
            if frame >= 2:
                pre_out[frame - 2, par] = pre[:, par * CH : (par + 1) * CH]
    times = first_time[...].reshape(3 * CH, CH)
    for frame in range(2):
        mixed = []
        for par in range(2):
            taps = jnp.concatenate([hidden_out[frame + k, par] for k in range(3)], axis=1)
            here = own[frame, par].reshape(CELLS, CH).astype(F32) + dot(taps, times)
            mixed.append(here.astype(BF16).reshape(COLS, HALF, CH))
        by_row = (row_before(mixed[1]), mixed[0], mixed[1])
        for row in range(3):
            for tap in range(3):
                lanes = pl.ds((row * 3 + tap) * CH, CH)
                for col in range(COLS // 2):
                    rows = pl.ds(frame * DOWN + col * HALF, HALF)
                    where = 2 * col + tap - 1
                    if where < 0:
                        cells_out[rows, lanes] = jnp.zeros((HALF, CH), BF16)
                    else:
                        cells_out[rows, lanes] = by_row[row][where]
    kernel = down_plane[...].reshape(9 * CH, WIDE)
    strided_out[...] = dot(cells_out[...], kernel).astype(BF16).reshape(2, DOWN, WIDE)


def middle_body(
    prior, own, cotans, down_time, last_time,
    lowered_out, grad_pre_out, grad_down_time_out, grad_last_out,
    spread, turned,
):
    spread[...] = cotans[...].reshape(HALF * 24, CH).astype(F32)
    cot = []
    for ahead in range(3):
        parts = []
        for col in range(4):
            halves = [
                spread[pl.ds(ahead * 8 + col * 2 + half, HALF, stride=24), :] for half in range(2)
            ]
            parts.append(jnp.concatenate(halves, axis=1))
        cot.append(jnp.concatenate(parts, axis=0).astype(BF16))
    grad_lowered = cot[0].astype(F32)
    for k in range(3):
        grad_lowered = grad_lowered + dot_nt(cot[2 - k], last_time[k])
    grad_lowered = grad_lowered.astype(BF16)
    taps = (prior[0], prior[1], own[0])
    pre = dot(taps[0], down_time[0]) + dot(taps[1], down_time[1]) + dot(taps[2], down_time[2])
    lowered = (pre * jax.nn.sigmoid(pre)).astype(BF16)
    grad_pre = (grad_lowered.astype(F32) * silu_slope(pre)).astype(BF16)
    grad_pre_out[...] = grad_pre
    wide = lowered.astype(F32)
    for col in range(4):
        for half in range(2):
            turned[pl.ds(col * 2 + half, HALF, stride=8), :] = wide[
                col * HALF : (col + 1) * HALF, half * CH : (half + 1) * CH
            ]
    lowered_out[...] = turned[...].astype(BF16).reshape(HALF, 8, CH)
    for k in range(3):
        down = dot_tn(taps[k], grad_pre)
        last = dot_tn(lowered, cot[2 - k])
        for half in range(2):
            lanes = slice(half * CH, (half + 1) * CH)
            grad_down_time_out[half, pl.ds(k * WIDE, WIDE), :] = down[:, lanes]
            grad_last_out[half, pl.ds(k * WIDE, WIDE), :] = last[:, lanes]


BACK = (
    (0, 0, 0, 0, 1, 1),
    (0, 1, 0, 1, 1, 0),
    (0, 1, 0, 0, 1, 2),
    (1, 0, 1, 0, 0, 1),
    (1, 0, 0, 0, 2, 1),
    (1, 1, 1, 1, 0, 0),
    (1, 1, 1, 0, 0, 2),
    (1, 1, 0, 1, 2, 0),
    (1, 1, 0, 0, 2, 2),
)


def back_body(
    own, ahead, down_time, down_plane, cells, hidden,
    grad_mixed_out, grad_first_time_out, grad_down_plane_out,
    shifted, kernels,
):
    current, following = own[...], ahead[...]
    even = dot_nt(current, down_time[2]) + dot_nt(following, down_time[0])
    odd = dot_nt(following, down_time[1])
    strided = [even.astype(BF16), odd.astype(BF16)]
    kernels[...] = jnp.zeros_like(kernels)
    for row_par, col_par, row_off, col_off, row, tap in BACK:
        rows = pl.ds((row_par * 2 + col_par) * CH, CH)
        lanes = pl.ds((row_off * 2 + col_off) * WIDE, WIDE)
        kernels[rows, lanes] = down_plane[row, tap]
    for frame in range(2):
        planes = strided[frame].reshape(4, HALF, WIDE)
        for row_off, rows in ((0, planes), (1, row_after(planes))):
            flat = rows.reshape(DOWN, WIDE)
            here = pl.ds((row_off * 2) * WIDE, WIDE)
            after = pl.ds((row_off * 2 + 1) * WIDE, WIDE)
            shifted[pl.ds(frame * DOWN, DOWN), here] = flat
            shifted[pl.ds(frame * DOWN, DOWN - HALF), after] = flat[HALF:]
            shifted[pl.ds(frame * DOWN + DOWN - HALF, HALF), after] = jnp.zeros((HALF, WIDE), BF16)
    mixed = dot_nt(shifted[...], kernels[...]).astype(BF16)
    for frame in range(2):
        for par in range(2):
            for col_par in range(2):
                lanes = slice((par * 2 + col_par) * CH, (par * 2 + col_par + 1) * CH)
                for col in range(4):
                    rows = slice(frame * DOWN + col * HALF, frame * DOWN + (col + 1) * HALF)
                    grad_mixed_out[frame, par, 2 * col + col_par] = mixed[rows, lanes]
    both = jnp.concatenate(strided, axis=0)
    down = dot_tn(cells[...], both)
    for half in range(2):
        grad_down_plane_out[half] = down[:, half * CH : (half + 1) * CH]
    cotan = grad_mixed_out[...].reshape(4 * CELLS, CH)
    for k in range(3):
        taps = hidden[pl.ds(k, 2)].reshape(4 * CELLS, CH)
        grad_first_time_out[pl.ds(k * CH, CH), :] = dot_tn(taps, cotan)


def last_body(
    core, own, ahead, first_time, pre, source, grad_first_time, grad_down_plane, grad_down_time, grad_last,
    mine_out, other_out,
    windows, flat,
):
    frames = [own[0], own[1], ahead[0], ahead[1]]
    kernels = jnp.concatenate([first_time[k] for k in range(3)], axis=1)
    cotans = []
    for frame in range(2):
        fill_windows(windows, frame * CELLS, source[frame, 0], source[frame, 1])
        parts = []
        for par in range(2):
            taps = [frames[frame + 2 - k][par].reshape(CELLS, CH) for k in range(3)]
            grad_hidden = dot_nt(jnp.concatenate(taps, axis=1), kernels)
            parts.append((grad_hidden * silu_slope(pre[frame, par])).astype(BF16))
        cotans.append(jnp.concatenate(parts, axis=1))
    product = dot_tn(windows[...], jnp.concatenate(cotans, axis=0))
    for row in range(3):
        for tap in range(3):
            at = (tap * 4 + row) * CH
            flat[pl.ds((row * 3 + tap) * CH, CH), :] = (
                product[at : at + CH, :CH] + product[at + CH : at + 2 * CH, CH:]
            )
    start = 9 * CH
    for grad in (grad_first_time, grad_down_plane, grad_down_time, grad_last):
        rows = grad.size // CH
        flat[pl.ds(start, rows), :] = grad[...].reshape(rows, CH)
        start += rows
    half = start // 2
    here = core[0]
    mine_out[...] = flat[pl.ds(pl.multiple_of(here * half, 16), half), :]
    other_out[...] = flat[pl.ds(pl.multiple_of((1 - here) * half, 16), half), :].astype(BF16)


def output_body(lowered, last_time, output, spread, padded):
    spread[...] = lowered[...].reshape(HALF * 8, CH).astype(F32)
    padded[pl.ds(0, 8), :] = jnp.zeros((8, WIDE), F32)
    for half in range(2):
        padded[pl.ds(8, DOWN), pl.ds(half * CH, CH)] = spread[pl.ds(half, DOWN, stride=2), :]
    total = padded[pl.ds(8, DOWN), :]
    for k in range(3):
        taps = padded[pl.ds(4 * k, DOWN), :].astype(BF16)
        total = total + dot(taps, last_time[k])
    output[...] = total.astype(BF16)


def from_behind(block, distance):
    devices = range(lax.axis_size("seq"))
    route = [(i - distance, i) for i in devices if i - distance in devices]
    return lax.ppermute(block, "seq", route)


def swap_cores(block):
    count = lax.axis_size("seq")
    return lax.ppermute(block, "seq", [(i, i ^ 1) for i in range(count)])


def exchange_clip(blocks):
    return lax.all_to_all(blocks, "clip", split_axis=0, concat_axis=0, tiled=True)


def exchange_seq(blocks):
    return lax.all_to_all(blocks, "seq", split_axis=0, concat_axis=0, tiled=True)


def exchange_depth(blocks):
    count = lax.axis_size("seq")
    groups = [list(range(core, count, 2)) for core in range(2)]
    return lax.all_to_all(
        blocks, "seq", split_axis=0, concat_axis=0, axis_index_groups=groups, tiled=True
    )


def sum_blocks(blocks):
    return jnp.sum(blocks.astype(F32), axis=0)


def sum_everywhere(mine, other):
    clips = lax.axis_size("clip")
    chips = lax.axis_size("seq") // 2
    core = lax.axis_index("seq") % 2
    other = swap_cores(other)
    half = (mine + other.astype(F32)).astype(BF16)
    part = sum_blocks(exchange_clip(half.reshape(clips, -1, CH)))
    part_rows = part.shape[0]
    chunk = 16 * (-(-part_rows // (16 * chips)))
    part = jnp.pad(part, ((0, chunk * chips - part_rows), (0, 0))).astype(BF16)
    piece = sum_blocks(exchange_depth(part.reshape(chips, chunk, CH))).astype(BF16)
    part = exchange_depth(jnp.broadcast_to(piece[None], (chips, chunk, CH)))
    part = part.reshape(-1, CH)[:part_rows]
    half = exchange_clip(jnp.broadcast_to(part[None], (clips, part_rows, CH)))
    half = half.reshape(-1, CH)
    other = swap_cores(half)
    first = jnp.where(core == 0, half, other)
    second = jnp.where(core == 0, other, half)
    return jnp.concatenate([first, second], axis=0)


def local(clip_in, first_plane, first_time, down_plane, down_time, last_time, cotan_out):
    source = clip_in[0].reshape(2, HALF, 2, COLS, CH).transpose(0, 2, 3, 1, 4)
    prior = from_behind(source, 1)
    rows = cotan_out[0].reshape(HALF, 8, CH)
    rows_ahead = jnp.pad(rows, ((0, 2), (0, 0), (0, 0)))
    cotans = jnp.concatenate([rows, rows_ahead[1 : HALF + 1], rows_ahead[2:]], axis=1)
    cotans = exchange_seq(cotans)
    pre_first, hidden, cells, strided = call(
        first_body,
        [
            ((2, 2, CELLS, CH), F32),
            ((4, 2, CELLS, CH), BF16),
            ((2 * DOWN, 9 * CH), BF16),
            ((2, DOWN, WIDE), BF16),
        ],
        [((4 * CELLS, 12 * CH), BF16), ((12 * CH, WIDE), BF16)],
        prior, source, first_plane, first_time, down_plane,
        flops=2000000000,
    )
    strided_prior = from_behind(strided, 1)
    lowered, grad_pre, grad_down_time, grad_last = call(
        middle_body,
        [
            ((HALF, 8, CH), BF16),
            ((DOWN, WIDE), BF16),
            ((2, 3 * WIDE, CH), F32),
            ((2, 3 * WIDE, CH), F32),
        ],
        [((HALF * 24, CH), F32), ((HALF * 8, CH), F32)],
        strided_prior, strided, cotans, down_time, last_time,
        flops=200000000,
    )
    grad_pre_next = from_behind(grad_pre, -1)
    grad_mixed, grad_first_time, grad_down_plane = call(
        back_body,
        [
            ((2, 2, COLS, HALF, CH), BF16),
            ((3 * CH, CH), F32),
            ((2, 9 * CH, CH), F32),
        ],
        [((2 * DOWN, 4 * WIDE), BF16), ((4 * CH, 4 * WIDE), BF16)],
        grad_pre, grad_pre_next, down_time, down_plane, cells, hidden,
        flops=600000000,
    )
    grad_mixed_next = from_behind(grad_mixed, -1)
    core = (lax.axis_index("seq") % 2).astype(jnp.int32).reshape(1)
    num_rows = (9 + 3 + 18 + 12 + 12) * CH
    mine, other = call(
        last_body,
        [((num_rows // 2, CH), F32), ((num_rows // 2, CH), BF16)],
        [((2 * CELLS, 12 * CH), BF16), ((num_rows, CH), F32)],
        core, grad_mixed, grad_mixed_next, first_time, pre_first, source,
        grad_first_time, grad_down_plane, grad_down_time, grad_last,
        smem=1,
        flops=800000000,
    )
    whole = sum_everywhere(mine, other)
    lowered_rows = exchange_seq(lowered)
    (output,) = call(
        output_body,
        [((DOWN, WIDE), BF16)],
        [((HALF * 8, CH), F32), ((DOWN + 8, WIDE), F32)],
        lowered_rows, last_time,
        flops=60000000,
    )

    result = [output.reshape(1, HALF, 1, 4, WIDE)]
    start = 0
    for shape in ((3, 3, CH, CH), (3, CH, CH), (3, 3, CH, WIDE), (3, WIDE, WIDE), (3, WIDE, WIDE)):
        rows = functools.reduce(lambda a, b: a * b, shape) // CH
        block = whole[start : start + rows]
        if shape[-1] == WIDE:
            block = jnp.concatenate([block[: rows // 2], block[rows // 2 :]], axis=1)
        result.append(block.reshape(shape))
        start += rows
    return tuple(result)


def solution(mesh):
    placed = (
        P("clip", "seq", None, None, None),
        P(),
        P(),
        P(),
        P(),
        P(),
        P("clip", None, "seq", None, None),
    )
    return jax.shard_map(
        local,
        mesh=mesh,
        in_specs=placed,
        out_specs=(P("clip", None, "seq", None, None), P(), P(), P(), P(), P()),
        check_vma=False,
    )
```

time: 205 us -> 174 us (0.85)
  matrix products: 32.8 us -> 0 us
  blocking collectives: 59 us -> 73.9 us
  starting transfers between devices: 56.1 us -> 41.5 us
  waiting for transfers between devices: 22.1 us -> 35.8 us
  local copies, waits for them, and re-layouts: 23.8 us -> 11.5 us
  Pallas kernels: 0 us -> 7.11 us
  other arithmetic: 7.73 us -> 3.1 us
    dot_general x72 -> x0, matrix products: 32.8 us -> none  [the longest x18 9.6 us: plane_conv_grad(): jnp.dot(window.reshape(-1, num_chans).T, flat_cotan, preferred_element_ty...]
    ppermute x4, waiting for transfers between devices: 3.98 us -> 20.4 us  [from_behind(): return lax.ppermute(block, 'seq', route)]
    all_to_all x3 -> x2, starting transfers between devices: 35.3 us -> 20.4 us  [exchange_seq(): lax.all_to_all(blocks, 'seq', split_axis=0, concat_axis=0, tiled=True)]
    all_to_all x1 -> x2, blocking collectives: 20.8 us -> 35.2 us  [exchange_clip(): lax.all_to_all(blocks, 'clip', split_axis=0, concat_axis=0, tiled=True)]
    slice x42 -> x5, local copies, waits for them, and re-layouts: 9.17 us -> 1.47 us  [the longest x2 0.8 us: local(): block = jnp.concatenate([block[:rows // 2], block[rows // 2:]], axis=1)]
    pallas_call x0 -> x5, Pallas kernels: none -> 7.11 us  [call(): pl.pallas_call(body, out_shape=[jax.ShapeDtypeStruct(shape, kind) for sha...]
    convert_element_type x11 -> x1, other arithmetic: 4.52 us -> 0.23 us  [sum_everywhere(): half = (mine + other.astype(F32)).astype(BF16)]
    unnamed x83 -> x32, local copies, waits for them, and re-layouts: 3.97 us -> 8.22 us
  transfers between devices with their start and end apart: 9 -> 8, of which waited for: 6 -> 6; matrix products, arithmetic and copies ran while one was open for 17% -> 0% of each run, Pallas kernels for 0% -> 1%
where the time goes in v2:
time: 174 us
  blocking collectives  73.9 us (42%)
  starting transfers between devices  41.5 us (24%)
  waiting for transfers between devices  35.8 us (21%)
  local copies, waits for them, and re-layouts  11.5 us (7%)
  Pallas kernels  7.11 us (4%)
  other arithmetic  3.1 us (2%)
    all_to_all x2, blocking collectives, exchange_depth(): lax.all_to_all(blocks, 'seq', split_axis=0, concat_axis=0, axis_index_gro...  38.7 us
    all_to_all x2, blocking collectives, exchange_clip(): lax.all_to_all(blocks, 'clip', split_axis=0, concat_axis=0, tiled=True)  35.2 us
    ppermute x4, waiting for transfers between devices, from_behind(): return lax.ppermute(block, 'seq', route)  20.4 us
    all_to_all x2, starting transfers between devices, exchange_seq(): lax.all_to_all(blocks, 'seq', split_axis=0, concat_axis=0, tiled=True)  20.4 us
    all_to_all x2, waiting for transfers between devices, exchange_seq(): lax.all_to_all(blocks, 'seq', split_axis=0, concat_axis=0, tiled=True)  12.9 us
    ppermute x4, starting transfers between devices, from_behind(): return lax.ppermute(block, 'seq', route)  11.9 us
    ppermute x2, starting transfers between devices, swap_cores(): return lax.ppermute(block, 'seq', [(i, i ^ 1) for i in range(count)])  9.21 us
    unnamed x32, local copies, waits for them, and re-layouts  8.22 us
  transfers between devices with their start and end apart: 8, of which 6 were waited for; matrix products, arithmetic and copies ran while one was open for 0% of the time, Pallas kernels for 1%

profile of v2, /device:TPU:1, one launch (start us, length us, event | category | flops | bytes accessed | tf_op | source)
XLA Modules:
  0.0 173.7 jit_solution(1254415839953566992)
XLA Ops:
  0.7 0.9 reshape_squeeze.7
  2.3 16.7 %all-to-all-start = ((bf16[32,24,128]{2,1,0:T(8,128)(2,1)}), bf16[32,24,128]{2,1,0:T(8,128)(2,1)S(1)}, u32[]{:S(2)}, u32[]{:S(2)}) async-start(bf16[32,24,128]{2,1,0:T(8,128)(2,1)} %pad_maximum_fusion.3), calls=%async_computation | async-start | bytes 393216 | tf_op jit(solution)/shard_map/all_to_all | solution.py:283
  19.2 3.7 %collective-permute-start = (bf16[2,2,8,32,128]{4,3,2,1,0:T(8,128)(2,1)S(1)}, bf16[2,2,8,32,128]{4,3,2,1,0:T(8,128)(2,1)S(1)}, u32[]{:S(2)}, u32[]{:S(2)}) collective-permute-start(bf16[2,2,8,32,128]{4,3,2,1,0:T(8,128)(2,1)S(1)} %bitcast.17), channel_id=1, source_target_pairs={{0,1},{1,2},{2,3},{3,4},{4,5},{5,6},{6,7},{7,8},{8,9},{9,10},{10,1... | collective-permute-start | bytes 786440 | tf_op jit(solution)/shard_map/ppermute | solution.py:270
  22.9 8.2 %collective-permute-done.prior = bf16[2,2,8,32,128]{4,3,2,1,0:T(8,128)(2,1)S(1)} collective-permute-done((bf16[2,2,8,32,128]{4,3,2,1,0:T(8,128)(2,1)S(1)}, bf16[2,2,8,32,128]{4,3,2,1,0:T(8,128)(2,1)S(1)}, u32[]{:S(2)}, u32[]{:S(2)}) %collective-permute-start) | collective-permute-done | bytes 262176 | tf_op jit(solution)/shard_map/ppermute | solution.py:270
  31.1 1.0 copy-done.14
  32.0 2.0 %shard_map.118 = (f32[2,2,256,128]{3,2,1,0:T(8,128)S(1)}, bf16[4,2,256,128]{3,2,1,0:T(8,128)(2,1)S(1)}, bf16[256,1152]{1,0:T(8,128)(2,1)S(1)}, bf16[2,128,256]{2,1,0:T(8,128)(2,1)S(1)}) custom-call(bf16[2,2,8,32,128]{4,3,2,1,0:T(8,128)(2,1)S(1)} %collective-permute-done.prior, bf16[2,2,8,32,128]{4,3,2,1,0:T(8,128)(2,1)S(1)} %bitcast.18, ...), custom_call_target="tpu_custom_call" | custom-call | flops 2000000000 | bytes 4000000 | tf_op jit(solution)/shard_map/pallas_call | solution.py:35
  34.9 0.8 copy-done.8
  35.7 4.4 %collective-permute-start.1 = (bf16[2,128,256]{2,1,0:T(8,128)(2,1)S(1)}, bf16[2,128,256]{2,1,0:T(8,128)(2,1)S(1)}, u32[]{:S(2)}, u32[]{:S(2)}) collective-permute-start(bf16[2,128,256]{2,1,0:T(8,128)(2,1)S(1)} %get-tuple-element.19.own), channel_id=1, source_target_pairs={{0,1},{1,2},{2,3},{3,4},{4,5},{5,6},{6,7},{7,8},{8,9},{9,10},{10,1... | collective-permute-start | bytes 393224 | tf_op jit(solution)/shard_map/ppermute | solution.py:270
  40.1 1.9 %collective-permute-done.1.prior = bf16[2,128,256]{2,1,0:T(8,128)(2,1)S(1)} collective-permute-done((bf16[2,128,256]{2,1,0:T(8,128)(2,1)S(1)}, bf16[2,128,256]{2,1,0:T(8,128)(2,1)S(1)}, u32[]{:S(2)}, u32[]{:S(2)}) %collective-permute-start.1) | collective-permute-done | bytes 131104 | tf_op jit(solution)/shard_map/ppermute | solution.py:270
  42.1 1.1 shard_map.119
  43.1 0.9 copy-done.2
  44.0 1.9 %collective-permute-start.2 = (bf16[128,256]{1,0:T(8,128)(2,1)S(1)}, bf16[128,256]{1,0:T(8,128)(2,1)S(1)}, u32[]{:S(2)}, u32[]{:S(2)}) collective-permute-start(bf16[128,256]{1,0:T(8,128)(2,1)S(1)} %get-tuple-element.21.own), channel_id=1, source_target_pairs={{1,0},{2,1},{3,2},{4,3},{5,4},{6,5},{7,6},{8,7},{9,8},{10,9},{11,1... | collective-permute-start | bytes 196616 | tf_op jit(solution)/shard_map/ppermute | solution.py:270
  45.9 4.4 %collective-permute-done.2.ahead = bf16[128,256]{1,0:T(8,128)(2,1)S(1)} collective-permute-done((bf16[128,256]{1,0:T(8,128)(2,1)S(1)}, bf16[128,256]{1,0:T(8,128)(2,1)S(1)}, u32[]{:S(2)}, u32[]{:S(2)}) %collective-permute-start.2) | collective-permute-done | bytes 65568 | tf_op jit(solution)/shard_map/ppermute | solution.py:270
  50.3 1.1 copy-done.5
  51.4 1.4 shard_map.121
  53.4 1.9 %collective-permute-start.3 = (bf16[2,2,8,32,128]{4,3,2,1,0:T(8,128)(2,1)}, bf16[2,2,8,32,128]{4,3,2,1,0:T(8,128)(2,1)S(1)}, u32[]{:S(2)}, u32[]{:S(2)}) collective-permute-start(bf16[2,2,8,32,128]{4,3,2,1,0:T(8,128)(2,1)} %get-tuple-element.24.own), channel_id=1, source_target_pairs={{1,0},{2,1},{3,2},{4,3},{5,4},{6,5},{7,6},{8,7},{9,8},{10,9},{11,1... | collective-permute-start | bytes 786440 | tf_op jit(solution)/shard_map/ppermute | solution.py:270
  55.4 6.0 %collective-permute-done.3.ahead = bf16[2,2,8,32,128]{4,3,2,1,0:T(8,128)(2,1)S(1)} collective-permute-done((bf16[2,2,8,32,128]{4,3,2,1,0:T(8,128)(2,1)}, bf16[2,2,8,32,128]{4,3,2,1,0:T(8,128)(2,1)S(1)}, u32[]{:S(2)}, u32[]{:S(2)}) %collective-permute-start.3) | collective-permute-done | bytes 262176 | tf_op jit(solution)/shard_map/ppermute | solution.py:270
  61.3 1.1 copy-done.3
  62.5 0.9 copy-done.11
  63.4 0.9 copy-done.13
  64.3 2.4 %shard_map.122 = (f32[3456,128]{1,0:T(8,128)S(1)}, bf16[3456,128]{1,0:T(8,128)(2,1)S(1)}) custom-call(s32[1]{0:T(128)} %bitcast.3.core, bf16[2,2,8,32,128]{4,3,2,1,0:T(8,128)(2,1)} %get-tuple-element.24.own, bf16[2,2,8,32,128]{4,3,2,1,0:T(8,128)(2,1)S(1)} %collective-permute-done.3.ahead, bf16[3,128,128]{2,1,0:T(8,128)(2,1)S(1)} %copy-done.13, ...), custom_call_target="tpu_custom_call" | custom-call | flops 800000000 | bytes 4000000 | tf_op jit(solution)/shard_map/pallas_call | solution.py:35
  66.7 1.9 %collective-permute-start.4 = (bf16[3456,128]{1,0:T(8,128)(2,1)S(1)}, bf16[3456,128]{1,0:T(8,128)(2,1)S(1)}, u32[]{:S(2)}, u32[]{:S(2)}) collective-permute-start(bf16[3456,128]{1,0:T(8,128)(2,1)S(1)} %get-tuple-element.31), channel_id=1, source_target_pairs={{0,1},{1,0},{2,3},{3,2},{4,5},{5,4},{6,7},{7,6},{8,9},{9,8},{10,11... | collective-permute-start | bytes 2654216 | tf_op jit(solution)/shard_map/ppermute | solution.py:275
  68.6 2.4 %collective-permute-done.4 = bf16[3456,128]{1,0:T(8,128)(2,1)S(1)} collective-permute-done((bf16[3456,128]{1,0:T(8,128)(2,1)S(1)}, bf16[3456,128]{1,0:T(8,128)(2,1)S(1)}, u32[]{:S(2)}, u32[]{:S(2)}) %collective-permute-start.4) | collective-permute-done | bytes 884768 | tf_op jit(solution)/shard_map/ppermute | solution.py:275
  71.2 20.6 %all_to_all.30 = bf16[16,216,128]{2,1,0:T(8,128)(2,1)S(1)} all-to-all(bf16[16,216,128]{2,1,0:T(8,128)(2,1)S(1)} %bitcast.20), channel_id=1, replica_groups=mesh['clip'=16,'seq'=32] {'clip'}, dimensions={0} | all-to-all | bytes 1769472 | tf_op jit(solution)/shard_map/all_to_all | solution.py:279
  92.0 24.3 %all_to_all.31 = bf16[16,16,128]{2,1,0:T(8,128)(2,1)S(1)} all-to-all(bf16[16,16,128]{2,1,0:T(8,128)(2,1)S(1)} %bitcast.27), channel_id=1, replica_groups={{0,2,4,6,8,10,12,14,16,18,20,22,24,26,28,30},{1,3,5,7,9,11,13,15,17,19,..., dimensions={0} | all-to-all | bytes 131072 | tf_op jit(solution)/shard_map/all_to_all | solution.py:289
  116.4 14.4 %all_to_all.32 = bf16[16,16,128]{2,1,0:T(8,128)(2,1)S(1)} all-to-all(bf16[16,16,128]{2,1,0:T(8,128)(2,1)S(1)} %broadcast_in_dim.4), channel_id=1, replica_groups={{0,2,4,6,8,10,12,14,16,18,20,22,24,26,28,30},{1,3,5,7,9,11,13,15,17,19,..., dimensions={0} | all-to-all | bytes 131072 | tf_op jit(solution)/shard_map/all_to_all | solution.py:289
  130.9 14.6 %all_to_all.33 = bf16[16,216,128]{2,1,0:T(8,128)(2,1)S(1)} all-to-all(bf16[16,216,128]{2,1,0:T(8,128)(2,1)S(1)} %broadcast_in_dim.5), channel_id=1, replica_groups=mesh['clip'=16,'seq'=32] {'clip'}, dimensions={0} | all-to-all | bytes 1769472 | tf_op jit(solution)/shard_map/all_to_all | solution.py:279
  145.5 7.3 %collective-permute-start.5 = (bf16[3456,128]{1,0:T(8,128)(2,1)S(1)}, bf16[3456,128]{1,0:T(8,128)(2,1)S(1)}, u32[]{:S(2)}, u32[]{:S(2)}) collective-permute-start(bf16[3456,128]{1,0:T(8,128)(2,1)S(1)} %bitcast.21), channel_id=1, source_target_pairs={{0,1},{1,0},{2,3},{3,2},{4,5},{5,4},{6,7},{7,6},{8,9},{9,8},{10,11... | collective-permute-start | bytes 2654216 | tf_op jit(solution)/shard_map/ppermute | solution.py:275
  152.8 3.7 %all-to-all-start.1 = ((bf16[32,8,128]{2,1,0:T(8,128)(2,1)}), bf16[32,8,128]{2,1,0:T(8,128)(2,1)S(1)}, u32[]{:S(2)}, u32[]{:S(2)}) async-start(bf16[32,8,128]{2,1,0:T(8,128)(2,1)} %get-tuple-element.20), calls=%async_computation.1 | async-start | bytes 131072 | tf_op jit(solution)/shard_map/all_to_all | solution.py:283
  156.4 12.9 %all-to-all-done.1.lowered = bf16[32,8,128]{2,1,0:T(8,128)(2,1)S(1)} async-done(((bf16[32,8,128]{2,1,0:T(8,128)(2,1)}), bf16[32,8,128]{2,1,0:T(8,128)(2,1)S(1)}, u32[]{:S(2)}, u32[]{:S(2)}) %all-to-all-start.1) | async-done | bytes 65568 | tf_op jit(solution)/shard_map/all_to_all | solution.py:283
  171.9 0.9 fusion
  172.8 1.0 pad_maximum_fusion.1
  (43 shorter events, 5.3 us)
Async XLA Ops:
  0.6 18.5 %copy-start.15 = (bf16[1,2,64,8,128]{4,3,2,1,0:T(8,128)(2,1)S(1)}, bf16[1,2,64,8,128]{4,3,2,1,0:T(8,128)(2,1)}, u32[]{:S(2)}) copy-start(bf16[1,2,64,8,128]{4,3,2,1,0:T(8,128)(2,1)} %param.7) | copy-start | bytes 786436
  0.6 30.4 %copy-start.12 = (bf16[3,128,128]{2,1,0:T(8,128)(2,1)S(1)}, bf16[3,128,128]{2,1,0:T(8,128)(2,1)}, u32[]{:S(2)}) copy-start(bf16[3,128,128]{2,1,0:T(8,128)(2,1)} %first_time.3) | copy-start | bytes 294916
  0.7 30.4 %copy-start.4 = (bf16[3,3,128,256]{3,2,1,0:T(8,128)(2,1)S(1)}, bf16[3,3,128,256]{3,2,1,0:T(8,128)(2,1)}, u32[]{:S(2)}) copy-start(bf16[3,3,128,256]{3,2,1,0:T(8,128)(2,1)} %down_plane.3) | copy-start | bytes 1769476
  2.3 39.7 %all-to-all-start = ((bf16[32,24,128]{2,1,0:T(8,128)(2,1)}), bf16[32,24,128]{2,1,0:T(8,128)(2,1)S(1)}, u32[]{:S(2)}, u32[]{:S(2)}) async-start(bf16[32,24,128]{2,1,0:T(8,128)(2,1)} %pad_maximum_fusion.3), calls=%async_computation | async-start | bytes 393216 | tf_op jit(solution)/shard_map/all_to_all | solution.py:283
  19.2 22.8 %copy-start = (bf16[3,256,256]{2,1,0:T(8,128)(2,1)S(1)}, bf16[3,256,256]{2,1,0:T(8,128)(2,1)}, u32[]{:S(2)}) copy-start(bf16[3,256,256]{2,1,0:T(8,128)(2,1)} %last_time.3) | copy-start | bytes 1179652
  19.2 22.8 %copy-start.1 = (bf16[3,256,256]{2,1,0:T(8,128)(2,1)S(1)}, bf16[3,256,256]{2,1,0:T(8,128)(2,1)}, u32[]{:S(2)}) copy-start(bf16[3,256,256]{2,1,0:T(8,128)(2,1)} %down_time.3) | copy-start | bytes 1179652
  19.2 11.8 %collective-permute-start = (bf16[2,2,8,32,128]{4,3,2,1,0:T(8,128)(2,1)S(1)}, bf16[2,2,8,32,128]{4,3,2,1,0:T(8,128)(2,1)S(1)}, u32[]{:S(2)}, u32[]{:S(2)}) collective-permute-start(bf16[2,2,8,32,128]{4,3,2,1,0:T(8,128)(2,1)S(1)} %bitcast.17), channel_id=1, source_target_pairs={{0,1},{1,2},{2,3},{3,4},{4,5},{5,6},{6,7},{7,8},{8,9},{9,10},{10,1... | collective-permute-start | bytes 786440 | tf_op jit(solution)/shard_map/ppermute | solution.py:270
  31.1 1.0 copy-start.14
  34.1 0.8 copy-start.6
  34.9 0.8 copy-start.8
  35.7 6.3 %collective-permute-start.1 = (bf16[2,128,256]{2,1,0:T(8,128)(2,1)S(1)}, bf16[2,128,256]{2,1,0:T(8,128)(2,1)S(1)}, u32[]{:S(2)}, u32[]{:S(2)}) collective-permute-start(bf16[2,128,256]{2,1,0:T(8,128)(2,1)S(1)} %get-tuple-element.19.own), channel_id=1, source_target_pairs={{0,1},{1,2},{2,3},{3,4},{4,5},{5,6},{6,7},{7,8},{8,9},{9,10},{10,1... | collective-permute-start | bytes 393224 | tf_op jit(solution)/shard_map/ppermute | solution.py:270
  42.0 8.3 %copy-start.7 = (bf16[256,1152]{1,0:T(8,128)(2,1)S(1)}, bf16[256,1152]{1,0:T(8,128)(2,1)}, u32[]{:S(2)}) copy-start(bf16[256,1152]{1,0:T(8,128)(2,1)} %copy-done.6) | copy-start | bytes 1769476
  42.0 8.2 %copy-start.9 = (bf16[4,2,256,128]{3,2,1,0:T(8,128)(2,1)S(1)}, bf16[4,2,256,128]{3,2,1,0:T(8,128)(2,1)}, u32[]{:S(2)}) copy-start(bf16[4,2,256,128]{3,2,1,0:T(8,128)(2,1)} %copy-done.8) | copy-start | bytes 1572868
  43.1 0.9 copy-start.2
  44.0 6.3 %collective-permute-start.2 = (bf16[128,256]{1,0:T(8,128)(2,1)S(1)}, bf16[128,256]{1,0:T(8,128)(2,1)S(1)}, u32[]{:S(2)}, u32[]{:S(2)}) collective-permute-start(bf16[128,256]{1,0:T(8,128)(2,1)S(1)} %get-tuple-element.21.own), channel_id=1, source_target_pairs={{1,0},{2,1},{3,2},{4,3},{5,4},{6,5},{7,6},{8,7},{9,8},{10,9},{11,1... | collective-permute-start | bytes 196616 | tf_op jit(solution)/shard_map/ppermute | solution.py:270
  50.3 1.1 copy-start.5
  52.8 0.7 copy-start.10
  53.4 7.9 %collective-permute-start.3 = (bf16[2,2,8,32,128]{4,3,2,1,0:T(8,128)(2,1)}, bf16[2,2,8,32,128]{4,3,2,1,0:T(8,128)(2,1)S(1)}, u32[]{:S(2)}, u32[]{:S(2)}) collective-permute-start(bf16[2,2,8,32,128]{4,3,2,1,0:T(8,128)(2,1)} %get-tuple-element.24.own), channel_id=1, source_target_pairs={{1,0},{2,1},{3,2},{4,3},{5,4},{6,5},{7,6},{8,7},{9,8},{10,9},{11,1... | collective-permute-start | bytes 786440 | tf_op jit(solution)/shard_map/ppermute | solution.py:270
  61.3 1.1 copy-start.3
  62.5 0.9 copy-start.11
  63.4 0.9 copy-start.13
  66.7 4.3 %collective-permute-start.4 = (bf16[3456,128]{1,0:T(8,128)(2,1)S(1)}, bf16[3456,128]{1,0:T(8,128)(2,1)S(1)}, u32[]{:S(2)}, u32[]{:S(2)}) collective-permute-start(bf16[3456,128]{1,0:T(8,128)(2,1)S(1)} %get-tuple-element.31), channel_id=1, source_target_pairs={{0,1},{1,0},{2,3},{3,2},{4,5},{5,4},{6,7},{7,6},{8,9},{9,8},{10,11... | collective-permute-start | bytes 2654216 | tf_op jit(solution)/shard_map/ppermute | solution.py:275
  145.5 24.8 %collective-permute-start.5 = (bf16[3456,128]{1,0:T(8,128)(2,1)S(1)}, bf16[3456,128]{1,0:T(8,128)(2,1)S(1)}, u32[]{:S(2)}, u32[]{:S(2)}) collective-permute-start(bf16[3456,128]{1,0:T(8,128)(2,1)S(1)} %bitcast.21), channel_id=1, source_target_pairs={{0,1},{1,0},{2,3},{3,2},{4,5},{5,4},{6,7},{7,6},{8,9},{9,8},{10,11... | collective-permute-start | bytes 2654216 | tf_op jit(solution)/shard_map/ppermute | solution.py:275
  152.8 16.6 %all-to-all-start.1 = ((bf16[32,8,128]{2,1,0:T(8,128)(2,1)}), bf16[32,8,128]{2,1,0:T(8,128)(2,1)S(1)}, u32[]{:S(2)}, u32[]{:S(2)}) async-start(bf16[32,8,128]{2,1,0:T(8,128)(2,1)} %get-tuple-element.20), calls=%async_computation.1 | async-start | bytes 131072 | tf_op jit(solution)/shard_map/all_to_all | solution.py:283

commit v3 on v2

--- a/solution.py
+++ b/solution.py
@@ -1,5 +1,3 @@
-import functools
-
 import jax
 import jax.numpy as jnp
 from jax import lax
@@ -38,7 +36,7 @@
         in_specs=[pl.BlockSpec(memory_space=space) for space in spaces],
         out_specs=[pl.BlockSpec(memory_space=pltpu.VMEM) for _ in outs],
         scratch_shapes=[pltpu.VMEM(shape, kind) for shape, kind in scratch],
-        compiler_params=pltpu.CompilerParams(vmem_limit_bytes=40 * 1024 * 1024),
+        compiler_params=pltpu.CompilerParams(vmem_limit_bytes=24 * 1024 * 1024),
         cost_estimate=pl.CostEstimate(flops=flops, bytes_accessed=4000000, transcendentals=0),
     )(*args)
 
@@ -81,8 +79,8 @@
 
 def first_body(
     prior, own, first_plane, first_time, down_plane,
-    pre_out, hidden_out, cells_out, strided_out,
-    windows, both,
+    pre_out, hidden_out, cells_out, strided_out, source_out,
+    spread, windows, both,
 ):
     both[...] = jnp.zeros_like(both)
     for tap in range(3):
@@ -94,7 +92,16 @@
                 both[rows, pl.ds(CH, CH)] = first_plane[row - 1, tap]
     for frame in range(4):
         source = prior if frame < 2 else own
-        fill_windows(windows, frame * CELLS, source[frame % 2, 0], source[frame % 2, 1])
+        spread[...] = source[frame % 2].astype(F32).reshape(2 * CELLS, CH)
+        planes = []
+        for par in range(2):
+            cols = [
+                spread[pl.ds(par * COLS + col, HALF, stride=2 * COLS), :] for col in range(COLS)
+            ]
+            planes.append(jnp.stack(cols, axis=0).astype(BF16))
+            if frame >= 2:
+                source_out[frame - 2, par] = planes[par]
+        fill_windows(windows, frame * CELLS, planes[0], planes[1])
     for frame in range(4):
         pre = dot(windows[pl.ds(frame * CELLS, CELLS), :], both[...])
         hid = (pre * jax.nn.sigmoid(pre)).astype(BF16)
@@ -107,7 +114,7 @@
         mixed = []
         for par in range(2):
             taps = jnp.concatenate([hidden_out[frame + k, par] for k in range(3)], axis=1)
-            here = own[frame, par].reshape(CELLS, CH).astype(F32) + dot(taps, times)
+            here = source_out[frame, par].reshape(CELLS, CH).astype(F32) + dot(taps, times)
             mixed.append(here.astype(BF16).reshape(COLS, HALF, CH))
         by_row = (row_before(mixed[1]), mixed[0], mixed[1])
         for row in range(3):
@@ -154,7 +161,7 @@
             turned[pl.ds(col * 2 + half, HALF, stride=8), :] = wide[
                 col * HALF : (col + 1) * HALF, half * CH : (half + 1) * CH
             ]
-    lowered_out[...] = turned[...].astype(BF16).reshape(HALF, 8, CH)
+    lowered_out[...] = turned[...].reshape(HALF // 2, 2, 8, CH).astype(BF16)
     for k in range(3):
         down = dot_tn(taps[k], grad_pre)
         last = dot_tn(lowered, cot[2 - k])
@@ -219,7 +226,8 @@
 
 
 def last_body(
-    core, own, ahead, first_time, pre, source, grad_first_time, grad_down_plane, grad_down_time, grad_last,
+    core, own, ahead, first_time, pre, source, lowered,
+    grad_first_time, grad_down_plane, grad_down_time, grad_last,
     mine_out, other_out,
     windows, flat,
 ):
@@ -249,11 +257,63 @@
     half = start // 2
     here = core[0]
     mine_out[...] = flat[pl.ds(pl.multiple_of(here * half, 16), half), :]
-    other_out[...] = flat[pl.ds(pl.multiple_of((1 - here) * half, 16), half), :].astype(BF16)
-
-
-def output_body(lowered, last_time, output, spread, padded):
-    spread[...] = lowered[...].reshape(HALF * 8, CH).astype(F32)
+    other_out[pl.ds(0, half), :] = flat[
+        pl.ds(pl.multiple_of((1 - here) * half, 16), half), :
+    ].astype(BF16)
+    away = lowered[:, pl.ds(1 - here, 1)].astype(F32).reshape(DOWN, CH)
+    other_out[pl.ds(half, DOWN), :] = away.astype(BF16)
+
+
+def sum_body(core, blocks, own, other, sent_out, padded):
+    rows = blocks.shape[1]
+    total = blocks[0].astype(F32)
+    for block in range(1, blocks.shape[0]):
+        total = total + blocks[block].astype(F32)
+    padded[...] = jnp.zeros_like(padded)
+    padded[pl.ds(0, rows), :] = total
+    chips = sent_out.shape[0]
+    sent_out[:, pl.ds(0, 16), :] = padded[...].reshape(chips, 16, CH).astype(BF16)
+    here = core[0]
+    mine = own[:, pl.ds(here, 1)].astype(F32).reshape(chips, 8, CH)
+    theirs = other[...].astype(F32).reshape(chips, 8, CH)
+    frames = [jnp.where(here == 0, mine, theirs), jnp.where(here == 0, theirs, mine)]
+    sent_out[:, pl.ds(16, 16), :] = jnp.concatenate(frames, axis=1).astype(BF16)
+
+
+def piece_body(received, piece_out):
+    chips = received.shape[0]
+    total = received[0, pl.ds(0, 16), :].astype(F32)
+    for chip in range(1, chips):
+        total = total + received[chip, pl.ds(0, 16), :].astype(F32)
+    piece = total.astype(BF16)
+    for chip in range(chips):
+        piece_out[chip] = piece
+
+
+def spread_body(pieces, part_out):
+    flat = pieces[...].reshape(-1, CH).astype(F32)
+    part = flat[: part_out.shape[1]].astype(BF16)
+    for block in range(part_out.shape[0]):
+        part_out[block] = part
+
+
+def results_body(core, mine, other, *rest):
+    outs, whole = rest[:-1], rest[-1]
+    here = core[0]
+    half = mine.shape[0]
+    whole[pl.ds(pl.multiple_of(here * half, 16), half), :] = mine[...]
+    whole[pl.ds(pl.multiple_of((1 - here) * half, 16), half), :] = other[...]
+    start = 0
+    for out in outs:
+        rows, lanes = out.shape
+        for part in range(lanes // CH):
+            out[:, pl.ds(part * CH, CH)] = whole[pl.ds(start, rows), :]
+            start += rows
+
+
+def output_body(received, last_time, output, spread, padded):
+    frames = received[:, pl.ds(16, 16), :]
+    spread[...] = frames.astype(F32).reshape(HALF * 8, CH)
     padded[pl.ds(0, 8), :] = jnp.zeros((8, WIDE), F32)
     for half in range(2):
         padded[pl.ds(8, DOWN), pl.ds(half * CH, CH)] = spread[pl.ds(half, DOWN, stride=2), :]
@@ -291,55 +351,30 @@
     )
 
 
-def sum_blocks(blocks):
-    return jnp.sum(blocks.astype(F32), axis=0)
-
-
-def sum_everywhere(mine, other):
-    clips = lax.axis_size("clip")
-    chips = lax.axis_size("seq") // 2
-    core = lax.axis_index("seq") % 2
-    other = swap_cores(other)
-    half = (mine + other.astype(F32)).astype(BF16)
-    part = sum_blocks(exchange_clip(half.reshape(clips, -1, CH)))
-    part_rows = part.shape[0]
-    chunk = 16 * (-(-part_rows // (16 * chips)))
-    part = jnp.pad(part, ((0, chunk * chips - part_rows), (0, 0))).astype(BF16)
-    piece = sum_blocks(exchange_depth(part.reshape(chips, chunk, CH))).astype(BF16)
-    part = exchange_depth(jnp.broadcast_to(piece[None], (chips, chunk, CH)))
-    part = part.reshape(-1, CH)[:part_rows]
-    half = exchange_clip(jnp.broadcast_to(part[None], (clips, part_rows, CH)))
-    half = half.reshape(-1, CH)
-    other = swap_cores(half)
-    first = jnp.where(core == 0, half, other)
-    second = jnp.where(core == 0, other, half)
-    return jnp.concatenate([first, second], axis=0)
-
-
 def local(clip_in, first_plane, first_time, down_plane, down_time, last_time, cotan_out):
-    source = clip_in[0].reshape(2, HALF, 2, COLS, CH).transpose(0, 2, 3, 1, 4)
-    prior = from_behind(source, 1)
+    prior = from_behind(clip_in[0], 1)
     rows = cotan_out[0].reshape(HALF, 8, CH)
     rows_ahead = jnp.pad(rows, ((0, 2), (0, 0), (0, 0)))
     cotans = jnp.concatenate([rows, rows_ahead[1 : HALF + 1], rows_ahead[2:]], axis=1)
     cotans = exchange_seq(cotans)
-    pre_first, hidden, cells, strided = call(
+    pre_first, hidden, cells, strided, source = call(
         first_body,
         [
             ((2, 2, CELLS, CH), F32),
             ((4, 2, CELLS, CH), BF16),
             ((2 * DOWN, 9 * CH), BF16),
             ((2, DOWN, WIDE), BF16),
+            ((2, 2, COLS, HALF, CH), BF16),
         ],
-        [((4 * CELLS, 12 * CH), BF16), ((12 * CH, WIDE), BF16)],
-        prior, source, first_plane, first_time, down_plane,
+        [((2 * CELLS, CH), F32), ((4 * CELLS, 12 * CH), BF16), ((12 * CH, WIDE), BF16)],
+        prior, clip_in[0], first_plane, first_time, down_plane,
         flops=2000000000,
     )
     strided_prior = from_behind(strided, 1)
     lowered, grad_pre, grad_down_time, grad_last = call(
         middle_body,
         [
-            ((HALF, 8, CH), BF16),
+            ((HALF // 2, 2, 8, CH), BF16),
             ((DOWN, WIDE), BF16),
             ((2, 3 * WIDE, CH), F32),
             ((2, 3 * WIDE, CH), F32),
@@ -362,36 +397,59 @@
     )
     grad_mixed_next = from_behind(grad_mixed, -1)
     core = (lax.axis_index("seq") % 2).astype(jnp.int32).reshape(1)
-    num_rows = (9 + 3 + 18 + 12 + 12) * CH
+    half_rows = (9 + 3 + 18 + 12 + 12) * CH // 2
     mine, other = call(
         last_body,
-        [((num_rows // 2, CH), F32), ((num_rows // 2, CH), BF16)],
-        [((2 * CELLS, 12 * CH), BF16), ((num_rows, CH), F32)],
-        core, grad_mixed, grad_mixed_next, first_time, pre_first, source,
+        [((half_rows, CH), F32), ((half_rows + DOWN, CH), BF16)],
+        [((2 * CELLS, 12 * CH), BF16), ((2 * half_rows, CH), F32)],
+        core, grad_mixed, grad_mixed_next, first_time, pre_first, source, lowered,
         grad_first_time, grad_down_plane, grad_down_time, grad_last,
         smem=1,
         flops=800000000,
     )
-    whole = sum_everywhere(mine, other)
-    lowered_rows = exchange_seq(lowered)
+
+    clips = lax.axis_size("clip")
+    chips = lax.axis_size("seq") // 2
+    other = swap_cores(other)
+    half = (mine + other[:half_rows].astype(F32)).astype(BF16)
+    part_rows = half_rows // clips
+    blocks = exchange_clip(half.reshape(clips, part_rows, CH))
+    (sent,) = call(
+        sum_body,
+        [((chips, 32, CH), BF16)],
+        [((16 * chips, CH), F32)],
+        core, blocks, lowered, other[half_rows:],
+        smem=1,
+    )
+    received = exchange_depth(sent)
+    (pieces,) = call(piece_body, [((chips, 16, CH), BF16)], [], received)
+    pieces = exchange_depth(pieces)
     (output,) = call(
         output_body,
         [((DOWN, WIDE), BF16)],
         [((HALF * 8, CH), F32), ((DOWN + 8, WIDE), F32)],
-        lowered_rows, last_time,
+        received, last_time,
         flops=60000000,
     )
-
-    result = [output.reshape(1, HALF, 1, 4, WIDE)]
-    start = 0
-    for shape in ((3, 3, CH, CH), (3, CH, CH), (3, 3, CH, WIDE), (3, WIDE, WIDE), (3, WIDE, WIDE)):
-        rows = functools.reduce(lambda a, b: a * b, shape) // CH
-        block = whole[start : start + rows]
-        if shape[-1] == WIDE:
-            block = jnp.concatenate([block[: rows // 2], block[rows // 2 :]], axis=1)
-        result.append(block.reshape(shape))
-        start += rows
-    return tuple(result)
+    (parts,) = call(spread_body, [((clips, part_rows, CH), BF16)], [], pieces)
+    half = exchange_clip(parts).reshape(half_rows, CH)
+    other = swap_cores(half)
+    grads = call(
+        results_body,
+        [
+            ((9 * CH, CH), BF16),
+            ((3 * CH, CH), BF16),
+            ((9 * CH, WIDE), BF16),
+            ((3 * WIDE, WIDE), BF16),
+            ((3 * WIDE, WIDE), BF16),
+        ],
+        [((2 * half_rows, CH), BF16)],
+        core, half, other,
+        smem=1,
+    )
+    shapes = ((3, 3, CH, CH), (3, CH, CH), (3, 3, CH, WIDE), (3, WIDE, WIDE), (3, WIDE, WIDE))
+    grads = [grad.reshape(shape) for grad, shape in zip(grads, shapes)]
+    return (output.reshape(1, HALF, 1, 4, WIDE), *grads)
 
 
 def solution(mesh):

time: 174 us -> 166 us (0.954)
  blocking collectives: 73.9 us -> 56 us
  starting transfers between devices: 41.5 us -> 44.6 us
  waiting for transfers between devices: 35.8 us -> 38.4 us
  local copies, waits for them, and re-layouts: 11.5 us -> 14.1 us
    all_to_all x2 -> x1, blocking collectives: 35.2 us -> 16 us  [exchange_clip(): lax.all_to_all(blocks, 'clip', split_axis=0, concat_axis=0, tiled=True)]
    all_to_all x0 -> x1, waiting for transfers between devices: none -> 14.2 us  [exchange_clip(): lax.all_to_all(blocks, 'clip', split_axis=0, concat_axis=0, tiled=True)]
    all_to_all x2 -> x1, waiting for transfers between devices: 12.9 us -> 0.01 us  [exchange_seq(): lax.all_to_all(blocks, 'seq', split_axis=0, concat_axis=0, tiled=True)]
    all_to_all x0 -> x1, starting transfers between devices: none -> 6.76 us  [exchange_clip(): lax.all_to_all(blocks, 'clip', split_axis=0, concat_axis=0, tiled=True)]
    unnamed x32, local copies, waits for them, and re-layouts: 8.22 us -> 12.6 us
    all_to_all x2 -> x1, starting transfers between devices: 20.4 us -> 16.7 us  [exchange_seq(): lax.all_to_all(blocks, 'seq', split_axis=0, concat_axis=0, tiled=True)]
    concatenate x2 -> x0, other arithmetic: 1.84 us -> none  [local(): block = jnp.concatenate([block[:rows // 2], block[rows // 2:]], axis=1)]
    pallas_call x5 -> x9, Pallas kernels: 7.11 us -> 8.81 us  [call(): pl.pallas_call(body, out_shape=[jax.ShapeDtypeStruct(shape, kind) for sha...]
  transfers between devices with their start and end apart: 8 -> 8, of which waited for: 6 -> 7; matrix products, arithmetic and copies ran while one was open for 0% -> 0% of each run, Pallas kernels for 1% -> 2%
where the time goes in v3:
time: 166 us; the launch traced here: 165 us
  blocking collectives  56 us (34%)
  starting transfers between devices  44.6 us (27%)
  waiting for transfers between devices  38.4 us (23%)
  local copies, waits for them, and re-layouts  14.1 us (8%)
  Pallas kernels  8.81 us (5%)
  other arithmetic  1.87 us (1%)
    all_to_all x2, blocking collectives, exchange_depth(): lax.all_to_all(blocks, 'seq', split_axis=0, concat_axis=0, axis_index_gro...  40 us
    ppermute x4, waiting for transfers between devices, from_behind(): return lax.ppermute(block, 'seq', route)  20.7 us
    all_to_all x1, starting transfers between devices, exchange_seq(): lax.all_to_all(blocks, 'seq', split_axis=0, concat_axis=0, tiled=True)  16.7 us
    all_to_all x1, blocking collectives, exchange_clip(): lax.all_to_all(blocks, 'clip', split_axis=0, concat_axis=0, tiled=True)  16 us
    all_to_all x1, waiting for transfers between devices, exchange_clip(): lax.all_to_all(blocks, 'clip', split_axis=0, concat_axis=0, tiled=True)  14.2 us
    unnamed x32, local copies, waits for them, and re-layouts  12.6 us
    ppermute x4, starting transfers between devices, from_behind(): return lax.ppermute(block, 'seq', route)  11.9 us
    ppermute x2, starting transfers between devices, swap_cores(): return lax.ppermute(block, 'seq', [(i, i ^ 1) for i in range(count)])  9.21 us
  transfers between devices with their start and end apart: 8, of which 7 were waited for; matrix products, arithmetic and copies ran while one was open for 0% of the time, Pallas kernels for 2%

profile of v3, /device:TPU:1, one launch (start us, length us, event | category | flops | bytes accessed | tf_op | source)
XLA Modules:
  0.0 164.6 jit_solution(14426169962365874719)
XLA Ops:
  2.2 16.7 %all-to-all-start = ((bf16[32,24,128]{2,1,0:T(8,128)(2,1)}), bf16[32,24,128]{2,1,0:T(8,128)(2,1)S(1)}, u32[]{:S(2)}, u32[]{:S(2)}) async-start(bf16[32,24,128]{2,1,0:T(8,128)(2,1)} %pad_maximum_fusion), calls=%async_computation | async-start | bytes 393216 | tf_op jit(solution)/shard_map/all_to_all | solution.py:343
  19.0 3.7 %collective-permute-start = (bf16[2,64,8,128]{3,2,1,0:T(8,128)(2,1)}, bf16[2,64,8,128]{3,2,1,0:T(8,128)(2,1)S(1)}, u32[]{:S(2)}, u32[]{:S(2)}) collective-permute-start(bf16[2,64,8,128]{3,2,1,0:T(8,128)(2,1)} %bitcast.12), channel_id=1, source_target_pairs={{0,1},{1,2},{2,3},{3,4},{4,5},{5,6},{6,7},{7,8},{8,9},{9,10},{10,1... | collective-permute-start | bytes 786440 | tf_op jit(solution)/shard_map/ppermute | solution.py:330
  22.7 8.4 %collective-permute-done.prior = bf16[2,64,8,128]{3,2,1,0:T(8,128)(2,1)S(1)} collective-permute-done((bf16[2,64,8,128]{3,2,1,0:T(8,128)(2,1)}, bf16[2,64,8,128]{3,2,1,0:T(8,128)(2,1)S(1)}, u32[]{:S(2)}, u32[]{:S(2)}) %collective-permute-start) | collective-permute-done | bytes 262176 | tf_op jit(solution)/shard_map/ppermute | solution.py:330
  31.1 1.1 copy-done.4
  33.1 1.0 copy-done.14
  34.1 0.9 copy-done.15
  35.0 2.3 %shard_map.118 = (f32[2,2,256,128]{3,2,1,0:T(8,128)S(1)}, bf16[4,2,256,128]{3,2,1,0:T(8,128)(2,1)S(1)}, bf16[256,1152]{1,0:T(8,128)(2,1)S(1)}, bf16[2,128,256]{2...) custom-call(bf16[2,64,8,128]{3,2,1,0:T(8,128)(2,1)S(1)} %collective-permute-done.prior, ...), custom_call_target="tpu_custom_call" | custom-call | flops 2000000000 | bytes 4000000 | tf_op jit(solution)/shard_map/pallas_call | solution.py:33
  39.8 4.4 %collective-permute-start.1 = (bf16[2,128,256]{2,1,0:T(8,128)(2,1)S(1)}, bf16[2,128,256]{2,1,0:T(8,128)(2,1)S(1)}, u32[]{:S(2)}, u32[]{:S(2)}) collective-permute-start(bf16[2,128,256]{2,1,0:T(8,128)(2,1)S(1)} %get-tuple-element.25.own), channel_id=1, source_target_pairs={{0,1},{1,2},{2,3},{3,4},{4,5},{5,6},{6,7},{7,8},{8,9},{9,10},{10,1... | collective-permute-start | bytes 393224 | tf_op jit(solution)/shard_map/ppermute | solution.py:330
  44.1 1.9 %collective-permute-done.1.prior = bf16[2,128,256]{2,1,0:T(8,128)(2,1)S(1)} collective-permute-done((bf16[2,128,256]{2,1,0:T(8,128)(2,1)S(1)}, bf16[2,128,256]{2,1,0:T(8,128)(2,1)S(1)}, u32[]{:S(2)}, u32[]{:S(2)}) %collective-permute-start.1) | collective-permute-done | bytes 131104 | tf_op jit(solution)/shard_map/ppermute | solution.py:330
  46.9 0.9 copy-done.2
  47.8 1.9 %collective-permute-start.2 = (bf16[128,256]{1,0:T(8,128)(2,1)S(1)}, bf16[128,256]{1,0:T(8,128)(2,1)S(1)}, u32[]{:S(2)}, u32[]{:S(2)}) collective-permute-start(bf16[128,256]{1,0:T(8,128)(2,1)S(1)} %get-tuple-element.26.own), channel_id=1, source_target_pairs={{1,0},{2,1},{3,2},{4,3},{5,4},{6,5},{7,6},{8,7},{9,8},{10,9},{11,1... | collective-permute-start | bytes 196616 | tf_op jit(solution)/shard_map/ppermute | solution.py:330
  49.7 4.4 %collective-permute-done.2.ahead = bf16[128,256]{1,0:T(8,128)(2,1)S(1)} collective-permute-done((bf16[128,256]{1,0:T(8,128)(2,1)S(1)}, bf16[128,256]{1,0:T(8,128)(2,1)S(1)}, u32[]{:S(2)}, u32[]{:S(2)}) %collective-permute-start.2) | collective-permute-done | bytes 65568 | tf_op jit(solution)/shard_map/ppermute | solution.py:330
  54.1 1.1 copy-done.5
  55.1 1.1 copy-done.7
  56.2 1.0 copy-done.11
  57.2 1.4 shard_map.120
  58.6 1.9 %collective-permute-start.3 = (bf16[2,2,8,32,128]{4,3,2,1,0:T(8,128)(2,1)}, bf16[2,2,8,32,128]{4,3,2,1,0:T(8,128)(2,1)S(1)}, u32[]{:S(2)}, u32[]{:S(2)}) collective-permute-start(bf16[2,2,8,32,128]{4,3,2,1,0:T(8,128)(2,1)} %get-tuple-element.29.own), channel_id=1, source_target_pairs={{1,0},{2,1},{3,2},{4,3},{5,4},{6,5},{7,6},{8,7},{9,8},{10,9},{11,1... | collective-permute-start | bytes 786440 | tf_op jit(solution)/shard_map/ppermute | solution.py:330
  60.6 6.0 %collective-permute-done.3.ahead = bf16[2,2,8,32,128]{4,3,2,1,0:T(8,128)(2,1)S(1)} collective-permute-done((bf16[2,2,8,32,128]{4,3,2,1,0:T(8,128)(2,1)}, bf16[2,2,8,32,128]{4,3,2,1,0:T(8,128)(2,1)S(1)}, u32[]{:S(2)}, u32[]{:S(2)}) %collective-permute-start.3) | collective-permute-done | bytes 262176 | tf_op jit(solution)/shard_map/ppermute | solution.py:330
  66.5 1.1 copy-done.3
  67.7 1.0 copy-done.9
  68.7 2.4 %shard_map.121 = (f32[3456,128]{1,0:T(8,128)S(1)}, bf16[3584,128]{1,0:T(8,128)(2,1)S(1)}) custom-call(s32[1]{0:T(128)} %bitcast.core, bf16[2,2,8,32,128]{4,3,2,1,0:T(8,128)(2,1)} %get-tuple-element.29.own, bf16[2,2,8,32,128]{4,3,2,1,0:T(8,128)(2,1)S(1)} %collective-permute-done.3.ahead, bf16[3,128,128]{2,1,0:T(8,128)(2,1)S(1)} %copy-done.13, ...), custom_call_target="tpu_custom_call" | custom-call | flops 800000000 | bytes 4000000 | tf_op jit(solution)/shard_map/pallas_call | solution.py:33
  71.1 1.9 %collective-permute-start.4 = (bf16[3584,128]{1,0:T(8,128)(2,1)S(1)}, bf16[3584,128]{1,0:T(8,128)(2,1)S(1)}, u32[]{:S(2)}, u32[]{:S(2)}) collective-permute-start(bf16[3584,128]{1,0:T(8,128)(2,1)S(1)} %get-tuple-element.38), channel_id=1, source_target_pairs={{0,1},{1,0},{2,3},{3,2},{4,5},{5,4},{6,7},{7,6},{8,9},{9,8},{10,11... | collective-permute-start | bytes 2752520 | tf_op jit(solution)/shard_map/ppermute | solution.py:335
  73.1 2.4 %collective-permute-done.4 = bf16[3584,128]{1,0:T(8,128)(2,1)S(1)} collective-permute-done((bf16[3584,128]{1,0:T(8,128)(2,1)S(1)}, bf16[3584,128]{1,0:T(8,128)(2,1)S(1)}, u32[]{:S(2)}, u32[]{:S(2)}) %collective-permute-start.4) | collective-permute-done | bytes 917536 | tf_op jit(solution)/shard_map/ppermute | solution.py:335
  75.5 1.2 add_convert_fusion
  76.7 6.8 %all-to-all-start.1 = ((bf16[16,216,128]{2,1,0:T(8,128)(2,1)}), bf16[16,216,128]{2,1,0:T(8,128)(2,1)S(1)}, u32[]{:S(2)}, u32[]{:S(2)}) async-start(bf16[16,216,128]{2,1,0:T(8,128)(2,1)} %bitcast.2), calls=%async_computation.1 | async-start | bytes 1769472 | tf_op jit(solution)/shard_map/all_to_all | solution.py:339
  83.4 14.2 %all-to-all-done.1.blocks = bf16[16,216,128]{2,1,0:T(8,128)(2,1)S(1)} async-done(((bf16[16,216,128]{2,1,0:T(8,128)(2,1)}), bf16[16,216,128]{2,1,0:T(8,128)(2,1)S(1)}, u32[]{:S(2)}, u32[]{:S(2)}) %all-to-all-start.1) | async-done | bytes 884768 | tf_op jit(solution)/shard_map/all_to_all | solution.py:339
  97.7 24.6 %all_to_all.25.received = bf16[16,32,128]{2,1,0:T(8,128)(2,1)S(1)} all-to-all(bf16[16,32,128]{2,1,0:T(8,128)(2,1)S(1)} %shard_map.122), channel_id=1, replica_groups={{0,2,4,6,8,10,12,14,16,18,20,22,24,26,28,30},{1,3,5,7,9,11,13,15,17,19,..., dimensions={0} | all-to-all | bytes 262144 | tf_op jit(solution)/shard_map/all_to_all | solution.py:349
  122.4 15.4 %all_to_all.26.pieces = bf16[16,16,128]{2,1,0:T(8,128)(2,1)S(1)} all-to-all(bf16[16,16,128]{2,1,0:T(8,128)(2,1)S(1)} %shard_map.124), channel_id=1, replica_groups={{0,2,4,6,8,10,12,14,16,18,20,22,24,26,28,30},{1,3,5,7,9,11,13,15,17,19,..., dimensions={0} | all-to-all | bytes 131072 | tf_op jit(solution)/shard_map/all_to_all | solution.py:349
  137.9 16.0 %all_to_all.27 = bf16[16,216,128]{2,1,0:T(8,128)(2,1)S(1)} all-to-all(bf16[16,216,128]{2,1,0:T(8,128)(2,1)S(1)} %shard_map.125), channel_id=1, replica_groups=mesh['clip'=16,'seq'=32] {'clip'}, dimensions={0} | all-to-all | bytes 1769472 | tf_op jit(solution)/shard_map/all_to_all | solution.py:339
  153.9 7.3 %collective-permute-start.5 = (bf16[3456,128]{1,0:T(8,128)(2,1)S(1)}, bf16[3456,128]{1,0:T(8,128)(2,1)S(1)}, u32[]{:S(2)}, u32[]{:S(2)}) collective-permute-start(bf16[3456,128]{1,0:T(8,128)(2,1)S(1)} %bitcast.10), channel_id=1, source_target_pairs={{0,1},{1,0},{2,3},{3,2},{4,5},{5,4},{6,7},{7,6},{8,9},{9,8},{10,11... | collective-permute-start | bytes 2654216 | tf_op jit(solution)/shard_map/ppermute | solution.py:335
  162.1 1.1 collective-permute-done.5.other
  163.2 1.4 shard_map.126
  (34 shorter events, 6.9 us)
Async XLA Ops:
  2.2 43.8 %all-to-all-start = ((bf16[32,24,128]{2,1,0:T(8,128)(2,1)}), bf16[32,24,128]{2,1,0:T(8,128)(2,1)S(1)}, u32[]{:S(2)}, u32[]{:S(2)}) async-start(bf16[32,24,128]{2,1,0:T(8,128)(2,1)} %pad_maximum_fusion), calls=%async_computation | async-start | bytes 393216 | tf_op jit(solution)/shard_map/all_to_all | solution.py:343
  19.0 27.1 %copy-start = (bf16[3,256,256]{2,1,0:T(8,128)(2,1)S(1)}, bf16[3,256,256]{2,1,0:T(8,128)(2,1)}, u32[]{:S(2)}) copy-start(bf16[3,256,256]{2,1,0:T(8,128)(2,1)} %last_time.3) | copy-start | bytes 1179652
  19.0 27.1 %copy-start.1 = (bf16[3,256,256]{2,1,0:T(8,128)(2,1)S(1)}, bf16[3,256,256]{2,1,0:T(8,128)(2,1)}, u32[]{:S(2)}) copy-start(bf16[3,256,256]{2,1,0:T(8,128)(2,1)} %down_time.3) | copy-start | bytes 1179652
  19.0 12.1 %collective-permute-start = (bf16[2,64,8,128]{3,2,1,0:T(8,128)(2,1)}, bf16[2,64,8,128]{3,2,1,0:T(8,128)(2,1)S(1)}, u32[]{:S(2)}, u32[]{:S(2)}) collective-permute-start(bf16[2,64,8,128]{3,2,1,0:T(8,128)(2,1)} %bitcast.12), channel_id=1, source_target_pairs={{0,1},{1,2},{2,3},{3,4},{4,5},{5,6},{6,7},{7,8},{8,9},{9,10},{10,1... | collective-permute-start | bytes 786440 | tf_op jit(solution)/shard_map/ppermute | solution.py:330
  31.1 1.1 copy-start.4
  32.2 0.9 copy-start.12
  33.1 1.0 copy-start.14
  34.1 0.9 copy-start.15
  37.3 0.8 copy-start.6
  38.1 0.8 copy-start.8
  39.0 0.8 copy-start.10
  39.8 26.8 %copy-start.13 = (bf16[3,128,128]{2,1,0:T(8,128)(2,1)S(1)}, bf16[3,128,128]{2,1,0:T(8,128)(2,1)}, u32[]{:S(2)}) copy-start(bf16[3,128,128]{2,1,0:T(8,128)(2,1)} %first_time.3) | copy-start | bytes 294916
  39.8 6.3 %collective-permute-start.1 = (bf16[2,128,256]{2,1,0:T(8,128)(2,1)S(1)}, bf16[2,128,256]{2,1,0:T(8,128)(2,1)S(1)}, u32[]{:S(2)}, u32[]{:S(2)}) collective-permute-start(bf16[2,128,256]{2,1,0:T(8,128)(2,1)S(1)} %get-tuple-element.25.own), channel_id=1, source_target_pairs={{0,1},{1,2},{2,3},{3,4},{4,5},{5,6},{6,7},{7,8},{8,9},{9,10},{10,1... | collective-permute-start | bytes 393224 | tf_op jit(solution)/shard_map/ppermute | solution.py:330
  46.9 0.9 copy-start.2
  47.8 6.3 %collective-permute-start.2 = (bf16[128,256]{1,0:T(8,128)(2,1)S(1)}, bf16[128,256]{1,0:T(8,128)(2,1)S(1)}, u32[]{:S(2)}, u32[]{:S(2)}) collective-permute-start(bf16[128,256]{1,0:T(8,128)(2,1)S(1)} %get-tuple-element.26.own), channel_id=1, source_target_pairs={{1,0},{2,1},{3,2},{4,3},{5,4},{6,5},{7,6},{8,7},{9,8},{10,9},{11,1... | collective-permute-start | bytes 196616 | tf_op jit(solution)/shard_map/ppermute | solution.py:330
  54.1 1.1 copy-start.5
  55.1 1.1 copy-start.7
  56.2 1.0 copy-start.11
  58.6 7.9 %collective-permute-start.3 = (bf16[2,2,8,32,128]{4,3,2,1,0:T(8,128)(2,1)}, bf16[2,2,8,32,128]{4,3,2,1,0:T(8,128)(2,1)S(1)}, u32[]{:S(2)}, u32[]{:S(2)}) collective-permute-start(bf16[2,2,8,32,128]{4,3,2,1,0:T(8,128)(2,1)} %get-tuple-element.29.own), channel_id=1, source_target_pairs={{1,0},{2,1},{3,2},{4,3},{5,4},{6,5},{7,6},{8,7},{9,8},{10,9},{11,1... | collective-permute-start | bytes 786440 | tf_op jit(solution)/shard_map/ppermute | solution.py:330
  66.5 1.1 copy-start.3
  67.7 1.0 copy-start.9
  71.1 4.4 %collective-permute-start.4 = (bf16[3584,128]{1,0:T(8,128)(2,1)S(1)}, bf16[3584,128]{1,0:T(8,128)(2,1)S(1)}, u32[]{:S(2)}, u32[]{:S(2)}) collective-permute-start(bf16[3584,128]{1,0:T(8,128)(2,1)S(1)} %get-tuple-element.38), channel_id=1, source_target_pairs={{0,1},{1,0},{2,3},{3,2},{4,5},{5,4},{6,7},{7,6},{8,9},{9,8},{10,11... | collective-permute-start | bytes 2752520 | tf_op jit(solution)/shard_map/ppermute | solution.py:335
  76.7 20.9 %all-to-all-start.1 = ((bf16[16,216,128]{2,1,0:T(8,128)(2,1)}), bf16[16,216,128]{2,1,0:T(8,128)(2,1)S(1)}, u32[]{:S(2)}, u32[]{:S(2)}) async-start(bf16[16,216,128]{2,1,0:T(8,128)(2,1)} %bitcast.2), calls=%async_computation.1 | async-start | bytes 1769472 | tf_op jit(solution)/shard_map/all_to_all | solution.py:339
  153.9 9.3 %collective-permute-start.5 = (bf16[3456,128]{1,0:T(8,128)(2,1)S(1)}, bf16[3456,128]{1,0:T(8,128)(2,1)S(1)}, u32[]{:S(2)}, u32[]{:S(2)}) collective-permute-start(bf16[3456,128]{1,0:T(8,128)(2,1)S(1)} %bitcast.10), channel_id=1, source_target_pairs={{0,1},{1,0},{2,3},{3,2},{4,5},{5,4},{6,7},{7,6},{8,9},{9,8},{10,11... | collective-permute-start | bytes 2654216 | tf_op jit(solution)/shard_map/ppermute | solution.py:335

commit v4 on v3

v4 whole, which is shorter than its diff:
```python
import jax
import jax.numpy as jnp
from jax import lax
from jax.experimental import pallas as pl
from jax.experimental.pallas import tpu as pltpu
from jax.sharding import PartitionSpec as P


F32 = jnp.float32
BF16 = jnp.bfloat16
COLS = 8
HALF = 32
CELLS = COLS * HALF
DOWN = CELLS // 2
CH = 128
WIDE = 256


def dot(left, right):
    return lax.dot_general(left, right, (((1,), (0,)), ((), ())), preferred_element_type=F32)


def dot_nt(left, right):
    return lax.dot_general(left, right, (((1,), (1,)), ((), ())), preferred_element_type=F32)


def dot_tn(left, right):
    return lax.dot_general(left, right, (((0,), (0,)), ((), ())), preferred_element_type=F32)


V, H, S = pltpu.VMEM, pltpu.HBM, pltpu.SMEM


def call(body, ins, outs, scratch=(), copies=0, flops=0):
    scratch = [pltpu.VMEM(shape, kind) for shape, kind in scratch]
    if copies:
        scratch.append(pltpu.SemaphoreType.DMA((copies,)))
    return pl.pallas_call(
        body,
        out_shape=[jax.ShapeDtypeStruct(shape, kind) for _, shape, kind in outs],
        in_specs=[pl.BlockSpec(memory_space=space) for space, _ in ins],
        out_specs=[pl.BlockSpec(memory_space=space) for space, _, _ in outs],
        scratch_shapes=scratch,
        compiler_params=pltpu.CompilerParams(vmem_limit_bytes=24 * 1024 * 1024),
        cost_estimate=pl.CostEstimate(flops=flops, bytes_accessed=2000000, transcendentals=0),
    )(*[array for _, array in ins])


def start(sems, *pairs):
    copies = [
        pltpu.make_async_copy(source, target, sems.at[at]) for at, source, target in pairs
    ]
    for copy in copies:
        copy.start()
    return copies


def row_before(planes):
    wide = planes.astype(F32)
    rolled = pltpu.roll(wide, 1, 1)
    at = lax.broadcasted_iota(jnp.int32, wide.shape, 1)
    return jnp.where(at == 0, 0.0, rolled).astype(BF16)


def row_after(planes):
    wide = planes.astype(F32)
    rolled = pltpu.roll(wide, HALF - 1, 1)
    at = lax.broadcasted_iota(jnp.int32, wide.shape, 1)
    return jnp.where(at == HALF - 1, 0.0, rolled).astype(BF16)


def fill_windows(windows, at, even, odd):
    by_row = (row_before(odd), even, odd, row_after(even))
    edge = jnp.zeros((HALF, CH), BF16)
    for row, planes in enumerate(by_row):
        flat = planes.reshape(CELLS, CH)
        for tap in range(3):
            lanes = pl.ds((tap * 4 + row) * CH, CH)
            if tap == 0:
                windows[pl.ds(at, HALF), lanes] = edge
                windows[pl.ds(at + HALF, CELLS - HALF), lanes] = flat[: CELLS - HALF]
            elif tap == 1:
                windows[pl.ds(at, CELLS), lanes] = flat
            else:
                windows[pl.ds(at, CELLS - HALF), lanes] = flat[HALF:]
                windows[pl.ds(at + CELLS - HALF, HALF), lanes] = edge


def silu_slope(preact):
    sigma = jax.nn.sigmoid(preact)
    return sigma * (1.0 + preact * (1.0 - sigma))


def first_body(
    prior, own_far, plane_far, time_far, down_far,
    pre_far, hidden_far, cells_far, source_far, strided_out,
    own, first_plane, first_time, down_plane, pre_out, hidden_out, cells_out, source_out,
    spread, windows, both, sems,
):
    loads = start(
        sems,
        (0, own_far, own),
        (1, plane_far, first_plane),
        (2, time_far, first_time),
        (3, down_far, down_plane),
    )
    both[...] = jnp.zeros_like(both)
    for frame in range(4):
        if frame == 2:
            loads[0].wait()
        source = prior if frame < 2 else own
        spread[...] = source[pl.ds(frame % 2 * 2 * CELLS, 2 * CELLS), :].astype(F32)
        planes = []
        for par in range(2):
            cols = [
                spread[pl.ds(par * COLS + col, HALF, stride=2 * COLS), :] for col in range(COLS)
            ]
            planes.append(jnp.stack(cols, axis=0).astype(BF16))
            if frame >= 2:
                source_out[frame - 2, par] = planes[par]
        fill_windows(windows, frame * CELLS, planes[0], planes[1])
    stores = start(sems, (4, source_out, source_far))
    loads[1].wait()
    for tap in range(3):
        for row in range(4):
            rows = pl.ds((tap * 4 + row) * CH, CH)
            if row < 3:
                both[rows, pl.ds(0, CH)] = first_plane[row, tap]
            if row > 0:
                both[rows, pl.ds(CH, CH)] = first_plane[row - 1, tap]
    for frame in range(4):
        pre = dot(windows[pl.ds(frame * CELLS, CELLS), :], both[...])
        hid = (pre * jax.nn.sigmoid(pre)).astype(BF16)
        for par in range(2):
            hidden_out[frame, par] = hid[:, par * CH : (par + 1) * CH]
            if frame >= 2:
                pre_out[frame - 2, par] = pre[:, par * CH : (par + 1) * CH]
    stores += start(sems, (5, pre_out, pre_far), (6, hidden_out, hidden_far))
    loads[2].wait()
    times = first_time[...].reshape(3 * CH, CH)
    for frame in range(2):
        mixed = []
        for par in range(2):
            taps = jnp.concatenate([hidden_out[frame + k, par] for k in range(3)], axis=1)
            here = source_out[frame, par].reshape(CELLS, CH).astype(F32) + dot(taps, times)
            mixed.append(here.astype(BF16).reshape(COLS, HALF, CH))
        by_row = (row_before(mixed[1]), mixed[0], mixed[1])
        for row in range(3):
            for tap in range(3):
                lanes = pl.ds((row * 3 + tap) * CH, CH)
                for col in range(COLS // 2):
                    rows = pl.ds(frame * DOWN + col * HALF, HALF)
                    where = 2 * col + tap - 1
                    if where < 0:
                        cells_out[rows, lanes] = jnp.zeros((HALF, CH), BF16)
                    else:
                        cells_out[rows, lanes] = by_row[row][where]
    stores += start(sems, (7, cells_out, cells_far))
    loads[3].wait()
    kernel = down_plane[...].reshape(9 * CH, WIDE)
    strided_out[...] = dot(cells_out[...], kernel).astype(BF16).reshape(2, DOWN, WIDE)
    for store in stores:
        store.wait()


def cotan_body(
    own, cotans, down_far, last_far,
    cot_out, grad_lowered_out, part_out, times_out,
    last_time, down_time, spread, sems,
):
    loads = start(sems, (0, last_far, last_time), (1, down_far, down_time))
    spread[...] = cotans[...].astype(F32).reshape(HALF * 24, CH)
    cot = []
    for ahead in range(3):
        parts = []
        for col in range(4):
            halves = [
                spread[pl.ds(ahead * 8 + col * 2 + half, HALF, stride=24), :] for half in range(2)
            ]
            parts.append(jnp.concatenate(halves, axis=1))
        cot.append(jnp.concatenate(parts, axis=0).astype(BF16))
        cot_out[ahead] = cot[ahead]
    loads[0].wait()
    grad_lowered = cot[0].astype(F32)
    for k in range(3):
        grad_lowered = grad_lowered + dot_nt(cot[2 - k], last_time[k])
    grad_lowered_out[...] = grad_lowered.astype(BF16)
    loads[1].wait()
    part_out[...] = dot(own[0], down_time[2])
    times_out[...] = down_time[pl.ds(0, 2)]


def middle_body(prior, part, times, grad_lowered, lowered_out, grad_pre_out):
    pre = dot(prior[0], times[0]) + dot(prior[1], times[1]) + part[...]
    lowered_out[...] = (pre * jax.nn.sigmoid(pre)).astype(BF16)
    grad_pre_out[...] = (grad_lowered[...].astype(F32) * silu_slope(pre)).astype(BF16)


BACK = (
    (0, 0, 0, 0, 1, 1),
    (0, 1, 0, 1, 1, 0),
    (0, 1, 0, 0, 1, 2),
    (1, 0, 1, 0, 0, 1),
    (1, 0, 0, 0, 2, 1),
    (1, 1, 1, 1, 0, 0),
    (1, 1, 1, 0, 0, 2),
    (1, 1, 0, 1, 2, 0),
    (1, 1, 0, 0, 2, 2),
)


def time_grads_body(
    grad_pre, lowered, cot, prior, own, down_far, plane_far,
    part_out, times_out, kernels_out, grad_down_time_out, grad_last_out, lowered_out,
    down_time, down_plane, turned, sems,
):
    loads = start(sems, (0, down_far, down_time), (1, plane_far, down_plane))
    kernels_out[...] = jnp.zeros_like(kernels_out)
    wide = lowered[...].astype(F32)
    for col in range(4):
        for half in range(2):
            turned[pl.ds(col * 2 + half, HALF, stride=8), :] = wide[
                col * HALF : (col + 1) * HALF, half * CH : (half + 1) * CH
            ]
    lowered_out[...] = turned[...].reshape(HALF // 2, 2, 8, CH).astype(BF16)
    taps = (prior[0], prior[1], own[0])
    for k in range(3):
        down = dot_tn(taps[k], grad_pre[...])
        last = dot_tn(lowered[...], cot[2 - k])
        for half in range(2):
            lanes = slice(half * CH, (half + 1) * CH)
            grad_down_time_out[half, pl.ds(k * WIDE, WIDE), :] = down[:, lanes]
            grad_last_out[half, pl.ds(k * WIDE, WIDE), :] = last[:, lanes]
    for load in loads:
        load.wait()
    part_out[...] = dot_nt(grad_pre[...], down_time[2])
    times_out[...] = down_time[pl.ds(0, 2)]
    for row_par, col_par, row_off, col_off, row, tap in BACK:
        rows = pl.ds((row_par * 2 + col_par) * CH, CH)
        lanes = pl.ds((row_off * 2 + col_off) * WIDE, WIDE)
        kernels_out[rows, lanes] = down_plane[row, tap]


def back_body(ahead, part, times, kernels, grad_strided_out, grad_mixed_out, shifted):
    following = ahead[...]
    even = part[...] + dot_nt(following, times[0])
    odd = dot_nt(following, times[1])
    for frame, strided in ((0, even.astype(BF16)), (1, odd.astype(BF16))):
        grad_strided_out[pl.ds(frame * DOWN, DOWN), :] = strided
        planes = strided.reshape(4, HALF, WIDE)
        for row_off, rows in ((0, planes), (1, row_after(planes))):
            flat = rows.reshape(DOWN, WIDE)
            here = pl.ds((row_off * 2) * WIDE, WIDE)
            after = pl.ds((row_off * 2 + 1) * WIDE, WIDE)
            shifted[pl.ds(frame * DOWN, DOWN), here] = flat
            shifted[pl.ds(frame * DOWN, DOWN - HALF), after] = flat[HALF:]
            shifted[pl.ds(frame * DOWN + DOWN - HALF, HALF), after] = jnp.zeros((HALF, WIDE), BF16)
    mixed = dot_nt(shifted[...], kernels[...]).astype(BF16)
    for frame in range(2):
        for par in range(2):
            for col_par in range(2):
                lanes = slice((par * 2 + col_par) * CH, (par * 2 + col_par + 1) * CH)
                for col in range(4):
                    rows = slice(frame * DOWN + col * HALF, frame * DOWN + (col + 1) * HALF)
                    grad_mixed_out[frame, par, 2 * col + col_par] = mixed[rows, lanes]


def plane_grads_body(
    core, grad_strided, grad_mixed, cells_far, hidden_far, source_far, pre_far, time_far,
    grad_down_time, grad_last, lowered,
    mine_out, other_out, windows_out, slope_out, part_out, time_out,
    cells, hidden, source, pre, flat, sems,
):
    loads = start(
        sems,
        (0, cells_far, cells),
        (1, hidden_far, hidden),
        (2, source_far, source),
        (3, pre_far, pre),
        (4, time_far, time_out),
    )
    rows = 2 * 3 * WIDE
    base = 3 * CH + 18 * CH
    flat[pl.ds(base, rows), :] = grad_down_time[...].reshape(rows, CH)
    flat[pl.ds(base + rows, rows), :] = grad_last[...].reshape(rows, CH)
    loads[0].wait()
    down = dot_tn(cells[...], grad_strided[...])
    for half in range(2):
        at = 3 * CH + half * 9 * CH
        flat[pl.ds(at, 9 * CH), :] = down[:, half * CH : (half + 1) * CH]
    cotan = grad_mixed[...].reshape(4 * CELLS, CH)
    loads[1].wait()
    for k in range(3):
        taps = hidden[pl.ds(k, 2)].reshape(4 * CELLS, CH)
        flat[pl.ds(k * CH, CH), :] = dot_tn(taps, cotan)
    here = core[0]
    half = mine_out.shape[0]
    mine_out[...] = flat[pl.ds(pl.multiple_of(here * half, 16), half), :]
    other_out[pl.ds(0, half), :] = flat[
        pl.ds(pl.multiple_of((1 - here) * half, 16), half), :
    ].astype(BF16)
    away = lowered[:, pl.ds(1 - here, 1)].astype(F32).reshape(DOWN, CH)
    other_out[pl.ds(half, DOWN), :] = away.astype(BF16)
    for load in loads[2:]:
        load.wait()
    for frame in range(2):
        fill_windows(windows_out, frame * CELLS, source[frame, 0], source[frame, 1])
    slope_out[...] = silu_slope(pre[...])
    for par in range(2):
        first, second = [grad_mixed[frame, par].reshape(CELLS, CH) for frame in range(2)]
        part_out[0, par] = dot_nt(first, time_out[2]) + dot_nt(second, time_out[1])
        part_out[1, par] = dot_nt(second, time_out[2])


def last_body(
    core, ahead, windows, slope, part, first_time,
    mine_out, other_out,
    flat,
):
    cotans = [[], []]
    for par in range(2):
        first, second = [ahead[frame, par].reshape(CELLS, CH) for frame in range(2)]
        hidden = (
            part[0, par] + dot_nt(first, first_time[0]),
            part[1, par] + dot_nt(first, first_time[1]) + dot_nt(second, first_time[0]),
        )
        for frame in range(2):
            cotans[frame].append((hidden[frame] * slope[frame, par]).astype(BF16))
    cotan = jnp.concatenate([jnp.concatenate(parts, axis=1) for parts in cotans], axis=0)
    product = dot_tn(windows[...], cotan)
    for row in range(3):
        for tap in range(3):
            at = (tap * 4 + row) * CH
            flat[pl.ds((row * 3 + tap) * CH, CH), :] = (
                product[at : at + CH, :CH] + product[at + CH : at + 2 * CH, CH:]
            )
    here = core[0]
    half = mine_out.shape[0]
    mine_out[...] = flat[pl.ds(pl.multiple_of(here * half, 16), half), :]
    other_out[...] = flat[pl.ds(pl.multiple_of((1 - here) * half, 16), half), :].astype(BF16)


def halves_body(early, early_other, late, late_other, half_out):
    rows, more = early.shape[0], late.shape[0]
    half_out[pl.ds(0, rows), :] = (
        early[...] + early_other[pl.ds(0, rows), :].astype(F32)
    ).astype(BF16)
    half_out[pl.ds(rows, more), :] = (late[...] + late_other[...].astype(F32)).astype(BF16)


def sum_body(core, blocks, own, other, sent_out, padded):
    rows = blocks.shape[1]
    total = blocks[0].astype(F32)
    for block in range(1, blocks.shape[0]):
        total = total + blocks[block].astype(F32)
    padded[...] = jnp.zeros_like(padded)
    padded[pl.ds(0, rows), :] = total
    chips = sent_out.shape[0]
    sent_out[:, pl.ds(0, 16), :] = padded[...].reshape(chips, 16, CH).astype(BF16)
    here = core[0]
    mine = own[:, pl.ds(here, 1)].astype(F32).reshape(chips, 8, CH)
    theirs = other[pl.ds(other.shape[0] - DOWN, DOWN), :].astype(F32).reshape(chips, 8, CH)
    frames = [jnp.where(here == 0, mine, theirs), jnp.where(here == 0, theirs, mine)]
    sent_out[:, pl.ds(16, 16), :] = jnp.concatenate(frames, axis=1).astype(BF16)


def piece_body(received, piece_out):
    chips = received.shape[0]
    total = received[0, pl.ds(0, 16), :].astype(F32)
    for chip in range(1, chips):
        total = total + received[chip, pl.ds(0, 16), :].astype(F32)
    piece = total.astype(BF16)
    for chip in range(chips):
        piece_out[chip] = piece


def spread_body(pieces, part_out):
    flat = pieces[...].reshape(-1, CH).astype(F32)
    part = flat[: part_out.shape[1]].astype(BF16)
    for block in range(part_out.shape[0]):
        part_out[block] = part


def results_body(core, mine, other, first_plane_out, *rest):
    outs, early, late = rest[:-2], rest[-2], rest[-1]
    here = core[0]
    rows, more = early.shape[0] // 2, late.shape[0] // 2
    for half, at in ((mine, here), (other, 1 - here)):
        early[pl.ds(pl.multiple_of(at * rows, 16), rows), :] = half[pl.ds(0, rows), :]
        late[pl.ds(pl.multiple_of(at * more, 16), more), :] = half[pl.ds(rows, more), :]
    first_plane_out[...] = late[...]
    first = 0
    for out in outs:
        count, lanes = out.shape
        for part in range(lanes // CH):
            out[:, pl.ds(part * CH, CH)] = early[pl.ds(first, count), :]
            first += count


def output_body(received, last_time, output, spread, padded):
    frames = received[:, pl.ds(16, 16), :]
    spread[...] = frames.astype(F32).reshape(HALF * 8, CH)
    padded[pl.ds(0, 8), :] = jnp.zeros((8, WIDE), F32)
    for half in range(2):
        padded[pl.ds(8, DOWN), pl.ds(half * CH, CH)] = spread[pl.ds(half, DOWN, stride=2), :]
    total = padded[pl.ds(8, DOWN), :]
    for k in range(3):
        taps = padded[pl.ds(4 * k, DOWN), :].astype(BF16)
        total = total + dot(taps, last_time[k])
    output[...] = total.astype(BF16)


def from_behind(block, distance):
    devices = range(lax.axis_size("seq"))
    route = [(i - distance, i) for i in devices if i - distance in devices]
    return lax.ppermute(block, "seq", route)


def swap_cores(block):
    count = lax.axis_size("seq")
    return lax.ppermute(block, "seq", [(i, i ^ 1) for i in range(count)])


def exchange_clip(blocks):
    return lax.all_to_all(blocks, "clip", split_axis=0, concat_axis=0, tiled=True)


def exchange_seq(blocks):
    return lax.all_to_all(blocks, "seq", split_axis=0, concat_axis=0, tiled=True)


def exchange_depth(blocks):
    count = lax.axis_size("seq")
    groups = [list(range(core, count, 2)) for core in range(2)]
    return lax.all_to_all(
        blocks, "seq", split_axis=0, concat_axis=0, axis_index_groups=groups, tiled=True
    )


def local(clip_in, first_plane, first_time, down_plane, down_time, last_time, cotan_out):
    own = clip_in.reshape(4 * CELLS, CH)
    prior = from_behind(own, 1)
    rows = cotan_out[0].reshape(HALF, 8, CH)
    rows_ahead = jnp.pad(rows, ((0, 2), (0, 0), (0, 0)))
    cotans = jnp.concatenate([rows, rows_ahead[1 : HALF + 1], rows_ahead[2:]], axis=1)
    cotans, prior = lax.optimization_barrier((cotans, prior))
    cotans = exchange_seq(cotans)
    frames = (2, 2, COLS, HALF, CH)
    flat_frames = (2, 2, CELLS, CH)
    far = [
        (H, flat_frames, F32),
        (H, (4, 2, CELLS, CH), BF16),
        (H, (2 * DOWN, 9 * CH), BF16),
        (H, frames, BF16),
    ]
    pre_first, hidden, cells, source, strided = call(
        first_body,
        [(V, prior), (H, own), (H, first_plane), (H, first_time), (H, down_plane)],
        [*far, (V, (2, DOWN, WIDE), BF16)],
        [
            ((4 * CELLS, CH), BF16),
            ((3, 3, CH, CH), BF16),
            ((3, CH, CH), BF16),
            ((3, 3, CH, WIDE), BF16),
            *[(shape, kind) for _, shape, kind in far],
            ((2 * CELLS, CH), F32),
            ((4 * CELLS, 12 * CH), BF16),
            ((12 * CH, WIDE), BF16),
        ],
        copies=8,
        flops=2000000000,
    )
    strided_prior = from_behind(strided, 1)
    times = (V, (2, WIDE, WIDE), BF16)
    cot, grad_lowered, part, near_times = call(
        cotan_body,
        [(V, strided), (V, cotans), (H, down_time), (H, last_time)],
        [(V, (3, DOWN, WIDE), BF16), (V, (DOWN, WIDE), BF16), (V, (DOWN, WIDE), F32), times],
        [((3, WIDE, WIDE), BF16), ((3, WIDE, WIDE), BF16), ((HALF * 24, CH), F32)],
        copies=2,
        flops=100000000,
    )
    lowered, grad_pre = call(
        middle_body,
        [(V, strided_prior), (V, part), (V, near_times), (V, grad_lowered)],
        [(V, (DOWN, WIDE), BF16), (V, (DOWN, WIDE), BF16)],
        flops=60000000,
    )
    grad_pre_next = from_behind(grad_pre, -1)
    part, near_times, kernels, grad_down_time, grad_last, lowered = call(
        time_grads_body,
        [
            (V, grad_pre), (V, lowered), (V, cot), (V, strided_prior), (V, strided),
            (H, down_time), (H, down_plane),
        ],
        [
            (V, (DOWN, WIDE), F32),
            times,
            (V, (4 * CH, 4 * WIDE), BF16),
            (V, (2, 3 * WIDE, CH), F32),
            (V, (2, 3 * WIDE, CH), F32),
            (V, (HALF // 2, 2, 8, CH), BF16),
        ],
        [((3, WIDE, WIDE), BF16), ((3, 3, CH, WIDE), BF16), ((HALF * 8, CH), F32)],
        copies=2,
        flops=120000000,
    )
    grad_strided, grad_mixed = call(
        back_body,
        [(V, grad_pre_next), (V, part), (V, near_times), (V, kernels)],
        [(V, (2 * DOWN, WIDE), BF16), (V, frames, BF16)],
        [((2 * DOWN, 4 * WIDE), BF16)],
        flops=300000000,
    )
    grad_mixed_next = from_behind(grad_mixed, -1)
    core = (lax.axis_index("seq") % 2).astype(jnp.int32).reshape(1)
    early_rows = (3 + 18 + 12 + 12) * CH
    late_rows = 9 * CH
    early, early_other, windows, slope, part, near_time = call(
        plane_grads_body,
        [
            (S, core), (V, grad_strided), (V, grad_mixed),
            (H, cells), (H, hidden), (H, source), (H, pre_first), (H, first_time),
            (V, grad_down_time), (V, grad_last), (V, lowered),
        ],
        [
            (V, (early_rows // 2, CH), F32),
            (V, (early_rows // 2 + DOWN, CH), BF16),
            (V, (2 * CELLS, 12 * CH), BF16),
            (V, flat_frames, F32),
            (V, flat_frames, F32),
            (V, (3, CH, CH), BF16),
        ],
        [
            ((2 * DOWN, 9 * CH), BF16),
            ((4, 2, CELLS, CH), BF16),
            (frames, BF16),
            (flat_frames, F32),
            ((early_rows, CH), F32),
        ],
        copies=5,
        flops=500000000,
    )
    early_other = swap_cores(early_other)
    late, late_other = call(
        last_body,
        [(S, core), (V, grad_mixed_next), (V, windows), (V, slope), (V, part), (V, near_time)],
        [(V, (late_rows // 2, CH), F32), (V, (late_rows // 2, CH), BF16)],
        [((late_rows, CH), F32)],
        flops=600000000,
    )
    late_other = swap_cores(late_other)

    clips = lax.axis_size("clip")
    chips = lax.axis_size("seq") // 2
    half_rows = (early_rows + late_rows) // 2
    part_rows = half_rows // clips
    (half,) = call(
        halves_body,
        [(V, early), (V, early_other), (V, late), (V, late_other)],
        [(V, (half_rows, CH), BF16)],
    )
    blocks = exchange_clip(half.reshape(clips, part_rows, CH))
    (sent,) = call(
        sum_body,
        [(S, core), (V, blocks), (V, lowered), (V, early_other)],
        [(V, (chips, 32, CH), BF16)],
        [((16 * chips, CH), F32)],
    )
    received = exchange_depth(sent)
    (pieces,) = call(piece_body, [(V, received)], [(V, (chips, 16, CH), BF16)])
    pieces = exchange_depth(pieces)
    (output,) = call(
        output_body,
        [(V, received), (V, last_time)],
        [(V, (DOWN, WIDE), BF16)],
        [((HALF * 8, CH), F32), ((DOWN + 8, WIDE), F32)],
        flops=60000000,
    )
    (parts,) = call(spread_body, [(V, pieces)], [(V, (clips, part_rows, CH), BF16)])
    half = exchange_clip(parts).reshape(half_rows, CH)
    other = swap_cores(half)
    grads = call(
        results_body,
        [(S, core), (V, half), (V, other)],
        [
            (V, (9 * CH, CH), BF16),
            (V, (3 * CH, CH), BF16),
            (V, (9 * CH, WIDE), BF16),
            (V, (3 * WIDE, WIDE), BF16),
            (V, (3 * WIDE, WIDE), BF16),
        ],
        [((early_rows, CH), BF16), ((late_rows, CH), BF16)],
    )
    shapes = ((3, 3, CH, CH), (3, CH, CH), (3, 3, CH, WIDE), (3, WIDE, WIDE), (3, WIDE, WIDE))
    grads = [grad.reshape(shape) for grad, shape in zip(grads, shapes)]
    return (output.reshape(1, HALF, 1, 4, WIDE), *grads)


def solution(mesh):
    placed = (
        P("clip", "seq", None, None, None),
        P(),
        P(),
        P(),
        P(),
        P(),
        P("clip", None, "seq", None, None),
    )
    return jax.shard_map(
        local,
        mesh=mesh,
        in_specs=placed,
        out_specs=(P("clip", None, "seq", None, None), P(), P(), P(), P(), P()),
        check_vma=False,
    )
```

time: 166 us -> 157 us (0.946)
  waiting for transfers between devices: 38.4 us -> 17.4 us
  blocking collectives: 56 us -> 69.9 us
  Pallas kernels: 8.81 us -> 14 us
  local copies, waits for them, and re-layouts: 14.1 us -> 11 us
  starting transfers between devices: 44.6 us -> 41.8 us
    all_to_all x1 -> x2, blocking collectives: 16 us -> 37 us  [exchange_clip(): lax.all_to_all(blocks, 'clip', split_axis=0, concat_axis=0, tiled=True)]
    all_to_all x1 -> x0, waiting for transfers between devices: 14.2 us -> none  [exchange_clip(): lax.all_to_all(blocks, 'clip', split_axis=0, concat_axis=0, tiled=True)]
    ppermute x4, waiting for transfers between devices: 20.7 us -> 8.13 us  [from_behind(): return lax.ppermute(block, 'seq', route)]
    all_to_all x2, blocking collectives: 40 us -> 32.9 us  [exchange_depth(): lax.all_to_all(blocks, 'seq', split_axis=0, concat_axis=0, axis_index_gro...]
    all_to_all x1, waiting for transfers between devices: 0.01 us -> 6.81 us  [exchange_seq(): lax.all_to_all(blocks, 'seq', split_axis=0, concat_axis=0, tiled=True)]
    all_to_all x1 -> x0, starting transfers between devices: 6.76 us -> none  [exchange_clip(): lax.all_to_all(blocks, 'clip', split_axis=0, concat_axis=0, tiled=True)]
    pallas_call x9 -> x13, Pallas kernels: 8.81 us -> 14 us  [call(): pl.pallas_call(body, out_shape=[jax.ShapeDtypeStruct(shape, kind) for _,...]
    unnamed x32 -> x28, local copies, waits for them, and re-layouts: 12.6 us -> 9.47 us
  transfers between devices with their start and end apart: 8 -> 8, of which waited for: 7 -> 5; matrix products, arithmetic and copies ran while one was open for 0% -> 1% of each run, Pallas kernels for 2% -> 5%
where the time goes in v4:
time: 157 us; the launch traced here: 156 us
  blocking collectives  69.9 us (45%)
  starting transfers between devices  41.8 us (27%)
  waiting for transfers between devices  17.4 us (11%)
  Pallas kernels  14 us (9%)
  local copies, waits for them, and re-layouts  11 us (7%)
    all_to_all x2, blocking collectives, exchange_clip(): lax.all_to_all(blocks, 'clip', split_axis=0, concat_axis=0, tiled=True)  37 us
    all_to_all x2, blocking collectives, exchange_depth(): lax.all_to_all(blocks, 'seq', split_axis=0, concat_axis=0, axis_index_gro...  32.9 us
    all_to_all x1, starting transfers between devices, exchange_seq(): lax.all_to_all(blocks, 'seq', split_axis=0, concat_axis=0, tiled=True)  16.5 us
    ppermute x4, starting transfers between devices, from_behind(): return lax.ppermute(block, 'seq', route)  14.6 us
    pallas_call x13, Pallas kernels, call(): pl.pallas_call(body, out_shape=[jax.ShapeDtypeStruct(shape, kind) for _,...  14 us
    ppermute x3, starting transfers between devices, swap_cores(): return lax.ppermute(block, 'seq', [(i, i ^ 1) for i in range(count)])  10.7 us
    unnamed x28, local copies, waits for them, and re-layouts  9.47 us
    ppermute x4, waiting for transfers between devices, from_behind(): return lax.ppermute(block, 'seq', route)  8.13 us
  transfers between devices with their start and end apart: 8, of which 5 were waited for; matrix products, arithmetic and copies ran while one was open for 1% of the time, Pallas kernels for 5%

profile of v4, /device:TPU:1, one launch (start us, length us, event | category | flops | bytes accessed | tf_op | source)
XLA Modules:
  0.0 155.6 jit_solution(13912527790997216775)
XLA Ops:
  0.6 4.9 %collective-permute-start = (bf16[1024,128]{1,0:T(8,128)(2,1)}, bf16[1024,128]{1,0:T(8,128)(2,1)S(1)}, u32[]{:S(2)}, u32[]{:S(2)}) collective-permute-start(bf16[1024,128]{1,0:T(8,128)(2,1)} %bitcast.13), channel_id=1, source_target_pairs={{0,1},{1,2},{2,3},{3,4},{4,5},{5,6},{6,7},{7,8},{8,9},{9,10},{10,1... | collective-permute-start | bytes 786440 | tf_op jit(solution)/shard_map/ppermute | solution.py:416
  5.6 0.9 reshape_squeeze.3
  7.2 2.8 %collective-permute-done.prior = bf16[1024,128]{1,0:T(8,128)(2,1)S(1)} collective-permute-done((bf16[1024,128]{1,0:T(8,128)(2,1)}, bf16[1024,128]{1,0:T(8,128)(2,1)S(1)}, u32[]{:S(2)}, u32[]{:S(2)}) %collective-permute-start) | collective-permute-done | bytes 262176 | tf_op jit(solution)/shard_map/ppermute | solution.py:416
  10.0 16.5 %all-to-all-start = ((bf16[32,24,128]{2,1,0:T(8,128)(2,1)}), bf16[32,24,128]{2,1,0:T(8,128)(2,1)S(1)}, u32[]{:S(2)}, u32[]{:S(2)}) async-start(bf16[32,24,128]{2,1,0:T(8,128)(2,1)} %pad_maximum_fusion), calls=%async_computation | async-start | bytes 393216 | tf_op jit(solution)/shard_map/all_to_all | solution.py:429
  26.5 1.1 copy-done.2
  27.6 0.9 copy-done.8
  28.5 1.0 copy-done.12
  29.4 0.9 copy-done.13
  30.4 3.5 %shard_map.118 = (f32[2,2,256,128]{3,2,1,0:T(8,128)S(1)}, bf16[4,2,256,128]{3,2,1,0:T(8,128)(2,1)S(1)}, bf16[256,1152]{1,0:T(8,128)(2,1)S(1)}, bf16[2,2,8,32,128...) custom-call(bf16[1024,128]{1,0:T(8,128)(2,1)S(1)} %collective-permute-done.prior, bf16[1024,128]{1,0:T(8,128)(2,1)S(1)} %bitcast.14, ...), custom_call_target="tpu_custom_call" | custom-call | flops 2000000000 | bytes 2000000 | tf_op jit(solution)/shard_map/pallas_call | solution.py:38
  34.6 3.7 %collective-permute-start.1 = (bf16[2,128,256]{2,1,0:T(8,128)(2,1)S(1)}, bf16[2,128,256]{2,1,0:T(8,128)(2,1)S(1)}, u32[]{:S(2)}, u32[]{:S(2)}) collective-permute-start(bf16[2,128,256]{2,1,0:T(8,128)(2,1)S(1)} %get-tuple-element.41.own), channel_id=1, source_target_pairs={{0,1},{1,2},{2,3},{3,4},{4,5},{5,6},{6,7},{7,8},{8,9},{9,10},{10,1... | collective-permute-start | bytes 393224 | tf_op jit(solution)/shard_map/ppermute | solution.py:416
  38.3 6.8 %all-to-all-done.cotans = bf16[32,24,128]{2,1,0:T(8,128)(2,1)S(1)} async-done(((bf16[32,24,128]{2,1,0:T(8,128)(2,1)}), bf16[32,24,128]{2,1,0:T(8,128)(2,1)S(1)}, u32[]{:S(2)}, u32[]{:S(2)}) %all-to-all-start) | async-done | bytes 196640 | tf_op jit(solution)/shard_map/all_to_all | solution.py:429
  45.1 1.0 shard_map.119
  48.3 3.6 %collective-permute-start.2 = (bf16[128,256]{1,0:T(8,128)(2,1)}, bf16[128,256]{1,0:T(8,128)(2,1)}, u32[]{:S(2)}, u32[]{:S(2)}) collective-permute-start(bf16[128,256]{1,0:T(8,128)(2,1)} %get-tuple-element.46.grad_pre), channel_id=1, source_target_pairs={{1,0},{2,1},{3,2},{4,3},{5,4},{6,5},{7,6},{8,7},{9,8},{10,9},{11,1... | collective-permute-start | bytes 196616 | tf_op jit(solution)/shard_map/ppermute | solution.py:416
  51.9 0.9 copy-done.7
  53.6 1.9 %shard_map.121 = (f32[128,256]{1,0:T(8,128)S(1)}, bf16[2,256,256]{2,1,0:T(8,128)(2,1)S(1)}, bf16[512,1024]{1,0:T(8,128)(2,1)S(1)}, f32[2,768,128]{2,1,0:T(8,128)...) custom-call(bf16[128,256]{1,0:T(8,128)(2,1)} %get-tuple-element.46.grad_pre, ...), custom_call_target="tpu_custom_call" | custom-call | flops 120000000 | bytes 2000000 | tf_op jit(solution)/shard_map/pallas_call | solution.py:38
  55.6 1.4 shard_map.122
  57.1 0.9 copy-done.5
  58.0 0.9 copy-done.9
  58.9 2.2 %shard_map.123 = (f32[2880,128]{1,0:T(8,128)S(1)}, bf16[3008,128]{1,0:T(8,128)(2,1)S(1)}, bf16[512,1536]{1,0:T(8,128)(2,1)S(1)}, f32[2,2,256,128]{3,2,1,0:T(8,12...) custom-call(s32[1]{0:T(128)} %bitcast.core, ...), custom_call_target="tpu_custom_call" | custom-call | flops 500000000 | bytes 2000000 | tf_op jit(solution)/shard_map/pallas_call | solution.py:38
  61.1 1.9 %collective-permute-start.3 = (bf16[3008,128]{1,0:T(8,128)(2,1)S(1)}, bf16[3008,128]{1,0:T(8,128)(2,1)S(1)}, u32[]{:S(2)}, u32[]{:S(2)}) collective-permute-start(bf16[3008,128]{1,0:T(8,128)(2,1)S(1)} %get-tuple-element.62), channel_id=1, source_target_pairs={{0,1},{1,0},{2,3},{3,2},{4,5},{5,4},{6,7},{7,6},{8,9},{9,8},{10,11... | collective-permute-start | bytes 2310152 | tf_op jit(solution)/shard_map/ppermute | solution.py:421
  63.1 2.4 %collective-permute-start.4 = (bf16[2,2,8,32,128]{4,3,2,1,0:T(8,128)(2,1)S(1)}, bf16[2,2,8,32,128]{4,3,2,1,0:T(8,128)(2,1)S(1)}, u32[]{:S(2)}, u32[]{:S(2)}) collective-permute-start(bf16[2,2,8,32,128]{4,3,2,1,0:T(8,128)(2,1)S(1)} %get-tuple-element.53.grad_mixed), channel_id=1, source_target_pairs={{1,0},{2,1},{3,2},{4,3},{5,4},{6,5},{7,6},{8,7},{9,8},{10,9},{11,1... | collective-permute-start | bytes 786440 | tf_op jit(solution)/shard_map/ppermute | solution.py:416
  65.5 5.3 %collective-permute-done.4.ahead = bf16[2,2,8,32,128]{4,3,2,1,0:T(8,128)(2,1)S(1)} collective-permute-done((bf16[2,2,8,32,128]{4,3,2,1,0:T(8,128)(2,1)S(1)}, bf16[2,2,8,32,128]{4,3,2,1,0:T(8,128)(2,1)S(1)}, u32[]{:S(2)}, u32[]{:S(2)}) %collective-permute-start.4) | collective-permute-done | bytes 262176 | tf_op jit(solution)/shard_map/ppermute | solution.py:416
  70.7 0.9 shard_map.124
  71.6 1.9 %collective-permute-start.5 = (bf16[576,128]{1,0:T(8,128)(2,1)S(1)}, bf16[576,128]{1,0:T(8,128)(2,1)S(1)}, u32[]{:S(2)}, u32[]{:S(2)}) collective-permute-start(bf16[576,128]{1,0:T(8,128)(2,1)S(1)} %get-tuple-element.68), channel_id=1, source_target_pairs={{0,1},{1,0},{2,3},{3,2},{4,5},{5,4},{6,7},{7,6},{8,9},{9,8},{10,11... | collective-permute-start | bytes 442376 | tf_op jit(solution)/shard_map/ppermute | solution.py:421
  73.6 1.3 collective-permute-done.5.late_other
  75.1 20.6 %all_to_all.25.blocks = bf16[16,216,128]{2,1,0:T(8,128)(2,1)S(1)} all-to-all(bf16[16,216,128]{2,1,0:T(8,128)(2,1)S(1)} %bitcast.10), channel_id=1, replica_groups=mesh['clip'=16,'seq'=32] {'clip'}, dimensions={0} | all-to-all | bytes 1769472 | tf_op jit(solution)/shard_map/all_to_all | solution.py:425
  95.8 17.5 %all_to_all.26.received = bf16[16,32,128]{2,1,0:T(8,128)(2,1)S(1)} all-to-all(bf16[16,32,128]{2,1,0:T(8,128)(2,1)S(1)} %shard_map.126), channel_id=1, replica_groups={{0,2,4,6,8,10,12,14,16,18,20,22,24,26,28,30},{1,3,5,7,9,11,13,15,17,19,..., dimensions={0} | all-to-all | bytes 262144 | tf_op jit(solution)/shard_map/all_to_all | solution.py:435
  113.3 15.5 %all_to_all.27.pieces = bf16[16,16,128]{2,1,0:T(8,128)(2,1)S(1)} all-to-all(bf16[16,16,128]{2,1,0:T(8,128)(2,1)S(1)} %shard_map.128), channel_id=1, replica_groups={{0,2,4,6,8,10,12,14,16,18,20,22,24,26,28,30},{1,3,5,7,9,11,13,15,17,19,..., dimensions={0} | all-to-all | bytes 131072 | tf_op jit(solution)/shard_map/all_to_all | solution.py:435
  128.9 16.4 %all_to_all.28 = bf16[16,216,128]{2,1,0:T(8,128)(2,1)S(1)} all-to-all(bf16[16,216,128]{2,1,0:T(8,128)(2,1)S(1)} %shard_map.129), channel_id=1, replica_groups=mesh['clip'=16,'seq'=32] {'clip'}, dimensions={0} | all-to-all | bytes 1769472 | tf_op jit(solution)/shard_map/all_to_all | solution.py:425
  145.3 6.9 %collective-permute-start.6 = (bf16[3456,128]{1,0:T(8,128)(2,1)S(1)}, bf16[3456,128]{1,0:T(8,128)(2,1)S(1)}, u32[]{:S(2)}, u32[]{:S(2)}) collective-permute-start(bf16[3456,128]{1,0:T(8,128)(2,1)S(1)} %bitcast.11), channel_id=1, source_target_pairs={{0,1},{1,0},{2,3},{3,2},{4,5},{5,4},{6,7},{7,6},{8,9},{9,8},{10,11... | collective-permute-start | bytes 2654216 | tf_op jit(solution)/shard_map/ppermute | solution.py:421
  153.1 1.1 collective-permute-done.6.other
  154.2 1.4 shard_map.130
  (33 shorter events, 5.8 us)
Async XLA Ops:
  0.6 9.4 %collective-permute-start = (bf16[1024,128]{1,0:T(8,128)(2,1)}, bf16[1024,128]{1,0:T(8,128)(2,1)S(1)}, u32[]{:S(2)}, u32[]{:S(2)}) collective-permute-start(bf16[1024,128]{1,0:T(8,128)(2,1)} %bitcast.13), channel_id=1, source_target_pairs={{0,1},{1,2},{2,3},{3,4},{4,5},{5,6},{6,7},{7,8},{8,9},{9,10},{10,1... | collective-permute-start | bytes 786440 | tf_op jit(solution)/shard_map/ppermute | solution.py:416
  10.0 35.1 %all-to-all-start = ((bf16[32,24,128]{2,1,0:T(8,128)(2,1)}), bf16[32,24,128]{2,1,0:T(8,128)(2,1)S(1)}, u32[]{:S(2)}, u32[]{:S(2)}) async-start(bf16[32,24,128]{2,1,0:T(8,128)(2,1)} %pad_maximum_fusion), calls=%async_computation | async-start | bytes 393216 | tf_op jit(solution)/shard_map/all_to_all | solution.py:429
  26.5 1.1 copy-start.2
  27.6 0.9 copy-start.8
  28.5 1.0 copy-start.12
  29.4 0.9 copy-start.13
  30.4 14.8 %copy-start = (bf16[3,256,256]{2,1,0:T(8,128)(2,1)S(1)}, bf16[3,256,256]{2,1,0:T(8,128)(2,1)}, u32[]{:S(2)}) copy-start(bf16[3,256,256]{2,1,0:T(8,128)(2,1)} %last_time.1) | copy-start | bytes 1179652
  30.4 14.8 %copy-start.1 = (bf16[3,256,256]{2,1,0:T(8,128)(2,1)S(1)}, bf16[3,256,256]{2,1,0:T(8,128)(2,1)}, u32[]{:S(2)}) copy-start(bf16[3,256,256]{2,1,0:T(8,128)(2,1)} %down_far.5) | copy-start | bytes 1179652
  33.9 0.7 copy-start.4
  34.6 17.2 %copy-start.3 = (bf16[3,3,128,256]{3,2,1,0:T(8,128)(2,1)S(1)}, bf16[3,3,128,256]{3,2,1,0:T(8,128)(2,1)}, u32[]{:S(2)}) copy-start(bf16[3,3,128,256]{3,2,1,0:T(8,128)(2,1)} %plane_far.3) | copy-start | bytes 1769476
  34.6 12.2 %collective-permute-start.1 = (bf16[2,128,256]{2,1,0:T(8,128)(2,1)S(1)}, bf16[2,128,256]{2,1,0:T(8,128)(2,1)S(1)}, u32[]{:S(2)}, u32[]{:S(2)}) collective-permute-start(bf16[2,128,256]{2,1,0:T(8,128)(2,1)S(1)} %get-tuple-element.41.own), channel_id=1, source_target_pairs={{0,1},{1,2},{2,3},{3,4},{4,5},{5,6},{6,7},{7,8},{8,9},{9,10},{10,1... | collective-permute-start | bytes 393224 | tf_op jit(solution)/shard_map/ppermute | solution.py:416
  46.1 0.7 copy-start.6
  47.6 0.6 copy-start.10
  48.3 7.3 %collective-permute-start.2 = (bf16[128,256]{1,0:T(8,128)(2,1)}, bf16[128,256]{1,0:T(8,128)(2,1)}, u32[]{:S(2)}, u32[]{:S(2)}) collective-permute-start(bf16[128,256]{1,0:T(8,128)(2,1)} %get-tuple-element.46.grad_pre), channel_id=1, source_target_pairs={{1,0},{2,1},{3,2},{4,3},{5,4},{6,5},{7,6},{8,7},{9,8},{10,9},{11,1... | collective-permute-start | bytes 196616 | tf_op jit(solution)/shard_map/ppermute | solution.py:416
  51.9 0.9 copy-start.7
  52.8 0.8 copy-start.11
  57.0 1.0 copy-start.5
  58.0 0.9 copy-start.9
  61.1 13.8 %collective-permute-start.3 = (bf16[3008,128]{1,0:T(8,128)(2,1)S(1)}, bf16[3008,128]{1,0:T(8,128)(2,1)S(1)}, u32[]{:S(2)}, u32[]{:S(2)}) collective-permute-start(bf16[3008,128]{1,0:T(8,128)(2,1)S(1)} %get-tuple-element.62), channel_id=1, source_target_pairs={{0,1},{1,0},{2,3},{3,2},{4,5},{5,4},{6,7},{7,6},{8,9},{9,8},{10,11... | collective-permute-start | bytes 2310152 | tf_op jit(solution)/shard_map/ppermute | solution.py:421
  63.1 7.7 %collective-permute-start.4 = (bf16[2,2,8,32,128]{4,3,2,1,0:T(8,128)(2,1)S(1)}, bf16[2,2,8,32,128]{4,3,2,1,0:T(8,128)(2,1)S(1)}, u32[]{:S(2)}, u32[]{:S(2)}) collective-permute-start(bf16[2,2,8,32,128]{4,3,2,1,0:T(8,128)(2,1)S(1)} %get-tuple-element.53.grad_mixed), channel_id=1, source_target_pairs={{1,0},{2,1},{3,2},{4,3},{5,4},{6,5},{7,6},{8,7},{9,8},{10,9},{11,1... | collective-permute-start | bytes 786440 | tf_op jit(solution)/shard_map/ppermute | solution.py:416
  71.6 3.3 %collective-permute-start.5 = (bf16[576,128]{1,0:T(8,128)(2,1)S(1)}, bf16[576,128]{1,0:T(8,128)(2,1)S(1)}, u32[]{:S(2)}, u32[]{:S(2)}) collective-permute-start(bf16[576,128]{1,0:T(8,128)(2,1)S(1)} %get-tuple-element.68), channel_id=1, source_target_pairs={{0,1},{1,0},{2,3},{3,2},{4,5},{5,4},{6,7},{7,6},{8,9},{9,8},{10,11... | collective-permute-start | bytes 442376 | tf_op jit(solution)/shard_map/ppermute | solution.py:421
  145.3 8.9 %collective-permute-start.6 = (bf16[3456,128]{1,0:T(8,128)(2,1)S(1)}, bf16[3456,128]{1,0:T(8,128)(2,1)S(1)}, u32[]{:S(2)}, u32[]{:S(2)}) collective-permute-start(bf16[3456,128]{1,0:T(8,128)(2,1)S(1)} %bitcast.11), channel_id=1, source_target_pairs={{0,1},{1,0},{2,3},{3,2},{4,5},{5,4},{6,7},{7,6},{8,9},{9,8},{10,11... | collective-permute-start | bytes 2654216 | tf_op jit(solution)/shard_map/ppermute | solution.py:421

commit v5 on v4

--- a/solution.py
+++ b/solution.py
@@ -14,6 +14,8 @@
 DOWN = CELLS // 2
 CH = 128
 WIDE = 256
+EARLY = (3 + 18 + 12 + 8) * CH
+LATE = (9 + 4) * CH
 
 
 def dot(left, right):
@@ -28,7 +30,20 @@
     return lax.dot_general(left, right, (((0,), (0,)), ((), ())), preferred_element_type=F32)
 
 
-V, H, S = pltpu.VMEM, pltpu.HBM, pltpu.SMEM
+V, P_, H, S = "vmem", "pinned", "hbm", "smem"
+SPACES = {V: pltpu.VMEM, P_: pltpu.VMEM, H: pltpu.HBM, S: pltpu.SMEM}
+
+
+def placed_input(space, array):
+    if space in (P_, H):
+        return pltpu.with_memory_space_constraint(array, SPACES[space])
+    return array
+
+
+def placed_output(space, shape, kind):
+    if space in (P_, H):
+        return SPACES[space](shape, kind)
+    return jax.ShapeDtypeStruct(shape, kind)
 
 
 def call(body, ins, outs, scratch=(), copies=0, flops=0):
@@ -37,13 +52,13 @@
         scratch.append(pltpu.SemaphoreType.DMA((copies,)))
     return pl.pallas_call(
         body,
-        out_shape=[jax.ShapeDtypeStruct(shape, kind) for _, shape, kind in outs],
-        in_specs=[pl.BlockSpec(memory_space=space) for space, _ in ins],
-        out_specs=[pl.BlockSpec(memory_space=space) for space, _, _ in outs],
+        out_shape=[placed_output(*out) for out in outs],
+        in_specs=[pl.BlockSpec(memory_space=SPACES[space]) for space, _ in ins],
+        out_specs=[pl.BlockSpec(memory_space=SPACES[space]) for space, _, _ in outs],
         scratch_shapes=scratch,
         compiler_params=pltpu.CompilerParams(vmem_limit_bytes=24 * 1024 * 1024),
         cost_estimate=pl.CostEstimate(flops=flops, bytes_accessed=2000000, transcendentals=0),
-    )(*[array for _, array in ins])
+    )(*[placed_input(*given) for given in ins])
 
 
 def start(sems, *pairs):
@@ -93,9 +108,8 @@
 
 def first_body(
     prior, own_far, plane_far, time_far, down_far,
-    pre_far, hidden_far, cells_far, source_far, strided_out,
-    own, first_plane, first_time, down_plane, pre_out, hidden_out, cells_out, source_out,
-    spread, windows, both, sems,
+    pre_out, hidden_out, cells_out, source_out, strided_out,
+    own, first_plane, first_time, down_plane, spread, windows, both, sems,
 ):
     loads = start(
         sems,
@@ -119,7 +133,6 @@
             if frame >= 2:
                 source_out[frame - 2, par] = planes[par]
         fill_windows(windows, frame * CELLS, planes[0], planes[1])
-    stores = start(sems, (4, source_out, source_far))
     loads[1].wait()
     for tap in range(3):
         for row in range(4):
@@ -135,7 +148,6 @@
             hidden_out[frame, par] = hid[:, par * CH : (par + 1) * CH]
             if frame >= 2:
                 pre_out[frame - 2, par] = pre[:, par * CH : (par + 1) * CH]
-    stores += start(sems, (5, pre_out, pre_far), (6, hidden_out, hidden_far))
     loads[2].wait()
     times = first_time[...].reshape(3 * CH, CH)
     for frame in range(2):
@@ -155,45 +167,54 @@
                         cells_out[rows, lanes] = jnp.zeros((HALF, CH), BF16)
                     else:
                         cells_out[rows, lanes] = by_row[row][where]
-    stores += start(sems, (7, cells_out, cells_far))
     loads[3].wait()
     kernel = down_plane[...].reshape(9 * CH, WIDE)
     strided_out[...] = dot(cells_out[...], kernel).astype(BF16).reshape(2, DOWN, WIDE)
-    for store in stores:
-        store.wait()
+
+
+def rows_body(rows, last_far, sent_out, last_time, spread, padded, turned, sems):
+    loads = start(sems, (0, last_far, last_time))
+    cotan = rows[...].astype(F32)
+    spread[...] = cotan.reshape(HALF * 8, CH)
+    for half in range(2):
+        padded[pl.ds(0, DOWN), pl.ds(half * CH, CH)] = spread[pl.ds(half, DOWN, stride=2), :]
+    padded[pl.ds(DOWN, 8), :] = jnp.zeros((8, WIDE), F32)
+    loads[0].wait()
+    total = padded[pl.ds(0, DOWN), :]
+    for k in range(3):
+        taps = padded[pl.ds(4 * (2 - k), DOWN), :].astype(BF16)
+        total = total + dot_nt(taps, last_time[k])
+    for half in range(2):
+        turned[pl.ds(half, DOWN, stride=2), :] = total[:, half * CH : (half + 1) * CH]
+    both = jnp.concatenate([turned[...].reshape(HALF, 8, CH), cotan], axis=1)
+    sent_out[...] = both.astype(BF16)
 
 
 def cotan_body(
-    own, cotans, down_far, last_far,
-    cot_out, grad_lowered_out, part_out, times_out,
-    last_time, down_time, spread, sems,
+    own, received, down_far,
+    grad_lowered_out, cot_out, part_out, times_out,
+    down_time, spread, sems,
 ):
-    loads = start(sems, (0, last_far, last_time), (1, down_far, down_time))
-    spread[...] = cotans[...].astype(F32).reshape(HALF * 24, CH)
-    cot = []
-    for ahead in range(3):
+    loads = start(sems, (0, down_far, down_time))
+    spread[...] = received[...].astype(F32).reshape(HALF * 16, CH)
+    for at, out in ((0, grad_lowered_out), (8, cot_out)):
         parts = []
         for col in range(4):
             halves = [
-                spread[pl.ds(ahead * 8 + col * 2 + half, HALF, stride=24), :] for half in range(2)
+                spread[pl.ds(at + col * 2 + half, HALF, stride=16), :] for half in range(2)
             ]
             parts.append(jnp.concatenate(halves, axis=1))
-        cot.append(jnp.concatenate(parts, axis=0).astype(BF16))
-        cot_out[ahead] = cot[ahead]
+        out[...] = jnp.concatenate(parts, axis=0).astype(BF16)
     loads[0].wait()
-    grad_lowered = cot[0].astype(F32)
-    for k in range(3):
-        grad_lowered = grad_lowered + dot_nt(cot[2 - k], last_time[k])
-    grad_lowered_out[...] = grad_lowered.astype(BF16)
-    loads[1].wait()
     part_out[...] = dot(own[0], down_time[2])
     times_out[...] = down_time[pl.ds(0, 2)]
 
 
-def middle_body(prior, part, times, grad_lowered, lowered_out, grad_pre_out):
+def middle_body(prior, part, times, grad_lowered, cot, lowered_out, sent_out):
     pre = dot(prior[0], times[0]) + dot(prior[1], times[1]) + part[...]
     lowered_out[...] = (pre * jax.nn.sigmoid(pre)).astype(BF16)
-    grad_pre_out[...] = (grad_lowered[...].astype(F32) * silu_slope(pre)).astype(BF16)
+    sent_out[pl.ds(0, DOWN), :] = (grad_lowered[...].astype(F32) * silu_slope(pre)).astype(BF16)
+    sent_out[pl.ds(DOWN, DOWN), :] = cot[...]
 
 
 BACK = (
@@ -210,7 +231,7 @@
 
 
 def time_grads_body(
-    grad_pre, lowered, cot, prior, own, down_far, plane_far,
+    sent, lowered, prior, own, down_far, plane_far,
     part_out, times_out, kernels_out, grad_down_time_out, grad_last_out, lowered_out,
     down_time, down_plane, turned, sems,
 ):
@@ -224,16 +245,18 @@
             ]
     lowered_out[...] = turned[...].reshape(HALF // 2, 2, 8, CH).astype(BF16)
     taps = (prior[0], prior[1], own[0])
+    grad_pre = sent[pl.ds(0, DOWN), :]
     for k in range(3):
-        down = dot_tn(taps[k], grad_pre[...])
-        last = dot_tn(lowered[...], cot[2 - k])
+        down = dot_tn(taps[k], grad_pre)
         for half in range(2):
             lanes = slice(half * CH, (half + 1) * CH)
             grad_down_time_out[half, pl.ds(k * WIDE, WIDE), :] = down[:, lanes]
-            grad_last_out[half, pl.ds(k * WIDE, WIDE), :] = last[:, lanes]
+    last = dot_tn(lowered[...], sent[pl.ds(DOWN, DOWN), :])
+    for half in range(2):
+        grad_last_out[half] = last[:, half * CH : (half + 1) * CH]
     for load in loads:
         load.wait()
-    part_out[...] = dot_nt(grad_pre[...], down_time[2])
+    part_out[...] = dot_nt(grad_pre, down_time[2])
     times_out[...] = down_time[pl.ds(0, 2)]
     for row_par, col_par, row_off, col_off, row, tap in BACK:
         rows = pl.ds((row_par * 2 + col_par) * CH, CH)
@@ -241,8 +264,12 @@
         kernels_out[rows, lanes] = down_plane[row, tap]
 
 
-def back_body(ahead, part, times, kernels, grad_strided_out, grad_mixed_out, shifted):
-    following = ahead[...]
+def back_body(ahead, part, times, kernels, grad_strided_out, sent_out, shifted):
+    following = ahead[pl.ds(0, DOWN), :]
+    for half in range(2):
+        sent_out[pl.ds(4 * CELLS + half * DOWN, DOWN), :] = ahead[
+            pl.ds(DOWN, DOWN), pl.ds(half * CH, CH)
+        ]
     even = part[...] + dot_nt(following, times[0])
     odd = dot_nt(following, times[1])
     for frame, strided in ((0, even.astype(BF16)), (1, odd.astype(BF16))):
@@ -262,34 +289,30 @@
                 lanes = slice((par * 2 + col_par) * CH, (par * 2 + col_par + 1) * CH)
                 for col in range(4):
                     rows = slice(frame * DOWN + col * HALF, frame * DOWN + (col + 1) * HALF)
-                    grad_mixed_out[frame, par, 2 * col + col_par] = mixed[rows, lanes]
+                    plane = (frame * 2 + par) * COLS + 2 * col + col_par
+                    sent_out[pl.ds(plane * HALF, HALF), :] = mixed[rows, lanes]
 
 
 def plane_grads_body(
-    core, grad_strided, grad_mixed, cells_far, hidden_far, source_far, pre_far, time_far,
-    grad_down_time, grad_last, lowered,
+    core, grad_strided, grad_mixed, cells, hidden, source, pre, time_far,
+    grad_down_time, grad_last, lowered, lowered_rows, ahead,
     mine_out, other_out, windows_out, slope_out, part_out, time_out,
-    cells, hidden, source, pre, flat, sems,
+    flat, sems,
 ):
-    loads = start(
-        sems,
-        (0, cells_far, cells),
-        (1, hidden_far, hidden),
-        (2, source_far, source),
-        (3, pre_far, pre),
-        (4, time_far, time_out),
-    )
-    rows = 2 * 3 * WIDE
+    loads = start(sems, (0, time_far, time_out))
     base = 3 * CH + 18 * CH
-    flat[pl.ds(base, rows), :] = grad_down_time[...].reshape(rows, CH)
-    flat[pl.ds(base + rows, rows), :] = grad_last[...].reshape(rows, CH)
-    loads[0].wait()
+    flat[pl.ds(base, 6 * WIDE), :] = grad_down_time[...].reshape(6 * WIDE, CH)
+    base += 6 * WIDE
+    flat[pl.ds(base, 2 * WIDE), :] = grad_last[...].reshape(2 * WIDE, CH)
+    base += 2 * WIDE
+    last = dot_tn(lowered[...], ahead[pl.ds(DOWN, DOWN), :])
+    for half in range(2):
+        flat[pl.ds(base + half * WIDE, WIDE), :] = last[:, half * CH : (half + 1) * CH]
     down = dot_tn(cells[...], grad_strided[...])
     for half in range(2):
         at = 3 * CH + half * 9 * CH
         flat[pl.ds(at, 9 * CH), :] = down[:, half * CH : (half + 1) * CH]
-    cotan = grad_mixed[...].reshape(4 * CELLS, CH)
-    loads[1].wait()
+    cotan = grad_mixed[pl.ds(0, 4 * CELLS), :]
     for k in range(3):
         taps = hidden[pl.ds(k, 2)].reshape(4 * CELLS, CH)
         flat[pl.ds(k * CH, CH), :] = dot_tn(taps, cotan)
@@ -299,27 +322,30 @@
     other_out[pl.ds(0, half), :] = flat[
         pl.ds(pl.multiple_of((1 - here) * half, 16), half), :
     ].astype(BF16)
-    away = lowered[:, pl.ds(1 - here, 1)].astype(F32).reshape(DOWN, CH)
+    away = lowered_rows[:, pl.ds(1 - here, 1)].astype(F32).reshape(DOWN, CH)
     other_out[pl.ds(half, DOWN), :] = away.astype(BF16)
-    for load in loads[2:]:
-        load.wait()
+    loads[0].wait()
     for frame in range(2):
         fill_windows(windows_out, frame * CELLS, source[frame, 0], source[frame, 1])
     slope_out[...] = silu_slope(pre[...])
     for par in range(2):
-        first, second = [grad_mixed[frame, par].reshape(CELLS, CH) for frame in range(2)]
+        first, second = [
+            grad_mixed[pl.ds((frame * 2 + par) * CELLS, CELLS), :] for frame in range(2)
+        ]
         part_out[0, par] = dot_nt(first, time_out[2]) + dot_nt(second, time_out[1])
         part_out[1, par] = dot_nt(second, time_out[2])
 
 
 def last_body(
-    core, ahead, windows, slope, part, first_time,
+    core, ahead, windows, slope, part, first_time, lowered, early_other,
     mine_out, other_out,
     flat,
 ):
     cotans = [[], []]
     for par in range(2):
-        first, second = [ahead[frame, par].reshape(CELLS, CH) for frame in range(2)]
+        first, second = [
+            ahead[pl.ds((frame * 2 + par) * CELLS, CELLS), :] for frame in range(2)
+        ]
         hidden = (
             part[0, par] + dot_nt(first, first_time[0]),
             part[1, par] + dot_nt(first, first_time[1]) + dot_nt(second, first_time[0]),
@@ -334,18 +360,25 @@
             flat[pl.ds((row * 3 + tap) * CH, CH), :] = (
                 product[at : at + CH, :CH] + product[at + CH : at + 2 * CH, CH:]
             )
+    further = [ahead[pl.ds(4 * CELLS + half * DOWN, DOWN), :] for half in range(2)]
+    for half in range(2):
+        flat[pl.ds(9 * CH + half * WIDE, WIDE), :] = dot_tn(lowered[...], further[half])
     here = core[0]
     half = mine_out.shape[0]
     mine_out[...] = flat[pl.ds(pl.multiple_of(here * half, 16), half), :]
-    other_out[...] = flat[pl.ds(pl.multiple_of((1 - here) * half, 16), half), :].astype(BF16)
-
-
-def halves_body(early, early_other, late, late_other, half_out):
+    rows = early_other.shape[0]
+    other_out[pl.ds(0, rows), :] = early_other[...]
+    other_out[pl.ds(rows, half), :] = flat[
+        pl.ds(pl.multiple_of((1 - here) * half, 16), half), :
+    ].astype(BF16)
+
+
+def halves_body(early, late, other, half_out):
     rows, more = early.shape[0], late.shape[0]
-    half_out[pl.ds(0, rows), :] = (
-        early[...] + early_other[pl.ds(0, rows), :].astype(F32)
+    half_out[pl.ds(0, rows), :] = (early[...] + other[pl.ds(0, rows), :].astype(F32)).astype(BF16)
+    half_out[pl.ds(rows, more), :] = (
+        late[...] + other[pl.ds(rows + DOWN, more), :].astype(F32)
     ).astype(BF16)
-    half_out[pl.ds(rows, more), :] = (late[...] + late_other[...].astype(F32)).astype(BF16)
 
 
 def sum_body(core, blocks, own, other, sent_out, padded):
@@ -359,7 +392,7 @@
     sent_out[:, pl.ds(0, 16), :] = padded[...].reshape(chips, 16, CH).astype(BF16)
     here = core[0]
     mine = own[:, pl.ds(here, 1)].astype(F32).reshape(chips, 8, CH)
-    theirs = other[pl.ds(other.shape[0] - DOWN, DOWN), :].astype(F32).reshape(chips, 8, CH)
+    theirs = other[pl.ds(EARLY // 2, DOWN), :].astype(F32).reshape(chips, 8, CH)
     frames = [jnp.where(here == 0, mine, theirs), jnp.where(here == 0, theirs, mine)]
     sent_out[:, pl.ds(16, 16), :] = jnp.concatenate(frames, axis=1).astype(BF16)
 
@@ -381,20 +414,25 @@
         part_out[block] = part
 
 
-def results_body(core, mine, other, first_plane_out, *rest):
-    outs, early, late = rest[:-2], rest[-2], rest[-1]
+def results_body(
+    core, mine, other,
+    first_plane_out, first_time_out, down_plane_out, down_time_out, last_time_out,
+    early, late,
+):
     here = core[0]
-    rows, more = early.shape[0] // 2, late.shape[0] // 2
+    rows, more = EARLY // 2, LATE // 2
     for half, at in ((mine, here), (other, 1 - here)):
         early[pl.ds(pl.multiple_of(at * rows, 16), rows), :] = half[pl.ds(0, rows), :]
         late[pl.ds(pl.multiple_of(at * more, 16), more), :] = half[pl.ds(rows, more), :]
-    first_plane_out[...] = late[...]
-    first = 0
-    for out in outs:
-        count, lanes = out.shape
-        for part in range(lanes // CH):
-            out[:, pl.ds(part * CH, CH)] = early[pl.ds(first, count), :]
-            first += count
+    first_plane_out[...] = late[pl.ds(0, 9 * CH), :]
+    first_time_out[...] = early[pl.ds(0, 3 * CH), :]
+    for half in range(2):
+        lanes = pl.ds(half * CH, CH)
+        down_plane_out[:, lanes] = early[pl.ds(3 * CH + half * 9 * CH, 9 * CH), :]
+        down_time_out[:, lanes] = early[pl.ds(21 * CH + half * 6 * CH, 6 * CH), :]
+        last_time_out[pl.ds(0, WIDE), lanes] = late[pl.ds(9 * CH + half * WIDE, WIDE), :]
+        last_time_out[pl.ds(WIDE, WIDE), lanes] = early[pl.ds(37 * CH + half * WIDE, WIDE), :]
+        last_time_out[pl.ds(2 * WIDE, WIDE), lanes] = early[pl.ds(33 * CH + half * WIDE, WIDE), :]
 
 
 def output_body(received, last_time, output, spread, padded):
@@ -440,130 +478,133 @@
 def local(clip_in, first_plane, first_time, down_plane, down_time, last_time, cotan_out):
     own = clip_in.reshape(4 * CELLS, CH)
     prior = from_behind(own, 1)
-    rows = cotan_out[0].reshape(HALF, 8, CH)
-    rows_ahead = jnp.pad(rows, ((0, 2), (0, 0), (0, 0)))
-    cotans = jnp.concatenate([rows, rows_ahead[1 : HALF + 1], rows_ahead[2:]], axis=1)
-    cotans, prior = lax.optimization_barrier((cotans, prior))
-    cotans = exchange_seq(cotans)
-    frames = (2, 2, COLS, HALF, CH)
+    (sent,) = call(
+        rows_body,
+        [(V, cotan_out[0].reshape(HALF, 8, CH)), (H, last_time)],
+        [(V, (HALF, 16, CH), BF16)],
+        [
+            ((3, WIDE, WIDE), BF16),
+            ((HALF * 8, CH), F32),
+            ((DOWN + 8, WIDE), F32),
+            ((HALF * 8, CH), F32),
+        ],
+        copies=1,
+        flops=60000000,
+    )
+    sent, prior = lax.optimization_barrier((sent, prior))
+    received = exchange_seq(sent)
     flat_frames = (2, 2, CELLS, CH)
-    far = [
-        (H, flat_frames, F32),
-        (H, (4, 2, CELLS, CH), BF16),
-        (H, (2 * DOWN, 9 * CH), BF16),
-        (H, frames, BF16),
-    ]
     pre_first, hidden, cells, source, strided = call(
         first_body,
         [(V, prior), (H, own), (H, first_plane), (H, first_time), (H, down_plane)],
-        [*far, (V, (2, DOWN, WIDE), BF16)],
+        [
+            (P_, flat_frames, F32),
+            (P_, (4, 2, CELLS, CH), BF16),
+            (P_, (2 * DOWN, 9 * CH), BF16),
+            (P_, (2, 2, COLS, HALF, CH), BF16),
+            (P_, (2, DOWN, WIDE), BF16),
+        ],
         [
             ((4 * CELLS, CH), BF16),
             ((3, 3, CH, CH), BF16),
             ((3, CH, CH), BF16),
             ((3, 3, CH, WIDE), BF16),
-            *[(shape, kind) for _, shape, kind in far],
             ((2 * CELLS, CH), F32),
             ((4 * CELLS, 12 * CH), BF16),
             ((12 * CH, WIDE), BF16),
         ],
-        copies=8,
+        copies=4,
         flops=2000000000,
     )
     strided_prior = from_behind(strided, 1)
-    times = (V, (2, WIDE, WIDE), BF16)
-    cot, grad_lowered, part, near_times = call(
+    times = (P_, (2, WIDE, WIDE), BF16)
+    down = (P_, (DOWN, WIDE), BF16)
+    grad_lowered, cot, part, near_times = call(
         cotan_body,
-        [(V, strided), (V, cotans), (H, down_time), (H, last_time)],
-        [(V, (3, DOWN, WIDE), BF16), (V, (DOWN, WIDE), BF16), (V, (DOWN, WIDE), F32), times],
-        [((3, WIDE, WIDE), BF16), ((3, WIDE, WIDE), BF16), ((HALF * 24, CH), F32)],
-        copies=2,
+        [(P_, strided), (V, received), (H, down_time)],
+        [down, down, (P_, (DOWN, WIDE), F32), times],
+        [((3, WIDE, WIDE), BF16), ((HALF * 16, CH), F32)],
+        copies=1,
         flops=100000000,
     )
-    lowered, grad_pre = call(
+    lowered, sent = call(
         middle_body,
-        [(V, strided_prior), (V, part), (V, near_times), (V, grad_lowered)],
-        [(V, (DOWN, WIDE), BF16), (V, (DOWN, WIDE), BF16)],
+        [(V, strided_prior), (P_, part), (P_, near_times), (P_, grad_lowered), (P_, cot)],
+        [down, (P_, (2 * DOWN, WIDE), BF16)],
         flops=60000000,
     )
-    grad_pre_next = from_behind(grad_pre, -1)
-    part, near_times, kernels, grad_down_time, grad_last, lowered = call(
+    ahead = from_behind(sent, -1)
+    part, near_times, kernels, grad_down_time, grad_last, lowered_rows = call(
         time_grads_body,
         [
-            (V, grad_pre), (V, lowered), (V, cot), (V, strided_prior), (V, strided),
+            (P_, sent), (P_, lowered), (V, strided_prior), (P_, strided),
             (H, down_time), (H, down_plane),
         ],
         [
-            (V, (DOWN, WIDE), F32),
+            (P_, (DOWN, WIDE), F32),
             times,
-            (V, (4 * CH, 4 * WIDE), BF16),
-            (V, (2, 3 * WIDE, CH), F32),
-            (V, (2, 3 * WIDE, CH), F32),
-            (V, (HALF // 2, 2, 8, CH), BF16),
+            (P_, (4 * CH, 4 * WIDE), BF16),
+            (P_, (2, 3 * WIDE, CH), F32),
+            (P_, (2, WIDE, CH), F32),
+            (P_, (HALF // 2, 2, 8, CH), BF16),
         ],
         [((3, WIDE, WIDE), BF16), ((3, 3, CH, WIDE), BF16), ((HALF * 8, CH), F32)],
         copies=2,
         flops=120000000,
     )
-    grad_strided, grad_mixed = call(
+    grad_strided, sent = call(
         back_body,
-        [(V, grad_pre_next), (V, part), (V, near_times), (V, kernels)],
-        [(V, (2 * DOWN, WIDE), BF16), (V, frames, BF16)],
+        [(V, ahead), (P_, part), (P_, near_times), (P_, kernels)],
+        [(P_, (2 * DOWN, WIDE), BF16), (P_, (4 * CELLS + 2 * DOWN, CH), BF16)],
         [((2 * DOWN, 4 * WIDE), BF16)],
         flops=300000000,
     )
-    grad_mixed_next = from_behind(grad_mixed, -1)
+    further = from_behind(sent, -1)
     core = (lax.axis_index("seq") % 2).astype(jnp.int32).reshape(1)
-    early_rows = (3 + 18 + 12 + 12) * CH
-    late_rows = 9 * CH
     early, early_other, windows, slope, part, near_time = call(
         plane_grads_body,
         [
-            (S, core), (V, grad_strided), (V, grad_mixed),
-            (H, cells), (H, hidden), (H, source), (H, pre_first), (H, first_time),
-            (V, grad_down_time), (V, grad_last), (V, lowered),
-        ],
-        [
-            (V, (early_rows // 2, CH), F32),
-            (V, (early_rows // 2 + DOWN, CH), BF16),
-            (V, (2 * CELLS, 12 * CH), BF16),
-            (V, flat_frames, F32),
-            (V, flat_frames, F32),
-            (V, (3, CH, CH), BF16),
-        ],
-        [
-            ((2 * DOWN, 9 * CH), BF16),
-            ((4, 2, CELLS, CH), BF16),
-            (frames, BF16),
-            (flat_frames, F32),
-            ((early_rows, CH), F32),
-        ],
-        copies=5,
+            (S, core), (P_, grad_strided), (P_, sent),
+            (P_, cells), (P_, hidden), (P_, source), (P_, pre_first), (H, first_time),
+            (P_, grad_down_time), (P_, grad_last), (P_, lowered), (P_, lowered_rows), (V, ahead),
+        ],
+        [
+            (P_, (EARLY // 2, CH), F32),
+            (P_, (EARLY // 2 + DOWN, CH), BF16),
+            (P_, (2 * CELLS, 12 * CH), BF16),
+            (P_, flat_frames, F32),
+            (P_, flat_frames, F32),
+            (P_, (3, CH, CH), BF16),
+        ],
+        [((EARLY, CH), F32)],
+        copies=1,
         flops=500000000,
     )
-    early_other = swap_cores(early_other)
-    late, late_other = call(
+    late, other = call(
         last_body,
-        [(S, core), (V, grad_mixed_next), (V, windows), (V, slope), (V, part), (V, near_time)],
-        [(V, (late_rows // 2, CH), F32), (V, (late_rows // 2, CH), BF16)],
-        [((late_rows, CH), F32)],
+        [
+            (S, core), (V, further), (P_, windows), (P_, slope), (P_, part), (P_, near_time),
+            (P_, lowered), (P_, early_other),
+        ],
+        [(P_, (LATE // 2, CH), F32), (P_, ((EARLY + LATE) // 2 + DOWN, CH), BF16)],
+        [((LATE, CH), F32)],
         flops=600000000,
     )
-    late_other = swap_cores(late_other)
 
     clips = lax.axis_size("clip")
     chips = lax.axis_size("seq") // 2
-    half_rows = (early_rows + late_rows) // 2
+    half_rows = (EARLY + LATE) // 2
     part_rows = half_rows // clips
+    other = swap_cores(other)
     (half,) = call(
         halves_body,
-        [(V, early), (V, early_other), (V, late), (V, late_other)],
-        [(V, (half_rows, CH), BF16)],
+        [(P_, early), (P_, late), (V, other)],
+        [(P_, (half_rows, CH), BF16)],
     )
     blocks = exchange_clip(half.reshape(clips, part_rows, CH))
     (sent,) = call(
         sum_body,
-        [(S, core), (V, blocks), (V, lowered), (V, early_other)],
+        [(S, core), (V, blocks), (P_, lowered_rows), (V, other)],
         [(V, (chips, 32, CH), BF16)],
         [((16 * chips, CH), F32)],
     )
@@ -590,7 +631,7 @@
             (V, (3 * WIDE, WIDE), BF16),
             (V, (3 * WIDE, WIDE), BF16),
         ],
-        [((early_rows, CH), BF16), ((late_rows, CH), BF16)],
+        [((EARLY, CH), BF16), ((LATE, CH), BF16)],
     )
     shapes = ((3, 3, CH, CH), (3, CH, CH), (3, 3, CH, WIDE), (3, WIDE, WIDE), (3, WIDE, WIDE))
     grads = [grad.reshape(shape) for grad, shape in zip(grads, shapes)]

time: 157 us -> 146 us (0.930)
  local copies, waits for them, and re-layouts: 11 us -> 4.12 us
  starting transfers between devices: 41.8 us -> 39.2 us
    unnamed x28 -> x10, local copies, waits for them, and re-layouts: 9.47 us -> 2.6 us
    ppermute x4, waiting for transfers between devices: 8.13 us -> 5.17 us  [from_behind(): return lax.ppermute(block, 'seq', route)]
    all_to_all x1, waiting for transfers between devices: 6.81 us -> 8.83 us  [exchange_seq(): lax.all_to_all(blocks, 'seq', split_axis=0, concat_axis=0, tiled=True)]
    ppermute x3 -> x2, starting transfers between devices: 10.7 us -> 8.82 us  [swap_cores(): return lax.ppermute(block, 'seq', [(i, i ^ 1) for i in range(count)])]
    ppermute x3 -> x2, waiting for transfers between devices: 2.49 us -> 3.58 us  [swap_cores(): return lax.ppermute(block, 'seq', [(i, i ^ 1) for i in range(count)])]
    pallas_call x13 -> x14, Pallas kernels: 14 us -> 13.4 us  [call(): pl.pallas_call(body, out_shape=[placed_output(*out) for out in outs], in_...]
  transfers between devices with their start and end apart: 8 -> 7, of which waited for: 5 -> 6; matrix products, arithmetic and copies ran while one was open for 1% -> 1% of each run, Pallas kernels for 5% -> 7%
where the time goes in v5:
time: 146 us; the launch traced here: 145 us
  blocking collectives  69.8 us (48%)
  starting transfers between devices  39.2 us (27%)
  waiting for transfers between devices  17.6 us (12%)
  Pallas kernels  13.4 us (9%)
  local copies, waits for them, and re-layouts  4.12 us (3%)
    all_to_all x2, blocking collectives, exchange_clip(): lax.all_to_all(blocks, 'clip', split_axis=0, concat_axis=0, tiled=True)  36.7 us
    all_to_all x2, blocking collectives, exchange_depth(): lax.all_to_all(blocks, 'seq', split_axis=0, concat_axis=0, axis_index_gro...  33.1 us
    all_to_all x1, starting transfers between devices, exchange_seq(): lax.all_to_all(blocks, 'seq', split_axis=0, concat_axis=0, tiled=True)  16.5 us
    ppermute x4, starting transfers between devices, from_behind(): return lax.ppermute(block, 'seq', route)  13.9 us
    pallas_call x14, Pallas kernels, call(): pl.pallas_call(body, out_shape=[placed_output(*out) for out in outs], in_...  13.4 us
    all_to_all x1, waiting for transfers between devices, exchange_seq(): lax.all_to_all(blocks, 'seq', split_axis=0, concat_axis=0, tiled=True)  8.83 us
    ppermute x2, starting transfers between devices, swap_cores(): return lax.ppermute(block, 'seq', [(i, i ^ 1) for i in range(count)])  8.82 us
    ppermute x4, waiting for transfers between devices, from_behind(): return lax.ppermute(block, 'seq', route)  5.17 us
  transfers between devices with their start and end apart: 7, of which 6 were waited for; matrix products, arithmetic and copies ran while one was open for 1% of the time, Pallas kernels for 7%

profile of v5, /device:TPU:1, one launch (start us, length us, event | category | flops | bytes accessed | tf_op | source)
XLA Modules:
  0.0 145.0 jit_solution(17292633507061875315)
XLA Ops:
  0.6 4.9 %collective-permute-start = (bf16[1024,128]{1,0:T(8,128)(2,1)}, bf16[1024,128]{1,0:T(8,128)(2,1)S(1)}, u32[]{:S(2)}, u32[]{:S(2)}) collective-permute-start(bf16[1024,128]{1,0:T(8,128)(2,1)} %bitcast.18), channel_id=1, source_target_pairs={{0,1},{1,2},{2,3},{3,4},{4,5},{5,6},{6,7},{7,8},{8,9},{9,10},{10,1... | collective-permute-start | bytes 786440 | tf_op jit(solution)/shard_map/ppermute | solution.py:454
  5.6 0.9 reshape_squeeze.3.rows
  6.5 2.0 %shard_map.118 = bf16[32,16,128]{2,1,0:T(8,128)(2,1)} custom-call(bf16[32,8,128]{2,1,0:T(8,128)(2,1)S(1)} %reshape_squeeze.3.rows, bf16[3,256,256]{2,1,0:T(8,128)(2,1)} %last_time.1), custom_call_target="tpu_custom_call" | custom-call | flops 60000000 | bytes 2000000 | tf_op jit(solution)/shard_map/pallas_call | solution.py:53
  8.4 1.6 %collective-permute-done.prior = bf16[1024,128]{1,0:T(8,128)(2,1)S(1)} collective-permute-done((bf16[1024,128]{1,0:T(8,128)(2,1)}, bf16[1024,128]{1,0:T(8,128)(2,1)S(1)}, u32[]{:S(2)}, u32[]{:S(2)}) %collective-permute-start) | collective-permute-done | bytes 262176 | tf_op jit(solution)/shard_map/ppermute | solution.py:454
  10.0 16.5 %all-to-all-start = ((bf16[32,16,128]{2,1,0:T(8,128)(2,1)}), bf16[32,16,128]{2,1,0:T(8,128)(2,1)S(1)}, u32[]{:S(2)}, u32[]{:S(2)}) async-start(bf16[32,16,128]{2,1,0:T(8,128)(2,1)} %shard_map.118), calls=%async_computation | async-start | bytes 262144 | tf_op jit(solution)/shard_map/all_to_all | solution.py:467
  26.5 3.5 %shard_map.119 = (f32[2,2,256,128]{3,2,1,0:T(8,128)S(1)}, bf16[4,2,256,128]{3,2,1,0:T(8,128)(2,1)S(1)}, bf16[256,1152]{1,0:T(8,128)(2,1)S(1)}, bf16[2,2,8,32,128...) custom-call(bf16[1024,128]{1,0:T(8,128)(2,1)S(1)} %collective-permute-done.prior, bf16[1024,128]{1,0:T(8,128)(2,1)} %bitcast.19, ...), custom_call_target="tpu_custom_call" | custom-call | flops 2000000000 | bytes 2000000 | tf_op jit(solution)/shard_map/pallas_call | solution.py:53
  30.0 3.5 %collective-permute-start.1 = (bf16[2,128,256]{2,1,0:T(8,128)(2,1)S(1)}, bf16[2,128,256]{2,1,0:T(8,128)(2,1)S(1)}, u32[]{:S(2)}, u32[]{:S(2)}) collective-permute-start(bf16[2,128,256]{2,1,0:T(8,128)(2,1)S(1)} %get-tuple-element.41.own), channel_id=1, source_target_pairs={{0,1},{1,2},{2,3},{3,4},{4,5},{5,6},{6,7},{7,8},{8,9},{9,10},{10,1... | collective-permute-start | bytes 393224 | tf_op jit(solution)/shard_map/ppermute | solution.py:454
  33.5 8.8 %all-to-all-done.received = bf16[32,16,128]{2,1,0:T(8,128)(2,1)S(1)} async-done(((bf16[32,16,128]{2,1,0:T(8,128)(2,1)}), bf16[32,16,128]{2,1,0:T(8,128)(2,1)S(1)}, u32[]{:S(2)}, u32[]{:S(2)}) %all-to-all-start) | async-done | bytes 131104 | tf_op jit(solution)/shard_map/all_to_all | solution.py:467
  42.4 1.2 shard_map.120
  43.6 0.2 shard_map.121
  43.8 3.5 %collective-permute-start.2 = (bf16[256,256]{1,0:T(8,128)(2,1)S(1)}, bf16[256,256]{1,0:T(8,128)(2,1)S(1)}, u32[]{:S(2)}, u32[]{:S(2)}) collective-permute-start(bf16[256,256]{1,0:T(8,128)(2,1)S(1)} %get-tuple-element.47.sent), channel_id=1, source_target_pairs={{1,0},{2,1},{3,2},{4,3},{5,4},{6,5},{7,6},{8,7},{9,8},{10,9},{11,1... | collective-permute-start | bytes 393224 | tf_op jit(solution)/shard_map/ppermute | solution.py:454
  47.3 1.5 %shard_map.122 = (f32[128,256]{1,0:T(8,128)S(1)}, bf16[2,256,256]{2,1,0:T(8,128)(2,1)S(1)}, bf16[512,1024]{1,0:T(8,128)(2,1)S(1)}, f32[2,768,128]{2,1,0:T(8,128)...) custom-call(bf16[256,256]{1,0:T(8,128)(2,1)S(1)} %get-tuple-element.47.sent, ...), custom_call_target="tpu_custom_call" | custom-call | flops 120000000 | bytes 2000000 | tf_op jit(solution)/shard_map/pallas_call | solution.py:53
  48.9 0.7 copy-done.3
  49.6 0.5 collective-permute-done.2.ahead
  50.1 0.6 shard_map.123
  50.7 1.9 %collective-permute-start.3 = (bf16[1280,128]{1,0:T(8,128)(2,1)S(1)}, bf16[1280,128]{1,0:T(8,128)(2,1)S(1)}, u32[]{:S(2)}, u32[]{:S(2)}) collective-permute-start(bf16[1280,128]{1,0:T(8,128)(2,1)S(1)} %get-tuple-element.53.grad_mixed), channel_id=1, source_target_pairs={{1,0},{2,1},{3,2},{4,3},{5,4},{6,5},{7,6},{8,7},{9,8},{10,9},{11,1... | collective-permute-start | bytes 983048 | tf_op jit(solution)/shard_map/ppermute | solution.py:454
  52.6 0.9 copy-done.2
  53.6 0.9 copy-done.4
  54.5 1.5 %shard_map.124 = (f32[2624,128]{1,0:T(8,128)S(1)}, bf16[2752,128]{1,0:T(8,128)(2,1)S(1)}, bf16[512,1536]{1,0:T(8,128)(2,1)S(1)}, f32[2,2,256,128]{3,2,1,0:T(8,12...) custom-call(s32[1]{0:T(128)} %bitcast.core, ...), custom_call_target="tpu_custom_call" | custom-call | flops 500000000 | bytes 2000000 | tf_op jit(solution)/shard_map/pallas_call | solution.py:53
  56.0 3.1 %collective-permute-done.3.ahead = bf16[1280,128]{1,0:T(8,128)(2,1)S(1)} collective-permute-done((bf16[1280,128]{1,0:T(8,128)(2,1)S(1)}, bf16[1280,128]{1,0:T(8,128)(2,1)S(1)}, u32[]{:S(2)}, u32[]{:S(2)}) %collective-permute-start.3) | collective-permute-done | bytes 327712 | tf_op jit(solution)/shard_map/ppermute | solution.py:454
  59.1 0.9 shard_map.125
  60.0 1.9 %collective-permute-start.4 = (bf16[3584,128]{1,0:T(8,128)(2,1)S(1)}, bf16[3584,128]{1,0:T(8,128)(2,1)S(1)}, u32[]{:S(2)}, u32[]{:S(2)}) collective-permute-start(bf16[3584,128]{1,0:T(8,128)(2,1)S(1)} %get-tuple-element.68), channel_id=1, source_target_pairs={{0,1},{1,0},{2,3},{3,2},{4,5},{5,4},{6,7},{7,6},{8,9},{9,8},{10,11... | collective-permute-start | bytes 2752520 | tf_op jit(solution)/shard_map/ppermute | solution.py:459
  61.9 2.4 %collective-permute-done.4.other = bf16[3584,128]{1,0:T(8,128)(2,1)S(1)} collective-permute-done((bf16[3584,128]{1,0:T(8,128)(2,1)S(1)}, bf16[3584,128]{1,0:T(8,128)(2,1)S(1)}, u32[]{:S(2)}, u32[]{:S(2)}) %collective-permute-start.4) | collective-permute-done | bytes 917536 | tf_op jit(solution)/shard_map/ppermute | solution.py:459
  64.5 20.6 %all_to_all.25.blocks = bf16[16,216,128]{2,1,0:T(8,128)(2,1)S(1)} all-to-all(bf16[16,216,128]{2,1,0:T(8,128)(2,1)S(1)} %bitcast.10), channel_id=1, replica_groups=mesh['clip'=16,'seq'=32] {'clip'}, dimensions={0} | all-to-all | bytes 1769472 | tf_op jit(solution)/shard_map/all_to_all | solution.py:463
  85.3 17.2 %all_to_all.26.received = bf16[16,32,128]{2,1,0:T(8,128)(2,1)S(1)} all-to-all(bf16[16,32,128]{2,1,0:T(8,128)(2,1)S(1)} %shard_map.127), channel_id=1, replica_groups={{0,2,4,6,8,10,12,14,16,18,20,22,24,26,28,30},{1,3,5,7,9,11,13,15,17,19,..., dimensions={0} | all-to-all | bytes 262144 | tf_op jit(solution)/shard_map/all_to_all | solution.py:473
  102.5 15.8 %all_to_all.27.pieces = bf16[16,16,128]{2,1,0:T(8,128)(2,1)S(1)} all-to-all(bf16[16,16,128]{2,1,0:T(8,128)(2,1)S(1)} %shard_map.129), channel_id=1, replica_groups={{0,2,4,6,8,10,12,14,16,18,20,22,24,26,28,30},{1,3,5,7,9,11,13,15,17,19,..., dimensions={0} | all-to-all | bytes 131072 | tf_op jit(solution)/shard_map/all_to_all | solution.py:473
  118.5 16.1 %all_to_all.28 = bf16[16,216,128]{2,1,0:T(8,128)(2,1)S(1)} all-to-all(bf16[16,216,128]{2,1,0:T(8,128)(2,1)S(1)} %shard_map.130), channel_id=1, replica_groups=mesh['clip'=16,'seq'=32] {'clip'}, dimensions={0} | all-to-all | bytes 1769472 | tf_op jit(solution)/shard_map/all_to_all | solution.py:463
  134.6 6.9 %collective-permute-start.5 = (bf16[3456,128]{1,0:T(8,128)(2,1)S(1)}, bf16[3456,128]{1,0:T(8,128)(2,1)S(1)}, u32[]{:S(2)}, u32[]{:S(2)}) collective-permute-start(bf16[3456,128]{1,0:T(8,128)(2,1)S(1)} %bitcast.11), channel_id=1, source_target_pairs={{0,1},{1,0},{2,3},{3,2},{4,5},{5,4},{6,7},{7,6},{8,9},{9,8},{10,11... | collective-permute-start | bytes 2654216 | tf_op jit(solution)/shard_map/ppermute | solution.py:459
  141.5 0.2 shard_map.128
  141.8 0.7 reshape.45
  142.4 1.1 collective-permute-done.5.other
  143.6 1.4 shard_map.131
  (12 shorter events, 0.5 us)
Async XLA Ops:
  0.6 9.4 %collective-permute-start = (bf16[1024,128]{1,0:T(8,128)(2,1)}, bf16[1024,128]{1,0:T(8,128)(2,1)S(1)}, u32[]{:S(2)}, u32[]{:S(2)}) collective-permute-start(bf16[1024,128]{1,0:T(8,128)(2,1)} %bitcast.18), channel_id=1, source_target_pairs={{0,1},{1,2},{2,3},{3,4},{4,5},{5,6},{6,7},{7,8},{8,9},{9,10},{10,1... | collective-permute-start | bytes 786440 | tf_op jit(solution)/shard_map/ppermute | solution.py:454
  10.0 32.3 %all-to-all-start = ((bf16[32,16,128]{2,1,0:T(8,128)(2,1)}), bf16[32,16,128]{2,1,0:T(8,128)(2,1)S(1)}, u32[]{:S(2)}, u32[]{:S(2)}) async-start(bf16[32,16,128]{2,1,0:T(8,128)(2,1)} %shard_map.118), calls=%async_computation | async-start | bytes 262144 | tf_op jit(solution)/shard_map/all_to_all | solution.py:467
  30.0 17.4 %copy-start.1 = (bf16[2,2,8,32,128]{4,3,2,1,0:T(8,128)(2,1)}, bf16[2,2,8,32,128]{4,3,2,1,0:T(8,128)(2,1)S(1)}, u32[]{:S(2)}) copy-start(bf16[2,2,8,32,128]{4,3,2,1,0:T(8,128)(2,1)S(1)} %get-tuple-element.56.source) | copy-start | bytes 786436
  30.0 13.6 %collective-permute-start.1 = (bf16[2,128,256]{2,1,0:T(8,128)(2,1)S(1)}, bf16[2,128,256]{2,1,0:T(8,128)(2,1)S(1)}, u32[]{:S(2)}, u32[]{:S(2)}) collective-permute-start(bf16[2,128,256]{2,1,0:T(8,128)(2,1)S(1)} %get-tuple-element.41.own), channel_id=1, source_target_pairs={{0,1},{1,2},{2,3},{3,4},{4,5},{5,6},{6,7},{7,8},{8,9},{9,10},{10,1... | collective-permute-start | bytes 393224 | tf_op jit(solution)/shard_map/ppermute | solution.py:454
  43.8 6.3 %collective-permute-start.2 = (bf16[256,256]{1,0:T(8,128)(2,1)S(1)}, bf16[256,256]{1,0:T(8,128)(2,1)S(1)}, u32[]{:S(2)}, u32[]{:S(2)}) collective-permute-start(bf16[256,256]{1,0:T(8,128)(2,1)S(1)} %get-tuple-element.47.sent), channel_id=1, source_target_pairs={{1,0},{2,1},{3,2},{4,3},{5,4},{6,5},{7,6},{8,7},{9,8},{10,9},{11,1... | collective-permute-start | bytes 393224 | tf_op jit(solution)/shard_map/ppermute | solution.py:454
  48.9 0.7 copy-start.3
  50.7 8.4 %collective-permute-start.3 = (bf16[1280,128]{1,0:T(8,128)(2,1)S(1)}, bf16[1280,128]{1,0:T(8,128)(2,1)S(1)}, u32[]{:S(2)}, u32[]{:S(2)}) collective-permute-start(bf16[1280,128]{1,0:T(8,128)(2,1)S(1)} %get-tuple-element.53.grad_mixed), channel_id=1, source_target_pairs={{1,0},{2,1},{3,2},{4,3},{5,4},{6,5},{7,6},{8,7},{9,8},{10,9},{11,1... | collective-permute-start | bytes 983048 | tf_op jit(solution)/shard_map/ppermute | solution.py:454
  52.6 1.0 copy-start.2
  53.6 0.9 copy-start.4
  60.0 4.4 %collective-permute-start.4 = (bf16[3584,128]{1,0:T(8,128)(2,1)S(1)}, bf16[3584,128]{1,0:T(8,128)(2,1)S(1)}, u32[]{:S(2)}, u32[]{:S(2)}) collective-permute-start(bf16[3584,128]{1,0:T(8,128)(2,1)S(1)} %get-tuple-element.68), channel_id=1, source_target_pairs={{0,1},{1,0},{2,3},{3,2},{4,5},{5,4},{6,7},{7,6},{8,9},{9,8},{10,11... | collective-permute-start | bytes 2752520 | tf_op jit(solution)/shard_map/ppermute | solution.py:459
  102.5 39.0 %copy-start = (bf16[3,256,256]{2,1,0:T(8,128)(2,1)S(1)}, bf16[3,256,256]{2,1,0:T(8,128)(2,1)}, u32[]{:S(2)}) copy-start(bf16[3,256,256]{2,1,0:T(8,128)(2,1)} %last_time.1) | copy-start | bytes 1179652
  134.6 8.9 %collective-permute-start.5 = (bf16[3456,128]{1,0:T(8,128)(2,1)S(1)}, bf16[3456,128]{1,0:T(8,128)(2,1)S(1)}, u32[]{:S(2)}, u32[]{:S(2)}) collective-permute-start(bf16[3456,128]{1,0:T(8,128)(2,1)S(1)} %bitcast.11), channel_id=1, source_target_pairs={{0,1},{1,0},{2,3},{3,2},{4,5},{5,4},{6,7},{7,6},{8,9},{9,8},{10,11... | collective-permute-start | bytes 2654216 | tf_op jit(solution)/shard_map/ppermute | solution.py:459

commit v6 on v5

--- a/solution.py
+++ b/solution.py
@@ -16,6 +16,7 @@
 WIDE = 256
 EARLY = (3 + 18 + 12 + 8) * CH
 LATE = (9 + 4) * CH
+NEAR = 4
 
 
 def dot(left, right):
@@ -106,55 +107,36 @@
     return sigma * (1.0 + preact * (1.0 - sigma))
 
 
+def parity_planes(source, frame, spread):
+    spread[...] = source[pl.ds(frame * 2 * CELLS, 2 * CELLS), :].astype(F32)
+    planes = []
+    for par in range(2):
+        cols = [spread[pl.ds(par * COLS + col, HALF, stride=2 * COLS), :] for col in range(COLS)]
+        planes.append(jnp.stack(cols, axis=0).astype(BF16))
+    return planes
+
+
 def first_body(
-    prior, own_far, plane_far, time_far, down_far,
-    pre_out, hidden_out, cells_out, source_out, strided_out,
-    own, first_plane, first_time, down_plane, spread, windows, both, sems,
+    prior, acts, both, time_far, down_far,
+    hidden_out, cells_out, strided_out,
+    first_time, down_plane, spread, windows, sems,
 ):
-    loads = start(
-        sems,
-        (0, own_far, own),
-        (1, plane_far, first_plane),
-        (2, time_far, first_time),
-        (3, down_far, down_plane),
-    )
-    both[...] = jnp.zeros_like(both)
-    for frame in range(4):
-        if frame == 2:
-            loads[0].wait()
-        source = prior if frame < 2 else own
-        spread[...] = source[pl.ds(frame % 2 * 2 * CELLS, 2 * CELLS), :].astype(F32)
-        planes = []
-        for par in range(2):
-            cols = [
-                spread[pl.ds(par * COLS + col, HALF, stride=2 * COLS), :] for col in range(COLS)
-            ]
-            planes.append(jnp.stack(cols, axis=0).astype(BF16))
-            if frame >= 2:
-                source_out[frame - 2, par] = planes[par]
-        fill_windows(windows, frame * CELLS, planes[0], planes[1])
-    loads[1].wait()
-    for tap in range(3):
-        for row in range(4):
-            rows = pl.ds((tap * 4 + row) * CH, CH)
-            if row < 3:
-                both[rows, pl.ds(0, CH)] = first_plane[row, tap]
-            if row > 0:
-                both[rows, pl.ds(CH, CH)] = first_plane[row - 1, tap]
-    for frame in range(4):
+    loads = start(sems, (0, time_far, first_time), (1, down_far, down_plane))
+    for frame in range(2):
+        fill_windows(windows, frame * CELLS, *parity_planes(prior, frame, spread))
+    for frame in range(2):
         pre = dot(windows[pl.ds(frame * CELLS, CELLS), :], both[...])
         hid = (pre * jax.nn.sigmoid(pre)).astype(BF16)
         for par in range(2):
             hidden_out[frame, par] = hid[:, par * CH : (par + 1) * CH]
-            if frame >= 2:
-                pre_out[frame - 2, par] = pre[:, par * CH : (par + 1) * CH]
-    loads[2].wait()
+    loads[0].wait()
     times = first_time[...].reshape(3 * CH, CH)
     for frame in range(2):
         mixed = []
         for par in range(2):
-            taps = jnp.concatenate([hidden_out[frame + k, par] for k in range(3)], axis=1)
-            here = source_out[frame, par].reshape(CELLS, CH).astype(F32) + dot(taps, times)
+            hid = [hidden_out[0, par], hidden_out[1, par], acts[0, par], acts[1, par]]
+            taps = jnp.concatenate(hid[frame : frame + 3], axis=1)
+            here = acts[2 + frame, par].astype(F32) + dot(taps, times)
             mixed.append(here.astype(BF16).reshape(COLS, HALF, CH))
         by_row = (row_before(mixed[1]), mixed[0], mixed[1])
         for row in range(3):
@@ -167,13 +149,20 @@
                         cells_out[rows, lanes] = jnp.zeros((HALF, CH), BF16)
                     else:
                         cells_out[rows, lanes] = by_row[row][where]
-    loads[3].wait()
+    loads[1].wait()
     kernel = down_plane[...].reshape(9 * CH, WIDE)
     strided_out[...] = dot(cells_out[...], kernel).astype(BF16).reshape(2, DOWN, WIDE)
 
 
-def rows_body(rows, last_far, sent_out, last_time, spread, padded, turned, sems):
-    loads = start(sems, (0, last_far, last_time))
+def own_body(
+    rows, last_far, own_far, plane_far,
+    sent_out, acts_out, pre_out, both_out,
+    last_time, own, first_plane, spread, padded, turned, cells, windows, sems,
+):
+    loads = start(
+        sems, (0, last_far, last_time), (1, own_far, own), (2, plane_far, first_plane)
+    )
+    both_out[...] = jnp.zeros_like(both_out)
     cotan = rows[...].astype(F32)
     spread[...] = cotan.reshape(HALF * 8, CH)
     for half in range(2):
@@ -188,6 +177,27 @@
         turned[pl.ds(half, DOWN, stride=2), :] = total[:, half * CH : (half + 1) * CH]
     both = jnp.concatenate([turned[...].reshape(HALF, 8, CH), cotan], axis=1)
     sent_out[...] = both.astype(BF16)
+
+    loads[1].wait()
+    for frame in range(2):
+        planes = parity_planes(own, frame, cells)
+        fill_windows(windows, frame * CELLS, *planes)
+        for par in range(2):
+            acts_out[2 + frame, par] = planes[par].reshape(CELLS, CH)
+    loads[2].wait()
+    for tap in range(3):
+        for row in range(4):
+            at = pl.ds((tap * 4 + row) * CH, CH)
+            if row < 3:
+                both_out[at, pl.ds(0, CH)] = first_plane[row, tap]
+            if row > 0:
+                both_out[at, pl.ds(CH, CH)] = first_plane[row - 1, tap]
+    for frame in range(2):
+        pre = dot(windows[pl.ds(frame * CELLS, CELLS), :], both_out[...])
+        hid = (pre * jax.nn.sigmoid(pre)).astype(BF16)
+        for par in range(2):
+            acts_out[frame, par] = hid[:, par * CH : (par + 1) * CH]
+            pre_out[frame, par] = pre[:, par * CH : (par + 1) * CH]
 
 
 def cotan_body(
@@ -232,7 +242,7 @@
 
 def time_grads_body(
     sent, lowered, prior, own, down_far, plane_far,
-    part_out, times_out, kernels_out, grad_down_time_out, grad_last_out, lowered_out,
+    part_out, times_out, kernels_out, grads_out, lowered_out,
     down_time, down_plane, turned, sems,
 ):
     loads = start(sems, (0, down_far, down_time), (1, plane_far, down_plane))
@@ -250,10 +260,10 @@
         down = dot_tn(taps[k], grad_pre)
         for half in range(2):
             lanes = slice(half * CH, (half + 1) * CH)
-            grad_down_time_out[half, pl.ds(k * WIDE, WIDE), :] = down[:, lanes]
+            grads_out[pl.ds((half * 3 + k) * WIDE, WIDE), :] = down[:, lanes]
     last = dot_tn(lowered[...], sent[pl.ds(DOWN, DOWN), :])
     for half in range(2):
-        grad_last_out[half] = last[:, half * CH : (half + 1) * CH]
+        grads_out[pl.ds((6 + half) * WIDE, WIDE), :] = last[:, half * CH : (half + 1) * CH]
     for load in loads:
         load.wait()
     part_out[...] = dot_nt(grad_pre, down_time[2])
@@ -294,17 +304,15 @@
 
 
 def plane_grads_body(
-    core, grad_strided, grad_mixed, cells, hidden, source, pre, time_far,
-    grad_down_time, grad_last, lowered, lowered_rows, ahead,
+    core, grad_strided, grad_mixed, cells, prior_hidden, acts, pre, time_far,
+    grads, lowered, lowered_rows, ahead,
     mine_out, other_out, windows_out, slope_out, part_out, time_out,
     flat, sems,
 ):
     loads = start(sems, (0, time_far, time_out))
     base = 3 * CH + 18 * CH
-    flat[pl.ds(base, 6 * WIDE), :] = grad_down_time[...].reshape(6 * WIDE, CH)
-    base += 6 * WIDE
-    flat[pl.ds(base, 2 * WIDE), :] = grad_last[...].reshape(2 * WIDE, CH)
-    base += 2 * WIDE
+    flat[pl.ds(base, 8 * WIDE), :] = grads[...]
+    base += 8 * WIDE
     last = dot_tn(lowered[...], ahead[pl.ds(DOWN, DOWN), :])
     for half in range(2):
         flat[pl.ds(base + half * WIDE, WIDE), :] = last[:, half * CH : (half + 1) * CH]
@@ -313,8 +321,10 @@
         at = 3 * CH + half * 9 * CH
         flat[pl.ds(at, 9 * CH), :] = down[:, half * CH : (half + 1) * CH]
     cotan = grad_mixed[pl.ds(0, 4 * CELLS), :]
+    early = prior_hidden[...].reshape(4 * CELLS, CH)
+    late = acts[pl.ds(0, 2)].reshape(4 * CELLS, CH)
     for k in range(3):
-        taps = hidden[pl.ds(k, 2)].reshape(4 * CELLS, CH)
+        taps = (early, jnp.concatenate([early[2 * CELLS :], late[: 2 * CELLS]], axis=0), late)[k]
         flat[pl.ds(k * CH, CH), :] = dot_tn(taps, cotan)
     here = core[0]
     half = mine_out.shape[0]
@@ -326,7 +336,8 @@
     other_out[pl.ds(half, DOWN), :] = away.astype(BF16)
     loads[0].wait()
     for frame in range(2):
-        fill_windows(windows_out, frame * CELLS, source[frame, 0], source[frame, 1])
+        planes = [acts[2 + frame, par].reshape(COLS, HALF, CH) for par in range(2)]
+        fill_windows(windows_out, frame * CELLS, *planes)
     slope_out[...] = silu_slope(pre[...])
     for par in range(2):
         first, second = [
@@ -388,22 +399,42 @@
         total = total + blocks[block].astype(F32)
     padded[...] = jnp.zeros_like(padded)
     padded[pl.ds(0, rows), :] = total
-    chips = sent_out.shape[0]
-    sent_out[:, pl.ds(0, 16), :] = padded[...].reshape(chips, 16, CH).astype(BF16)
     here = core[0]
+    chips = own.shape[0]
     mine = own[:, pl.ds(here, 1)].astype(F32).reshape(chips, 8, CH)
     theirs = other[pl.ds(EARLY // 2, DOWN), :].astype(F32).reshape(chips, 8, CH)
     frames = [jnp.where(here == 0, mine, theirs), jnp.where(here == 0, theirs, mine)]
-    sent_out[:, pl.ds(16, 16), :] = jnp.concatenate(frames, axis=1).astype(BF16)
+    frames = jnp.concatenate(frames, axis=1)
+    near = sent_out.shape[0]
+    share = padded.shape[0] // near
+    for chip in range(near):
+        sent_out[chip, pl.ds(0, share), :] = padded[pl.ds(chip * share, share), :].astype(BF16)
+        for far in range(chips // near):
+            sent_out[chip, pl.ds(share + far * 16, 16), :] = frames[far * near + chip].astype(BF16)
+
+
+def first_rows(received, share):
+    total = received[0, pl.ds(0, share), :].astype(F32)
+    for chip in range(1, received.shape[0]):
+        total = total + received[chip, pl.ds(0, share), :].astype(F32)
+    return total.astype(BF16)
+
+
+def near_body(received, sent_out):
+    near, far = received.shape[0], sent_out.shape[0]
+    share = sent_out.shape[1] - near * 16
+    piece = first_rows(received, share)
+    for there in range(far):
+        sent_out[there, pl.ds(0, share), :] = piece
+        for chip in range(near):
+            sent_out[there, pl.ds(share + chip * 16, 16), :] = received[
+                chip, pl.ds(share + there * 16, 16), :
+            ]
 
 
 def piece_body(received, piece_out):
-    chips = received.shape[0]
-    total = received[0, pl.ds(0, 16), :].astype(F32)
-    for chip in range(1, chips):
-        total = total + received[chip, pl.ds(0, 16), :].astype(F32)
-    piece = total.astype(BF16)
-    for chip in range(chips):
+    piece = first_rows(received, piece_out.shape[1])
+    for chip in range(piece_out.shape[0]):
         piece_out[chip] = piece
 
 
@@ -436,8 +467,10 @@
 
 
 def output_body(received, last_time, output, spread, padded):
-    frames = received[:, pl.ds(16, 16), :]
-    spread[...] = frames.astype(F32).reshape(HALF * 8, CH)
+    share = received.shape[1] - 16 * HALF // 2 // received.shape[0]
+    for far in range(received.shape[0]):
+        rows = received.shape[1] - share
+        spread[pl.ds(far * rows, rows), :] = received[far, pl.ds(share, rows), :].astype(F32)
     padded[pl.ds(0, 8), :] = jnp.zeros((8, WIDE), F32)
     for half in range(2):
         padded[pl.ds(8, DOWN), pl.ds(half * CH, CH)] = spread[pl.ds(half, DOWN, stride=2), :]
@@ -467,6 +500,125 @@
     return lax.all_to_all(blocks, "seq", split_axis=0, concat_axis=0, tiled=True)
 
 
+def exchange_chips(blocks, near):
+    count = lax.axis_size("seq") // 2
+    runs = [list(range(first, first + NEAR)) for first in range(0, count, NEAR)]
+    if not near:
+        runs = [list(place) for place in zip(*runs)]
+    groups = [[2 * chip + core for chip in run] for run in runs for core in range(2)]
+    return lax.all_to_all(
+        blocks, "seq", split_axis=0, concat_axis=0, axis_index_groups=groups, tiled=True
+    )
+
+
+def sum_body(core, blocks, own, other, sent_out, padded):
+    rows = blocks.shape[1]
+    total = blocks[0].astype(F32)
+    for block in range(1, blocks.shape[0]):
+        total = total + blocks[block].astype(F32)
+    padded[...] = jnp.zeros_like(padded)
+    padded[pl.ds(0, rows), :] = total
+    here = core[0]
+    chips = own.shape[0]
+    mine = own[:, pl.ds(here, 1)].astype(F32).reshape(chips, 8, CH)
+    theirs = other[pl.ds(EARLY // 2, DOWN), :].astype(F32).reshape(chips, 8, CH)
+    frames = [jnp.where(here == 0, mine, theirs), jnp.where(here == 0, theirs, mine)]
+    frames = jnp.concatenate(frames, axis=1)
+    near = sent_out.shape[0]
+    share = padded.shape[0] // near
+    for chip in range(near):
+        sent_out[chip, pl.ds(0, share), :] = padded[pl.ds(chip * share, share), :].astype(BF16)
+        for far in range(chips // near):
+            sent_out[chip, pl.ds(share + far * 16, 16), :] = frames[far * near + chip].astype(BF16)
+
+
+def first_rows(received, share):
+    total = received[0, pl.ds(0, share), :].astype(F32)
+    for chip in range(1, received.shape[0]):
+        total = total + received[chip, pl.ds(0, share), :].astype(F32)
+    return total.astype(BF16)
+
+
+def near_body(received, sent_out):
+    near, far = received.shape[0], sent_out.shape[0]
+    share = sent_out.shape[1] - near * 16
+    piece = first_rows(received, share)
+    for there in range(far):
+        sent_out[there, pl.ds(0, share), :] = piece
+        for chip in range(near):
+            sent_out[there, pl.ds(share + chip * 16, 16), :] = received[
+                chip, pl.ds(share + there * 16, 16), :
+            ]
+
+
+def piece_body(received, piece_out):
+    piece = first_rows(received, piece_out.shape[1])
+    for chip in range(piece_out.shape[0]):
+        piece_out[chip] = piece
+
+
+def spread_body(pieces, part_out):
+    flat = pieces[...].reshape(-1, CH).astype(F32)
+    part = flat[: part_out.shape[1]].astype(BF16)
+    for block in range(part_out.shape[0]):
+        part_out[block] = part
+
+
+def results_body(
+    core, mine, other,
+    first_plane_out, first_time_out, down_plane_out, down_time_out, last_time_out,
+    early, late,
+):
+    here = core[0]
+    rows, more = EARLY // 2, LATE // 2
+    for half, at in ((mine, here), (other, 1 - here)):
+        early[pl.ds(pl.multiple_of(at * rows, 16), rows), :] = half[pl.ds(0, rows), :]
+        late[pl.ds(pl.multiple_of(at * more, 16), more), :] = half[pl.ds(rows, more), :]
+    first_plane_out[...] = late[pl.ds(0, 9 * CH), :]
+    first_time_out[...] = early[pl.ds(0, 3 * CH), :]
+    for half in range(2):
+        lanes = pl.ds(half * CH, CH)
+        down_plane_out[:, lanes] = early[pl.ds(3 * CH + half * 9 * CH, 9 * CH), :]
+        down_time_out[:, lanes] = early[pl.ds(21 * CH + half * 6 * CH, 6 * CH), :]
+        last_time_out[pl.ds(0, WIDE), lanes] = late[pl.ds(9 * CH + half * WIDE, WIDE), :]
+        last_time_out[pl.ds(WIDE, WIDE), lanes] = early[pl.ds(37 * CH + half * WIDE, WIDE), :]
+        last_time_out[pl.ds(2 * WIDE, WIDE), lanes] = early[pl.ds(33 * CH + half * WIDE, WIDE), :]
+
+
+def output_body(received, last_time, output, spread, padded):
+    share = received.shape[1] - 16 * HALF // 2 // received.shape[0]
+    for far in range(received.shape[0]):
+        rows = received.shape[1] - share
+        spread[pl.ds(far * rows, rows), :] = received[far, pl.ds(share, rows), :].astype(F32)
+    padded[pl.ds(0, 8), :] = jnp.zeros((8, WIDE), F32)
+    for half in range(2):
+        padded[pl.ds(8, DOWN), pl.ds(half * CH, CH)] = spread[pl.ds(half, DOWN, stride=2), :]
+    total = padded[pl.ds(8, DOWN), :]
+    for k in range(3):
+        taps = padded[pl.ds(4 * k, DOWN), :].astype(BF16)
+        total = total + dot(taps, last_time[k])
+    output[...] = total.astype(BF16)
+
+
+def from_behind(block, distance):
+    devices = range(lax.axis_size("seq"))
+    route = [(i - distance, i) for i in devices if i - distance in devices]
+    return lax.ppermute(block, "seq", route)
+
+
+def swap_cores(block):
+    count = lax.axis_size("seq")
+    return lax.ppermute(block, "seq", [(i, i ^ 1) for i in range(count)])
+
+
+def exchange_clip(blocks):
+    return lax.all_to_all(blocks, "clip", split_axis=0, concat_axis=0, tiled=True)
+
+
+def exchange_seq(blocks):
+    return lax.all_to_all(blocks, "seq", split_axis=0, concat_axis=0, tiled=True)
+
+
 def exchange_depth(blocks):
     count = lax.axis_size("seq")
     groups = [list(range(core, count, 2)) for core in range(2)]
@@ -478,43 +630,47 @@
 def local(clip_in, first_plane, first_time, down_plane, down_time, last_time, cotan_out):
     own = clip_in.reshape(4 * CELLS, CH)
     prior = from_behind(own, 1)
-    (sent,) = call(
-        rows_body,
-        [(V, cotan_out[0].reshape(HALF, 8, CH)), (H, last_time)],
-        [(V, (HALF, 16, CH), BF16)],
+    flat_frames = (2, 2, CELLS, CH)
+    sent, acts, pre_first, both = call(
+        own_body,
+        [(V, cotan_out[0].reshape(HALF, 8, CH)), (H, last_time), (H, own), (H, first_plane)],
+        [
+            (V, (HALF, 16, CH), BF16),
+            (P_, (4, 2, CELLS, CH), BF16),
+            (P_, flat_frames, F32),
+            (P_, (12 * CH, WIDE), BF16),
+        ],
         [
             ((3, WIDE, WIDE), BF16),
+            ((4 * CELLS, CH), BF16),
+            ((3, 3, CH, CH), BF16),
             ((HALF * 8, CH), F32),
             ((DOWN + 8, WIDE), F32),
             ((HALF * 8, CH), F32),
-        ],
-        copies=1,
-        flops=60000000,
+            ((2 * CELLS, CH), F32),
+            ((2 * CELLS, 12 * CH), BF16),
+        ],
+        copies=3,
+        flops=600000000,
     )
     sent, prior = lax.optimization_barrier((sent, prior))
     received = exchange_seq(sent)
-    flat_frames = (2, 2, CELLS, CH)
-    pre_first, hidden, cells, source, strided = call(
+    prior_hidden, cells, strided = call(
         first_body,
-        [(V, prior), (H, own), (H, first_plane), (H, first_time), (H, down_plane)],
-        [
-            (P_, flat_frames, F32),
-            (P_, (4, 2, CELLS, CH), BF16),
+        [(V, prior), (P_, acts), (P_, both), (H, first_time), (H, down_plane)],
+        [
+            (P_, flat_frames, BF16),
             (P_, (2 * DOWN, 9 * CH), BF16),
-            (P_, (2, 2, COLS, HALF, CH), BF16),
             (P_, (2, DOWN, WIDE), BF16),
         ],
         [
-            ((4 * CELLS, CH), BF16),
-            ((3, 3, CH, CH), BF16),
             ((3, CH, CH), BF16),
             ((3, 3, CH, WIDE), BF16),
             ((2 * CELLS, CH), F32),
-            ((4 * CELLS, 12 * CH), BF16),
-            ((12 * CH, WIDE), BF16),
-        ],
-        copies=4,
-        flops=2000000000,
+            ((2 * CELLS, 12 * CH), BF16),
+        ],
+        copies=2,
+        flops=1000000000,
     )
     strided_prior = from_behind(strided, 1)
     times = (P_, (2, WIDE, WIDE), BF16)
@@ -534,7 +690,7 @@
         flops=60000000,
     )
     ahead = from_behind(sent, -1)
-    part, near_times, kernels, grad_down_time, grad_last, lowered_rows = call(
+    part, near_times, kernels, time_grads, lowered_rows = call(
         time_grads_body,
         [
             (P_, sent), (P_, lowered), (V, strided_prior), (P_, strided),
@@ -544,8 +700,7 @@
             (P_, (DOWN, WIDE), F32),
             times,
             (P_, (4 * CH, 4 * WIDE), BF16),
-            (P_, (2, 3 * WIDE, CH), F32),
-            (P_, (2, WIDE, CH), F32),
+            (P_, (8 * WIDE, CH), F32),
             (P_, (HALF // 2, 2, 8, CH), BF16),
         ],
         [((3, WIDE, WIDE), BF16), ((3, 3, CH, WIDE), BF16), ((HALF * 8, CH), F32)],
@@ -565,8 +720,8 @@
         plane_grads_body,
         [
             (S, core), (P_, grad_strided), (P_, sent),
-            (P_, cells), (P_, hidden), (P_, source), (P_, pre_first), (H, first_time),
-            (P_, grad_down_time), (P_, grad_last), (P_, lowered), (P_, lowered_rows), (V, ahead),
+            (P_, cells), (P_, prior_hidden), (P_, acts), (P_, pre_first), (H, first_time),
+            (P_, time_grads), (P_, lowered), (P_, lowered_rows), (V, ahead),
         ],
         [
             (P_, (EARLY // 2, CH), F32),
@@ -602,15 +757,19 @@
         [(P_, (half_rows, CH), BF16)],
     )
     blocks = exchange_clip(half.reshape(clips, part_rows, CH))
+    far = chips // NEAR
+    share = 16 * (-(-part_rows // (16 * NEAR)))
     (sent,) = call(
         sum_body,
         [(S, core), (V, blocks), (P_, lowered_rows), (V, other)],
-        [(V, (chips, 32, CH), BF16)],
-        [((16 * chips, CH), F32)],
-    )
-    received = exchange_depth(sent)
-    (pieces,) = call(piece_body, [(V, received)], [(V, (chips, 16, CH), BF16)])
-    pieces = exchange_depth(pieces)
+        [(V, (NEAR, share + far * 16, CH), BF16)],
+        [((NEAR * share, CH), F32)],
+    )
+    received = exchange_chips(sent, True)
+    (sent,) = call(near_body, [(V, received)], [(V, (far, share + NEAR * 16, CH), BF16)])
+    received = exchange_chips(sent, False)
+    (pieces,) = call(piece_body, [(V, received)], [(V, (NEAR, share, CH), BF16)])
+    pieces = exchange_chips(pieces, True)
     (output,) = call(
         output_body,
         [(V, received), (V, last_time)],

time: 146 us -> 148 us (1.014)
  local copies, waits for them, and re-layouts: 4.12 us -> 8.2 us
  waiting for transfers between devices: 17.6 us -> 14.7 us
  starting transfers between devices: 39.2 us -> 42 us
  blocking collectives: 69.8 us -> 68.2 us
    unnamed x10 -> x20, local copies, waits for them, and re-layouts: 2.6 us -> 6.68 us
    ppermute x2, starting transfers between devices: 8.82 us -> 11.6 us  [swap_cores(): return lax.ppermute(block, 'seq', [(i, i ^ 1) for i in range(count)])]
    ppermute x4, waiting for transfers between devices: 5.17 us -> 3.02 us  [from_behind(): return lax.ppermute(block, 'seq', route)]
    pallas_call x14 -> x15, Pallas kernels: 13.4 us -> 12.9 us  [call(): pl.pallas_call(body, out_shape=[placed_output(*out) for out in outs], in_...]
    all_to_all x2 -> x3, blocking collectives: 33.1 us -> 32.9 us  [exchange_chips(): lax.all_to_all(blocks, 'seq', split_axis=0, concat_axis=0, axis_index_gro...]
  transfers between devices with their start and end apart: 7 -> 7, of which waited for: 6 -> 6; matrix products, arithmetic and copies ran while one was open for 1% -> 1% of each run, Pallas kernels for 7% -> 6%
where the time goes in v6:
time: 148 us; the launch traced here: 147 us
  blocking collectives  68.2 us (46%)
  starting transfers between devices  42 us (28%)
  waiting for transfers between devices  14.7 us (10%)
  Pallas kernels  12.9 us (9%)
  local copies, waits for them, and re-layouts  8.2 us (6%)
    all_to_all x2, blocking collectives, exchange_clip(): lax.all_to_all(blocks, 'clip', split_axis=0, concat_axis=0, tiled=True)  35.3 us
    all_to_all x3, blocking collectives, exchange_chips(): lax.all_to_all(blocks, 'seq', split_axis=0, concat_axis=0, axis_index_gro...  32.9 us
    all_to_all x1, starting transfers between devices, exchange_seq(): lax.all_to_all(blocks, 'seq', split_axis=0, concat_axis=0, tiled=True)  16.5 us
    ppermute x4, starting transfers between devices, from_behind(): return lax.ppermute(block, 'seq', route)  13.9 us
    pallas_call x15, Pallas kernels, call(): pl.pallas_call(body, out_shape=[placed_output(*out) for out in outs], in_...  12.9 us
    ppermute x2, starting transfers between devices, swap_cores(): return lax.ppermute(block, 'seq', [(i, i ^ 1) for i in range(count)])  11.6 us
    all_to_all x1, waiting for transfers between devices, exchange_seq(): lax.all_to_all(blocks, 'seq', split_axis=0, concat_axis=0, tiled=True)  8.1 us
    unnamed x20, local copies, waits for them, and re-layouts  6.68 us
  transfers between devices with their start and end apart: 7, of which 6 were waited for; matrix products, arithmetic and copies ran while one was open for 1% of the time, Pallas kernels for 6%

profile of v6, /device:TPU:1, one launch (start us, length us, event | category | flops | bytes accessed | tf_op | source)
XLA Modules:
  0.0 146.8 jit_solution(8578107236458643187)
XLA Ops:
  0.6 4.9 %collective-permute-start = (bf16[1024,128]{1,0:T(8,128)(2,1)}, bf16[1024,128]{1,0:T(8,128)(2,1)S(1)}, u32[]{:S(2)}, u32[]{:S(2)}) collective-permute-start(bf16[1024,128]{1,0:T(8,128)(2,1)} %bitcast.18), channel_id=1, source_target_pairs={{0,1},{1,2},{2,3},{3,4},{4,5},{5,6},{6,7},{7,8},{8,9},{9,10},{10,1... | collective-permute-start | bytes 786440 | tf_op jit(solution)/shard_map/ppermute | solution.py:606
  5.6 0.9 reshape_squeeze.3.rows
  6.5 2.5 %shard_map.118 = (bf16[32,16,128]{2,1,0:T(8,128)(2,1)}, bf16[4,2,256,128]{3,2,1,0:T(8,128)(2,1)S(1)}, f32[2,2,256,128]{3,2,1,0:T(8,128)S(1)}, bf16[1536,256]{1,0:T(8,128)(2,1)S(1)}) custom-call(bf16[32,8,128]{2,1,0:T(8,128)(2,1)S(1)} %reshape_squeeze.3.rows, bf16[3,256,256]{2,1,0:T(8,128)(2,1)} %last_time.1, bf16[1024,128]{1,0:T(8,128)(2,1)} %bitcast.19, ...), custom_call_target="tpu_custom_call" | custom-call | flops 600000000 | bytes 2000000 | tf_op jit(solution)/shard_map/pallas_call | solution.py:54
  9.0 0.9 copy-done.8
  10.0 16.5 %all-to-all-start = ((bf16[32,16,128]{2,1,0:T(8,128)(2,1)}), bf16[32,16,128]{2,1,0:T(8,128)(2,1)S(1)}, u32[]{:S(2)}, u32[]{:S(2)}) async-start(bf16[32,16,128]{2,1,0:T(8,128)(2,1)} %get-tuple-element.46), calls=%async_computation | async-start | bytes 262144 | tf_op jit(solution)/shard_map/all_to_all | solution.py:619
  26.5 1.1 copy-done.9
  27.6 2.4 %shard_map.119 = (bf16[2,2,256,128]{3,2,1,0:T(8,128)(2,1)S(1)}, bf16[256,1152]{1,0:T(8,128)(2,1)S(1)}, bf16[2,128,256]{2,1,0:T(8,128)(2,1)S(1)}) custom-call(bf16[1024,128]{1,0:T(8,128)(2,1)S(1)} %collective-permute-done.prior, bf16[4,2,256,128]{3,2,1,0:T(8,128)(2,1)S(1)} %get-tuple-element.43.acts, bf16[1536,256]{1,0:T(8,128)(2,1)S(1)} %copy-done.9, ...), custom_call_target="tpu_custom_call" | custom-call | flops 1000000000 | bytes 2000000 | tf_op jit(solution)/shard_map/pallas_call | solution.py:54
  30.0 0.7 copy-done.4
  30.7 3.5 %collective-permute-start.1 = (bf16[2,128,256]{2,1,0:T(8,128)(2,1)S(1)}, bf16[2,128,256]{2,1,0:T(8,128)(2,1)S(1)}, u32[]{:S(2)}, u32[]{:S(2)}) collective-permute-start(bf16[2,128,256]{2,1,0:T(8,128)(2,1)S(1)} %get-tuple-element.45.own), channel_id=1, source_target_pairs={{0,1},{1,2},{2,3},{3,4},{4,5},{5,6},{6,7},{7,8},{8,9},{9,10},{10,1... | collective-permute-start | bytes 393224 | tf_op jit(solution)/shard_map/ppermute | solution.py:606
  34.3 8.1 %all-to-all-done.received = bf16[32,16,128]{2,1,0:T(8,128)(2,1)S(1)} async-done(((bf16[32,16,128]{2,1,0:T(8,128)(2,1)}), bf16[32,16,128]{2,1,0:T(8,128)(2,1)S(1)}, u32[]{:S(2)}, u32[]{:S(2)}) %all-to-all-start) | async-done | bytes 131104 | tf_op jit(solution)/shard_map/all_to_all | solution.py:619
  42.4 1.2 shard_map.120
  43.8 3.5 %collective-permute-start.2 = (bf16[256,256]{1,0:T(8,128)(2,1)S(1)}, bf16[256,256]{1,0:T(8,128)(2,1)S(1)}, u32[]{:S(2)}, u32[]{:S(2)}) collective-permute-start(bf16[256,256]{1,0:T(8,128)(2,1)S(1)} %get-tuple-element.51.sent), channel_id=1, source_target_pairs={{1,0},{2,1},{3,2},{4,3},{5,4},{6,5},{7,6},{8,7},{9,8},{10,9},{11,1... | collective-permute-start | bytes 393224 | tf_op jit(solution)/shard_map/ppermute | solution.py:606
  47.3 1.5 %shard_map.122 = (f32[128,256]{1,0:T(8,128)S(1)}, bf16[2,256,256]{2,1,0:T(8,128)(2,1)S(1)}, bf16[512,1024]{1,0:T(8,128)(2,1)S(1)}, f32[2048,128]{1,0:T(8,128)S(1)}, bf16[16,2,8,128]{3,2,1,0:T(8,128)(2,1)S(1)}) custom-call(bf16[256,256]{1,0:T(8,128)(2,1)S(1)} %get-tuple-element.51.sent, bf16[128,256]{1,0:T(8,128)(2,1)S(1)} %get-tuple-element.52.lowered, ...), custom_call_target="tpu_custom_call" | custom-call | flops 120000000 | bytes 2000000 | tf_op jit(solution)/shard_map/pallas_call | solution.py:54
  50.7 0.6 copy-done.6
  51.3 1.9 %collective-permute-start.3 = (bf16[1280,128]{1,0:T(8,128)(2,1)S(1)}, bf16[1280,128]{1,0:T(8,128)(2,1)S(1)}, u32[]{:S(2)}, u32[]{:S(2)}) collective-permute-start(bf16[1280,128]{1,0:T(8,128)(2,1)S(1)} %get-tuple-element.57.grad_mixed), channel_id=1, source_target_pairs={{1,0},{2,1},{3,2},{4,3},{5,4},{6,5},{7,6},{8,7},{9,8},{10,9},{11,1... | collective-permute-start | bytes 983048 | tf_op jit(solution)/shard_map/ppermute | solution.py:606
  53.3 0.8 copy-done.2
  54.1 0.9 copy-done.5
  55.1 0.9 copy-done.7
  56.0 1.5 %shard_map.124 = (f32[2624,128]{1,0:T(8,128)S(1)}, bf16[2752,128]{1,0:T(8,128)(2,1)S(1)}, bf16[512,1536]{1,0:T(8,128)(2,1)S(1)}, f32[2,2,256,128]{3,2,1,0:T(8,12...) custom-call(s32[1]{0:T(128)} %bitcast.core, bf16[256,256]{1,0:T(8,128)(2,1)S(1)} %copy-done.7, ...), custom_call_target="tpu_custom_call" | custom-call | flops 500000000 | bytes 2000000 | tf_op jit(solution)/shard_map/pallas_call | solution.py:54
  57.4 2.3 %collective-permute-done.3.ahead = bf16[1280,128]{1,0:T(8,128)(2,1)S(1)} collective-permute-done((bf16[1280,128]{1,0:T(8,128)(2,1)S(1)}, bf16[1280,128]{1,0:T(8,128)(2,1)S(1)}, u32[]{:S(2)}, u32[]{:S(2)}) %collective-permute-start.3) | collective-permute-done | bytes 327712 | tf_op jit(solution)/shard_map/ppermute | solution.py:606
  59.7 0.9 shard_map.125
  60.6 1.9 %collective-permute-start.4 = (bf16[3584,128]{1,0:T(8,128)(2,1)S(1)}, bf16[3584,128]{1,0:T(8,128)(2,1)S(1)}, u32[]{:S(2)}, u32[]{:S(2)}) collective-permute-start(bf16[3584,128]{1,0:T(8,128)(2,1)S(1)} %get-tuple-element.70), channel_id=1, source_target_pairs={{0,1},{1,0},{2,3},{3,2},{4,5},{5,4},{6,7},{7,6},{8,9},{9,8},{10,11... | collective-permute-start | bytes 2752520 | tf_op jit(solution)/shard_map/ppermute | solution.py:611
  62.6 2.4 %collective-permute-done.4.other = bf16[3584,128]{1,0:T(8,128)(2,1)S(1)} collective-permute-done((bf16[3584,128]{1,0:T(8,128)(2,1)S(1)}, bf16[3584,128]{1,0:T(8,128)(2,1)S(1)}, u32[]{:S(2)}, u32[]{:S(2)}) %collective-permute-start.4) | collective-permute-done | bytes 917536 | tf_op jit(solution)/shard_map/ppermute | solution.py:611
  65.2 20.8 %all_to_all.30.blocks = bf16[16,216,128]{2,1,0:T(8,128)(2,1)S(1)} all-to-all(bf16[16,216,128]{2,1,0:T(8,128)(2,1)S(1)} %bitcast.10), channel_id=1, replica_groups=mesh['clip'=16,'seq'=32] {'clip'}, dimensions={0} | all-to-all | bytes 1769472 | tf_op jit(solution)/shard_map/all_to_all | solution.py:615
  86.1 9.1 %all_to_all.31.received = bf16[4,128,128]{2,1,0:T(8,128)(2,1)S(1)} all-to-all(bf16[4,128,128]{2,1,0:T(8,128)(2,1)S(1)} %shard_map.127), channel_id=1, replica_groups={{0,2,4,6},{1,3,5,7},{8,10,12,14},{9,11,13,15},{16,18,20,22},{17,19,21,2..., dimensions={0} | all-to-all | bytes 262144 | tf_op jit(solution)/shard_map/all_to_all | solution.py:509
  95.2 16.3 %all_to_all.32.received = bf16[4,128,128]{2,1,0:T(8,128)(2,1)S(1)} all-to-all(bf16[4,128,128]{2,1,0:T(8,128)(2,1)S(1)} %shard_map.128), channel_id=1, replica_groups={{0,8,16,24},{1,9,17,25},{2,10,18,26},{3,11,19,27},{4,12,20,28},{5,13,21..., dimensions={0} | all-to-all | bytes 262144 | tf_op jit(solution)/shard_map/all_to_all | solution.py:509
  111.6 7.4 %all_to_all.33.pieces = bf16[4,64,128]{2,1,0:T(8,128)(2,1)S(1)} all-to-all(bf16[4,64,128]{2,1,0:T(8,128)(2,1)S(1)} %shard_map.130), channel_id=1, replica_groups={{0,2,4,6},{1,3,5,7},{8,10,12,14},{9,11,13,15},{16,18,20,22},{17,19,21,2..., dimensions={0} | all-to-all | bytes 131072 | tf_op jit(solution)/shard_map/all_to_all | solution.py:509
  119.1 14.6 %all_to_all.34 = bf16[16,216,128]{2,1,0:T(8,128)(2,1)S(1)} all-to-all(bf16[16,216,128]{2,1,0:T(8,128)(2,1)S(1)} %shard_map.131), channel_id=1, replica_groups=mesh['clip'=16,'seq'=32] {'clip'}, dimensions={0} | all-to-all | bytes 1769472 | tf_op jit(solution)/shard_map/all_to_all | solution.py:615
  133.7 9.7 %collective-permute-start.5 = (bf16[3456,128]{1,0:T(8,128)(2,1)S(1)}, bf16[3456,128]{1,0:T(8,128)(2,1)S(1)}, u32[]{:S(2)}, u32[]{:S(2)}) collective-permute-start(bf16[3456,128]{1,0:T(8,128)(2,1)S(1)} %bitcast.11), channel_id=1, source_target_pairs={{0,1},{1,0},{2,3},{3,2},{4,5},{5,4},{6,7},{7,6},{8,9},{9,8},{10,11... | collective-permute-start | bytes 2654216 | tf_op jit(solution)/shard_map/ppermute | solution.py:611
  143.6 0.7 reshape.45
  144.3 1.1 collective-permute-done.5.other
  145.4 1.4 shard_map.132
  (24 shorter events, 2.9 us)
Async XLA Ops:
  0.6 9.4 %collective-permute-start = (bf16[1024,128]{1,0:T(8,128)(2,1)}, bf16[1024,128]{1,0:T(8,128)(2,1)S(1)}, u32[]{:S(2)}, u32[]{:S(2)}) collective-permute-start(bf16[1024,128]{1,0:T(8,128)(2,1)} %bitcast.18), channel_id=1, source_target_pairs={{0,1},{1,2},{2,3},{3,4},{4,5},{5,6},{6,7},{7,8},{8,9},{9,10},{10,1... | collective-permute-start | bytes 786440 | tf_op jit(solution)/shard_map/ppermute | solution.py:606
  9.0 0.9 copy-start.8
  10.0 32.3 %all-to-all-start = ((bf16[32,16,128]{2,1,0:T(8,128)(2,1)}), bf16[32,16,128]{2,1,0:T(8,128)(2,1)S(1)}, u32[]{:S(2)}, u32[]{:S(2)}) async-start(bf16[32,16,128]{2,1,0:T(8,128)(2,1)} %get-tuple-element.46), calls=%async_computation | async-start | bytes 262144 | tf_op jit(solution)/shard_map/all_to_all | solution.py:619
  26.5 1.1 copy-start.9
  30.0 0.7 copy-start.4
  30.7 12.8 %collective-permute-start.1 = (bf16[2,128,256]{2,1,0:T(8,128)(2,1)S(1)}, bf16[2,128,256]{2,1,0:T(8,128)(2,1)S(1)}, u32[]{:S(2)}, u32[]{:S(2)}) collective-permute-start(bf16[2,128,256]{2,1,0:T(8,128)(2,1)S(1)} %get-tuple-element.45.own), channel_id=1, source_target_pairs={{0,1},{1,2},{2,3},{3,4},{4,5},{5,6},{6,7},{7,8},{8,9},{9,10},{10,1... | collective-permute-start | bytes 393224 | tf_op jit(solution)/shard_map/ppermute | solution.py:606
  43.8 6.3 %collective-permute-start.2 = (bf16[256,256]{1,0:T(8,128)(2,1)S(1)}, bf16[256,256]{1,0:T(8,128)(2,1)S(1)}, u32[]{:S(2)}, u32[]{:S(2)}) collective-permute-start(bf16[256,256]{1,0:T(8,128)(2,1)S(1)} %get-tuple-element.51.sent), channel_id=1, source_target_pairs={{1,0},{2,1},{3,2},{4,3},{5,4},{6,5},{7,6},{8,7},{9,8},{10,9},{11,1... | collective-permute-start | bytes 393224 | tf_op jit(solution)/shard_map/ppermute | solution.py:606
  48.9 0.6 copy-start.1
  50.7 0.7 copy-start.6
  51.3 8.4 %collective-permute-start.3 = (bf16[1280,128]{1,0:T(8,128)(2,1)S(1)}, bf16[1280,128]{1,0:T(8,128)(2,1)S(1)}, u32[]{:S(2)}, u32[]{:S(2)}) collective-permute-start(bf16[1280,128]{1,0:T(8,128)(2,1)S(1)} %get-tuple-element.57.grad_mixed), channel_id=1, source_target_pairs={{1,0},{2,1},{3,2},{4,3},{5,4},{6,5},{7,6},{8,7},{9,8},{10,9},{11,1... | collective-permute-start | bytes 983048 | tf_op jit(solution)/shard_map/ppermute | solution.py:606
  53.3 0.8 copy-start.2
  54.1 0.9 copy-start.5
  55.1 0.9 copy-start.7
  60.6 4.4 %collective-permute-start.4 = (bf16[3584,128]{1,0:T(8,128)(2,1)S(1)}, bf16[3584,128]{1,0:T(8,128)(2,1)S(1)}, u32[]{:S(2)}, u32[]{:S(2)}) collective-permute-start(bf16[3584,128]{1,0:T(8,128)(2,1)S(1)} %get-tuple-element.70), channel_id=1, source_target_pairs={{0,1},{1,0},{2,3},{3,2},{4,5},{5,4},{6,7},{7,6},{8,9},{9,8},{10,11... | collective-permute-start | bytes 2752520 | tf_op jit(solution)/shard_map/ppermute | solution.py:611
  65.2 20.8 %copy-start.3 = (bf16[16,2,8,128]{3,2,1,0:T(8,128)(2,1)S(1)}, bf16[16,2,8,128]{3,2,1,0:T(8,128)(2,1)}, u32[]{:S(2)}) copy-start(bf16[16,2,8,128]{3,2,1,0:T(8,128)(2,1)} %copy-done.1) | copy-start | bytes 196612
  111.6 31.8 %copy-start = (bf16[3,256,256]{2,1,0:T(8,128)(2,1)S(1)}, bf16[3,256,256]{2,1,0:T(8,128)(2,1)}, u32[]{:S(2)}) copy-start(bf16[3,256,256]{2,1,0:T(8,128)(2,1)} %last_time.1) | copy-start | bytes 1179652
  133.7 11.8 %collective-permute-start.5 = (bf16[3456,128]{1,0:T(8,128)(2,1)S(1)}, bf16[3456,128]{1,0:T(8,128)(2,1)S(1)}, u32[]{:S(2)}, u32[]{:S(2)}) collective-permute-start(bf16[3456,128]{1,0:T(8,128)(2,1)S(1)} %bitcast.11), channel_id=1, source_target_pairs={{0,1},{1,0},{2,3},{3,2},{4,5},{5,4},{6,7},{7,6},{8,9},{9,8},{10,11... | collective-permute-start | bytes 2654216 | tf_op jit(solution)/shard_map/ppermute | solution.py:611

commit v7 on v6

--- a/solution.py
+++ b/solution.py
@@ -14,6 +14,10 @@
 DOWN = CELLS // 2
 CH = 128
 WIDE = 256
+STRIDED_AT = 9 * 2 * DOWN
+KEPT = STRIDED_AT + 2 * DOWN
+LOWERED_AT = 8 * WIDE
+PART_AT = LOWERED_AT + 2 * DOWN
 EARLY = (3 + 18 + 12 + 8) * CH
 LATE = (9 + 4) * CH
 NEAR = 4
@@ -47,7 +51,7 @@
     return jax.ShapeDtypeStruct(shape, kind)
 
 
-def call(body, ins, outs, scratch=(), copies=0, flops=0):
+def call(body, ins, outs, scratch=(), copies=0):
     scratch = [pltpu.VMEM(shape, kind) for shape, kind in scratch]
     if copies:
         scratch.append(pltpu.SemaphoreType.DMA((copies,)))
@@ -58,7 +62,7 @@
         out_specs=[pl.BlockSpec(memory_space=SPACES[space]) for space, _, _ in outs],
         scratch_shapes=scratch,
         compiler_params=pltpu.CompilerParams(vmem_limit_bytes=24 * 1024 * 1024),
-        cost_estimate=pl.CostEstimate(flops=flops, bytes_accessed=2000000, transcendentals=0),
+        cost_estimate=pl.CostEstimate(flops=1000, bytes_accessed=8000000, transcendentals=0),
     )(*[placed_input(*given) for given in ins])
 
 
@@ -116,42 +120,59 @@
     return planes
 
 
-def first_body(
-    prior, acts, both, time_far, down_far,
-    hidden_out, cells_out, strided_out,
-    first_time, down_plane, spread, windows, sems,
-):
-    loads = start(sems, (0, time_far, first_time), (1, down_far, down_plane))
+def cells_of(kept):
+    return jnp.concatenate([kept[pl.ds(tap * 2 * DOWN, 2 * DOWN), :] for tap in range(9)], axis=1)
+
+
+def prior_body(prior, own_acts, both, acts_out, spread, windows):
     for frame in range(2):
         fill_windows(windows, frame * CELLS, *parity_planes(prior, frame, spread))
+    acts_out[pl.ds(2, 4)] = own_acts[...]
     for frame in range(2):
         pre = dot(windows[pl.ds(frame * CELLS, CELLS), :], both[...])
         hid = (pre * jax.nn.sigmoid(pre)).astype(BF16)
         for par in range(2):
-            hidden_out[frame, par] = hid[:, par * CH : (par + 1) * CH]
+            acts_out[frame, par] = hid[:, par * CH : (par + 1) * CH]
+
+
+def first_body(
+    acts, time_far, plane_far, down_far,
+    kept_out, strided_out, part_out, times_out,
+    first_time, down_plane, down_time, sems,
+):
+    loads = start(
+        sems, (0, time_far, first_time), (1, plane_far, down_plane), (2, down_far, down_time)
+    )
     loads[0].wait()
     times = first_time[...].reshape(3 * CH, CH)
     for frame in range(2):
         mixed = []
         for par in range(2):
-            hid = [hidden_out[0, par], hidden_out[1, par], acts[0, par], acts[1, par]]
-            taps = jnp.concatenate(hid[frame : frame + 3], axis=1)
-            here = acts[2 + frame, par].astype(F32) + dot(taps, times)
+            taps = jnp.concatenate([acts[frame + k, par] for k in range(3)], axis=1)
+            here = acts[4 + frame, par].astype(F32) + dot(taps, times)
             mixed.append(here.astype(BF16).reshape(COLS, HALF, CH))
         by_row = (row_before(mixed[1]), mixed[0], mixed[1])
         for row in range(3):
             for tap in range(3):
-                lanes = pl.ds((row * 3 + tap) * CH, CH)
+                at = (row * 3 + tap) * 2 * DOWN + frame * DOWN
                 for col in range(COLS // 2):
-                    rows = pl.ds(frame * DOWN + col * HALF, HALF)
+                    rows = pl.ds(at + col * HALF, HALF)
                     where = 2 * col + tap - 1
                     if where < 0:
-                        cells_out[rows, lanes] = jnp.zeros((HALF, CH), BF16)
+                        kept_out[rows, :] = jnp.zeros((HALF, CH), BF16)
                     else:
-                        cells_out[rows, lanes] = by_row[row][where]
+                        kept_out[rows, :] = by_row[row][where]
     loads[1].wait()
     kernel = down_plane[...].reshape(9 * CH, WIDE)
-    strided_out[...] = dot(cells_out[...], kernel).astype(BF16).reshape(2, DOWN, WIDE)
+    strided = dot(cells_of(kept_out), kernel).astype(BF16).reshape(2, DOWN, WIDE)
+    strided_out[...] = strided
+    for half in range(2):
+        kept_out[pl.ds(STRIDED_AT + half * DOWN, DOWN), :] = strided[
+            0, :, half * CH : (half + 1) * CH
+        ]
+    loads[2].wait()
+    part_out[...] = dot(strided[0], down_time[2])
+    times_out[...] = down_time[pl.ds(0, 2)]
 
 
 def own_body(
@@ -201,11 +222,10 @@
 
 
 def cotan_body(
-    own, received, down_far,
-    grad_lowered_out, cot_out, part_out, times_out,
-    down_time, spread, sems,
+    received,
+    grad_lowered_out, cot_out,
+    spread,
 ):
-    loads = start(sems, (0, down_far, down_time))
     spread[...] = received[...].astype(F32).reshape(HALF * 16, CH)
     for at, out in ((0, grad_lowered_out), (8, cot_out)):
         parts = []
@@ -215,9 +235,6 @@
             ]
             parts.append(jnp.concatenate(halves, axis=1))
         out[...] = jnp.concatenate(parts, axis=0).astype(BF16)
-    loads[0].wait()
-    part_out[...] = dot(own[0], down_time[2])
-    times_out[...] = down_time[pl.ds(0, 2)]
 
 
 def middle_body(prior, part, times, grad_lowered, cot, lowered_out, sent_out):
@@ -241,20 +258,20 @@
 
 
 def time_grads_body(
-    sent, lowered, prior, own, down_far, plane_far,
-    part_out, times_out, kernels_out, grads_out, lowered_out,
-    down_time, down_plane, turned, sems,
+    sent, lowered, prior, kept, down_far, plane_far,
+    times_out, kernels_out, grads_out,
+    down_time, down_plane, sems,
 ):
     loads = start(sems, (0, down_far, down_time), (1, plane_far, down_plane))
     kernels_out[...] = jnp.zeros_like(kernels_out)
     wide = lowered[...].astype(F32)
     for col in range(4):
         for half in range(2):
-            turned[pl.ds(col * 2 + half, HALF, stride=8), :] = wide[
+            grads_out[pl.ds(LOWERED_AT + col * 2 + half, HALF, stride=8), :] = wide[
                 col * HALF : (col + 1) * HALF, half * CH : (half + 1) * CH
             ]
-    lowered_out[...] = turned[...].reshape(HALF // 2, 2, 8, CH).astype(BF16)
-    taps = (prior[0], prior[1], own[0])
+    own = [kept[pl.ds(STRIDED_AT + half * DOWN, DOWN), :] for half in range(2)]
+    taps = (prior[0], prior[1], jnp.concatenate(own, axis=1))
     grad_pre = sent[pl.ds(0, DOWN), :]
     for k in range(3):
         down = dot_tn(taps[k], grad_pre)
@@ -266,7 +283,9 @@
         grads_out[pl.ds((6 + half) * WIDE, WIDE), :] = last[:, half * CH : (half + 1) * CH]
     for load in loads:
         load.wait()
-    part_out[...] = dot_nt(grad_pre, down_time[2])
+    part = dot_nt(grad_pre, down_time[2])
+    for half in range(2):
+        grads_out[pl.ds(PART_AT + half * DOWN, DOWN), :] = part[:, half * CH : (half + 1) * CH]
     times_out[...] = down_time[pl.ds(0, 2)]
     for row_par, col_par, row_off, col_off, row, tap in BACK:
         rows = pl.ds((row_par * 2 + col_par) * CH, CH)
@@ -274,16 +293,19 @@
         kernels_out[rows, lanes] = down_plane[row, tap]
 
 
-def back_body(ahead, part, times, kernels, grad_strided_out, sent_out, shifted):
+def grad_strided_of(grads, ahead, times):
     following = ahead[pl.ds(0, DOWN), :]
+    part = [grads[pl.ds(PART_AT + half * DOWN, DOWN), :] for half in range(2)]
+    even = jnp.concatenate(part, axis=1) + dot_nt(following, times[0])
+    return even.astype(BF16), dot_nt(following, times[1]).astype(BF16)
+
+
+def back_body(ahead, grads, times, kernels, sent_out, shifted):
     for half in range(2):
         sent_out[pl.ds(4 * CELLS + half * DOWN, DOWN), :] = ahead[
             pl.ds(DOWN, DOWN), pl.ds(half * CH, CH)
         ]
-    even = part[...] + dot_nt(following, times[0])
-    odd = dot_nt(following, times[1])
-    for frame, strided in ((0, even.astype(BF16)), (1, odd.astype(BF16))):
-        grad_strided_out[pl.ds(frame * DOWN, DOWN), :] = strided
+    for frame, strided in enumerate(grad_strided_of(grads, ahead, times)):
         planes = strided.reshape(4, HALF, WIDE)
         for row_off, rows in ((0, planes), (1, row_after(planes))):
             flat = rows.reshape(DOWN, WIDE)
@@ -304,39 +326,41 @@
 
 
 def plane_grads_body(
-    core, grad_strided, grad_mixed, cells, prior_hidden, acts, pre, time_far,
-    grads, lowered, lowered_rows, ahead,
+    core, grad_mixed, kept, acts, pre, time_far, down_far,
+    grads, lowered, ahead,
     mine_out, other_out, windows_out, slope_out, part_out, time_out,
-    flat, sems,
+    flat, rows_here, times, sems,
 ):
-    loads = start(sems, (0, time_far, time_out))
+    loads = start(sems, (0, time_far, time_out), (1, down_far, times))
     base = 3 * CH + 18 * CH
-    flat[pl.ds(base, 8 * WIDE), :] = grads[...]
+    flat[pl.ds(base, 8 * WIDE), :] = grads[pl.ds(0, 8 * WIDE), :]
     base += 8 * WIDE
     last = dot_tn(lowered[...], ahead[pl.ds(DOWN, DOWN), :])
     for half in range(2):
         flat[pl.ds(base + half * WIDE, WIDE), :] = last[:, half * CH : (half + 1) * CH]
-    down = dot_tn(cells[...], grad_strided[...])
+    loads[1].wait()
+    grad_strided = jnp.concatenate(grad_strided_of(grads, ahead, times), axis=0)
+    down = dot_tn(cells_of(kept), grad_strided)
     for half in range(2):
         at = 3 * CH + half * 9 * CH
         flat[pl.ds(at, 9 * CH), :] = down[:, half * CH : (half + 1) * CH]
     cotan = grad_mixed[pl.ds(0, 4 * CELLS), :]
-    early = prior_hidden[...].reshape(4 * CELLS, CH)
-    late = acts[pl.ds(0, 2)].reshape(4 * CELLS, CH)
     for k in range(3):
-        taps = (early, jnp.concatenate([early[2 * CELLS :], late[: 2 * CELLS]], axis=0), late)[k]
+        taps = acts[pl.ds(k, 2)].reshape(4 * CELLS, CH)
         flat[pl.ds(k * CH, CH), :] = dot_tn(taps, cotan)
     here = core[0]
-    half = mine_out.shape[0]
-    mine_out[...] = flat[pl.ds(pl.multiple_of(here * half, 16), half), :]
+    half = EARLY // 2
+    mine_out[pl.ds(0, half), :] = flat[pl.ds(pl.multiple_of(here * half, 16), half), :]
     other_out[pl.ds(0, half), :] = flat[
         pl.ds(pl.multiple_of((1 - here) * half, 16), half), :
     ].astype(BF16)
-    away = lowered_rows[:, pl.ds(1 - here, 1)].astype(F32).reshape(DOWN, CH)
+    rows_here[...] = grads[pl.ds(LOWERED_AT, 2 * DOWN), :].reshape(HALF // 2, 2, 8, CH)
+    mine_out[pl.ds(half, DOWN), :] = rows_here[:, pl.ds(here, 1)].reshape(DOWN, CH)
+    away = rows_here[:, pl.ds(1 - here, 1)].reshape(DOWN, CH)
     other_out[pl.ds(half, DOWN), :] = away.astype(BF16)
     loads[0].wait()
     for frame in range(2):
-        planes = [acts[2 + frame, par].reshape(COLS, HALF, CH) for par in range(2)]
+        planes = [acts[4 + frame, par].reshape(COLS, HALF, CH) for par in range(2)]
         fill_windows(windows_out, frame * CELLS, *planes)
     slope_out[...] = silu_slope(pre[...])
     for par in range(2):
@@ -384,33 +408,36 @@
     ].astype(BF16)
 
 
-def halves_body(early, late, other, half_out):
-    rows, more = early.shape[0], late.shape[0]
-    half_out[pl.ds(0, rows), :] = (early[...] + other[pl.ds(0, rows), :].astype(F32)).astype(BF16)
+def halves_body(core, early, late, other, half_out, frames_out):
+    rows, more = EARLY // 2, LATE // 2
+    half_out[pl.ds(0, rows), :] = (
+        early[pl.ds(0, rows), :] + other[pl.ds(0, rows), :].astype(F32)
+    ).astype(BF16)
+    here = core[0]
+    chips = HALF // 2
+    mine = early[pl.ds(rows, DOWN), :].reshape(chips, 8, CH)
+    theirs = other[pl.ds(rows, DOWN), :].astype(F32).reshape(chips, 8, CH)
+    frames = [jnp.where(here == 0, mine, theirs), jnp.where(here == 0, theirs, mine)]
+    frames_out[...] = jnp.concatenate(frames, axis=1).astype(BF16)
     half_out[pl.ds(rows, more), :] = (
         late[...] + other[pl.ds(rows + DOWN, more), :].astype(F32)
     ).astype(BF16)
 
 
-def sum_body(core, blocks, own, other, sent_out, padded):
+def sum_body(blocks, frames, sent_out, padded):
     rows = blocks.shape[1]
     total = blocks[0].astype(F32)
     for block in range(1, blocks.shape[0]):
         total = total + blocks[block].astype(F32)
     padded[...] = jnp.zeros_like(padded)
     padded[pl.ds(0, rows), :] = total
-    here = core[0]
-    chips = own.shape[0]
-    mine = own[:, pl.ds(here, 1)].astype(F32).reshape(chips, 8, CH)
-    theirs = other[pl.ds(EARLY // 2, DOWN), :].astype(F32).reshape(chips, 8, CH)
-    frames = [jnp.where(here == 0, mine, theirs), jnp.where(here == 0, theirs, mine)]
-    frames = jnp.concatenate(frames, axis=1)
+    chips = frames.shape[0]
     near = sent_out.shape[0]
     share = padded.shape[0] // near
     for chip in range(near):
         sent_out[chip, pl.ds(0, share), :] = padded[pl.ds(chip * share, share), :].astype(BF16)
         for far in range(chips // near):
-            sent_out[chip, pl.ds(share + far * 16, 16), :] = frames[far * near + chip].astype(BF16)
+            sent_out[chip, pl.ds(share + far * 16, 16), :] = frames[far * near + chip]
 
 
 def first_rows(received, share):
@@ -511,122 +538,6 @@
     )
 
 
-def sum_body(core, blocks, own, other, sent_out, padded):
-    rows = blocks.shape[1]
-    total = blocks[0].astype(F32)
-    for block in range(1, blocks.shape[0]):
-        total = total + blocks[block].astype(F32)
-    padded[...] = jnp.zeros_like(padded)
-    padded[pl.ds(0, rows), :] = total
-    here = core[0]
-    chips = own.shape[0]
-    mine = own[:, pl.ds(here, 1)].astype(F32).reshape(chips, 8, CH)
-    theirs = other[pl.ds(EARLY // 2, DOWN), :].astype(F32).reshape(chips, 8, CH)
-    frames = [jnp.where(here == 0, mine, theirs), jnp.where(here == 0, theirs, mine)]
-    frames = jnp.concatenate(frames, axis=1)
-    near = sent_out.shape[0]
-    share = padded.shape[0] // near
-    for chip in range(near):
-        sent_out[chip, pl.ds(0, share), :] = padded[pl.ds(chip * share, share), :].astype(BF16)
-        for far in range(chips // near):
-            sent_out[chip, pl.ds(share + far * 16, 16), :] = frames[far * near + chip].astype(BF16)
-
-
-def first_rows(received, share):
-    total = received[0, pl.ds(0, share), :].astype(F32)
-    for chip in range(1, received.shape[0]):
-        total = total + received[chip, pl.ds(0, share), :].astype(F32)
-    return total.astype(BF16)
-
-
-def near_body(received, sent_out):
-    near, far = received.shape[0], sent_out.shape[0]
-    share = sent_out.shape[1] - near * 16
-    piece = first_rows(received, share)
-    for there in range(far):
-        sent_out[there, pl.ds(0, share), :] = piece
-        for chip in range(near):
-            sent_out[there, pl.ds(share + chip * 16, 16), :] = received[
-                chip, pl.ds(share + there * 16, 16), :
-            ]
-
-
-def piece_body(received, piece_out):
-    piece = first_rows(received, piece_out.shape[1])
-    for chip in range(piece_out.shape[0]):
-        piece_out[chip] = piece
-
-
-def spread_body(pieces, part_out):
-    flat = pieces[...].reshape(-1, CH).astype(F32)
-    part = flat[: part_out.shape[1]].astype(BF16)
-    for block in range(part_out.shape[0]):
-        part_out[block] = part
-
-
-def results_body(
-    core, mine, other,
-    first_plane_out, first_time_out, down_plane_out, down_time_out, last_time_out,
-    early, late,
-):
-    here = core[0]
-    rows, more = EARLY // 2, LATE // 2
-    for half, at in ((mine, here), (other, 1 - here)):
-        early[pl.ds(pl.multiple_of(at * rows, 16), rows), :] = half[pl.ds(0, rows), :]
-        late[pl.ds(pl.multiple_of(at * more, 16), more), :] = half[pl.ds(rows, more), :]
-    first_plane_out[...] = late[pl.ds(0, 9 * CH), :]
-    first_time_out[...] = early[pl.ds(0, 3 * CH), :]
-    for half in range(2):
-        lanes = pl.ds(half * CH, CH)
-        down_plane_out[:, lanes] = early[pl.ds(3 * CH + half * 9 * CH, 9 * CH), :]
-        down_time_out[:, lanes] = early[pl.ds(21 * CH + half * 6 * CH, 6 * CH), :]
-        last_time_out[pl.ds(0, WIDE), lanes] = late[pl.ds(9 * CH + half * WIDE, WIDE), :]
-        last_time_out[pl.ds(WIDE, WIDE), lanes] = early[pl.ds(37 * CH + half * WIDE, WIDE), :]
-        last_time_out[pl.ds(2 * WIDE, WIDE), lanes] = early[pl.ds(33 * CH + half * WIDE, WIDE), :]
-
-
-def output_body(received, last_time, output, spread, padded):
-    share = received.shape[1] - 16 * HALF // 2 // received.shape[0]
-    for far in range(received.shape[0]):
-        rows = received.shape[1] - share
-        spread[pl.ds(far * rows, rows), :] = received[far, pl.ds(share, rows), :].astype(F32)
-    padded[pl.ds(0, 8), :] = jnp.zeros((8, WIDE), F32)
-    for half in range(2):
-        padded[pl.ds(8, DOWN), pl.ds(half * CH, CH)] = spread[pl.ds(half, DOWN, stride=2), :]
-    total = padded[pl.ds(8, DOWN), :]
-    for k in range(3):
-        taps = padded[pl.ds(4 * k, DOWN), :].astype(BF16)
-        total = total + dot(taps, last_time[k])
-    output[...] = total.astype(BF16)
-
-
-def from_behind(block, distance):
-    devices = range(lax.axis_size("seq"))
-    route = [(i - distance, i) for i in devices if i - distance in devices]
-    return lax.ppermute(block, "seq", route)
-
-
-def swap_cores(block):
-    count = lax.axis_size("seq")
-    return lax.ppermute(block, "seq", [(i, i ^ 1) for i in range(count)])
-
-
-def exchange_clip(blocks):
-    return lax.all_to_all(blocks, "clip", split_axis=0, concat_axis=0, tiled=True)
-
-
-def exchange_seq(blocks):
-    return lax.all_to_all(blocks, "seq", split_axis=0, concat_axis=0, tiled=True)
-
-
-def exchange_depth(blocks):
-    count = lax.axis_size("seq")
-    groups = [list(range(core, count, 2)) for core in range(2)]
-    return lax.all_to_all(
-        blocks, "seq", split_axis=0, concat_axis=0, axis_index_groups=groups, tiled=True
-    )
-
-
 def local(clip_in, first_plane, first_time, down_plane, down_time, last_time, cotan_out):
     own = clip_in.reshape(4 * CELLS, CH)
     prior = from_behind(own, 1)
@@ -651,89 +562,83 @@
             ((2 * CELLS, 12 * CH), BF16),
         ],
         copies=3,
-        flops=600000000,
-    )
-    sent, prior = lax.optimization_barrier((sent, prior))
+    )
+    (acts,) = call(
+        prior_body,
+        [(V, prior), (P_, acts), (P_, both)],
+        [(P_, (6, 2, CELLS, CH), BF16)],
+        [((2 * CELLS, CH), F32), ((2 * CELLS, 12 * CH), BF16)],
+    )
+    sent, acts = lax.optimization_barrier((sent, acts))
     received = exchange_seq(sent)
-    prior_hidden, cells, strided = call(
+    times = (P_, (2, WIDE, WIDE), BF16)
+    kept, strided, part, near_times = call(
         first_body,
-        [(V, prior), (P_, acts), (P_, both), (H, first_time), (H, down_plane)],
-        [
-            (P_, flat_frames, BF16),
-            (P_, (2 * DOWN, 9 * CH), BF16),
+        [
+            (P_, acts), (H, first_time), (H, down_plane), (H, down_time),
+        ],
+        [
+            (P_, (KEPT, CH), BF16),
             (P_, (2, DOWN, WIDE), BF16),
+            (P_, (DOWN, WIDE), F32),
+            times,
         ],
         [
             ((3, CH, CH), BF16),
             ((3, 3, CH, WIDE), BF16),
-            ((2 * CELLS, CH), F32),
-            ((2 * CELLS, 12 * CH), BF16),
-        ],
-        copies=2,
-        flops=1000000000,
+            ((3, WIDE, WIDE), BF16),
+        ],
+        copies=3,
     )
     strided_prior = from_behind(strided, 1)
-    times = (P_, (2, WIDE, WIDE), BF16)
     down = (P_, (DOWN, WIDE), BF16)
-    grad_lowered, cot, part, near_times = call(
-        cotan_body,
-        [(P_, strided), (V, received), (H, down_time)],
-        [down, down, (P_, (DOWN, WIDE), F32), times],
-        [((3, WIDE, WIDE), BF16), ((HALF * 16, CH), F32)],
-        copies=1,
-        flops=100000000,
+    grad_lowered, cot = call(
+        cotan_body, [(V, received)], [down, down], [((HALF * 16, CH), F32)]
     )
     lowered, sent = call(
         middle_body,
         [(V, strided_prior), (P_, part), (P_, near_times), (P_, grad_lowered), (P_, cot)],
         [down, (P_, (2 * DOWN, WIDE), BF16)],
-        flops=60000000,
     )
     ahead = from_behind(sent, -1)
-    part, near_times, kernels, time_grads, lowered_rows = call(
+    near_times, kernels, time_grads = call(
         time_grads_body,
         [
-            (P_, sent), (P_, lowered), (V, strided_prior), (P_, strided),
+            (P_, sent), (P_, lowered), (V, strided_prior), (P_, kept),
             (H, down_time), (H, down_plane),
         ],
         [
-            (P_, (DOWN, WIDE), F32),
             times,
             (P_, (4 * CH, 4 * WIDE), BF16),
-            (P_, (8 * WIDE, CH), F32),
-            (P_, (HALF // 2, 2, 8, CH), BF16),
-        ],
-        [((3, WIDE, WIDE), BF16), ((3, 3, CH, WIDE), BF16), ((HALF * 8, CH), F32)],
+            (P_, (PART_AT + 2 * DOWN, CH), F32),
+        ],
+        [((3, WIDE, WIDE), BF16), ((3, 3, CH, WIDE), BF16)],
         copies=2,
-        flops=120000000,
-    )
-    grad_strided, sent = call(
+    )
+    (sent,) = call(
         back_body,
-        [(V, ahead), (P_, part), (P_, near_times), (P_, kernels)],
-        [(P_, (2 * DOWN, WIDE), BF16), (P_, (4 * CELLS + 2 * DOWN, CH), BF16)],
+        [(V, ahead), (P_, time_grads), (P_, near_times), (P_, kernels)],
+        [(P_, (4 * CELLS + 2 * DOWN, CH), BF16)],
         [((2 * DOWN, 4 * WIDE), BF16)],
-        flops=300000000,
     )
     further = from_behind(sent, -1)
     core = (lax.axis_index("seq") % 2).astype(jnp.int32).reshape(1)
     early, early_other, windows, slope, part, near_time = call(
         plane_grads_body,
         [
-            (S, core), (P_, grad_strided), (P_, sent),
-            (P_, cells), (P_, prior_hidden), (P_, acts), (P_, pre_first), (H, first_time),
-            (P_, time_grads), (P_, lowered), (P_, lowered_rows), (V, ahead),
-        ],
-        [
-            (P_, (EARLY // 2, CH), F32),
+            (S, core), (P_, sent), (P_, kept), (P_, acts), (P_, pre_first),
+            (H, first_time), (H, down_time), (P_, time_grads), (P_, lowered), (V, ahead),
+        ],
+        [
+            (P_, (EARLY // 2 + DOWN, CH), F32),
             (P_, (EARLY // 2 + DOWN, CH), BF16),
             (P_, (2 * CELLS, 12 * CH), BF16),
             (P_, flat_frames, F32),
             (P_, flat_frames, F32),
             (P_, (3, CH, CH), BF16),
         ],
-        [((EARLY, CH), F32)],
-        copies=1,
-        flops=500000000,
+        [((EARLY, CH), F32), ((HALF // 2, 2, 8, CH), F32), ((3, WIDE, WIDE), BF16)],
+        copies=2,
     )
     late, other = call(
         last_body,
@@ -743,7 +648,6 @@
         ],
         [(P_, (LATE // 2, CH), F32), (P_, ((EARLY + LATE) // 2 + DOWN, CH), BF16)],
         [((LATE, CH), F32)],
-        flops=600000000,
     )
 
     clips = lax.axis_size("clip")
@@ -751,17 +655,17 @@
     half_rows = (EARLY + LATE) // 2
     part_rows = half_rows // clips
     other = swap_cores(other)
-    (half,) = call(
+    half, frames = call(
         halves_body,
-        [(P_, early), (P_, late), (V, other)],
-        [(P_, (half_rows, CH), BF16)],
+        [(S, core), (P_, early), (P_, late), (V, other)],
+        [(P_, (half_rows, CH), BF16), (V, (chips, 16, CH), BF16)],
     )
     blocks = exchange_clip(half.reshape(clips, part_rows, CH))
     far = chips // NEAR
     share = 16 * (-(-part_rows // (16 * NEAR)))
     (sent,) = call(
         sum_body,
-        [(S, core), (V, blocks), (P_, lowered_rows), (V, other)],
+        [(V, blocks), (V, frames)],
         [(V, (NEAR, share + far * 16, CH), BF16)],
         [((NEAR * share, CH), F32)],
     )
@@ -775,7 +679,6 @@
         [(V, received), (V, last_time)],
         [(V, (DOWN, WIDE), BF16)],
         [((HALF * 8, CH), F32), ((DOWN + 8, WIDE), F32)],
-        flops=60000000,
     )
     (parts,) = call(spread_body, [(V, pieces)], [(V, (clips, part_rows, CH), BF16)])
     half = exchange_clip(parts).reshape(half_rows, CH)

time: 148 us -> 148 us (level)
  local copies, waits for them, and re-layouts: 8.2 us -> 2.57 us
  waiting for transfers between devices: 14.7 us -> 18.9 us
  Pallas kernels: 12.9 us -> 14.4 us
    unnamed x20 -> x6, local copies, waits for them, and re-layouts: 6.68 us -> 1.05 us
    all_to_all x1, waiting for transfers between devices: 8.1 us -> 10.2 us  [exchange_seq(): lax.all_to_all(blocks, 'seq', split_axis=0, concat_axis=0, tiled=True)]
    ppermute x4, waiting for transfers between devices: 3.02 us -> 5.1 us  [from_behind(): return lax.ppermute(block, 'seq', route)]
    pallas_call x15 -> x16, Pallas kernels: 12.9 us -> 14.4 us  [call(): pl.pallas_call(body, out_shape=[placed_output(*out) for out in outs], in_...]
where the time goes in v7:
time: 148 us; the launch traced here: 147 us
  blocking collectives  68.2 us (46%)
  starting transfers between devices  42.2 us (29%)
  waiting for transfers between devices  18.9 us (13%)
  Pallas kernels  14.4 us (10%)
  local copies, waits for them, and re-layouts  2.57 us (2%)
    all_to_all x2, blocking collectives, exchange_clip(): lax.all_to_all(blocks, 'clip', split_axis=0, concat_axis=0, tiled=True)  35.2 us
    all_to_all x3, blocking collectives, exchange_chips(): lax.all_to_all(blocks, 'seq', split_axis=0, concat_axis=0, axis_index_gro...  33 us
    all_to_all x1, starting transfers between devices, exchange_seq(): lax.all_to_all(blocks, 'seq', split_axis=0, concat_axis=0, tiled=True)  16.5 us
    pallas_call x16, Pallas kernels, call(): pl.pallas_call(body, out_shape=[placed_output(*out) for out in outs], in_...  14.4 us
    ppermute x4, starting transfers between devices, from_behind(): return lax.ppermute(block, 'seq', route)  14.1 us
    ppermute x2, starting transfers between devices, swap_cores(): return lax.ppermute(block, 'seq', [(i, i ^ 1) for i in range(count)])  11.6 us
    all_to_all x1, waiting for transfers between devices, exchange_seq(): lax.all_to_all(blocks, 'seq', split_axis=0, concat_axis=0, tiled=True)  10.2 us
    ppermute x4, waiting for transfers between devices, from_behind(): return lax.ppermute(block, 'seq', route)  5.1 us
  transfers between devices with their start and end apart: 7, of which 6 were waited for; matrix products, arithmetic and copies ran while one was open for 1% of the time, Pallas kernels for 6%

profile of v7, /device:TPU:1, one launch (start us, length us, event | category | flops | bytes accessed | tf_op | source)
XLA Modules:
  0.0 147.1 jit_solution(15079595216733251127)
XLA Ops:
  0.6 4.9 %collective-permute-start = (bf16[1024,128]{1,0:T(8,128)(2,1)}, bf16[1024,128]{1,0:T(8,128)(2,1)S(1)}, u32[]{:S(2)}, u32[]{:S(2)}) collective-permute-start(bf16[1024,128]{1,0:T(8,128)(2,1)} %bitcast.13), channel_id=1, source_target_pairs={{0,1},{1,2},{2,3},{3,4},{4,5},{5,6},{6,7},{7,8},{8,9},{9,10},{10,1... | collective-permute-start | bytes 786440 | tf_op jit(solution)/shard_map/ppermute | solution.py:514
  5.6 0.9 reshape_squeeze.3.rows
  6.5 2.5 %shard_map.118 = (bf16[32,16,128]{2,1,0:T(8,128)(2,1)}, bf16[4,2,256,128]{3,2,1,0:T(8,128)(2,1)S(1)}, f32[2,2,256,128]{3,2,1,0:T(8,128)S(1)}, bf16[1536,256]{1,0:T(8,128)(2,1)S(1)}) custom-call(bf16[32,8,128]{2,1,0:T(8,128)(2,1)S(1)} %reshape_squeeze.3.rows, bf16[3,256,256]{2,1,0:T(8,128)(2,1)} %last_time.1, bf16[1024,128]{1,0:T(8,128)(2,1)} %bitcast.14, ...), custom_call_target="tpu_custom_call" | custom-call | flops 1000 | bytes 8000000 | tf_op jit(solution)/shard_map/pallas_call | solution.py:58
  9.0 1.1 collective-permute-done.prior
  10.0 0.8 shard_map.119.acts
  10.9 16.5 %all-to-all-start = ((bf16[32,16,128]{2,1,0:T(8,128)(2,1)}), bf16[32,16,128]{2,1,0:T(8,128)(2,1)S(1)}, u32[]{:S(2)}, u32[]{:S(2)}) async-start(bf16[32,16,128]{2,1,0:T(8,128)(2,1)} %get-tuple-element.45), calls=%async_computation | async-start | bytes 262144 | tf_op jit(solution)/shard_map/all_to_all | solution.py:527
  27.4 2.1 %shard_map.120 = (bf16[2560,128]{1,0:T(8,128)(2,1)S(1)}, bf16[2,128,256]{2,1,0:T(8,128)(2,1)S(1)}, f32[128,256]{1,0:T(8,128)S(1)}, bf16[2,256,256]{2,1,0:T(8,128)(2,1)S(1)}) custom-call(bf16[6,2,256,128]{3,2,1,0:T(8,128)(2,1)S(1)} %shard_map.119.acts, bf16[3,128,128]{2,1,0:T(8,128)(2,1)} %time_far.3, bf16[3,3,128,256]{3,2,1,0:T(8,128)(2,1)} %plane_far.5, ...), custom_call_target="tpu_custom_call" | custom-call | flops 1000 | bytes 8000000 | tf_op jit(solution)/shard_map/pallas_call | solution.py:58
  29.5 3.5 %collective-permute-start.1 = (bf16[2,128,256]{2,1,0:T(8,128)(2,1)S(1)}, bf16[2,128,256]{2,1,0:T(8,128)(2,1)S(1)}, u32[]{:S(2)}, u32[]{:S(2)}) collective-permute-start(bf16[2,128,256]{2,1,0:T(8,128)(2,1)S(1)} %get-tuple-element.42), channel_id=1, source_target_pairs={{0,1},{1,2},{2,3},{3,4},{4,5},{5,6},{6,7},{7,8},{8,9},{9,10},{10,1... | collective-permute-start | bytes 393224 | tf_op jit(solution)/shard_map/ppermute | solution.py:514
  33.0 10.2 %all-to-all-done.received = bf16[32,16,128]{2,1,0:T(8,128)(2,1)S(1)} async-done(((bf16[32,16,128]{2,1,0:T(8,128)(2,1)}), bf16[32,16,128]{2,1,0:T(8,128)(2,1)S(1)}, u32[]{:S(2)}, u32[]{:S(2)}) %all-to-all-start) | async-done | bytes 131104 | tf_op jit(solution)/shard_map/all_to_all | solution.py:527
  43.4 0.2 shard_map.122
  43.6 3.7 %collective-permute-start.2 = (bf16[256,256]{1,0:T(8,128)(2,1)S(1)}, bf16[256,256]{1,0:T(8,128)(2,1)S(1)}, u32[]{:S(2)}, u32[]{:S(2)}) collective-permute-start(bf16[256,256]{1,0:T(8,128)(2,1)S(1)} %get-tuple-element.48.sent), channel_id=1, source_target_pairs={{1,0},{2,1},{3,2},{4,3},{5,4},{6,5},{7,6},{8,7},{9,8},{10,9},{11,1... | collective-permute-start | bytes 393224 | tf_op jit(solution)/shard_map/ppermute | solution.py:514
  47.3 1.5 %shard_map.123 = (bf16[2,256,256]{2,1,0:T(8,128)(2,1)S(1)}, bf16[512,1024]{1,0:T(8,128)(2,1)S(1)}, f32[2560,128]{1,0:T(8,128)S(1)}) custom-call(bf16[256,256]{1,0:T(8,128)(2,1)S(1)} %get-tuple-element.48.sent, bf16[128,256]{1,0:T(8,128)(2,1)S(1)} %get-tuple-element.49.lowered, bf16[2,128,256]{2,1,0:T(8,128)(2,1)S(1)} %collective-permute-done.1.prior, ...), custom_call_target="tpu_custom_call" | custom-call | flops 1000 | bytes 8000000 | tf_op jit(solution)/shard_map/pallas_call | solution.py:58
  48.8 1.1 collective-permute-done.2.ahead
  49.9 0.6 shard_map.124.grad_mixed
  50.5 1.9 %collective-permute-start.3 = (bf16[1280,128]{1,0:T(8,128)(2,1)S(1)}, bf16[1280,128]{1,0:T(8,128)(2,1)}, u32[]{:S(2)}, u32[]{:S(2)}) collective-permute-start(bf16[1280,128]{1,0:T(8,128)(2,1)S(1)} %shard_map.124.grad_mixed), channel_id=1, source_target_pairs={{1,0},{2,1},{3,2},{4,3},{5,4},{6,5},{7,6},{8,7},{9,8},{10,9},{11,1... | collective-permute-start | bytes 983048 | tf_op jit(solution)/shard_map/ppermute | solution.py:514
  52.4 1.0 copy-done.2
  53.5 2.5 %shard_map.125 = (f32[2752,128]{1,0:T(8,128)S(1)}, bf16[2752,128]{1,0:T(8,128)(2,1)S(1)}, bf16[512,1536]{1,0:T(8,128)(2,1)S(1)}, f32[2,2,256,128]{3,2,1,0:T(8,12...) custom-call(s32[1]{0:T(128)} %bitcast.core, bf16[1280,128]{1,0:T(8,128)(2,1)S(1)} %shard_map.124.grad_mixed, ...), custom_call_target="tpu_custom_call" | custom-call | flops 1000 | bytes 8000000 | tf_op jit(solution)/shard_map/pallas_call | solution.py:58
  56.0 3.0 %collective-permute-done.3.ahead = bf16[1280,128]{1,0:T(8,128)(2,1)} collective-permute-done((bf16[1280,128]{1,0:T(8,128)(2,1)S(1)}, bf16[1280,128]{1,0:T(8,128)(2,1)}, u32[]{:S(2)}, u32[]{:S(2)}) %collective-permute-start.3) | collective-permute-done | bytes 327712 | tf_op jit(solution)/shard_map/ppermute | solution.py:514
  59.0 1.9 %shard_map.126 = (f32[832,128]{1,0:T(8,128)S(1)}, bf16[3584,128]{1,0:T(8,128)(2,1)S(1)}) custom-call(s32[1]{0:T(128)} %bitcast.core, bf16[1280,128]{1,0:T(8,128)(2,1)} %collective-permute-done.3.ahead, bf16[512,1536]{1,0:T(8,128)(2,1)S(1)} %get-tuple-element.56.windows, f32[2,2,256,128]{3,2,1,0:T(8,128)S(1)} %get-tuple-element.57.slope, ...), custom_call_target="tpu_custom_call" | custom-call | flops 1000 | bytes 8000000 | tf_op jit(solution)/shard_map/pallas_call | solution.py:58
  60.9 1.9 %collective-permute-start.4 = (bf16[3584,128]{1,0:T(8,128)(2,1)S(1)}, bf16[3584,128]{1,0:T(8,128)(2,1)S(1)}, u32[]{:S(2)}, u32[]{:S(2)}) collective-permute-start(bf16[3584,128]{1,0:T(8,128)(2,1)S(1)} %get-tuple-element.62), channel_id=1, source_target_pairs={{0,1},{1,0},{2,3},{3,2},{4,5},{5,4},{6,7},{7,6},{8,9},{9,8},{10,11... | collective-permute-start | bytes 2752520 | tf_op jit(solution)/shard_map/ppermute | solution.py:519
  62.9 2.4 %collective-permute-done.4.other = bf16[3584,128]{1,0:T(8,128)(2,1)S(1)} collective-permute-done((bf16[3584,128]{1,0:T(8,128)(2,1)S(1)}, bf16[3584,128]{1,0:T(8,128)(2,1)S(1)}, u32[]{:S(2)}, u32[]{:S(2)}) %collective-permute-start.4) | collective-permute-done | bytes 917536 | tf_op jit(solution)/shard_map/ppermute | solution.py:519
  65.3 0.2 shard_map.127
  65.4 20.6 %all_to_all.30.blocks = bf16[16,216,128]{2,1,0:T(8,128)(2,1)S(1)} all-to-all(bf16[16,216,128]{2,1,0:T(8,128)(2,1)S(1)} %bitcast.12), channel_id=1, replica_groups=mesh['clip'=16,'seq'=32] {'clip'}, dimensions={0} | all-to-all | bytes 1769472 | tf_op jit(solution)/shard_map/all_to_all | solution.py:523
  86.2 9.1 %all_to_all.31.received = bf16[4,128,128]{2,1,0:T(8,128)(2,1)S(1)} all-to-all(bf16[4,128,128]{2,1,0:T(8,128)(2,1)S(1)} %shard_map.128), channel_id=1, replica_groups={{0,2,4,6},{1,3,5,7},{8,10,12,14},{9,11,13,15},{16,18,20,22},{17,19,21,2..., dimensions={0} | all-to-all | bytes 262144 | tf_op jit(solution)/shard_map/all_to_all | solution.py:536
  95.3 16.5 %all_to_all.32.received = bf16[4,128,128]{2,1,0:T(8,128)(2,1)S(1)} all-to-all(bf16[4,128,128]{2,1,0:T(8,128)(2,1)S(1)} %shard_map.129), channel_id=1, replica_groups={{0,8,16,24},{1,9,17,25},{2,10,18,26},{3,11,19,27},{4,12,20,28},{5,13,21..., dimensions={0} | all-to-all | bytes 262144 | tf_op jit(solution)/shard_map/all_to_all | solution.py:536
  111.9 7.4 %all_to_all.33.pieces = bf16[4,64,128]{2,1,0:T(8,128)(2,1)S(1)} all-to-all(bf16[4,64,128]{2,1,0:T(8,128)(2,1)S(1)} %shard_map.131), channel_id=1, replica_groups={{0,2,4,6},{1,3,5,7},{8,10,12,14},{9,11,13,15},{16,18,20,22},{17,19,21,2..., dimensions={0} | all-to-all | bytes 131072 | tf_op jit(solution)/shard_map/all_to_all | solution.py:536
  119.4 14.6 %all_to_all.34 = bf16[16,216,128]{2,1,0:T(8,128)(2,1)S(1)} all-to-all(bf16[16,216,128]{2,1,0:T(8,128)(2,1)S(1)} %shard_map.132), channel_id=1, replica_groups=mesh['clip'=16,'seq'=32] {'clip'}, dimensions={0} | all-to-all | bytes 1769472 | tf_op jit(solution)/shard_map/all_to_all | solution.py:523
  133.9 9.7 %collective-permute-start.5 = (bf16[3456,128]{1,0:T(8,128)(2,1)S(1)}, bf16[3456,128]{1,0:T(8,128)(2,1)S(1)}, u32[]{:S(2)}, u32[]{:S(2)}) collective-permute-start(bf16[3456,128]{1,0:T(8,128)(2,1)S(1)} %bitcast.10), channel_id=1, source_target_pairs={{0,1},{1,0},{2,3},{3,2},{4,5},{5,4},{6,7},{7,6},{8,9},{9,8},{10,11... | collective-permute-start | bytes 2654216 | tf_op jit(solution)/shard_map/ppermute | solution.py:519
  143.7 0.2 shard_map.130
  143.9 0.7 reshape.45
  144.6 1.1 collective-permute-done.5.other
  145.7 1.4 shard_map.133
  (11 shorter events, 0.4 us)
Async XLA Ops:
  0.6 9.4 %collective-permute-start = (bf16[1024,128]{1,0:T(8,128)(2,1)}, bf16[1024,128]{1,0:T(8,128)(2,1)S(1)}, u32[]{:S(2)}, u32[]{:S(2)}) collective-permute-start(bf16[1024,128]{1,0:T(8,128)(2,1)} %bitcast.13), channel_id=1, source_target_pairs={{0,1},{1,2},{2,3},{3,4},{4,5},{5,6},{6,7},{7,8},{8,9},{9,10},{10,1... | collective-permute-start | bytes 786440 | tf_op jit(solution)/shard_map/ppermute | solution.py:514
  9.0 1.9 %copy-start.1 = (f32[2,2,256,128]{3,2,1,0:T(8,128)}, f32[2,2,256,128]{3,2,1,0:T(8,128)S(1)}, u32[]{:S(2)}) copy-start(f32[2,2,256,128]{3,2,1,0:T(8,128)S(1)} %get-tuple-element.54.pre) | copy-start | bytes 1572868
  10.9 32.4 %all-to-all-start = ((bf16[32,16,128]{2,1,0:T(8,128)(2,1)}), bf16[32,16,128]{2,1,0:T(8,128)(2,1)S(1)}, u32[]{:S(2)}, u32[]{:S(2)}) async-start(bf16[32,16,128]{2,1,0:T(8,128)(2,1)} %get-tuple-element.45), calls=%async_computation | async-start | bytes 262144 | tf_op jit(solution)/shard_map/all_to_all | solution.py:527
  29.5 13.9 %collective-permute-start.1 = (bf16[2,128,256]{2,1,0:T(8,128)(2,1)S(1)}, bf16[2,128,256]{2,1,0:T(8,128)(2,1)S(1)}, u32[]{:S(2)}, u32[]{:S(2)}) collective-permute-start(bf16[2,128,256]{2,1,0:T(8,128)(2,1)S(1)} %get-tuple-element.42), channel_id=1, source_target_pairs={{0,1},{1,2},{2,3},{3,4},{4,5},{5,6},{6,7},{7,8},{8,9},{9,10},{10,1... | collective-permute-start | bytes 393224 | tf_op jit(solution)/shard_map/ppermute | solution.py:514
  43.6 6.3 %collective-permute-start.2 = (bf16[256,256]{1,0:T(8,128)(2,1)S(1)}, bf16[256,256]{1,0:T(8,128)(2,1)S(1)}, u32[]{:S(2)}, u32[]{:S(2)}) collective-permute-start(bf16[256,256]{1,0:T(8,128)(2,1)S(1)} %get-tuple-element.48.sent), channel_id=1, source_target_pairs={{1,0},{2,1},{3,2},{4,3},{5,4},{6,5},{7,6},{8,7},{9,8},{10,9},{11,1... | collective-permute-start | bytes 393224 | tf_op jit(solution)/shard_map/ppermute | solution.py:514
  50.5 8.5 %collective-permute-start.3 = (bf16[1280,128]{1,0:T(8,128)(2,1)S(1)}, bf16[1280,128]{1,0:T(8,128)(2,1)}, u32[]{:S(2)}, u32[]{:S(2)}) collective-permute-start(bf16[1280,128]{1,0:T(8,128)(2,1)S(1)} %shard_map.124.grad_mixed), channel_id=1, source_target_pairs={{1,0},{2,1},{3,2},{4,3},{5,4},{6,5},{7,6},{8,7},{9,8},{10,9},{11,1... | collective-permute-start | bytes 983048 | tf_op jit(solution)/shard_map/ppermute | solution.py:514
  52.4 1.0 copy-start.2
  60.9 4.4 %collective-permute-start.4 = (bf16[3584,128]{1,0:T(8,128)(2,1)S(1)}, bf16[3584,128]{1,0:T(8,128)(2,1)S(1)}, u32[]{:S(2)}, u32[]{:S(2)}) collective-permute-start(bf16[3584,128]{1,0:T(8,128)(2,1)S(1)} %get-tuple-element.62), channel_id=1, source_target_pairs={{0,1},{1,0},{2,3},{3,2},{4,5},{5,4},{6,7},{7,6},{8,9},{9,8},{10,11... | collective-permute-start | bytes 2752520 | tf_op jit(solution)/shard_map/ppermute | solution.py:519
  111.8 31.8 %copy-start = (bf16[3,256,256]{2,1,0:T(8,128)(2,1)S(1)}, bf16[3,256,256]{2,1,0:T(8,128)(2,1)}, u32[]{:S(2)}) copy-start(bf16[3,256,256]{2,1,0:T(8,128)(2,1)} %last_time.1) | copy-start | bytes 1179652
  133.9 11.8 %collective-permute-start.5 = (bf16[3456,128]{1,0:T(8,128)(2,1)S(1)}, bf16[3456,128]{1,0:T(8,128)(2,1)S(1)}, u32[]{:S(2)}, u32[]{:S(2)}) collective-permute-start(bf16[3456,128]{1,0:T(8,128)(2,1)S(1)} %bitcast.10), channel_id=1, source_target_pairs={{0,1},{1,0},{2,3},{3,2},{4,5},{5,4},{6,7},{7,6},{8,9},{9,8},{10,11... | collective-permute-start | bytes 2654216 | tf_op jit(solution)/shard_map/ppermute | solution.py:519

commit v8 on v7

--- a/solution.py
+++ b/solution.py
@@ -51,7 +51,7 @@
     return jax.ShapeDtypeStruct(shape, kind)
 
 
-def call(body, ins, outs, scratch=(), copies=0):
+def call(body, ins, outs, scratch=(), copies=0, cost=8000000):
     scratch = [pltpu.VMEM(shape, kind) for shape, kind in scratch]
     if copies:
         scratch.append(pltpu.SemaphoreType.DMA((copies,)))
@@ -62,7 +62,7 @@
         out_specs=[pl.BlockSpec(memory_space=SPACES[space]) for space, _, _ in outs],
         scratch_shapes=scratch,
         compiler_params=pltpu.CompilerParams(vmem_limit_bytes=24 * 1024 * 1024),
-        cost_estimate=pl.CostEstimate(flops=1000, bytes_accessed=8000000, transcendentals=0),
+        cost_estimate=pl.CostEstimate(flops=1000, bytes_accessed=cost, transcendentals=0),
     )(*[placed_input(*given) for given in ins])
 
 
@@ -175,15 +175,8 @@
     times_out[...] = down_time[pl.ds(0, 2)]
 
 
-def own_body(
-    rows, last_far, own_far, plane_far,
-    sent_out, acts_out, pre_out, both_out,
-    last_time, own, first_plane, spread, padded, turned, cells, windows, sems,
-):
-    loads = start(
-        sems, (0, last_far, last_time), (1, own_far, own), (2, plane_far, first_plane)
-    )
-    both_out[...] = jnp.zeros_like(both_out)
+def rows_body(rows, last_far, sent_out, last_time, spread, padded, turned, sems):
+    loads = start(sems, (0, last_far, last_time))
     cotan = rows[...].astype(F32)
     spread[...] = cotan.reshape(HALF * 8, CH)
     for half in range(2):
@@ -199,13 +192,21 @@
     both = jnp.concatenate([turned[...].reshape(HALF, 8, CH), cotan], axis=1)
     sent_out[...] = both.astype(BF16)
 
-    loads[1].wait()
+
+def own_body(
+    own_far, plane_far,
+    acts_out, pre_out, both_out,
+    own, first_plane, cells, windows, sems,
+):
+    loads = start(sems, (0, own_far, own), (1, plane_far, first_plane))
+    both_out[...] = jnp.zeros_like(both_out)
+    loads[0].wait()
     for frame in range(2):
         planes = parity_planes(own, frame, cells)
         fill_windows(windows, frame * CELLS, *planes)
         for par in range(2):
             acts_out[2 + frame, par] = planes[par].reshape(CELLS, CH)
-    loads[2].wait()
+    loads[1].wait()
     for tap in range(3):
         for row in range(4):
             at = pl.ds((tap * 4 + row) * CH, CH)
@@ -542,26 +543,34 @@
     own = clip_in.reshape(4 * CELLS, CH)
     prior = from_behind(own, 1)
     flat_frames = (2, 2, CELLS, CH)
-    sent, acts, pre_first, both = call(
+    (sent,) = call(
+        rows_body,
+        [(V, cotan_out[0].reshape(HALF, 8, CH)), (H, last_time)],
+        [(V, (HALF, 16, CH), BF16)],
+        [
+            ((3, WIDE, WIDE), BF16),
+            ((HALF * 8, CH), F32),
+            ((DOWN + 8, WIDE), F32),
+            ((HALF * 8, CH), F32),
+        ],
+        copies=1,
+    )
+    received = exchange_seq(sent)
+    acts, pre_first, both = call(
         own_body,
-        [(V, cotan_out[0].reshape(HALF, 8, CH)), (H, last_time), (H, own), (H, first_plane)],
-        [
-            (V, (HALF, 16, CH), BF16),
+        [(H, own), (H, first_plane)],
+        [
             (P_, (4, 2, CELLS, CH), BF16),
             (P_, flat_frames, F32),
             (P_, (12 * CH, WIDE), BF16),
         ],
         [
-            ((3, WIDE, WIDE), BF16),
             ((4 * CELLS, CH), BF16),
             ((3, 3, CH, CH), BF16),
-            ((HALF * 8, CH), F32),
-            ((DOWN + 8, WIDE), F32),
-            ((HALF * 8, CH), F32),
             ((2 * CELLS, CH), F32),
             ((2 * CELLS, 12 * CH), BF16),
         ],
-        copies=3,
+        copies=2,
     )
     (acts,) = call(
         prior_body,
@@ -569,8 +578,6 @@
         [(P_, (6, 2, CELLS, CH), BF16)],
         [((2 * CELLS, CH), F32), ((2 * CELLS, 12 * CH), BF16)],
     )
-    sent, acts = lax.optimization_barrier((sent, acts))
-    received = exchange_seq(sent)
     times = (P_, (2, WIDE, WIDE), BF16)
     kept, strided, part, near_times = call(
         first_body,

time: 148 us -> 151 us (1.020)
  blocking collectives: 68.2 us -> 74.6 us
  waiting for transfers between devices: 18.9 us -> 16.5 us
  starting transfers between devices: 42.2 us -> 40 us
    all_to_all x1, waiting for transfers between devices: 10.2 us -> 0.01 us  [exchange_seq(): lax.all_to_all(blocks, 'seq', split_axis=0, concat_axis=0, tiled=True)]
    ppermute x4, waiting for transfers between devices: 5.1 us -> 13 us  [from_behind(): return lax.ppermute(block, 'seq', route)]
    all_to_all x3, blocking collectives: 33 us -> 39.4 us  [exchange_chips(): lax.all_to_all(blocks, 'seq', split_axis=0, concat_axis=0, axis_index_gro...]
    ppermute x4, starting transfers between devices: 14.1 us -> 11.6 us  [from_behind(): return lax.ppermute(block, 'seq', route)]
    pallas_call x16 -> x17, Pallas kernels: 14.4 us -> 15.9 us  [call(): pl.pallas_call(body, out_shape=[placed_output(*out) for out in outs], in_...]
  transfers between devices with their start and end apart: 7 -> 7, of which waited for: 6 -> 6; matrix products, arithmetic and copies ran while one was open for 1% -> 0% of each run, Pallas kernels for 6% -> 6%
where the time goes in v8:
time: 151 us; the launch traced here: 150 us
  blocking collectives  74.6 us (49%)
  starting transfers between devices  40 us (26%)
  waiting for transfers between devices  16.5 us (11%)
  Pallas kernels  15.9 us (11%)
  local copies, waits for them, and re-layouts  2.57 us (2%)
    all_to_all x3, blocking collectives, exchange_chips(): lax.all_to_all(blocks, 'seq', split_axis=0, concat_axis=0, axis_index_gro...  39.4 us
    all_to_all x2, blocking collectives, exchange_clip(): lax.all_to_all(blocks, 'clip', split_axis=0, concat_axis=0, tiled=True)  35.2 us
    all_to_all x1, starting transfers between devices, exchange_seq(): lax.all_to_all(blocks, 'seq', split_axis=0, concat_axis=0, tiled=True)  16.8 us
    pallas_call x17, Pallas kernels, call(): pl.pallas_call(body, out_shape=[placed_output(*out) for out in outs], in_...  15.9 us
    ppermute x4, waiting for transfers between devices, from_behind(): return lax.ppermute(block, 'seq', route)  13 us
    ppermute x2, starting transfers between devices, swap_cores(): return lax.ppermute(block, 'seq', [(i, i ^ 1) for i in range(count)])  11.6 us
    ppermute x4, starting transfers between devices, from_behind(): return lax.ppermute(block, 'seq', route)  11.6 us
    ppermute x2, waiting for transfers between devices, swap_cores(): return lax.ppermute(block, 'seq', [(i, i ^ 1) for i in range(count)])  3.58 us
  transfers between devices with their start and end apart: 7, of which 6 were waited for; matrix products, arithmetic and copies ran while one was open for 0% of the time, Pallas kernels for 6%

profile of v8, /device:TPU:1, one launch (start us, length us, event | category | flops | bytes accessed | tf_op | source)
XLA Modules:
  0.0 150.5 jit_solution(6505860384302441177)
XLA Ops:
  0.6 0.9 reshape_squeeze.3.rows
  1.5 2.0 %shard_map.121 = bf16[32,16,128]{2,1,0:T(8,128)(2,1)} custom-call(bf16[32,8,128]{2,1,0:T(8,128)(2,1)S(1)} %reshape_squeeze.3.rows, bf16[3,256,256]{2,1,0:T(8,128)(2,1)} %last_time.1), custom_call_target="tpu_custom_call" | custom-call | flops 1000 | bytes 8000000 | tf_op jit(solution)/shard_map/pallas_call | solution.py:58
  3.5 16.8 %all-to-all-start = ((bf16[32,16,128]{2,1,0:T(8,128)(2,1)}), bf16[32,16,128]{2,1,0:T(8,128)(2,1)S(1)}, u32[]{:S(2)}, u32[]{:S(2)}) async-start(bf16[32,16,128]{2,1,0:T(8,128)(2,1)} %shard_map.121), calls=%async_computation | async-start | bytes 262144 | tf_op jit(solution)/shard_map/all_to_all | solution.py:528
  20.2 3.5 %collective-permute-start = (bf16[1024,128]{1,0:T(8,128)(2,1)}, bf16[1024,128]{1,0:T(8,128)(2,1)S(1)}, u32[]{:S(2)}, u32[]{:S(2)}) collective-permute-start(bf16[1024,128]{1,0:T(8,128)(2,1)} %bitcast.13), channel_id=1, source_target_pairs={{0,1},{1,2},{2,3},{3,4},{4,5},{5,6},{6,7},{7,8},{8,9},{9,10},{10,1... | collective-permute-start | bytes 786440 | tf_op jit(solution)/shard_map/ppermute | solution.py:515
  23.8 2.0 %shard_map.118 = (bf16[4,2,256,128]{3,2,1,0:T(8,128)(2,1)S(1)}, f32[2,2,256,128]{3,2,1,0:T(8,128)S(1)}, bf16[1536,256]{1,0:T(8,128)(2,1)S(1)}) custom-call(bf16[1024,128]{1,0:T(8,128)(2,1)} %bitcast.14, bf16[3,3,128,128]{3,2,1,0:T(8,128)(2,1)} %plane_far.3), custom_call_target="tpu_custom_call" | custom-call | flops 1000 | bytes 8000000 | tf_op jit(solution)/shard_map/pallas_call | solution.py:58
  25.8 4.6 %collective-permute-done.prior = bf16[1024,128]{1,0:T(8,128)(2,1)S(1)} collective-permute-done((bf16[1024,128]{1,0:T(8,128)(2,1)}, bf16[1024,128]{1,0:T(8,128)(2,1)S(1)}, u32[]{:S(2)}, u32[]{:S(2)}) %collective-permute-start) | collective-permute-done | bytes 262176 | tf_op jit(solution)/shard_map/ppermute | solution.py:515
  30.4 0.8 shard_map.119.acts
  31.3 2.1 %shard_map.120 = (bf16[2560,128]{1,0:T(8,128)(2,1)S(1)}, bf16[2,128,256]{2,1,0:T(8,128)(2,1)S(1)}, f32[128,256]{1,0:T(8,128)S(1)}, bf16[2,256,256]{2,1,0:T(8,128)(2,1)S(1)}) custom-call(bf16[6,2,256,128]{3,2,1,0:T(8,128)(2,1)S(1)} %shard_map.119.acts, bf16[3,128,128]{2,1,0:T(8,128)(2,1)} %time_far.3, bf16[3,3,128,256]{3,2,1,0:T(8,128)(2,1)} %plane_far.5, ...), custom_call_target="tpu_custom_call" | custom-call | flops 1000 | bytes 8000000 | tf_op jit(solution)/shard_map/pallas_call | solution.py:58
  33.4 4.3 %collective-permute-start.1 = (bf16[2,128,256]{2,1,0:T(8,128)(2,1)S(1)}, bf16[2,128,256]{2,1,0:T(8,128)(2,1)S(1)}, u32[]{:S(2)}, u32[]{:S(2)}) collective-permute-start(bf16[2,128,256]{2,1,0:T(8,128)(2,1)S(1)} %get-tuple-element.37), channel_id=1, source_target_pairs={{0,1},{1,2},{2,3},{3,4},{4,5},{5,6},{6,7},{7,8},{8,9},{9,10},{10,1... | collective-permute-start | bytes 393224 | tf_op jit(solution)/shard_map/ppermute | solution.py:515
  37.8 1.8 %collective-permute-done.1.prior = bf16[2,128,256]{2,1,0:T(8,128)(2,1)S(1)} collective-permute-done((bf16[2,128,256]{2,1,0:T(8,128)(2,1)S(1)}, bf16[2,128,256]{2,1,0:T(8,128)(2,1)S(1)}, u32[]{:S(2)}, u32[]{:S(2)}) %collective-permute-start.1) | collective-permute-done | bytes 131104 | tf_op jit(solution)/shard_map/ppermute | solution.py:515
  39.6 0.2 shard_map.123
  39.8 1.9 %collective-permute-start.2 = (bf16[256,256]{1,0:T(8,128)(2,1)S(1)}, bf16[256,256]{1,0:T(8,128)(2,1)S(1)}, u32[]{:S(2)}, u32[]{:S(2)}) collective-permute-start(bf16[256,256]{1,0:T(8,128)(2,1)S(1)} %get-tuple-element.42.sent), channel_id=1, source_target_pairs={{1,0},{2,1},{3,2},{4,3},{5,4},{6,5},{7,6},{8,7},{9,8},{10,9},{11,1... | collective-permute-start | bytes 393224 | tf_op jit(solution)/shard_map/ppermute | solution.py:515
  41.8 1.5 %shard_map.124 = (bf16[2,256,256]{2,1,0:T(8,128)(2,1)S(1)}, bf16[512,1024]{1,0:T(8,128)(2,1)S(1)}, f32[2560,128]{1,0:T(8,128)S(1)}) custom-call(bf16[256,256]{1,0:T(8,128)(2,1)S(1)} %get-tuple-element.42.sent, bf16[128,256]{1,0:T(8,128)(2,1)S(1)} %get-tuple-element.43.lowered, bf16[2,128,256]{2,1,0:T(8,128)(2,1)S(1)} %collective-permute-done.1.prior, ...), custom_call_target="tpu_custom_call" | custom-call | flops 1000 | bytes 8000000 | tf_op jit(solution)/shard_map/pallas_call | solution.py:58
  43.3 3.6 %collective-permute-done.2.ahead = bf16[256,256]{1,0:T(8,128)(2,1)S(1)} collective-permute-done((bf16[256,256]{1,0:T(8,128)(2,1)S(1)}, bf16[256,256]{1,0:T(8,128)(2,1)S(1)}, u32[]{:S(2)}, u32[]{:S(2)}) %collective-permute-start.2) | collective-permute-done | bytes 131104 | tf_op jit(solution)/shard_map/ppermute | solution.py:515
  46.8 0.6 shard_map.125.grad_mixed
  47.4 1.9 %collective-permute-start.3 = (bf16[1280,128]{1,0:T(8,128)(2,1)S(1)}, bf16[1280,128]{1,0:T(8,128)(2,1)}, u32[]{:S(2)}, u32[]{:S(2)}) collective-permute-start(bf16[1280,128]{1,0:T(8,128)(2,1)S(1)} %shard_map.125.grad_mixed), channel_id=1, source_target_pairs={{1,0},{2,1},{3,2},{4,3},{5,4},{6,5},{7,6},{8,7},{9,8},{10,9},{11,1... | collective-permute-start | bytes 983048 | tf_op jit(solution)/shard_map/ppermute | solution.py:515
  49.4 1.0 copy-done.2
  50.4 2.5 %shard_map.126 = (f32[2752,128]{1,0:T(8,128)S(1)}, bf16[2752,128]{1,0:T(8,128)(2,1)S(1)}, bf16[512,1536]{1,0:T(8,128)(2,1)S(1)}, f32[2,2,256,128]{3,2,1,0:T(8,12...) custom-call(s32[1]{0:T(128)} %bitcast.core, bf16[1280,128]{1,0:T(8,128)(2,1)S(1)} %shard_map.125.grad_mixed, ...), custom_call_target="tpu_custom_call" | custom-call | flops 1000 | bytes 8000000 | tf_op jit(solution)/shard_map/pallas_call | solution.py:58
  53.0 3.0 %collective-permute-done.3.ahead = bf16[1280,128]{1,0:T(8,128)(2,1)} collective-permute-done((bf16[1280,128]{1,0:T(8,128)(2,1)S(1)}, bf16[1280,128]{1,0:T(8,128)(2,1)}, u32[]{:S(2)}, u32[]{:S(2)}) %collective-permute-start.3) | collective-permute-done | bytes 327712 | tf_op jit(solution)/shard_map/ppermute | solution.py:515
  55.9 1.9 %shard_map.127 = (f32[832,128]{1,0:T(8,128)S(1)}, bf16[3584,128]{1,0:T(8,128)(2,1)S(1)}) custom-call(s32[1]{0:T(128)} %bitcast.core, bf16[1280,128]{1,0:T(8,128)(2,1)} %collective-permute-done.3.ahead, bf16[512,1536]{1,0:T(8,128)(2,1)S(1)} %get-tuple-element.50.windows, f32[2,2,256,128]{3,2,1,0:T(8,128)S(1)} %get-tuple-element.51.slope, ...), custom_call_target="tpu_custom_call" | custom-call | flops 1000 | bytes 8000000 | tf_op jit(solution)/shard_map/pallas_call | solution.py:58
  57.9 1.9 %collective-permute-start.4 = (bf16[3584,128]{1,0:T(8,128)(2,1)S(1)}, bf16[3584,128]{1,0:T(8,128)(2,1)S(1)}, u32[]{:S(2)}, u32[]{:S(2)}) collective-permute-start(bf16[3584,128]{1,0:T(8,128)(2,1)S(1)} %get-tuple-element.56), channel_id=1, source_target_pairs={{0,1},{1,0},{2,3},{3,2},{4,5},{5,4},{6,7},{7,6},{8,9},{9,8},{10,11... | collective-permute-start | bytes 2752520 | tf_op jit(solution)/shard_map/ppermute | solution.py:520
  59.8 2.4 %collective-permute-done.4.other = bf16[3584,128]{1,0:T(8,128)(2,1)S(1)} collective-permute-done((bf16[3584,128]{1,0:T(8,128)(2,1)S(1)}, bf16[3584,128]{1,0:T(8,128)(2,1)S(1)}, u32[]{:S(2)}, u32[]{:S(2)}) %collective-permute-start.4) | collective-permute-done | bytes 917536 | tf_op jit(solution)/shard_map/ppermute | solution.py:520
  62.4 20.6 %all_to_all.30.blocks = bf16[16,216,128]{2,1,0:T(8,128)(2,1)S(1)} all-to-all(bf16[16,216,128]{2,1,0:T(8,128)(2,1)S(1)} %bitcast.12), channel_id=1, replica_groups=mesh['clip'=16,'seq'=32] {'clip'}, dimensions={0} | all-to-all | bytes 1769472 | tf_op jit(solution)/shard_map/all_to_all | solution.py:524
  83.2 11.5 %all_to_all.31.received = bf16[4,128,128]{2,1,0:T(8,128)(2,1)S(1)} all-to-all(bf16[4,128,128]{2,1,0:T(8,128)(2,1)S(1)} %shard_map.129), channel_id=1, replica_groups={{0,2,4,6},{1,3,5,7},{8,10,12,14},{9,11,13,15},{16,18,20,22},{17,19,21,2..., dimensions={0} | all-to-all | bytes 262144 | tf_op jit(solution)/shard_map/all_to_all | solution.py:537
  94.7 20.5 %all_to_all.32.received = bf16[4,128,128]{2,1,0:T(8,128)(2,1)S(1)} all-to-all(bf16[4,128,128]{2,1,0:T(8,128)(2,1)S(1)} %shard_map.130), channel_id=1, replica_groups={{0,8,16,24},{1,9,17,25},{2,10,18,26},{3,11,19,27},{4,12,20,28},{5,13,21..., dimensions={0} | all-to-all | bytes 262144 | tf_op jit(solution)/shard_map/all_to_all | solution.py:537
  115.2 7.4 %all_to_all.33.pieces = bf16[4,64,128]{2,1,0:T(8,128)(2,1)S(1)} all-to-all(bf16[4,64,128]{2,1,0:T(8,128)(2,1)S(1)} %shard_map.132), channel_id=1, replica_groups={{0,2,4,6},{1,3,5,7},{8,10,12,14},{9,11,13,15},{16,18,20,22},{17,19,21,2..., dimensions={0} | all-to-all | bytes 131072 | tf_op jit(solution)/shard_map/all_to_all | solution.py:537
  122.7 14.6 %all_to_all.34 = bf16[16,216,128]{2,1,0:T(8,128)(2,1)S(1)} all-to-all(bf16[16,216,128]{2,1,0:T(8,128)(2,1)S(1)} %shard_map.133), channel_id=1, replica_groups=mesh['clip'=16,'seq'=32] {'clip'}, dimensions={0} | all-to-all | bytes 1769472 | tf_op jit(solution)/shard_map/all_to_all | solution.py:524
  137.3 9.7 %collective-permute-start.5 = (bf16[3456,128]{1,0:T(8,128)(2,1)S(1)}, bf16[3456,128]{1,0:T(8,128)(2,1)S(1)}, u32[]{:S(2)}, u32[]{:S(2)}) collective-permute-start(bf16[3456,128]{1,0:T(8,128)(2,1)S(1)} %bitcast.10), channel_id=1, source_target_pairs={{0,1},{1,0},{2,3},{3,2},{4,5},{5,4},{6,7},{7,6},{8,9},{9,8},{10,11... | collective-permute-start | bytes 2654216 | tf_op jit(solution)/shard_map/ppermute | solution.py:520
  147.0 0.2 shard_map.131
  147.3 0.7 reshape.45
  147.9 1.1 collective-permute-done.5.other
  149.1 1.4 shard_map.134
  (12 shorter events, 0.5 us)
Async XLA Ops:
  3.5 34.2 %all-to-all-start = ((bf16[32,16,128]{2,1,0:T(8,128)(2,1)}), bf16[32,16,128]{2,1,0:T(8,128)(2,1)S(1)}, u32[]{:S(2)}, u32[]{:S(2)}) async-start(bf16[32,16,128]{2,1,0:T(8,128)(2,1)} %shard_map.121), calls=%async_computation | async-start | bytes 262144 | tf_op jit(solution)/shard_map/all_to_all | solution.py:528
  20.2 10.2 %collective-permute-start = (bf16[1024,128]{1,0:T(8,128)(2,1)}, bf16[1024,128]{1,0:T(8,128)(2,1)S(1)}, u32[]{:S(2)}, u32[]{:S(2)}) collective-permute-start(bf16[1024,128]{1,0:T(8,128)(2,1)} %bitcast.13), channel_id=1, source_target_pairs={{0,1},{1,2},{2,3},{3,4},{4,5},{5,6},{6,7},{7,8},{8,9},{9,10},{10,1... | collective-permute-start | bytes 786440 | tf_op jit(solution)/shard_map/ppermute | solution.py:515
  25.8 7.6 %copy-start.1 = (f32[2,2,256,128]{3,2,1,0:T(8,128)}, f32[2,2,256,128]{3,2,1,0:T(8,128)S(1)}, u32[]{:S(2)}) copy-start(f32[2,2,256,128]{3,2,1,0:T(8,128)S(1)} %get-tuple-element.48.pre) | copy-start | bytes 1572868
  33.4 6.2 %collective-permute-start.1 = (bf16[2,128,256]{2,1,0:T(8,128)(2,1)S(1)}, bf16[2,128,256]{2,1,0:T(8,128)(2,1)S(1)}, u32[]{:S(2)}, u32[]{:S(2)}) collective-permute-start(bf16[2,128,256]{2,1,0:T(8,128)(2,1)S(1)} %get-tuple-element.37), channel_id=1, source_target_pairs={{0,1},{1,2},{2,3},{3,4},{4,5},{5,6},{6,7},{7,8},{8,9},{9,10},{10,1... | collective-permute-start | bytes 393224 | tf_op jit(solution)/shard_map/ppermute | solution.py:515
  39.8 7.0 %collective-permute-start.2 = (bf16[256,256]{1,0:T(8,128)(2,1)S(1)}, bf16[256,256]{1,0:T(8,128)(2,1)S(1)}, u32[]{:S(2)}, u32[]{:S(2)}) collective-permute-start(bf16[256,256]{1,0:T(8,128)(2,1)S(1)} %get-tuple-element.42.sent), channel_id=1, source_target_pairs={{1,0},{2,1},{3,2},{4,3},{5,4},{6,5},{7,6},{8,7},{9,8},{10,9},{11,1... | collective-permute-start | bytes 393224 | tf_op jit(solution)/shard_map/ppermute | solution.py:515
  47.4 8.5 %collective-permute-start.3 = (bf16[1280,128]{1,0:T(8,128)(2,1)S(1)}, bf16[1280,128]{1,0:T(8,128)(2,1)}, u32[]{:S(2)}, u32[]{:S(2)}) collective-permute-start(bf16[1280,128]{1,0:T(8,128)(2,1)S(1)} %shard_map.125.grad_mixed), channel_id=1, source_target_pairs={{1,0},{2,1},{3,2},{4,3},{5,4},{6,5},{7,6},{8,7},{9,8},{10,9},{11,1... | collective-permute-start | bytes 983048 | tf_op jit(solution)/shard_map/ppermute | solution.py:515
  49.4 1.0 copy-start.2
  57.9 4.4 %collective-permute-start.4 = (bf16[3584,128]{1,0:T(8,128)(2,1)S(1)}, bf16[3584,128]{1,0:T(8,128)(2,1)S(1)}, u32[]{:S(2)}, u32[]{:S(2)}) collective-permute-start(bf16[3584,128]{1,0:T(8,128)(2,1)S(1)} %get-tuple-element.56), channel_id=1, source_target_pairs={{0,1},{1,0},{2,3},{3,2},{4,5},{5,4},{6,7},{7,6},{8,9},{9,8},{10,11... | collective-permute-start | bytes 2752520 | tf_op jit(solution)/shard_map/ppermute | solution.py:520
  115.2 31.8 %copy-start = (bf16[3,256,256]{2,1,0:T(8,128)(2,1)S(1)}, bf16[3,256,256]{2,1,0:T(8,128)(2,1)}, u32[]{:S(2)}) copy-start(bf16[3,256,256]{2,1,0:T(8,128)(2,1)} %last_time.1) | copy-start | bytes 1179652
  137.3 11.8 %collective-permute-start.5 = (bf16[3456,128]{1,0:T(8,128)(2,1)S(1)}, bf16[3456,128]{1,0:T(8,128)(2,1)S(1)}, u32[]{:S(2)}, u32[]{:S(2)}) collective-permute-start(bf16[3456,128]{1,0:T(8,128)(2,1)S(1)} %bitcast.10), channel_id=1, source_target_pairs={{0,1},{1,0},{2,3},{3,2},{4,5},{5,4},{6,7},{7,6},{8,9},{9,8},{10,11... | collective-permute-start | bytes 2654216 | tf_op jit(solution)/shard_map/ppermute | solution.py:520

commit v9 on v8

--- a/solution.py
+++ b/solution.py
@@ -20,7 +20,6 @@
 PART_AT = LOWERED_AT + 2 * DOWN
 EARLY = (3 + 18 + 12 + 8) * CH
 LATE = (9 + 4) * CH
-NEAR = 4
 
 
 def dot(left, right):
@@ -51,7 +50,7 @@
     return jax.ShapeDtypeStruct(shape, kind)
 
 
-def call(body, ins, outs, scratch=(), copies=0, cost=8000000):
+def call(body, ins, outs, scratch=(), copies=0, flops=1000, size=8000000):
     scratch = [pltpu.VMEM(shape, kind) for shape, kind in scratch]
     if copies:
         scratch.append(pltpu.SemaphoreType.DMA((copies,)))
@@ -62,7 +61,7 @@
         out_specs=[pl.BlockSpec(memory_space=SPACES[space]) for space, _, _ in outs],
         scratch_shapes=scratch,
         compiler_params=pltpu.CompilerParams(vmem_limit_bytes=24 * 1024 * 1024),
-        cost_estimate=pl.CostEstimate(flops=1000, bytes_accessed=cost, transcendentals=0),
+        cost_estimate=pl.CostEstimate(flops=flops, bytes_accessed=size, transcendentals=0),
     )(*[placed_input(*given) for given in ins])
 
 
@@ -175,7 +174,9 @@
     times_out[...] = down_time[pl.ds(0, 2)]
 
 
-def rows_body(rows, last_far, sent_out, last_time, spread, padded, turned, sems):
+def rows_body(
+    core, rows, last_far, mine_out, away_out, last_time, spread, padded, turned, frames, sems
+):
     loads = start(sems, (0, last_far, last_time))
     cotan = rows[...].astype(F32)
     spread[...] = cotan.reshape(HALF * 8, CH)
@@ -190,7 +191,17 @@
     for half in range(2):
         turned[pl.ds(half, DOWN, stride=2), :] = total[:, half * CH : (half + 1) * CH]
     both = jnp.concatenate([turned[...].reshape(HALF, 8, CH), cotan], axis=1)
-    sent_out[...] = both.astype(BF16)
+    frames[...] = both.reshape(HALF // 2, 2, 16, CH)
+    here = core[0]
+    mine_out[...] = frames[:, pl.ds(here, 1)].reshape(HALF // 2, 16, CH).astype(BF16)
+    away_out[...] = frames[:, pl.ds(1 - here, 1)].reshape(HALF // 2, 16, CH).astype(BF16)
+
+
+def join_body(core, mine, theirs, sent_out):
+    here = core[0]
+    own, other = mine[...].astype(F32), theirs[...].astype(F32)
+    sent_out[:, pl.ds(0, 16), :] = jnp.where(here == 0, own, other).astype(BF16)
+    sent_out[:, pl.ds(16, 16), :] = jnp.where(here == 0, other, own).astype(BF16)
 
 
 def own_body(
@@ -339,16 +350,27 @@
     last = dot_tn(lowered[...], ahead[pl.ds(DOWN, DOWN), :])
     for half in range(2):
         flat[pl.ds(base + half * WIDE, WIDE), :] = last[:, half * CH : (half + 1) * CH]
-    loads[1].wait()
-    grad_strided = jnp.concatenate(grad_strided_of(grads, ahead, times), axis=0)
-    down = dot_tn(cells_of(kept), grad_strided)
-    for half in range(2):
-        at = 3 * CH + half * 9 * CH
-        flat[pl.ds(at, 9 * CH), :] = down[:, half * CH : (half + 1) * CH]
     cotan = grad_mixed[pl.ds(0, 4 * CELLS), :]
     for k in range(3):
         taps = acts[pl.ds(k, 2)].reshape(4 * CELLS, CH)
         flat[pl.ds(k * CH, CH), :] = dot_tn(taps, cotan)
+    for frame in range(2):
+        planes = [acts[4 + frame, par].reshape(COLS, HALF, CH) for par in range(2)]
+        fill_windows(windows_out, frame * CELLS, *planes)
+    slope_out[...] = silu_slope(pre[...])
+    loads[0].wait()
+    for par in range(2):
+        first, second = [
+            grad_mixed[pl.ds((frame * 2 + par) * CELLS, CELLS), :] for frame in range(2)
+        ]
+        part_out[0, par] = dot_nt(first, time_out[2]) + dot_nt(second, time_out[1])
+        part_out[1, par] = dot_nt(second, time_out[2])
+    loads[1].wait()
+    grad_strided = jnp.concatenate(grad_strided_of(grads, ahead, times), axis=0)
+    down = dot_tn(cells_of(kept), grad_strided)
+    for half in range(2):
+        at = 3 * CH + half * 9 * CH
+        flat[pl.ds(at, 9 * CH), :] = down[:, half * CH : (half + 1) * CH]
     here = core[0]
     half = EARLY // 2
     mine_out[pl.ds(0, half), :] = flat[pl.ds(pl.multiple_of(here * half, 16), half), :]
@@ -359,17 +381,6 @@
     mine_out[pl.ds(half, DOWN), :] = rows_here[:, pl.ds(here, 1)].reshape(DOWN, CH)
     away = rows_here[:, pl.ds(1 - here, 1)].reshape(DOWN, CH)
     other_out[pl.ds(half, DOWN), :] = away.astype(BF16)
-    loads[0].wait()
-    for frame in range(2):
-        planes = [acts[4 + frame, par].reshape(COLS, HALF, CH) for par in range(2)]
-        fill_windows(windows_out, frame * CELLS, *planes)
-    slope_out[...] = silu_slope(pre[...])
-    for par in range(2):
-        first, second = [
-            grad_mixed[pl.ds((frame * 2 + par) * CELLS, CELLS), :] for frame in range(2)
-        ]
-        part_out[0, par] = dot_nt(first, time_out[2]) + dot_nt(second, time_out[1])
-        part_out[1, par] = dot_nt(second, time_out[2])
 
 
 def last_body(
@@ -433,35 +444,18 @@
     padded[...] = jnp.zeros_like(padded)
     padded[pl.ds(0, rows), :] = total
     chips = frames.shape[0]
-    near = sent_out.shape[0]
-    share = padded.shape[0] // near
-    for chip in range(near):
+    share = padded.shape[0] // chips
+    for chip in range(chips):
         sent_out[chip, pl.ds(0, share), :] = padded[pl.ds(chip * share, share), :].astype(BF16)
-        for far in range(chips // near):
-            sent_out[chip, pl.ds(share + far * 16, 16), :] = frames[far * near + chip]
-
-
-def first_rows(received, share):
+        sent_out[chip, pl.ds(share, 16), :] = frames[chip]
+
+
+def piece_body(received, piece_out):
+    share = piece_out.shape[1]
     total = received[0, pl.ds(0, share), :].astype(F32)
     for chip in range(1, received.shape[0]):
         total = total + received[chip, pl.ds(0, share), :].astype(F32)
-    return total.astype(BF16)
-
-
-def near_body(received, sent_out):
-    near, far = received.shape[0], sent_out.shape[0]
-    share = sent_out.shape[1] - near * 16
-    piece = first_rows(received, share)
-    for there in range(far):
-        sent_out[there, pl.ds(0, share), :] = piece
-        for chip in range(near):
-            sent_out[there, pl.ds(share + chip * 16, 16), :] = received[
-                chip, pl.ds(share + there * 16, 16), :
-            ]
-
-
-def piece_body(received, piece_out):
-    piece = first_rows(received, piece_out.shape[1])
+    piece = total.astype(BF16)
     for chip in range(piece_out.shape[0]):
         piece_out[chip] = piece
 
@@ -495,10 +489,8 @@
 
 
 def output_body(received, last_time, output, spread, padded):
-    share = received.shape[1] - 16 * HALF // 2 // received.shape[0]
-    for far in range(received.shape[0]):
-        rows = received.shape[1] - share
-        spread[pl.ds(far * rows, rows), :] = received[far, pl.ds(share, rows), :].astype(F32)
+    frames = received[:, pl.ds(received.shape[1] - 16, 16), :]
+    spread[...] = frames.astype(F32).reshape(HALF * 8, CH)
     padded[pl.ds(0, 8), :] = jnp.zeros((8, WIDE), F32)
     for half in range(2):
         padded[pl.ds(8, DOWN), pl.ds(half * CH, CH)] = spread[pl.ds(half, DOWN, stride=2), :]
@@ -524,16 +516,9 @@
     return lax.all_to_all(blocks, "clip", split_axis=0, concat_axis=0, tiled=True)
 
 
-def exchange_seq(blocks):
-    return lax.all_to_all(blocks, "seq", split_axis=0, concat_axis=0, tiled=True)
-
-
-def exchange_chips(blocks, near):
-    count = lax.axis_size("seq") // 2
-    runs = [list(range(first, first + NEAR)) for first in range(0, count, NEAR)]
-    if not near:
-        runs = [list(place) for place in zip(*runs)]
-    groups = [[2 * chip + core for chip in run] for run in runs for core in range(2)]
+def exchange_chips(blocks):
+    count = lax.axis_size("seq")
+    groups = [list(range(core, count, 2)) for core in range(2)]
     return lax.all_to_all(
         blocks, "seq", split_axis=0, concat_axis=0, axis_index_groups=groups, tiled=True
     )
@@ -543,19 +528,21 @@
     own = clip_in.reshape(4 * CELLS, CH)
     prior = from_behind(own, 1)
     flat_frames = (2, 2, CELLS, CH)
-    (sent,) = call(
+    core = (lax.axis_index("seq") % 2).astype(jnp.int32).reshape(1)
+    mine, away = call(
         rows_body,
-        [(V, cotan_out[0].reshape(HALF, 8, CH)), (H, last_time)],
-        [(V, (HALF, 16, CH), BF16)],
+        [(S, core), (V, cotan_out[0].reshape(HALF, 8, CH)), (H, last_time)],
+        [(P_, (HALF // 2, 16, CH), BF16), (V, (HALF // 2, 16, CH), BF16)],
         [
             ((3, WIDE, WIDE), BF16),
             ((HALF * 8, CH), F32),
             ((DOWN + 8, WIDE), F32),
             ((HALF * 8, CH), F32),
+            ((HALF // 2, 2, 16, CH), F32),
         ],
         copies=1,
     )
-    received = exchange_seq(sent)
+    theirs = swap_cores(away)
     acts, pre_first, both = call(
         own_body,
         [(H, own), (H, first_plane)],
@@ -574,11 +561,18 @@
     )
     (acts,) = call(
         prior_body,
-        [(V, prior), (P_, acts), (P_, both)],
+        [(P_, prior), (P_, acts), (P_, both)],
         [(P_, (6, 2, CELLS, CH), BF16)],
         [((2 * CELLS, CH), F32), ((2 * CELLS, 12 * CH), BF16)],
     )
     times = (P_, (2, WIDE, WIDE), BF16)
+    theirs, acts = lax.optimization_barrier((theirs, acts))
+    (sent,) = call(
+        join_body,
+        [(S, core), (P_, mine), (P_, theirs)],
+        [(V, (HALF // 2, HALF, CH), BF16)],
+    )
+    received = exchange_chips(sent).reshape(HALF, 16, CH)
     kept, strided, part, near_times = call(
         first_body,
         [
@@ -600,18 +594,18 @@
     strided_prior = from_behind(strided, 1)
     down = (P_, (DOWN, WIDE), BF16)
     grad_lowered, cot = call(
-        cotan_body, [(V, received)], [down, down], [((HALF * 16, CH), F32)]
+        cotan_body, [(P_, received)], [down, down], [((HALF * 16, CH), F32)]
     )
     lowered, sent = call(
         middle_body,
-        [(V, strided_prior), (P_, part), (P_, near_times), (P_, grad_lowered), (P_, cot)],
+        [(P_, strided_prior), (P_, part), (P_, near_times), (P_, grad_lowered), (P_, cot)],
         [down, (P_, (2 * DOWN, WIDE), BF16)],
     )
     ahead = from_behind(sent, -1)
     near_times, kernels, time_grads = call(
         time_grads_body,
         [
-            (P_, sent), (P_, lowered), (V, strided_prior), (P_, kept),
+            (P_, sent), (P_, lowered), (P_, strided_prior), (P_, kept),
             (H, down_time), (H, down_plane),
         ],
         [
@@ -624,17 +618,16 @@
     )
     (sent,) = call(
         back_body,
-        [(V, ahead), (P_, time_grads), (P_, near_times), (P_, kernels)],
+        [(P_, ahead), (P_, time_grads), (P_, near_times), (P_, kernels)],
         [(P_, (4 * CELLS + 2 * DOWN, CH), BF16)],
         [((2 * DOWN, 4 * WIDE), BF16)],
     )
     further = from_behind(sent, -1)
-    core = (lax.axis_index("seq") % 2).astype(jnp.int32).reshape(1)
     early, early_other, windows, slope, part, near_time = call(
         plane_grads_body,
         [
             (S, core), (P_, sent), (P_, kept), (P_, acts), (P_, pre_first),
-            (H, first_time), (H, down_time), (P_, time_grads), (P_, lowered), (V, ahead),
+            (H, first_time), (H, down_time), (P_, time_grads), (P_, lowered), (P_, ahead),
         ],
         [
             (P_, (EARLY // 2 + DOWN, CH), F32),
@@ -650,11 +643,13 @@
     late, other = call(
         last_body,
         [
-            (S, core), (V, further), (P_, windows), (P_, slope), (P_, part), (P_, near_time),
+            (S, core), (P_, further), (P_, windows), (P_, slope), (P_, part), (P_, near_time),
             (P_, lowered), (P_, early_other),
         ],
         [(P_, (LATE // 2, CH), F32), (P_, ((EARLY + LATE) // 2 + DOWN, CH), BF16)],
         [((LATE, CH), F32)],
+        flops=600000000,
+        size=2000000,
     )
 
     clips = lax.axis_size("clip")
@@ -668,19 +663,16 @@
         [(P_, (half_rows, CH), BF16), (V, (chips, 16, CH), BF16)],
     )
     blocks = exchange_clip(half.reshape(clips, part_rows, CH))
-    far = chips // NEAR
-    share = 16 * (-(-part_rows // (16 * NEAR)))
+    share = 16 * (-(-part_rows // (16 * chips)))
     (sent,) = call(
         sum_body,
         [(V, blocks), (V, frames)],
-        [(V, (NEAR, share + far * 16, CH), BF16)],
-        [((NEAR * share, CH), F32)],
-    )
-    received = exchange_chips(sent, True)
-    (sent,) = call(near_body, [(V, received)], [(V, (far, share + NEAR * 16, CH), BF16)])
-    received = exchange_chips(sent, False)
-    (pieces,) = call(piece_body, [(V, received)], [(V, (NEAR, share, CH), BF16)])
-    pieces = exchange_chips(pieces, True)
+        [(V, (chips, share + 16, CH), BF16)],
+        [((chips * share, CH), F32)],
+    )
+    received = exchange_chips(sent)
+    (pieces,) = call(piece_body, [(V, received)], [(V, (chips, share, CH), BF16)])
+    pieces = exchange_chips(pieces)
     (output,) = call(
         output_body,
         [(V, received), (V, last_time)],

time: 151 us -> 146 us (0.967)
  blocking collectives: 74.6 us -> 71.6 us
  Pallas kernels: 15.9 us -> 14.2 us
    ppermute x4, waiting for transfers between devices: 13 us -> 6.36 us  [from_behind(): return lax.ppermute(block, 'seq', route)]
    all_to_all x1, starting transfers between devices: 16.8 us -> 10.8 us  [exchange_chips(): lax.all_to_all(blocks, 'seq', split_axis=0, concat_axis=0, axis_index_gro...]
    all_to_all x1, waiting for transfers between devices: 0.01 us -> 5.7 us  [exchange_chips(): lax.all_to_all(blocks, 'seq', split_axis=0, concat_axis=0, axis_index_gro...]
    ppermute x4, starting transfers between devices: 11.6 us -> 16.5 us  [from_behind(): return lax.ppermute(block, 'seq', route)]
    all_to_all x3 -> x2, blocking collectives: 39.4 us -> 34.8 us  [exchange_chips(): lax.all_to_all(blocks, 'seq', split_axis=0, concat_axis=0, axis_index_gro...]
    ppermute x2 -> x3, starting transfers between devices: 11.6 us -> 14 us  [swap_cores(): return lax.ppermute(block, 'seq', [(i, i ^ 1) for i in range(count)])]
    pallas_call x17, Pallas kernels: 15.9 us -> 14.2 us  [call(): pl.pallas_call(body, out_shape=[placed_output(*out) for out in outs], in_...]
    all_to_all x2, blocking collectives: 35.2 us -> 36.7 us  [exchange_clip(): lax.all_to_all(blocks, 'clip', split_axis=0, concat_axis=0, tiled=True)]
  transfers between devices with their start and end apart: 7 -> 8, of which waited for: 6 -> 5; matrix products, arithmetic and copies ran while one was open for 0% -> 1% of each run, Pallas kernels for 6% -> 7%
where the time goes in v9:
time: 146 us; the launch traced here: 145 us
  blocking collectives  71.6 us (49%)
  starting transfers between devices  41.3 us (28%)
  waiting for transfers between devices  15.6 us (11%)
  Pallas kernels  14.2 us (10%)
  local copies, waits for them, and re-layouts  1.52 us (1%)
    all_to_all x2, blocking collectives, exchange_clip(): lax.all_to_all(blocks, 'clip', split_axis=0, concat_axis=0, tiled=True)  36.7 us
    all_to_all x2, blocking collectives, exchange_chips(): lax.all_to_all(blocks, 'seq', split_axis=0, concat_axis=0, axis_index_gro...  34.8 us
    ppermute x4, starting transfers between devices, from_behind(): return lax.ppermute(block, 'seq', route)  16.5 us
    pallas_call x17, Pallas kernels, call(): pl.pallas_call(body, out_shape=[placed_output(*out) for out in outs], in_...  14.2 us
    ppermute x3, starting transfers between devices, swap_cores(): return lax.ppermute(block, 'seq', [(i, i ^ 1) for i in range(count)])  14 us
    all_to_all x1, starting transfers between devices, exchange_chips(): lax.all_to_all(blocks, 'seq', split_axis=0, concat_axis=0, axis_index_gro...  10.8 us
    ppermute x4, waiting for transfers between devices, from_behind(): return lax.ppermute(block, 'seq', route)  6.36 us
    all_to_all x1, waiting for transfers between devices, exchange_chips(): lax.all_to_all(blocks, 'seq', split_axis=0, concat_axis=0, axis_index_gro...  5.7 us
  transfers between devices with their start and end apart: 8, of which 5 were waited for; matrix products, arithmetic and copies ran while one was open for 1% of the time, Pallas kernels for 7%

profile of v9, /device:TPU:1, one launch (start us, length us, event | category | flops | bytes accessed | tf_op | source)
XLA Modules:
  0.0 145.1 jit_solution(12278330797241344954)
XLA Ops:
  0.6 4.9 %collective-permute-start.1 = (bf16[1024,128]{1,0:T(8,128)(2,1)}, bf16[1024,128]{1,0:T(8,128)(2,1)S(1)}, u32[]{:S(2)}, u32[]{:S(2)}) collective-permute-start(bf16[1024,128]{1,0:T(8,128)(2,1)} %bitcast.15), channel_id=1, source_target_pairs={{0,1},{1,2},{2,3},{3,4},{4,5},{5,6},{6,7},{7,8},{8,9},{9,10},{10,1... | collective-permute-start | bytes 786440 | tf_op jit(solution)/shard_map/ppermute | solution.py:507
  5.6 0.9 reshape_squeeze.3.rows
  6.5 1.3 shard_map.118
  7.8 5.2 %collective-permute-start = (bf16[16,16,128]{2,1,0:T(8,128)(2,1)S(1)}, bf16[16,16,128]{2,1,0:T(8,128)(2,1)S(1)}, u32[]{:S(2)}, u32[]{:S(2)}) collective-permute-start(bf16[16,16,128]{2,1,0:T(8,128)(2,1)S(1)} %get-tuple-element.39), channel_id=1, source_target_pairs={{0,1},{1,0},{2,3},{3,2},{4,5},{5,4},{6,7},{7,6},{8,9},{9,8},{10,11... | collective-permute-start | bytes 196616 | tf_op jit(solution)/shard_map/ppermute | solution.py:512
  13.0 2.0 %shard_map.119 = (bf16[4,2,256,128]{3,2,1,0:T(8,128)(2,1)S(1)}, f32[2,2,256,128]{3,2,1,0:T(8,128)S(1)}, bf16[1536,256]{1,0:T(8,128)(2,1)S(1)}) custom-call(bf16[1024,128]{1,0:T(8,128)(2,1)} %bitcast.16, bf16[3,3,128,128]{3,2,1,0:T(8,128)(2,1)} %plane_far.3), custom_call_target="tpu_custom_call" | custom-call | flops 1000 | bytes 8000000 | tf_op jit(solution)/shard_map/pallas_call | solution.py:57
  15.0 0.8 shard_map.120.acts
  15.9 0.7 shard_map.122
  16.5 10.8 %all-to-all-start = ((bf16[16,32,128]{2,1,0:T(8,128)(2,1)}), bf16[16,32,128]{2,1,0:T(8,128)(2,1)S(1)}, u32[]{:S(2)}, u32[]{:S(2)}) async-start(bf16[16,32,128]{2,1,0:T(8,128)(2,1)} %shard_map.122), calls=%async_computation | async-start | bytes 262144 | tf_op jit(solution)/shard_map/all_to_all | solution.py:522
  27.3 2.1 %shard_map.121 = (bf16[2560,128]{1,0:T(8,128)(2,1)S(1)}, bf16[2,128,256]{2,1,0:T(8,128)(2,1)S(1)}, f32[128,256]{1,0:T(8,128)S(1)}, bf16[2,256,256]{2,1,0:T(8,128)(2,1)S(1)}) custom-call(bf16[6,2,256,128]{3,2,1,0:T(8,128)(2,1)S(1)} %shard_map.120.acts, bf16[3,128,128]{2,1,0:T(8,128)(2,1)} %time_far.3, bf16[3,3,128,256]{3,2,1,0:T(8,128)(2,1)} %plane_far.5, ...), custom_call_target="tpu_custom_call" | custom-call | flops 1000 | bytes 8000000 | tf_op jit(solution)/shard_map/pallas_call | solution.py:57
  29.4 4.2 %collective-permute-start.2 = (bf16[2,128,256]{2,1,0:T(8,128)(2,1)S(1)}, bf16[2,128,256]{2,1,0:T(8,128)(2,1)S(1)}, u32[]{:S(2)}, u32[]{:S(2)}) collective-permute-start(bf16[2,128,256]{2,1,0:T(8,128)(2,1)S(1)} %get-tuple-element.43), channel_id=1, source_target_pairs={{0,1},{1,2},{2,3},{3,4},{4,5},{5,6},{6,7},{7,8},{8,9},{9,10},{10,1... | collective-permute-start | bytes 393224 | tf_op jit(solution)/shard_map/ppermute | solution.py:507
  33.7 5.7 %all-to-all-done = bf16[16,32,128]{2,1,0:T(8,128)(2,1)S(1)} async-done(((bf16[16,32,128]{2,1,0:T(8,128)(2,1)}), bf16[16,32,128]{2,1,0:T(8,128)(2,1)S(1)}, u32[]{:S(2)}, u32[]{:S(2)}) %all-to-all-start) | async-done | bytes 131104 | tf_op jit(solution)/shard_map/all_to_all | solution.py:522
  39.5 0.2 shard_map.124
  39.7 5.4 %collective-permute-start.3 = (bf16[256,256]{1,0:T(8,128)(2,1)S(1)}, bf16[256,256]{1,0:T(8,128)(2,1)S(1)}, u32[]{:S(2)}, u32[]{:S(2)}) collective-permute-start(bf16[256,256]{1,0:T(8,128)(2,1)S(1)} %get-tuple-element.50.sent), channel_id=1, source_target_pairs={{1,0},{2,1},{3,2},{4,3},{5,4},{6,5},{7,6},{8,7},{9,8},{10,9},{11,1... | collective-permute-start | bytes 393224 | tf_op jit(solution)/shard_map/ppermute | solution.py:507
  45.1 1.5 %shard_map.125 = (bf16[2,256,256]{2,1,0:T(8,128)(2,1)S(1)}, bf16[512,1024]{1,0:T(8,128)(2,1)S(1)}, f32[2560,128]{1,0:T(8,128)S(1)}) custom-call(bf16[256,256]{1,0:T(8,128)(2,1)S(1)} %get-tuple-element.50.sent, bf16[128,256]{1,0:T(8,128)(2,1)S(1)} %get-tuple-element.51.lowered, bf16[2,128,256]{2,1,0:T(8,128)(2,1)S(1)} %collective-permute-done.2.prior, ...), custom_call_target="tpu_custom_call" | custom-call | flops 1000 | bytes 8000000 | tf_op jit(solution)/shard_map/pallas_call | solution.py:57
  46.7 1.8 %collective-permute-done.3.ahead = bf16[256,256]{1,0:T(8,128)(2,1)S(1)} collective-permute-done((bf16[256,256]{1,0:T(8,128)(2,1)S(1)}, bf16[256,256]{1,0:T(8,128)(2,1)S(1)}, u32[]{:S(2)}, u32[]{:S(2)}) %collective-permute-start.3) | collective-permute-done | bytes 131104 | tf_op jit(solution)/shard_map/ppermute | solution.py:507
  48.5 0.6 shard_map.126.grad_mixed
  49.1 1.9 %collective-permute-start.4 = (bf16[1280,128]{1,0:T(8,128)(2,1)S(1)}, bf16[1280,128]{1,0:T(8,128)(2,1)S(1)}, u32[]{:S(2)}, u32[]{:S(2)}) collective-permute-start(bf16[1280,128]{1,0:T(8,128)(2,1)S(1)} %shard_map.126.grad_mixed), channel_id=1, source_target_pairs={{1,0},{2,1},{3,2},{4,3},{5,4},{6,5},{7,6},{8,7},{9,8},{10,9},{11,1... | collective-permute-start | bytes 983048 | tf_op jit(solution)/shard_map/ppermute | solution.py:507
  51.0 1.9 %shard_map.127 = (f32[2752,128]{1,0:T(8,128)S(1)}, bf16[2752,128]{1,0:T(8,128)(2,1)S(1)}, bf16[512,1536]{1,0:T(8,128)(2,1)S(1)}, f32[2,2,256,128]{3,2,1,0:T(8,12...) custom-call(s32[1]{0:T(128)} %bitcast.core, bf16[1280,128]{1,0:T(8,128)(2,1)S(1)} %shard_map.126.grad_mixed, ...), custom_call_target="tpu_custom_call" | custom-call | flops 1000 | bytes 8000000 | tf_op jit(solution)/shard_map/pallas_call | solution.py:57
  52.9 4.6 %collective-permute-done.4.ahead = bf16[1280,128]{1,0:T(8,128)(2,1)S(1)} collective-permute-done((bf16[1280,128]{1,0:T(8,128)(2,1)S(1)}, bf16[1280,128]{1,0:T(8,128)(2,1)S(1)}, u32[]{:S(2)}, u32[]{:S(2)}) %collective-permute-start.4) | collective-permute-done | bytes 327712 | tf_op jit(solution)/shard_map/ppermute | solution.py:507
  57.4 0.9 shard_map.128
  58.4 1.9 %collective-permute-start.5 = (bf16[3584,128]{1,0:T(8,128)(2,1)S(1)}, bf16[3584,128]{1,0:T(8,128)(2,1)S(1)}, u32[]{:S(2)}, u32[]{:S(2)}) collective-permute-start(bf16[3584,128]{1,0:T(8,128)(2,1)S(1)} %get-tuple-element.64), channel_id=1, source_target_pairs={{0,1},{1,0},{2,3},{3,2},{4,5},{5,4},{6,7},{7,6},{8,9},{9,8},{10,11... | collective-permute-start | bytes 2752520 | tf_op jit(solution)/shard_map/ppermute | solution.py:512
  60.3 2.4 %collective-permute-done.5.other = bf16[3584,128]{1,0:T(8,128)(2,1)S(1)} collective-permute-done((bf16[3584,128]{1,0:T(8,128)(2,1)S(1)}, bf16[3584,128]{1,0:T(8,128)(2,1)S(1)}, u32[]{:S(2)}, u32[]{:S(2)}) %collective-permute-start.5) | collective-permute-done | bytes 917536 | tf_op jit(solution)/shard_map/ppermute | solution.py:512
  62.7 0.2 shard_map.129
  62.9 20.6 %all_to_all.25.blocks = bf16[16,216,128]{2,1,0:T(8,128)(2,1)S(1)} all-to-all(bf16[16,216,128]{2,1,0:T(8,128)(2,1)S(1)} %bitcast.13), channel_id=1, replica_groups=mesh['clip'=16,'seq'=32] {'clip'}, dimensions={0} | all-to-all | bytes 1769472 | tf_op jit(solution)/shard_map/all_to_all | solution.py:516
  83.6 19.0 %all_to_all.26.received = bf16[16,32,128]{2,1,0:T(8,128)(2,1)S(1)} all-to-all(bf16[16,32,128]{2,1,0:T(8,128)(2,1)S(1)} %shard_map.130), channel_id=1, replica_groups={{0,2,4,6,8,10,12,14,16,18,20,22,24,26,28,30},{1,3,5,7,9,11,13,15,17,19,..., dimensions={0} | all-to-all | bytes 262144 | tf_op jit(solution)/shard_map/all_to_all | solution.py:522
  102.6 15.8 %all_to_all.27.pieces = bf16[16,16,128]{2,1,0:T(8,128)(2,1)S(1)} all-to-all(bf16[16,16,128]{2,1,0:T(8,128)(2,1)S(1)} %shard_map.132), channel_id=1, replica_groups={{0,2,4,6,8,10,12,14,16,18,20,22,24,26,28,30},{1,3,5,7,9,11,13,15,17,19,..., dimensions={0} | all-to-all | bytes 131072 | tf_op jit(solution)/shard_map/all_to_all | solution.py:522
  118.6 16.1 %all_to_all.28 = bf16[16,216,128]{2,1,0:T(8,128)(2,1)S(1)} all-to-all(bf16[16,216,128]{2,1,0:T(8,128)(2,1)S(1)} %shard_map.133), channel_id=1, replica_groups=mesh['clip'=16,'seq'=32] {'clip'}, dimensions={0} | all-to-all | bytes 1769472 | tf_op jit(solution)/shard_map/all_to_all | solution.py:516
  134.7 6.9 %collective-permute-start.6 = (bf16[3456,128]{1,0:T(8,128)(2,1)S(1)}, bf16[3456,128]{1,0:T(8,128)(2,1)S(1)}, u32[]{:S(2)}, u32[]{:S(2)}) collective-permute-start(bf16[3456,128]{1,0:T(8,128)(2,1)S(1)} %bitcast.11), channel_id=1, source_target_pairs={{0,1},{1,0},{2,3},{3,2},{4,5},{5,4},{6,7},{7,6},{8,9},{9,8},{10,11... | collective-permute-start | bytes 2654216 | tf_op jit(solution)/shard_map/ppermute | solution.py:512
  141.6 0.2 shard_map.131
  141.9 0.7 reshape.49
  142.5 1.1 collective-permute-done.6.other
  143.7 1.4 shard_map.134
  (9 shorter events, 0.4 us)
Async XLA Ops:
  0.6 14.3 %collective-permute-start.1 = (bf16[1024,128]{1,0:T(8,128)(2,1)}, bf16[1024,128]{1,0:T(8,128)(2,1)S(1)}, u32[]{:S(2)}, u32[]{:S(2)}) collective-permute-start(bf16[1024,128]{1,0:T(8,128)(2,1)} %bitcast.15), channel_id=1, source_target_pairs={{0,1},{1,2},{2,3},{3,4},{4,5},{5,6},{6,7},{7,8},{8,9},{9,10},{10,1... | collective-permute-start | bytes 786440 | tf_op jit(solution)/shard_map/ppermute | solution.py:507
  7.8 8.0 %collective-permute-start = (bf16[16,16,128]{2,1,0:T(8,128)(2,1)S(1)}, bf16[16,16,128]{2,1,0:T(8,128)(2,1)S(1)}, u32[]{:S(2)}, u32[]{:S(2)}) collective-permute-start(bf16[16,16,128]{2,1,0:T(8,128)(2,1)S(1)} %get-tuple-element.39), channel_id=1, source_target_pairs={{0,1},{1,0},{2,3},{3,2},{4,5},{5,4},{6,7},{7,6},{8,9},{9,8},{10,11... | collective-permute-start | bytes 196616 | tf_op jit(solution)/shard_map/ppermute | solution.py:512
  16.5 22.8 %all-to-all-start = ((bf16[16,32,128]{2,1,0:T(8,128)(2,1)}), bf16[16,32,128]{2,1,0:T(8,128)(2,1)S(1)}, u32[]{:S(2)}, u32[]{:S(2)}) async-start(bf16[16,32,128]{2,1,0:T(8,128)(2,1)} %shard_map.122), calls=%async_computation | async-start | bytes 262144 | tf_op jit(solution)/shard_map/all_to_all | solution.py:522
  29.4 10.0 %collective-permute-start.2 = (bf16[2,128,256]{2,1,0:T(8,128)(2,1)S(1)}, bf16[2,128,256]{2,1,0:T(8,128)(2,1)S(1)}, u32[]{:S(2)}, u32[]{:S(2)}) collective-permute-start(bf16[2,128,256]{2,1,0:T(8,128)(2,1)S(1)} %get-tuple-element.43), channel_id=1, source_target_pairs={{0,1},{1,2},{2,3},{3,4},{4,5},{5,6},{6,7},{7,8},{8,9},{9,10},{10,1... | collective-permute-start | bytes 393224 | tf_op jit(solution)/shard_map/ppermute | solution.py:507
  39.7 8.8 %collective-permute-start.3 = (bf16[256,256]{1,0:T(8,128)(2,1)S(1)}, bf16[256,256]{1,0:T(8,128)(2,1)S(1)}, u32[]{:S(2)}, u32[]{:S(2)}) collective-permute-start(bf16[256,256]{1,0:T(8,128)(2,1)S(1)} %get-tuple-element.50.sent), channel_id=1, source_target_pairs={{1,0},{2,1},{3,2},{4,3},{5,4},{6,5},{7,6},{8,7},{9,8},{10,9},{11,1... | collective-permute-start | bytes 393224 | tf_op jit(solution)/shard_map/ppermute | solution.py:507
  49.1 8.4 %collective-permute-start.4 = (bf16[1280,128]{1,0:T(8,128)(2,1)S(1)}, bf16[1280,128]{1,0:T(8,128)(2,1)S(1)}, u32[]{:S(2)}, u32[]{:S(2)}) collective-permute-start(bf16[1280,128]{1,0:T(8,128)(2,1)S(1)} %shard_map.126.grad_mixed), channel_id=1, source_target_pairs={{1,0},{2,1},{3,2},{4,3},{5,4},{6,5},{7,6},{8,7},{9,8},{10,9},{11,1... | collective-permute-start | bytes 983048 | tf_op jit(solution)/shard_map/ppermute | solution.py:507
  58.4 4.4 %collective-permute-start.5 = (bf16[3584,128]{1,0:T(8,128)(2,1)S(1)}, bf16[3584,128]{1,0:T(8,128)(2,1)S(1)}, u32[]{:S(2)}, u32[]{:S(2)}) collective-permute-start(bf16[3584,128]{1,0:T(8,128)(2,1)S(1)} %get-tuple-element.64), channel_id=1, source_target_pairs={{0,1},{1,0},{2,3},{3,2},{4,5},{5,4},{6,7},{7,6},{8,9},{9,8},{10,11... | collective-permute-start | bytes 2752520 | tf_op jit(solution)/shard_map/ppermute | solution.py:512
  102.6 39.0 %copy-start = (bf16[3,256,256]{2,1,0:T(8,128)(2,1)S(1)}, bf16[3,256,256]{2,1,0:T(8,128)(2,1)}, u32[]{:S(2)}) copy-start(bf16[3,256,256]{2,1,0:T(8,128)(2,1)} %last_time.1) | copy-start | bytes 1179652
  134.7 8.9 %collective-permute-start.6 = (bf16[3456,128]{1,0:T(8,128)(2,1)S(1)}, bf16[3456,128]{1,0:T(8,128)(2,1)S(1)}, u32[]{:S(2)}, u32[]{:S(2)}) collective-permute-start(bf16[3456,128]{1,0:T(8,128)(2,1)S(1)} %bitcast.11), channel_id=1, source_target_pairs={{0,1},{1,0},{2,3},{3,2},{4,5},{5,4},{6,7},{7,6},{8,9},{9,8},{10,11... | collective-permute-start | bytes 2654216 | tf_op jit(solution)/shard_map/ppermute | solution.py:512

commit v10 on v9

--- a/solution.py
+++ b/solution.py
@@ -18,8 +18,7 @@
 KEPT = STRIDED_AT + 2 * DOWN
 LOWERED_AT = 8 * WIDE
 PART_AT = LOWERED_AT + 2 * DOWN
-EARLY = (3 + 18 + 12 + 8) * CH
-LATE = (9 + 4) * CH
+GRADS = (9 + 3 + 18 + 12 + 12) * CH
 
 
 def dot(left, right):
@@ -270,12 +269,16 @@
 
 
 def time_grads_body(
-    sent, lowered, prior, kept, down_far, plane_far,
-    times_out, kernels_out, grads_out,
-    down_time, down_plane, sems,
+    sent, lowered, prior, kept, acts, pre, down_far, plane_far,
+    times_out, kernels_out, grads_out, windows_out, slope_out,
+    down_plane, sems,
 ):
-    loads = start(sems, (0, down_far, down_time), (1, plane_far, down_plane))
+    loads = start(sems, (0, down_far, times_out), (1, plane_far, down_plane))
     kernels_out[...] = jnp.zeros_like(kernels_out)
+    for frame in range(2):
+        planes = [acts[4 + frame, par].reshape(COLS, HALF, CH) for par in range(2)]
+        fill_windows(windows_out, frame * CELLS, *planes)
+    slope_out[...] = silu_slope(pre[...])
     wide = lowered[...].astype(F32)
     for col in range(4):
         for half in range(2):
@@ -295,84 +298,84 @@
         grads_out[pl.ds((6 + half) * WIDE, WIDE), :] = last[:, half * CH : (half + 1) * CH]
     for load in loads:
         load.wait()
-    part = dot_nt(grad_pre, down_time[2])
+    part = dot_nt(grad_pre, times_out[2])
     for half in range(2):
         grads_out[pl.ds(PART_AT + half * DOWN, DOWN), :] = part[:, half * CH : (half + 1) * CH]
-    times_out[...] = down_time[pl.ds(0, 2)]
     for row_par, col_par, row_off, col_off, row, tap in BACK:
         rows = pl.ds((row_par * 2 + col_par) * CH, CH)
         lanes = pl.ds((row_off * 2 + col_off) * WIDE, WIDE)
         kernels_out[rows, lanes] = down_plane[row, tap]
 
 
-def grad_strided_of(grads, ahead, times):
-    following = ahead[pl.ds(0, DOWN), :]
+def back_body(
+    core, ahead, further, grads, times, kernels, kept, acts, windows, slope, lowered, time_far,
+    mine_out, other_out,
+    shifted, mixed, flat, rows_here, first_time, sems,
+):
+    loads = start(sems, (0, time_far, first_time))
+    near, far = ahead[pl.ds(0, DOWN), :], further[pl.ds(0, DOWN), :]
     part = [grads[pl.ds(PART_AT + half * DOWN, DOWN), :] for half in range(2)]
-    even = jnp.concatenate(part, axis=1) + dot_nt(following, times[0])
-    return even.astype(BF16), dot_nt(following, times[1]).astype(BF16)
-
-
-def back_body(ahead, grads, times, kernels, sent_out, shifted):
-    for half in range(2):
-        sent_out[pl.ds(4 * CELLS + half * DOWN, DOWN), :] = ahead[
-            pl.ds(DOWN, DOWN), pl.ds(half * CH, CH)
-        ]
-    for frame, strided in enumerate(grad_strided_of(grads, ahead, times)):
-        planes = strided.reshape(4, HALF, WIDE)
+    strided = [
+        jnp.concatenate(part, axis=1) + dot_nt(near, times[0]),
+        dot_nt(near, times[1]),
+        dot_nt(near, times[2]) + dot_nt(far, times[0]),
+        dot_nt(far, times[1]),
+    ]
+    strided = [frame.astype(BF16) for frame in strided]
+    for frame in range(4):
+        planes = strided[frame].reshape(4, HALF, WIDE)
         for row_off, rows in ((0, planes), (1, row_after(planes))):
-            flat = rows.reshape(DOWN, WIDE)
+            cells = rows.reshape(DOWN, WIDE)
             here = pl.ds((row_off * 2) * WIDE, WIDE)
             after = pl.ds((row_off * 2 + 1) * WIDE, WIDE)
-            shifted[pl.ds(frame * DOWN, DOWN), here] = flat
-            shifted[pl.ds(frame * DOWN, DOWN - HALF), after] = flat[HALF:]
+            shifted[pl.ds(frame * DOWN, DOWN), here] = cells
+            shifted[pl.ds(frame * DOWN, DOWN - HALF), after] = cells[HALF:]
             shifted[pl.ds(frame * DOWN + DOWN - HALF, HALF), after] = jnp.zeros((HALF, WIDE), BF16)
-    mixed = dot_nt(shifted[...], kernels[...]).astype(BF16)
-    for frame in range(2):
+    product = dot_nt(shifted[...], kernels[...]).astype(BF16)
+    for frame in range(4):
         for par in range(2):
             for col_par in range(2):
                 lanes = slice((par * 2 + col_par) * CH, (par * 2 + col_par + 1) * CH)
                 for col in range(4):
                     rows = slice(frame * DOWN + col * HALF, frame * DOWN + (col + 1) * HALF)
                     plane = (frame * 2 + par) * COLS + 2 * col + col_par
-                    sent_out[pl.ds(plane * HALF, HALF), :] = mixed[rows, lanes]
-
-
-def plane_grads_body(
-    core, grad_mixed, kept, acts, pre, time_far, down_far,
-    grads, lowered, ahead,
-    mine_out, other_out, windows_out, slope_out, part_out, time_out,
-    flat, rows_here, times, sems,
-):
-    loads = start(sems, (0, time_far, time_out), (1, down_far, times))
-    base = 3 * CH + 18 * CH
-    flat[pl.ds(base, 8 * WIDE), :] = grads[pl.ds(0, 8 * WIDE), :]
-    base += 8 * WIDE
-    last = dot_tn(lowered[...], ahead[pl.ds(DOWN, DOWN), :])
+                    mixed[pl.ds(plane * HALF, HALF), :] = product[rows, lanes]
+
+    loads[0].wait()
+    taps = jnp.concatenate([first_time[k] for k in range(3)], axis=1)
+    cotans = []
+    for frame in range(2):
+        parts = []
+        for par in range(2):
+            frames = [
+                mixed[pl.ds(((frame + 2 - k) * 2 + par) * CELLS, CELLS), :] for k in range(3)
+            ]
+            grad_hidden = dot_nt(jnp.concatenate(frames, axis=1), taps)
+            parts.append((grad_hidden * slope[frame, par]).astype(BF16))
+        cotans.append(jnp.concatenate(parts, axis=1))
+    product = dot_tn(windows[...], jnp.concatenate(cotans, axis=0))
+    for row in range(3):
+        for tap in range(3):
+            at = (tap * 4 + row) * CH
+            flat[pl.ds((row * 3 + tap) * CH, CH), :] = (
+                product[at : at + CH, :CH] + product[at + CH : at + 2 * CH, CH:]
+            )
+    cotan = mixed[pl.ds(0, 4 * CELLS), :]
+    for k in range(3):
+        flat[pl.ds((9 + k) * CH, CH), :] = dot_tn(acts[pl.ds(k, 2)].reshape(4 * CELLS, CH), cotan)
+    down = dot_tn(cells_of(kept), jnp.concatenate(strided[:2], axis=0))
+    last = [dot_tn(lowered[...], sent[pl.ds(DOWN, DOWN), :]) for sent in (further, ahead)]
+    flat[pl.ds(30 * CH, 12 * CH), :] = grads[pl.ds(0, 12 * CH), :]
     for half in range(2):
-        flat[pl.ds(base + half * WIDE, WIDE), :] = last[:, half * CH : (half + 1) * CH]
-    cotan = grad_mixed[pl.ds(0, 4 * CELLS), :]
-    for k in range(3):
-        taps = acts[pl.ds(k, 2)].reshape(4 * CELLS, CH)
-        flat[pl.ds(k * CH, CH), :] = dot_tn(taps, cotan)
-    for frame in range(2):
-        planes = [acts[4 + frame, par].reshape(COLS, HALF, CH) for par in range(2)]
-        fill_windows(windows_out, frame * CELLS, *planes)
-    slope_out[...] = silu_slope(pre[...])
-    loads[0].wait()
-    for par in range(2):
-        first, second = [
-            grad_mixed[pl.ds((frame * 2 + par) * CELLS, CELLS), :] for frame in range(2)
-        ]
-        part_out[0, par] = dot_nt(first, time_out[2]) + dot_nt(second, time_out[1])
-        part_out[1, par] = dot_nt(second, time_out[2])
-    loads[1].wait()
-    grad_strided = jnp.concatenate(grad_strided_of(grads, ahead, times), axis=0)
-    down = dot_tn(cells_of(kept), grad_strided)
-    for half in range(2):
-        at = 3 * CH + half * 9 * CH
-        flat[pl.ds(at, 9 * CH), :] = down[:, half * CH : (half + 1) * CH]
+        lanes = slice(half * CH, (half + 1) * CH)
+        flat[pl.ds((12 + half * 9) * CH, 9 * CH), :] = down[:, lanes]
+        base = (42 + half * 6) * CH
+        for k in range(2):
+            flat[pl.ds(base + k * WIDE, WIDE), :] = last[k][:, lanes]
+        flat[pl.ds(base + 2 * WIDE, WIDE), :] = grads[pl.ds((6 + half) * WIDE, WIDE), :]
+
     here = core[0]
-    half = EARLY // 2
+    half = GRADS // 2
     mine_out[pl.ds(0, half), :] = flat[pl.ds(pl.multiple_of(here * half, 16), half), :]
     other_out[pl.ds(0, half), :] = flat[
         pl.ds(pl.multiple_of((1 - here) * half, 16), half), :
@@ -383,57 +386,15 @@
     other_out[pl.ds(half, DOWN), :] = away.astype(BF16)
 
 
-def last_body(
-    core, ahead, windows, slope, part, first_time, lowered, early_other,
-    mine_out, other_out,
-    flat,
-):
-    cotans = [[], []]
-    for par in range(2):
-        first, second = [
-            ahead[pl.ds((frame * 2 + par) * CELLS, CELLS), :] for frame in range(2)
-        ]
-        hidden = (
-            part[0, par] + dot_nt(first, first_time[0]),
-            part[1, par] + dot_nt(first, first_time[1]) + dot_nt(second, first_time[0]),
-        )
-        for frame in range(2):
-            cotans[frame].append((hidden[frame] * slope[frame, par]).astype(BF16))
-    cotan = jnp.concatenate([jnp.concatenate(parts, axis=1) for parts in cotans], axis=0)
-    product = dot_tn(windows[...], cotan)
-    for row in range(3):
-        for tap in range(3):
-            at = (tap * 4 + row) * CH
-            flat[pl.ds((row * 3 + tap) * CH, CH), :] = (
-                product[at : at + CH, :CH] + product[at + CH : at + 2 * CH, CH:]
-            )
-    further = [ahead[pl.ds(4 * CELLS + half * DOWN, DOWN), :] for half in range(2)]
-    for half in range(2):
-        flat[pl.ds(9 * CH + half * WIDE, WIDE), :] = dot_tn(lowered[...], further[half])
-    here = core[0]
-    half = mine_out.shape[0]
-    mine_out[...] = flat[pl.ds(pl.multiple_of(here * half, 16), half), :]
-    rows = early_other.shape[0]
-    other_out[pl.ds(0, rows), :] = early_other[...]
-    other_out[pl.ds(rows, half), :] = flat[
-        pl.ds(pl.multiple_of((1 - here) * half, 16), half), :
-    ].astype(BF16)
-
-
-def halves_body(core, early, late, other, half_out, frames_out):
-    rows, more = EARLY // 2, LATE // 2
-    half_out[pl.ds(0, rows), :] = (
-        early[pl.ds(0, rows), :] + other[pl.ds(0, rows), :].astype(F32)
-    ).astype(BF16)
+def halves_body(core, own, other, half_out, frames_out):
+    rows = half_out.shape[0]
+    half_out[...] = (own[pl.ds(0, rows), :] + other[pl.ds(0, rows), :].astype(F32)).astype(BF16)
     here = core[0]
     chips = HALF // 2
-    mine = early[pl.ds(rows, DOWN), :].reshape(chips, 8, CH)
+    mine = own[pl.ds(rows, DOWN), :].reshape(chips, 8, CH)
     theirs = other[pl.ds(rows, DOWN), :].astype(F32).reshape(chips, 8, CH)
     frames = [jnp.where(here == 0, mine, theirs), jnp.where(here == 0, theirs, mine)]
     frames_out[...] = jnp.concatenate(frames, axis=1).astype(BF16)
-    half_out[pl.ds(rows, more), :] = (
-        late[...] + other[pl.ds(rows + DOWN, more), :].astype(F32)
-    ).astype(BF16)
 
 
 def sum_body(blocks, frames, sent_out, padded):
@@ -467,25 +428,18 @@
         part_out[block] = part
 
 
-def results_body(
-    core, mine, other,
-    first_plane_out, first_time_out, down_plane_out, down_time_out, last_time_out,
-    early, late,
-):
+def results_body(core, mine, other, *rest):
+    outs, whole = rest[:-1], rest[-1]
     here = core[0]
-    rows, more = EARLY // 2, LATE // 2
-    for half, at in ((mine, here), (other, 1 - here)):
-        early[pl.ds(pl.multiple_of(at * rows, 16), rows), :] = half[pl.ds(0, rows), :]
-        late[pl.ds(pl.multiple_of(at * more, 16), more), :] = half[pl.ds(rows, more), :]
-    first_plane_out[...] = late[pl.ds(0, 9 * CH), :]
-    first_time_out[...] = early[pl.ds(0, 3 * CH), :]
-    for half in range(2):
-        lanes = pl.ds(half * CH, CH)
-        down_plane_out[:, lanes] = early[pl.ds(3 * CH + half * 9 * CH, 9 * CH), :]
-        down_time_out[:, lanes] = early[pl.ds(21 * CH + half * 6 * CH, 6 * CH), :]
-        last_time_out[pl.ds(0, WIDE), lanes] = late[pl.ds(9 * CH + half * WIDE, WIDE), :]
-        last_time_out[pl.ds(WIDE, WIDE), lanes] = early[pl.ds(37 * CH + half * WIDE, WIDE), :]
-        last_time_out[pl.ds(2 * WIDE, WIDE), lanes] = early[pl.ds(33 * CH + half * WIDE, WIDE), :]
+    half = mine.shape[0]
+    whole[pl.ds(pl.multiple_of(here * half, 16), half), :] = mine[...]
+    whole[pl.ds(pl.multiple_of((1 - here) * half, 16), half), :] = other[...]
+    first = 0
+    for out in outs:
+        rows, lanes = out.shape
+        for part in range(lanes // CH):
+            out[:, pl.ds(part * CH, CH)] = whole[pl.ds(first, rows), :]
+            first += rows
 
 
 def output_body(received, last_time, output, spread, padded):
@@ -602,64 +556,51 @@
         [down, (P_, (2 * DOWN, WIDE), BF16)],
     )
     ahead = from_behind(sent, -1)
-    near_times, kernels, time_grads = call(
+    further = from_behind(sent, -2)
+    all_times, kernels, time_grads, windows, slope = call(
         time_grads_body,
         [
-            (P_, sent), (P_, lowered), (P_, strided_prior), (P_, kept),
-            (H, down_time), (H, down_plane),
-        ],
-        [
-            times,
+            (P_, sent), (P_, lowered), (P_, strided_prior), (P_, kept), (P_, acts),
+            (P_, pre_first), (H, down_time), (H, down_plane),
+        ],
+        [
+            (P_, (3, WIDE, WIDE), BF16),
             (P_, (4 * CH, 4 * WIDE), BF16),
             (P_, (PART_AT + 2 * DOWN, CH), F32),
-        ],
-        [((3, WIDE, WIDE), BF16), ((3, 3, CH, WIDE), BF16)],
-        copies=2,
-    )
-    (sent,) = call(
-        back_body,
-        [(P_, ahead), (P_, time_grads), (P_, near_times), (P_, kernels)],
-        [(P_, (4 * CELLS + 2 * DOWN, CH), BF16)],
-        [((2 * DOWN, 4 * WIDE), BF16)],
-    )
-    further = from_behind(sent, -1)
-    early, early_other, windows, slope, part, near_time = call(
-        plane_grads_body,
-        [
-            (S, core), (P_, sent), (P_, kept), (P_, acts), (P_, pre_first),
-            (H, first_time), (H, down_time), (P_, time_grads), (P_, lowered), (P_, ahead),
-        ],
-        [
-            (P_, (EARLY // 2 + DOWN, CH), F32),
-            (P_, (EARLY // 2 + DOWN, CH), BF16),
             (P_, (2 * CELLS, 12 * CH), BF16),
             (P_, flat_frames, F32),
-            (P_, flat_frames, F32),
-            (P_, (3, CH, CH), BF16),
-        ],
-        [((EARLY, CH), F32), ((HALF // 2, 2, 8, CH), F32), ((3, WIDE, WIDE), BF16)],
+        ],
+        [((3, 3, CH, WIDE), BF16)],
         copies=2,
     )
-    late, other = call(
-        last_body,
-        [
-            (S, core), (P_, further), (P_, windows), (P_, slope), (P_, part), (P_, near_time),
-            (P_, lowered), (P_, early_other),
-        ],
-        [(P_, (LATE // 2, CH), F32), (P_, ((EARLY + LATE) // 2 + DOWN, CH), BF16)],
-        [((LATE, CH), F32)],
+    half_rows = GRADS // 2
+    mine, other = call(
+        back_body,
+        [
+            (S, core), (P_, ahead), (P_, further), (P_, time_grads), (P_, all_times),
+            (P_, kernels), (P_, kept), (P_, acts), (P_, windows), (P_, slope), (P_, lowered),
+            (H, first_time),
+        ],
+        [(P_, (half_rows + DOWN, CH), F32), (P_, (half_rows + DOWN, CH), BF16)],
+        [
+            ((4 * DOWN, 4 * WIDE), BF16),
+            ((8 * CELLS, CH), BF16),
+            ((GRADS, CH), F32),
+            ((HALF // 2, 2, 8, CH), F32),
+            ((3, CH, CH), BF16),
+        ],
+        copies=1,
         flops=600000000,
         size=2000000,
     )
 
     clips = lax.axis_size("clip")
     chips = lax.axis_size("seq") // 2
-    half_rows = (EARLY + LATE) // 2
     part_rows = half_rows // clips
     other = swap_cores(other)
     half, frames = call(
         halves_body,
-        [(S, core), (P_, early), (P_, late), (V, other)],
+        [(S, core), (P_, mine), (V, other)],
         [(P_, (half_rows, CH), BF16), (V, (chips, 16, CH), BF16)],
     )
     blocks = exchange_clip(half.reshape(clips, part_rows, CH))
@@ -692,7 +633,7 @@
             (V, (3 * WIDE, WIDE), BF16),
             (V, (3 * WIDE, WIDE), BF16),
         ],
-        [((EARLY, CH), BF16), ((LATE, CH), BF16)],
+        [((GRADS, CH), BF16)],
     )
     shapes = ((3, 3, CH, CH), (3, CH, CH), (3, 3, CH, WIDE), (3, WIDE, WIDE), (3, WIDE, WIDE))
     grads = [grad.reshape(shape) for grad, shape in zip(grads, shapes)]

time: 146 us -> 141 us (0.966)
  waiting for transfers between devices: 15.6 us -> 12.7 us
    ppermute x4, waiting for transfers between devices: 6.36 us -> 3.38 us  [from_behind(): return lax.ppermute(block, 'seq', route)]
    pallas_call x17 -> x15, Pallas kernels: 14.2 us -> 13.9 us  [call(): pl.pallas_call(body, out_shape=[placed_output(*out) for out in outs], in_...]
  transfers between devices with their start and end apart: 8 -> 8, of which waited for: 5 -> 4; matrix products, arithmetic and copies ran while one was open for 1% -> 1% of each run, Pallas kernels for 7% -> 6%
where the time goes in v10:
time: 141 us; the launch traced here: 140 us
  blocking collectives  70.8 us (50%)
  starting transfers between devices  40.6 us (29%)
  Pallas kernels  13.9 us (10%)
  waiting for transfers between devices  12.7 us (9%)
  local copies, waits for them, and re-layouts  1.52 us (1%)
    all_to_all x2, blocking collectives, exchange_clip(): lax.all_to_all(blocks, 'clip', split_axis=0, concat_axis=0, tiled=True)  36.7 us
    all_to_all x2, blocking collectives, exchange_chips(): lax.all_to_all(blocks, 'seq', split_axis=0, concat_axis=0, axis_index_gro...  34.1 us
    ppermute x4, starting transfers between devices, from_behind(): return lax.ppermute(block, 'seq', route)  15.9 us
    ppermute x3, starting transfers between devices, swap_cores(): return lax.ppermute(block, 'seq', [(i, i ^ 1) for i in range(count)])  14 us
    pallas_call x15, Pallas kernels, call(): pl.pallas_call(body, out_shape=[placed_output(*out) for out in outs], in_...  13.9 us
    all_to_all x1, starting transfers between devices, exchange_chips(): lax.all_to_all(blocks, 'seq', split_axis=0, concat_axis=0, axis_index_gro...  10.8 us
    all_to_all x1, waiting for transfers between devices, exchange_chips(): lax.all_to_all(blocks, 'seq', split_axis=0, concat_axis=0, axis_index_gro...  5.7 us
    ppermute x3, waiting for transfers between devices, swap_cores(): return lax.ppermute(block, 'seq', [(i, i ^ 1) for i in range(count)])  3.58 us
  transfers between devices with their start and end apart: 8, of which 4 were waited for; matrix products, arithmetic and copies ran while one was open for 1% of the time, Pallas kernels for 6%

profile of v10, /device:TPU:1, one launch (start us, length us, event | category | flops | bytes accessed | tf_op | source)
XLA Modules:
  0.0 140.4 jit_solution(13899085286511909005)
XLA Ops:
  0.6 4.9 %collective-permute-start.1 = (bf16[1024,128]{1,0:T(8,128)(2,1)}, bf16[1024,128]{1,0:T(8,128)(2,1)S(1)}, u32[]{:S(2)}, u32[]{:S(2)}) collective-permute-start(bf16[1024,128]{1,0:T(8,128)(2,1)} %bitcast.15), channel_id=1, source_target_pairs={{0,1},{1,2},{2,3},{3,4},{4,5},{5,6},{6,7},{7,8},{8,9},{9,10},{10,1... | collective-permute-start | bytes 786440 | tf_op jit(solution)/shard_map/ppermute | solution.py:461
  5.6 0.9 reshape_squeeze.3.rows
  6.5 1.3 shard_map.118
  7.8 5.2 %collective-permute-start = (bf16[16,16,128]{2,1,0:T(8,128)(2,1)S(1)}, bf16[16,16,128]{2,1,0:T(8,128)(2,1)S(1)}, u32[]{:S(2)}, u32[]{:S(2)}) collective-permute-start(bf16[16,16,128]{2,1,0:T(8,128)(2,1)S(1)} %get-tuple-element.35), channel_id=1, source_target_pairs={{0,1},{1,0},{2,3},{3,2},{4,5},{5,4},{6,7},{7,6},{8,9},{9,8},{10,11... | collective-permute-start | bytes 196616 | tf_op jit(solution)/shard_map/ppermute | solution.py:466
  13.0 2.0 %shard_map.119 = (bf16[4,2,256,128]{3,2,1,0:T(8,128)(2,1)S(1)}, f32[2,2,256,128]{3,2,1,0:T(8,128)S(1)}, bf16[1536,256]{1,0:T(8,128)(2,1)S(1)}) custom-call(bf16[1024,128]{1,0:T(8,128)(2,1)} %bitcast.16, bf16[3,3,128,128]{3,2,1,0:T(8,128)(2,1)} %plane_far.3), custom_call_target="tpu_custom_call" | custom-call | flops 1000 | bytes 8000000 | tf_op jit(solution)/shard_map/pallas_call | solution.py:56
  15.0 0.8 shard_map.120.acts
  15.9 0.7 shard_map.122
  16.5 10.8 %all-to-all-start = ((bf16[16,32,128]{2,1,0:T(8,128)(2,1)}), bf16[16,32,128]{2,1,0:T(8,128)(2,1)S(1)}, u32[]{:S(2)}, u32[]{:S(2)}) async-start(bf16[16,32,128]{2,1,0:T(8,128)(2,1)} %shard_map.122), calls=%async_computation | async-start | bytes 262144 | tf_op jit(solution)/shard_map/all_to_all | solution.py:476
  27.3 2.1 %shard_map.121 = (bf16[2560,128]{1,0:T(8,128)(2,1)S(1)}, bf16[2,128,256]{2,1,0:T(8,128)(2,1)S(1)}, f32[128,256]{1,0:T(8,128)S(1)}, bf16[2,256,256]{2,1,0:T(8,128)(2,1)S(1)}) custom-call(bf16[6,2,256,128]{3,2,1,0:T(8,128)(2,1)S(1)} %shard_map.120.acts, bf16[3,128,128]{2,1,0:T(8,128)(2,1)} %time_far.3, bf16[3,3,128,256]{3,2,1,0:T(8,128)(2,1)} %plane_far.5, ...), custom_call_target="tpu_custom_call" | custom-call | flops 1000 | bytes 8000000 | tf_op jit(solution)/shard_map/pallas_call | solution.py:56
  29.4 4.2 %collective-permute-start.2 = (bf16[2,128,256]{2,1,0:T(8,128)(2,1)S(1)}, bf16[2,128,256]{2,1,0:T(8,128)(2,1)S(1)}, u32[]{:S(2)}, u32[]{:S(2)}) collective-permute-start(bf16[2,128,256]{2,1,0:T(8,128)(2,1)S(1)} %get-tuple-element.39), channel_id=1, source_target_pairs={{0,1},{1,2},{2,3},{3,4},{4,5},{5,6},{6,7},{7,8},{8,9},{9,10},{10,1... | collective-permute-start | bytes 393224 | tf_op jit(solution)/shard_map/ppermute | solution.py:461
  33.7 5.7 %all-to-all-done = bf16[16,32,128]{2,1,0:T(8,128)(2,1)S(1)} async-done(((bf16[16,32,128]{2,1,0:T(8,128)(2,1)}), bf16[16,32,128]{2,1,0:T(8,128)(2,1)S(1)}, u32[]{:S(2)}, u32[]{:S(2)}) %all-to-all-start) | async-done | bytes 131104 | tf_op jit(solution)/shard_map/all_to_all | solution.py:476
  39.4 0.1 shard_map.123
  39.5 0.2 shard_map.124
  39.7 1.3 collective-permute-start.4
  41.0 5.4 %collective-permute-start.3 = (bf16[256,256]{1,0:T(8,128)(2,1)S(1)}, bf16[256,256]{1,0:T(8,128)(2,1)S(1)}, u32[]{:S(2)}, u32[]{:S(2)}) collective-permute-start(bf16[256,256]{1,0:T(8,128)(2,1)S(1)} %get-tuple-element.46.sent), channel_id=1, source_target_pairs={{1,0},{2,1},{3,2},{4,3},{5,4},{6,5},{7,6},{8,7},{9,8},{10,9},{11,1... | collective-permute-start | bytes 393224 | tf_op jit(solution)/shard_map/ppermute | solution.py:461
  46.4 1.5 %shard_map.125 = (bf16[3,256,256]{2,1,0:T(8,128)(2,1)S(1)}, bf16[512,1024]{1,0:T(8,128)(2,1)S(1)}, f32[2560,128]{1,0:T(8,128)S(1)}, bf16[512,1536]{1,0:T(8,128)(2,1)S(1)}, f32[2,2,256,128]{3,2,1,0:T(8,128)S(1)}) custom-call(bf16[256,256]{1,0:T(8,128)(2,1)S(1)} %get-tuple-element.46.sent, bf16[128,256]{1,0:T(8,128)(2,1)S(1)} %get-tuple-element.47.lowered, ...), custom_call_target="tpu_custom_call" | custom-call | flops 1000 | bytes 8000000 | tf_op jit(solution)/shard_map/pallas_call | solution.py:56
  48.0 3.4 %collective-permute-done.3.ahead = bf16[256,256]{1,0:T(8,128)(2,1)S(1)} collective-permute-done((bf16[256,256]{1,0:T(8,128)(2,1)S(1)}, bf16[256,256]{1,0:T(8,128)(2,1)S(1)}, u32[]{:S(2)}, u32[]{:S(2)}) %collective-permute-start.3) | collective-permute-done | bytes 131104 | tf_op jit(solution)/shard_map/ppermute | solution.py:461
  51.3 3.1 %shard_map.126 = (f32[3584,128]{1,0:T(8,128)S(1)}, bf16[3584,128]{1,0:T(8,128)(2,1)S(1)}) custom-call(s32[1]{0:T(128)} %bitcast.core, bf16[256,256]{1,0:T(8,128)(2,1)S(1)} %collective-permute-done.3.ahead, bf16[256,256]{1,0:T(8,128)(2,1)S(1)} %collective-permute-done.4.further, f32[2560,128]{1,0:T(8,128)S(1)} %get-tuple-element.50.grads, ...), custom_call_target="tpu_custom_call" | custom-call | flops 600000000 | bytes 2000000 | tf_op jit(solution)/shard_map/pallas_call | solution.py:56
  54.4 1.9 %collective-permute-start.5 = (bf16[3584,128]{1,0:T(8,128)(2,1)S(1)}, bf16[3584,128]{1,0:T(8,128)(2,1)S(1)}, u32[]{:S(2)}, u32[]{:S(2)}) collective-permute-start(bf16[3584,128]{1,0:T(8,128)(2,1)S(1)} %get-tuple-element.56), channel_id=1, source_target_pairs={{0,1},{1,0},{2,3},{3,2},{4,5},{5,4},{6,7},{7,6},{8,9},{9,8},{10,11... | collective-permute-start | bytes 2752520 | tf_op jit(solution)/shard_map/ppermute | solution.py:466
  56.4 2.4 %collective-permute-done.5.other = bf16[3584,128]{1,0:T(8,128)(2,1)S(1)} collective-permute-done((bf16[3584,128]{1,0:T(8,128)(2,1)S(1)}, bf16[3584,128]{1,0:T(8,128)(2,1)S(1)}, u32[]{:S(2)}, u32[]{:S(2)}) %collective-permute-start.5) | collective-permute-done | bytes 917536 | tf_op jit(solution)/shard_map/ppermute | solution.py:466
  58.8 0.2 shard_map.127
  59.0 20.6 %all_to_all.25.blocks = bf16[16,216,128]{2,1,0:T(8,128)(2,1)S(1)} all-to-all(bf16[16,216,128]{2,1,0:T(8,128)(2,1)S(1)} %bitcast.13), channel_id=1, replica_groups=mesh['clip'=16,'seq'=32] {'clip'}, dimensions={0} | all-to-all | bytes 1769472 | tf_op jit(solution)/shard_map/all_to_all | solution.py:470
  79.6 0.1 shard_map.128
  79.7 18.3 %all_to_all.26.received = bf16[16,32,128]{2,1,0:T(8,128)(2,1)S(1)} all-to-all(bf16[16,32,128]{2,1,0:T(8,128)(2,1)S(1)} %shard_map.128), channel_id=1, replica_groups={{0,2,4,6,8,10,12,14,16,18,20,22,24,26,28,30},{1,3,5,7,9,11,13,15,17,19,..., dimensions={0} | all-to-all | bytes 262144 | tf_op jit(solution)/shard_map/all_to_all | solution.py:476
  98.0 15.8 %all_to_all.27.pieces = bf16[16,16,128]{2,1,0:T(8,128)(2,1)S(1)} all-to-all(bf16[16,16,128]{2,1,0:T(8,128)(2,1)S(1)} %shard_map.130), channel_id=1, replica_groups={{0,2,4,6,8,10,12,14,16,18,20,22,24,26,28,30},{1,3,5,7,9,11,13,15,17,19,..., dimensions={0} | all-to-all | bytes 131072 | tf_op jit(solution)/shard_map/all_to_all | solution.py:476
  113.8 0.1 shard_map.131
  114.0 16.1 %all_to_all.28 = bf16[16,216,128]{2,1,0:T(8,128)(2,1)S(1)} all-to-all(bf16[16,216,128]{2,1,0:T(8,128)(2,1)S(1)} %shard_map.131), channel_id=1, replica_groups=mesh['clip'=16,'seq'=32] {'clip'}, dimensions={0} | all-to-all | bytes 1769472 | tf_op jit(solution)/shard_map/all_to_all | solution.py:470
  130.1 6.9 %collective-permute-start.6 = (bf16[3456,128]{1,0:T(8,128)(2,1)S(1)}, bf16[3456,128]{1,0:T(8,128)(2,1)S(1)}, u32[]{:S(2)}, u32[]{:S(2)}) collective-permute-start(bf16[3456,128]{1,0:T(8,128)(2,1)S(1)} %bitcast.11), channel_id=1, source_target_pairs={{0,1},{1,0},{2,3},{3,2},{4,5},{5,4},{6,7},{7,6},{8,9},{9,8},{10,11... | collective-permute-start | bytes 2654216 | tf_op jit(solution)/shard_map/ppermute | solution.py:466
  137.0 0.2 shard_map.129
  137.2 0.7 reshape.49
  137.9 1.1 collective-permute-done.6.other
  139.0 1.4 %shard_map.132 = (bf16[1152,128]{1,0:T(8,128)(2,1)}, bf16[384,128]{1,0:T(8,128)(2,1)}, bf16[1152,256]{1,0:T(8,128)(2,1)}, bf16[768,256]{1,0:T(8,128)(2,1)}, bf16[768,256]{1,0:T(8,128)(2,1)}) custom-call(s32[1]{0:T(128)} %bitcast.core, bf16[3456,128]{1,0:T(8,128)(2,1)S(1)} %bitcast.12, bf16[3456,128]{1,0:T(8,128)(2,1)S(1)} %collective-permute-done.6.other), custom_call_target="tpu_custom_call" | custom-call | flops 1000 | bytes 8000000 | tf_op jit(solution)/shard_map/pallas_call | solution.py:56
  (7 shorter events, 0.0 us)
Async XLA Ops:
  0.6 14.3 %collective-permute-start.1 = (bf16[1024,128]{1,0:T(8,128)(2,1)}, bf16[1024,128]{1,0:T(8,128)(2,1)S(1)}, u32[]{:S(2)}, u32[]{:S(2)}) collective-permute-start(bf16[1024,128]{1,0:T(8,128)(2,1)} %bitcast.15), channel_id=1, source_target_pairs={{0,1},{1,2},{2,3},{3,4},{4,5},{5,6},{6,7},{7,8},{8,9},{9,10},{10,1... | collective-permute-start | bytes 786440 | tf_op jit(solution)/shard_map/ppermute | solution.py:461
  7.8 8.0 %collective-permute-start = (bf16[16,16,128]{2,1,0:T(8,128)(2,1)S(1)}, bf16[16,16,128]{2,1,0:T(8,128)(2,1)S(1)}, u32[]{:S(2)}, u32[]{:S(2)}) collective-permute-start(bf16[16,16,128]{2,1,0:T(8,128)(2,1)S(1)} %get-tuple-element.35), channel_id=1, source_target_pairs={{0,1},{1,0},{2,3},{3,2},{4,5},{5,4},{6,7},{7,6},{8,9},{9,8},{10,11... | collective-permute-start | bytes 196616 | tf_op jit(solution)/shard_map/ppermute | solution.py:466
  16.5 22.8 %all-to-all-start = ((bf16[16,32,128]{2,1,0:T(8,128)(2,1)}), bf16[16,32,128]{2,1,0:T(8,128)(2,1)S(1)}, u32[]{:S(2)}, u32[]{:S(2)}) async-start(bf16[16,32,128]{2,1,0:T(8,128)(2,1)} %shard_map.122), calls=%async_computation | async-start | bytes 262144 | tf_op jit(solution)/shard_map/all_to_all | solution.py:476
  29.4 10.0 %collective-permute-start.2 = (bf16[2,128,256]{2,1,0:T(8,128)(2,1)S(1)}, bf16[2,128,256]{2,1,0:T(8,128)(2,1)S(1)}, u32[]{:S(2)}, u32[]{:S(2)}) collective-permute-start(bf16[2,128,256]{2,1,0:T(8,128)(2,1)S(1)} %get-tuple-element.39), channel_id=1, source_target_pairs={{0,1},{1,2},{2,3},{3,4},{4,5},{5,6},{6,7},{7,8},{8,9},{9,10},{10,1... | collective-permute-start | bytes 393224 | tf_op jit(solution)/shard_map/ppermute | solution.py:461
  39.7 8.2 %collective-permute-start.4 = (bf16[256,256]{1,0:T(8,128)(2,1)S(1)}, bf16[256,256]{1,0:T(8,128)(2,1)S(1)}, u32[]{:S(2)}, u32[]{:S(2)}) collective-permute-start(bf16[256,256]{1,0:T(8,128)(2,1)S(1)} %get-tuple-element.46.sent), channel_id=1, source_target_pairs={{2,0},{3,1},{4,2},{5,3},{6,4},{7,5},{8,6},{9,7},{10,8},{11,9},{12,... | collective-permute-start | bytes 393224 | tf_op jit(solution)/shard_map/ppermute | solution.py:461
  41.0 10.3 %collective-permute-start.3 = (bf16[256,256]{1,0:T(8,128)(2,1)S(1)}, bf16[256,256]{1,0:T(8,128)(2,1)S(1)}, u32[]{:S(2)}, u32[]{:S(2)}) collective-permute-start(bf16[256,256]{1,0:T(8,128)(2,1)S(1)} %get-tuple-element.46.sent), channel_id=1, source_target_pairs={{1,0},{2,1},{3,2},{4,3},{5,4},{6,5},{7,6},{8,7},{9,8},{10,9},{11,1... | collective-permute-start | bytes 393224 | tf_op jit(solution)/shard_map/ppermute | solution.py:461
  54.4 4.4 %collective-permute-start.5 = (bf16[3584,128]{1,0:T(8,128)(2,1)S(1)}, bf16[3584,128]{1,0:T(8,128)(2,1)S(1)}, u32[]{:S(2)}, u32[]{:S(2)}) collective-permute-start(bf16[3584,128]{1,0:T(8,128)(2,1)S(1)} %get-tuple-element.56), channel_id=1, source_target_pairs={{0,1},{1,0},{2,3},{3,2},{4,5},{5,4},{6,7},{7,6},{8,9},{9,8},{10,11... | collective-permute-start | bytes 2752520 | tf_op jit(solution)/shard_map/ppermute | solution.py:466
  98.0 39.0 %copy-start = (bf16[3,256,256]{2,1,0:T(8,128)(2,1)S(1)}, bf16[3,256,256]{2,1,0:T(8,128)(2,1)}, u32[]{:S(2)}) copy-start(bf16[3,256,256]{2,1,0:T(8,128)(2,1)} %last_time.1) | copy-start | bytes 1179652
  130.1 8.9 %collective-permute-start.6 = (bf16[3456,128]{1,0:T(8,128)(2,1)S(1)}, bf16[3456,128]{1,0:T(8,128)(2,1)S(1)}, u32[]{:S(2)}, u32[]{:S(2)}) collective-permute-start(bf16[3456,128]{1,0:T(8,128)(2,1)S(1)} %bitcast.11), channel_id=1, source_target_pairs={{0,1},{1,0},{2,3},{3,2},{4,5},{5,4},{6,7},{7,6},{8,9},{9,8},{10,11... | collective-permute-start | bytes 2654216 | tf_op jit(solution)/shard_map/ppermute | solution.py:466

commit v11 on v10

--- a/solution.py
+++ b/solution.py
@@ -173,9 +173,7 @@
     times_out[...] = down_time[pl.ds(0, 2)]
 
 
-def rows_body(
-    core, rows, last_far, mine_out, away_out, last_time, spread, padded, turned, frames, sems
-):
+def rows_body(rows, last_far, sent_out, last_time, spread, padded, turned, sems):
     loads = start(sems, (0, last_far, last_time))
     cotan = rows[...].astype(F32)
     spread[...] = cotan.reshape(HALF * 8, CH)
@@ -190,17 +188,7 @@
     for half in range(2):
         turned[pl.ds(half, DOWN, stride=2), :] = total[:, half * CH : (half + 1) * CH]
     both = jnp.concatenate([turned[...].reshape(HALF, 8, CH), cotan], axis=1)
-    frames[...] = both.reshape(HALF // 2, 2, 16, CH)
-    here = core[0]
-    mine_out[...] = frames[:, pl.ds(here, 1)].reshape(HALF // 2, 16, CH).astype(BF16)
-    away_out[...] = frames[:, pl.ds(1 - here, 1)].reshape(HALF // 2, 16, CH).astype(BF16)
-
-
-def join_body(core, mine, theirs, sent_out):
-    here = core[0]
-    own, other = mine[...].astype(F32), theirs[...].astype(F32)
-    sent_out[:, pl.ds(0, 16), :] = jnp.where(here == 0, own, other).astype(BF16)
-    sent_out[:, pl.ds(16, 16), :] = jnp.where(here == 0, other, own).astype(BF16)
+    sent_out[...] = both.astype(BF16)
 
 
 def own_body(
@@ -467,7 +455,17 @@
 
 
 def exchange_clip(blocks):
-    return lax.all_to_all(blocks, "clip", split_axis=0, concat_axis=0, tiled=True)
+    count = lax.axis_size("clip")
+    side = round(count**0.5)
+    rows = [list(range(first, first + side)) for first in range(0, count, side)]
+    path = [clip for at, row in enumerate(rows) for clip in (row if at % 2 == 0 else row[::-1])]
+    return lax.all_to_all(
+        blocks, "clip", split_axis=0, concat_axis=0, axis_index_groups=[path], tiled=True
+    )
+
+
+def exchange_seq(blocks):
+    return lax.all_to_all(blocks, "seq", split_axis=0, concat_axis=0, tiled=True)
 
 
 def exchange_chips(blocks):
@@ -483,20 +481,18 @@
     prior = from_behind(own, 1)
     flat_frames = (2, 2, CELLS, CH)
     core = (lax.axis_index("seq") % 2).astype(jnp.int32).reshape(1)
-    mine, away = call(
+    (sent,) = call(
         rows_body,
-        [(S, core), (V, cotan_out[0].reshape(HALF, 8, CH)), (H, last_time)],
-        [(P_, (HALF // 2, 16, CH), BF16), (V, (HALF // 2, 16, CH), BF16)],
+        [(V, cotan_out[0].reshape(HALF, 8, CH)), (H, last_time)],
+        [(V, (HALF, 16, CH), BF16)],
         [
             ((3, WIDE, WIDE), BF16),
             ((HALF * 8, CH), F32),
             ((DOWN + 8, WIDE), F32),
             ((HALF * 8, CH), F32),
-            ((HALF // 2, 2, 16, CH), F32),
         ],
         copies=1,
     )
-    theirs = swap_cores(away)
     acts, pre_first, both = call(
         own_body,
         [(H, own), (H, first_plane)],
@@ -520,13 +516,8 @@
         [((2 * CELLS, CH), F32), ((2 * CELLS, 12 * CH), BF16)],
     )
     times = (P_, (2, WIDE, WIDE), BF16)
-    theirs, acts = lax.optimization_barrier((theirs, acts))
-    (sent,) = call(
-        join_body,
-        [(S, core), (P_, mine), (P_, theirs)],
-        [(V, (HALF // 2, HALF, CH), BF16)],
-    )
-    received = exchange_chips(sent).reshape(HALF, 16, CH)
+    sent, acts = lax.optimization_barrier((sent, acts))
+    received = exchange_seq(sent)
     kept, strided, part, near_times = call(
         first_body,
         [

time: 141 us -> 140 us (level)
  waiting for transfers between devices: 12.7 us -> 17.1 us
  starting transfers between devices: 40.6 us -> 37.8 us
  blocking collectives: 70.8 us -> 68.3 us
    ppermute x3 -> x2, starting transfers between devices: 14 us -> 8.33 us  [swap_cores(): return lax.ppermute(block, 'seq', [(i, i ^ 1) for i in range(count)])]
    all_to_all x1, starting transfers between devices: 10.8 us -> 16.1 us  [exchange_seq(): lax.all_to_all(blocks, 'seq', split_axis=0, concat_axis=0, tiled=True)]
    all_to_all x1, waiting for transfers between devices: 5.7 us -> 10.2 us  [exchange_seq(): lax.all_to_all(blocks, 'seq', split_axis=0, concat_axis=0, tiled=True)]
    ppermute x4, starting transfers between devices: 15.9 us -> 13.4 us  [from_behind(): return lax.ppermute(block, 'seq', route)]
    all_to_all x2, blocking collectives: 34.1 us -> 32.2 us  [exchange_chips(): lax.all_to_all(blocks, 'seq', split_axis=0, concat_axis=0, axis_index_gro...]
    pallas_call x15 -> x14, Pallas kernels: 13.9 us -> 13.9 us  [call(): pl.pallas_call(body, out_shape=[placed_output(*out) for out in outs], in_...]
    ppermute x3 -> x2, waiting for transfers between devices: 3.58 us -> 3.58 us  [swap_cores(): return lax.ppermute(block, 'seq', [(i, i ^ 1) for i in range(count)])]
  transfers between devices with their start and end apart: 8 -> 7, of which waited for: 4 -> 4; matrix products, arithmetic and copies ran while one was open for 1% -> 1% of each run, Pallas kernels for 6% -> 6%
where the time goes in v11:
time: 140 us
  blocking collectives  68.3 us (49%)
  starting transfers between devices  37.8 us (27%)
  waiting for transfers between devices  17.1 us (12%)
  Pallas kernels  13.9 us (10%)
  local copies, waits for them, and re-layouts  1.53 us (1%)
    all_to_all x2, blocking collectives, exchange_clip(): lax.all_to_all(blocks, 'clip', split_axis=0, concat_axis=0, axis_index_gr...  36.1 us
    all_to_all x2, blocking collectives, exchange_chips(): lax.all_to_all(blocks, 'seq', split_axis=0, concat_axis=0, axis_index_gro...  32.2 us
    all_to_all x1, starting transfers between devices, exchange_seq(): lax.all_to_all(blocks, 'seq', split_axis=0, concat_axis=0, tiled=True)  16.1 us
    pallas_call x14, Pallas kernels, call(): pl.pallas_call(body, out_shape=[placed_output(*out) for out in outs], in_...  13.9 us
    ppermute x4, starting transfers between devices, from_behind(): return lax.ppermute(block, 'seq', route)  13.4 us
    all_to_all x1, waiting for transfers between devices, exchange_seq(): lax.all_to_all(blocks, 'seq', split_axis=0, concat_axis=0, tiled=True)  10.2 us
    ppermute x2, starting transfers between devices, swap_cores(): return lax.ppermute(block, 'seq', [(i, i ^ 1) for i in range(count)])  8.33 us
    ppermute x2, waiting for transfers between devices, swap_cores(): return lax.ppermute(block, 'seq', [(i, i ^ 1) for i in range(count)])  3.58 us
  transfers between devices with their start and end apart: 7, of which 4 were waited for; matrix products, arithmetic and copies ran while one was open for 1% of the time, Pallas kernels for 6%

profile of v11, /device:TPU:1, one launch (start us, length us, event | category | flops | bytes accessed | tf_op | source)
XLA Modules:
  0.0 139.5 jit_solution(10267227903672622556)
XLA Ops:
  0.6 4.9 %collective-permute-start = (bf16[1024,128]{1,0:T(8,128)(2,1)}, bf16[1024,128]{1,0:T(8,128)(2,1)S(1)}, u32[]{:S(2)}, u32[]{:S(2)}) collective-permute-start(bf16[1024,128]{1,0:T(8,128)(2,1)} %bitcast.13), channel_id=1, source_target_pairs={{0,1},{1,2},{2,3},{3,4},{4,5},{5,6},{6,7},{7,8},{8,9},{9,10},{10,1... | collective-permute-start | bytes 786440 | tf_op jit(solution)/shard_map/ppermute | solution.py:449
  5.6 2.0 %shard_map.119 = (bf16[4,2,256,128]{3,2,1,0:T(8,128)(2,1)S(1)}, f32[2,2,256,128]{3,2,1,0:T(8,128)S(1)}, bf16[1536,256]{1,0:T(8,128)(2,1)S(1)}) custom-call(bf16[1024,128]{1,0:T(8,128)(2,1)} %bitcast.14, bf16[3,3,128,128]{3,2,1,0:T(8,128)(2,1)} %plane_far.3), custom_call_target="tpu_custom_call" | custom-call | flops 1000 | bytes 8000000 | tf_op jit(solution)/shard_map/pallas_call | solution.py:56
  7.6 0.9 reshape_squeeze.3.rows
  8.5 2.0 %shard_map.118 = bf16[32,16,128]{2,1,0:T(8,128)(2,1)} custom-call(bf16[32,8,128]{2,1,0:T(8,128)(2,1)S(1)} %reshape_squeeze.3.rows, bf16[3,256,256]{2,1,0:T(8,128)(2,1)} %last_time.1), custom_call_target="tpu_custom_call" | custom-call | flops 1000 | bytes 8000000 | tf_op jit(solution)/shard_map/pallas_call | solution.py:56
  10.4 0.0 collective-permute-done.prior
  10.4 0.8 shard_map.120.acts
  11.3 16.1 %all-to-all-start = ((bf16[32,16,128]{2,1,0:T(8,128)(2,1)}), bf16[32,16,128]{2,1,0:T(8,128)(2,1)S(1)}, u32[]{:S(2)}, u32[]{:S(2)}) async-start(bf16[32,16,128]{2,1,0:T(8,128)(2,1)} %shard_map.118), calls=%async_computation | async-start | bytes 262144 | tf_op jit(solution)/shard_map/all_to_all | solution.py:468
  27.4 2.1 %shard_map.121 = (bf16[2560,128]{1,0:T(8,128)(2,1)S(1)}, bf16[2,128,256]{2,1,0:T(8,128)(2,1)S(1)}, f32[128,256]{1,0:T(8,128)S(1)}, bf16[2,256,256]{2,1,0:T(8,128)(2,1)S(1)}) custom-call(bf16[6,2,256,128]{3,2,1,0:T(8,128)(2,1)S(1)} %shard_map.120.acts, bf16[3,128,128]{2,1,0:T(8,128)(2,1)} %time_far.3, bf16[3,3,128,256]{3,2,1,0:T(8,128)(2,1)} %plane_far.5, ...), custom_call_target="tpu_custom_call" | custom-call | flops 1000 | bytes 8000000 | tf_op jit(solution)/shard_map/pallas_call | solution.py:56
  29.5 3.5 %collective-permute-start.1 = (bf16[2,128,256]{2,1,0:T(8,128)(2,1)S(1)}, bf16[2,128,256]{2,1,0:T(8,128)(2,1)S(1)}, u32[]{:S(2)}, u32[]{:S(2)}) collective-permute-start(bf16[2,128,256]{2,1,0:T(8,128)(2,1)S(1)} %get-tuple-element.36), channel_id=1, source_target_pairs={{0,1},{1,2},{2,3},{3,4},{4,5},{5,6},{6,7},{7,8},{8,9},{9,10},{10,1... | collective-permute-start | bytes 393224 | tf_op jit(solution)/shard_map/ppermute | solution.py:449
  33.0 10.2 %all-to-all-done.received = bf16[32,16,128]{2,1,0:T(8,128)(2,1)S(1)} async-done(((bf16[32,16,128]{2,1,0:T(8,128)(2,1)}), bf16[32,16,128]{2,1,0:T(8,128)(2,1)S(1)}, u32[]{:S(2)}, u32[]{:S(2)}) %all-to-all-start) | async-done | bytes 131104 | tf_op jit(solution)/shard_map/all_to_all | solution.py:468
  43.2 0.1 shard_map.122
  43.3 0.0 collective-permute-done.1.prior
  43.3 0.2 shard_map.123
  43.6 1.3 collective-permute-start.3
  44.9 3.7 %collective-permute-start.2 = (bf16[256,256]{1,0:T(8,128)(2,1)S(1)}, bf16[256,256]{1,0:T(8,128)(2,1)S(1)}, u32[]{:S(2)}, u32[]{:S(2)}) collective-permute-start(bf16[256,256]{1,0:T(8,128)(2,1)S(1)} %get-tuple-element.42.sent), channel_id=1, source_target_pairs={{1,0},{2,1},{3,2},{4,3},{5,4},{6,5},{7,6},{8,7},{9,8},{10,9},{11,1... | collective-permute-start | bytes 393224 | tf_op jit(solution)/shard_map/ppermute | solution.py:449
  48.6 1.5 %shard_map.124 = (bf16[3,256,256]{2,1,0:T(8,128)(2,1)S(1)}, bf16[512,1024]{1,0:T(8,128)(2,1)S(1)}, f32[2560,128]{1,0:T(8,128)S(1)}, bf16[512,1536]{1,0:T(8,128)(2,1)S(1)}, f32[2,2,256,128]{3,2,1,0:T(8,128)S(1)}) custom-call(bf16[256,256]{1,0:T(8,128)(2,1)S(1)} %get-tuple-element.42.sent, bf16[128,256]{1,0:T(8,128)(2,1)S(1)} %get-tuple-element.43.lowered, ...), custom_call_target="tpu_custom_call" | custom-call | flops 1000 | bytes 8000000 | tf_op jit(solution)/shard_map/pallas_call | solution.py:56
  50.1 3.4 %collective-permute-done.2.ahead = bf16[256,256]{1,0:T(8,128)(2,1)S(1)} collective-permute-done((bf16[256,256]{1,0:T(8,128)(2,1)S(1)}, bf16[256,256]{1,0:T(8,128)(2,1)S(1)}, u32[]{:S(2)}, u32[]{:S(2)}) %collective-permute-start.2) | collective-permute-done | bytes 131104 | tf_op jit(solution)/shard_map/ppermute | solution.py:449
  53.4 3.1 %shard_map.125 = (f32[3584,128]{1,0:T(8,128)S(1)}, bf16[3584,128]{1,0:T(8,128)(2,1)S(1)}) custom-call(s32[1]{0:T(128)} %bitcast.core, bf16[256,256]{1,0:T(8,128)(2,1)S(1)} %collective-permute-done.2.ahead, bf16[256,256]{1,0:T(8,128)(2,1)S(1)} %collective-permute-done.3.further, f32[2560,128]{1,0:T(8,128)S(1)} %get-tuple-element.46.grads, ...), custom_call_target="tpu_custom_call" | custom-call | flops 600000000 | bytes 2000000 | tf_op jit(solution)/shard_map/pallas_call | solution.py:56
  56.6 1.9 %collective-permute-start.4 = (bf16[3584,128]{1,0:T(8,128)(2,1)S(1)}, bf16[3584,128]{1,0:T(8,128)(2,1)S(1)}, u32[]{:S(2)}, u32[]{:S(2)}) collective-permute-start(bf16[3584,128]{1,0:T(8,128)(2,1)S(1)} %get-tuple-element.52), channel_id=1, source_target_pairs={{0,1},{1,0},{2,3},{3,2},{4,5},{5,4},{6,7},{7,6},{8,9},{9,8},{10,11... | collective-permute-start | bytes 2752520 | tf_op jit(solution)/shard_map/ppermute | solution.py:454
  58.5 2.4 %collective-permute-done.4.other = bf16[3584,128]{1,0:T(8,128)(2,1)S(1)} collective-permute-done((bf16[3584,128]{1,0:T(8,128)(2,1)S(1)}, bf16[3584,128]{1,0:T(8,128)(2,1)S(1)}, u32[]{:S(2)}, u32[]{:S(2)}) %collective-permute-start.4) | collective-permute-done | bytes 917536 | tf_op jit(solution)/shard_map/ppermute | solution.py:454
  60.9 0.2 shard_map.126
  61.1 20.6 %all_to_all.25.blocks = bf16[16,216,128]{2,1,0:T(8,128)(2,1)S(1)} all-to-all(bf16[16,216,128]{2,1,0:T(8,128)(2,1)S(1)} %bitcast.12), channel_id=1, replica_groups={{0,32,64,96,224,192,160,128,256,288,320,352,480,448,416,384},{1,33,65,9..., dimensions={0} | all-to-all | bytes 1769472 | tf_op jit(solution)/shard_map/all_to_all | solution.py:462
  81.7 0.1 shard_map.127
  81.8 15.5 %all_to_all.26.received = bf16[16,32,128]{2,1,0:T(8,128)(2,1)S(1)} all-to-all(bf16[16,32,128]{2,1,0:T(8,128)(2,1)S(1)} %shard_map.127), channel_id=1, replica_groups={{0,2,4,6,8,10,12,14,16,18,20,22,24,26,28,30},{1,3,5,7,9,11,13,15,17,19,..., dimensions={0} | all-to-all | bytes 262144 | tf_op jit(solution)/shard_map/all_to_all | solution.py:474
  97.4 16.7 %all_to_all.27.pieces = bf16[16,16,128]{2,1,0:T(8,128)(2,1)S(1)} all-to-all(bf16[16,16,128]{2,1,0:T(8,128)(2,1)S(1)} %shard_map.129), channel_id=1, replica_groups={{0,2,4,6,8,10,12,14,16,18,20,22,24,26,28,30},{1,3,5,7,9,11,13,15,17,19,..., dimensions={0} | all-to-all | bytes 131072 | tf_op jit(solution)/shard_map/all_to_all | solution.py:474
  114.1 0.1 shard_map.130
  114.2 15.5 %all_to_all.28 = bf16[16,216,128]{2,1,0:T(8,128)(2,1)S(1)} all-to-all(bf16[16,216,128]{2,1,0:T(8,128)(2,1)S(1)} %shard_map.130), channel_id=1, replica_groups={{0,32,64,96,224,192,160,128,256,288,320,352,480,448,416,384},{1,33,65,9..., dimensions={0} | all-to-all | bytes 1769472 | tf_op jit(solution)/shard_map/all_to_all | solution.py:462
  129.7 6.4 %collective-permute-start.5 = (bf16[3456,128]{1,0:T(8,128)(2,1)S(1)}, bf16[3456,128]{1,0:T(8,128)(2,1)S(1)}, u32[]{:S(2)}, u32[]{:S(2)}) collective-permute-start(bf16[3456,128]{1,0:T(8,128)(2,1)S(1)} %bitcast.10), channel_id=1, source_target_pairs={{0,1},{1,0},{2,3},{3,2},{4,5},{5,4},{6,7},{7,6},{8,9},{9,8},{10,11... | collective-permute-start | bytes 2654216 | tf_op jit(solution)/shard_map/ppermute | solution.py:454
  136.1 0.2 shard_map.128
  136.3 0.7 reshape.45
  137.0 1.1 collective-permute-done.5.other
  138.1 1.4 %shard_map.131 = (bf16[1152,128]{1,0:T(8,128)(2,1)}, bf16[384,128]{1,0:T(8,128)(2,1)}, bf16[1152,256]{1,0:T(8,128)(2,1)}, bf16[768,256]{1,0:T(8,128)(2,1)}, bf16[768,256]{1,0:T(8,128)(2,1)}) custom-call(s32[1]{0:T(128)} %bitcast.core, bf16[3456,128]{1,0:T(8,128)(2,1)S(1)} %bitcast.11, bf16[3456,128]{1,0:T(8,128)(2,1)S(1)} %collective-permute-done.5.other), custom_call_target="tpu_custom_call" | custom-call | flops 1000 | bytes 8000000 | tf_op jit(solution)/shard_map/pallas_call | solution.py:56
  (4 shorter events, 0.0 us)
Async XLA Ops:
  0.6 9.8 %collective-permute-start = (bf16[1024,128]{1,0:T(8,128)(2,1)}, bf16[1024,128]{1,0:T(8,128)(2,1)S(1)}, u32[]{:S(2)}, u32[]{:S(2)}) collective-permute-start(bf16[1024,128]{1,0:T(8,128)(2,1)} %bitcast.13), channel_id=1, source_target_pairs={{0,1},{1,2},{2,3},{3,4},{4,5},{5,6},{6,7},{7,8},{8,9},{9,10},{10,1... | collective-permute-start | bytes 786440 | tf_op jit(solution)/shard_map/ppermute | solution.py:449
  11.3 31.9 %all-to-all-start = ((bf16[32,16,128]{2,1,0:T(8,128)(2,1)}), bf16[32,16,128]{2,1,0:T(8,128)(2,1)S(1)}, u32[]{:S(2)}, u32[]{:S(2)}) async-start(bf16[32,16,128]{2,1,0:T(8,128)(2,1)} %shard_map.118), calls=%async_computation | async-start | bytes 262144 | tf_op jit(solution)/shard_map/all_to_all | solution.py:468
  29.5 13.8 %collective-permute-start.1 = (bf16[2,128,256]{2,1,0:T(8,128)(2,1)S(1)}, bf16[2,128,256]{2,1,0:T(8,128)(2,1)S(1)}, u32[]{:S(2)}, u32[]{:S(2)}) collective-permute-start(bf16[2,128,256]{2,1,0:T(8,128)(2,1)S(1)} %get-tuple-element.36), channel_id=1, source_target_pairs={{0,1},{1,2},{2,3},{3,4},{4,5},{5,6},{6,7},{7,8},{8,9},{9,10},{10,1... | collective-permute-start | bytes 393224 | tf_op jit(solution)/shard_map/ppermute | solution.py:449
  43.6 6.5 %collective-permute-start.3 = (bf16[256,256]{1,0:T(8,128)(2,1)S(1)}, bf16[256,256]{1,0:T(8,128)(2,1)S(1)}, u32[]{:S(2)}, u32[]{:S(2)}) collective-permute-start(bf16[256,256]{1,0:T(8,128)(2,1)S(1)} %get-tuple-element.42.sent), channel_id=1, source_target_pairs={{2,0},{3,1},{4,2},{5,3},{6,4},{7,5},{8,6},{9,7},{10,8},{11,9},{12,... | collective-permute-start | bytes 393224 | tf_op jit(solution)/shard_map/ppermute | solution.py:449
  44.9 8.6 %collective-permute-start.2 = (bf16[256,256]{1,0:T(8,128)(2,1)S(1)}, bf16[256,256]{1,0:T(8,128)(2,1)S(1)}, u32[]{:S(2)}, u32[]{:S(2)}) collective-permute-start(bf16[256,256]{1,0:T(8,128)(2,1)S(1)} %get-tuple-element.42.sent), channel_id=1, source_target_pairs={{1,0},{2,1},{3,2},{4,3},{5,4},{6,5},{7,6},{8,7},{9,8},{10,9},{11,1... | collective-permute-start | bytes 393224 | tf_op jit(solution)/shard_map/ppermute | solution.py:449
  56.6 4.4 %collective-permute-start.4 = (bf16[3584,128]{1,0:T(8,128)(2,1)S(1)}, bf16[3584,128]{1,0:T(8,128)(2,1)S(1)}, u32[]{:S(2)}, u32[]{:S(2)}) collective-permute-start(bf16[3584,128]{1,0:T(8,128)(2,1)S(1)} %get-tuple-element.52), channel_id=1, source_target_pairs={{0,1},{1,0},{2,3},{3,2},{4,5},{5,4},{6,7},{7,6},{8,9},{9,8},{10,11... | collective-permute-start | bytes 2752520 | tf_op jit(solution)/shard_map/ppermute | solution.py:454
  97.3 38.8 %copy-start = (bf16[3,256,256]{2,1,0:T(8,128)(2,1)S(1)}, bf16[3,256,256]{2,1,0:T(8,128)(2,1)}, u32[]{:S(2)}) copy-start(bf16[3,256,256]{2,1,0:T(8,128)(2,1)} %last_time.1) | copy-start | bytes 1179652
  129.7 8.4 %collective-permute-start.5 = (bf16[3456,128]{1,0:T(8,128)(2,1)S(1)}, bf16[3456,128]{1,0:T(8,128)(2,1)S(1)}, u32[]{:S(2)}, u32[]{:S(2)}) collective-permute-start(bf16[3456,128]{1,0:T(8,128)(2,1)S(1)} %bitcast.10), channel_id=1, source_target_pairs={{0,1},{1,0},{2,3},{3,2},{4,5},{5,4},{6,7},{7,6},{8,9},{9,8},{10,11... | collective-permute-start | bytes 2654216 | tf_op jit(solution)/shard_map/ppermute | solution.py:454

commit v12 on v11

--- a/solution.py
+++ b/solution.py
@@ -135,7 +135,7 @@
 
 def first_body(
     acts, time_far, plane_far, down_far,
-    kept_out, strided_out, part_out, times_out,
+    kept_out, strided_out, times_out,
     first_time, down_plane, down_time, sems,
 ):
     loads = start(
@@ -169,8 +169,7 @@
             0, :, half * CH : (half + 1) * CH
         ]
     loads[2].wait()
-    part_out[...] = dot(strided[0], down_time[2])
-    times_out[...] = down_time[pl.ds(0, 2)]
+    times_out[...] = down_time[...]
 
 
 def rows_body(rows, last_far, sent_out, last_time, spread, padded, turned, sems):
@@ -236,8 +235,8 @@
         out[...] = jnp.concatenate(parts, axis=0).astype(BF16)
 
 
-def middle_body(prior, part, times, grad_lowered, cot, lowered_out, sent_out):
-    pre = dot(prior[0], times[0]) + dot(prior[1], times[1]) + part[...]
+def middle_body(prior, own, times, grad_lowered, cot, lowered_out, sent_out):
+    pre = dot(prior[0], times[0]) + dot(prior[1], times[1]) + dot(own[0], times[2])
     lowered_out[...] = (pre * jax.nn.sigmoid(pre)).astype(BF16)
     sent_out[pl.ds(0, DOWN), :] = (grad_lowered[...].astype(F32) * silu_slope(pre)).astype(BF16)
     sent_out[pl.ds(DOWN, DOWN), :] = cot[...]
@@ -509,16 +508,16 @@
         ],
         copies=2,
     )
+    sent, prior, acts = lax.optimization_barrier((sent, prior, acts))
+    received = exchange_seq(sent)
     (acts,) = call(
         prior_body,
         [(P_, prior), (P_, acts), (P_, both)],
         [(P_, (6, 2, CELLS, CH), BF16)],
         [((2 * CELLS, CH), F32), ((2 * CELLS, 12 * CH), BF16)],
     )
-    times = (P_, (2, WIDE, WIDE), BF16)
-    sent, acts = lax.optimization_barrier((sent, acts))
-    received = exchange_seq(sent)
-    kept, strided, part, near_times = call(
+    times = (P_, (3, WIDE, WIDE), BF16)
+    kept, strided, near_times = call(
         first_body,
         [
             (P_, acts), (H, first_time), (H, down_plane), (H, down_time),
@@ -526,7 +525,6 @@
         [
             (P_, (KEPT, CH), BF16),
             (P_, (2, DOWN, WIDE), BF16),
-            (P_, (DOWN, WIDE), F32),
             times,
         ],
         [
@@ -543,7 +541,7 @@
     )
     lowered, sent = call(
         middle_body,
-        [(P_, strided_prior), (P_, part), (P_, near_times), (P_, grad_lowered), (P_, cot)],
+        [(P_, strided_prior), (P_, strided), (P_, near_times), (P_, grad_lowered), (P_, cot)],
         [down, (P_, (2 * DOWN, WIDE), BF16)],
     )
     ahead = from_behind(sent, -1)

time: 140 us -> 140 us (level)
  no operation moved by 1% of the time
where the time goes in v12:
time: 140 us; the launch traced here: 139 us
  blocking collectives  69.2 us (49%)
  starting transfers between devices  37.7 us (27%)
  waiting for transfers between devices  16.4 us (12%)
  Pallas kernels  13.8 us (10%)
  local copies, waits for them, and re-layouts  1.53 us (1%)
    all_to_all x2, blocking collectives, exchange_clip(): lax.all_to_all(blocks, 'clip', split_axis=0, concat_axis=0, axis_index_gr...  36.1 us
    all_to_all x2, blocking collectives, exchange_chips(): lax.all_to_all(blocks, 'seq', split_axis=0, concat_axis=0, axis_index_gro...  33.1 us
    all_to_all x1, starting transfers between devices, exchange_seq(): lax.all_to_all(blocks, 'seq', split_axis=0, concat_axis=0, tiled=True)  16.1 us
    pallas_call x14, Pallas kernels, call(): pl.pallas_call(body, out_shape=[placed_output(*out) for out in outs], in_...  13.8 us
    ppermute x4, starting transfers between devices, from_behind(): return lax.ppermute(block, 'seq', route)  13.3 us
    all_to_all x1, waiting for transfers between devices, exchange_seq(): lax.all_to_all(blocks, 'seq', split_axis=0, concat_axis=0, tiled=True)  9.5 us
    ppermute x2, starting transfers between devices, swap_cores(): return lax.ppermute(block, 'seq', [(i, i ^ 1) for i in range(count)])  8.33 us
    ppermute x2, waiting for transfers between devices, swap_cores(): return lax.ppermute(block, 'seq', [(i, i ^ 1) for i in range(count)])  3.58 us
  transfers between devices with their start and end apart: 7, of which 4 were waited for; matrix products, arithmetic and copies ran while one was open for 1% of the time, Pallas kernels for 6%

profile of v12, /device:TPU:1, one launch (start us, length us, event | category | flops | bytes accessed | tf_op | source)
XLA Modules:
  0.0 139.4 jit_solution(8295034694306047387)
XLA Ops:
  0.6 4.9 %collective-permute-start = (bf16[1024,128]{1,0:T(8,128)(2,1)}, bf16[1024,128]{1,0:T(8,128)(2,1)S(1)}, u32[]{:S(2)}, u32[]{:S(2)}) collective-permute-start(bf16[1024,128]{1,0:T(8,128)(2,1)} %bitcast.13), channel_id=1, source_target_pairs={{0,1},{1,2},{2,3},{3,4},{4,5},{5,6},{6,7},{7,8},{8,9},{9,10},{10,1... | collective-permute-start | bytes 786440 | tf_op jit(solution)/shard_map/ppermute | solution.py:448
  5.6 2.0 %shard_map.119 = (bf16[4,2,256,128]{3,2,1,0:T(8,128)(2,1)S(1)}, f32[2,2,256,128]{3,2,1,0:T(8,128)S(1)}, bf16[1536,256]{1,0:T(8,128)(2,1)S(1)}) custom-call(bf16[1024,128]{1,0:T(8,128)(2,1)} %bitcast.14, bf16[3,3,128,128]{3,2,1,0:T(8,128)(2,1)} %plane_far.3), custom_call_target="tpu_custom_call" | custom-call | flops 1000 | bytes 8000000 | tf_op jit(solution)/shard_map/pallas_call | solution.py:56
  7.6 0.9 reshape_squeeze.3.rows
  8.5 2.0 %shard_map.118 = bf16[32,16,128]{2,1,0:T(8,128)(2,1)} custom-call(bf16[32,8,128]{2,1,0:T(8,128)(2,1)S(1)} %reshape_squeeze.3.rows, bf16[3,256,256]{2,1,0:T(8,128)(2,1)} %last_time.1), custom_call_target="tpu_custom_call" | custom-call | flops 1000 | bytes 8000000 | tf_op jit(solution)/shard_map/pallas_call | solution.py:56
  10.4 0.0 collective-permute-done.prior
  10.4 16.1 %all-to-all-start = ((bf16[32,16,128]{2,1,0:T(8,128)(2,1)}), bf16[32,16,128]{2,1,0:T(8,128)(2,1)S(1)}, u32[]{:S(2)}, u32[]{:S(2)}) async-start(bf16[32,16,128]{2,1,0:T(8,128)(2,1)} %shard_map.118), calls=%async_computation | async-start | bytes 262144 | tf_op jit(solution)/shard_map/all_to_all | solution.py:467
  26.5 0.8 shard_map.120.acts
  27.4 1.9 %shard_map.121 = (bf16[2560,128]{1,0:T(8,128)(2,1)S(1)}, bf16[2,128,256]{2,1,0:T(8,128)(2,1)S(1)}, bf16[3,256,256]{2,1,0:T(8,128)(2,1)S(1)}) custom-call(bf16[6,2,256,128]{3,2,1,0:T(8,128)(2,1)S(1)} %shard_map.120.acts, bf16[3,128,128]{2,1,0:T(8,128)(2,1)} %time_far.3, bf16[3,3,128,256]{3,2,1,0:T(8,128)(2,1)} %plane_far.5, bf16[3,256,256]{2,1,0:T(8,128)(2,1)} %down_far.3), custom_call_target="tpu_custom_call" | custom-call | flops 1000 | bytes 8000000 | tf_op jit(solution)/shard_map/pallas_call | solution.py:56
  29.3 3.5 %collective-permute-start.1 = (bf16[2,128,256]{2,1,0:T(8,128)(2,1)S(1)}, bf16[2,128,256]{2,1,0:T(8,128)(2,1)S(1)}, u32[]{:S(2)}, u32[]{:S(2)}) collective-permute-start(bf16[2,128,256]{2,1,0:T(8,128)(2,1)S(1)} %get-tuple-element.37.own), channel_id=1, source_target_pairs={{0,1},{1,2},{2,3},{3,4},{4,5},{5,6},{6,7},{7,8},{8,9},{9,10},{10,1... | collective-permute-start | bytes 393224 | tf_op jit(solution)/shard_map/ppermute | solution.py:448
  32.9 9.5 %all-to-all-done.received = bf16[32,16,128]{2,1,0:T(8,128)(2,1)S(1)} async-done(((bf16[32,16,128]{2,1,0:T(8,128)(2,1)}), bf16[32,16,128]{2,1,0:T(8,128)(2,1)S(1)}, u32[]{:S(2)}, u32[]{:S(2)}) %all-to-all-start) | async-done | bytes 131104 | tf_op jit(solution)/shard_map/all_to_all | solution.py:467
  42.4 0.1 shard_map.122
  42.5 0.3 shard_map.123
  42.7 1.3 collective-permute-start.3
  44.0 3.5 %collective-permute-start.2 = (bf16[256,256]{1,0:T(8,128)(2,1)S(1)}, bf16[256,256]{1,0:T(8,128)(2,1)S(1)}, u32[]{:S(2)}, u32[]{:S(2)}) collective-permute-start(bf16[256,256]{1,0:T(8,128)(2,1)S(1)} %get-tuple-element.42.sent), channel_id=1, source_target_pairs={{1,0},{2,1},{3,2},{4,3},{5,4},{6,5},{7,6},{8,7},{9,8},{10,9},{11,1... | collective-permute-start | bytes 393224 | tf_op jit(solution)/shard_map/ppermute | solution.py:448
  47.6 1.5 %shard_map.124 = (bf16[3,256,256]{2,1,0:T(8,128)(2,1)S(1)}, bf16[512,1024]{1,0:T(8,128)(2,1)S(1)}, f32[2560,128]{1,0:T(8,128)S(1)}, bf16[512,1536]{1,0:T(8,128)(2,1)S(1)}, f32[2,2,256,128]{3,2,1,0:T(8,128)S(1)}) custom-call(bf16[256,256]{1,0:T(8,128)(2,1)S(1)} %get-tuple-element.42.sent, bf16[128,256]{1,0:T(8,128)(2,1)S(1)} %get-tuple-element.43.lowered, ...), custom_call_target="tpu_custom_call" | custom-call | flops 1000 | bytes 8000000 | tf_op jit(solution)/shard_map/pallas_call | solution.py:56
  49.1 0.0 collective-permute-done.3.further
  49.1 3.4 %collective-permute-done.2.ahead = bf16[256,256]{1,0:T(8,128)(2,1)S(1)} collective-permute-done((bf16[256,256]{1,0:T(8,128)(2,1)S(1)}, bf16[256,256]{1,0:T(8,128)(2,1)S(1)}, u32[]{:S(2)}, u32[]{:S(2)}) %collective-permute-start.2) | collective-permute-done | bytes 131104 | tf_op jit(solution)/shard_map/ppermute | solution.py:448
  52.5 3.1 %shard_map.125 = (f32[3584,128]{1,0:T(8,128)S(1)}, bf16[3584,128]{1,0:T(8,128)(2,1)S(1)}) custom-call(s32[1]{0:T(128)} %bitcast.core, bf16[256,256]{1,0:T(8,128)(2,1)S(1)} %collective-permute-done.2.ahead, bf16[256,256]{1,0:T(8,128)(2,1)S(1)} %collective-permute-done.3.further, f32[2560,128]{1,0:T(8,128)S(1)} %get-tuple-element.46.grads, ...), custom_call_target="tpu_custom_call" | custom-call | flops 600000000 | bytes 2000000 | tf_op jit(solution)/shard_map/pallas_call | solution.py:56
  55.6 1.9 %collective-permute-start.4 = (bf16[3584,128]{1,0:T(8,128)(2,1)S(1)}, bf16[3584,128]{1,0:T(8,128)(2,1)S(1)}, u32[]{:S(2)}, u32[]{:S(2)}) collective-permute-start(bf16[3584,128]{1,0:T(8,128)(2,1)S(1)} %get-tuple-element.52), channel_id=1, source_target_pairs={{0,1},{1,0},{2,3},{3,2},{4,5},{5,4},{6,7},{7,6},{8,9},{9,8},{10,11... | collective-permute-start | bytes 2752520 | tf_op jit(solution)/shard_map/ppermute | solution.py:453
  57.5 2.4 %collective-permute-done.4.other = bf16[3584,128]{1,0:T(8,128)(2,1)S(1)} collective-permute-done((bf16[3584,128]{1,0:T(8,128)(2,1)S(1)}, bf16[3584,128]{1,0:T(8,128)(2,1)S(1)}, u32[]{:S(2)}, u32[]{:S(2)}) %collective-permute-start.4) | collective-permute-done | bytes 917536 | tf_op jit(solution)/shard_map/ppermute | solution.py:453
  59.9 0.2 shard_map.126
  60.1 20.6 %all_to_all.25.blocks = bf16[16,216,128]{2,1,0:T(8,128)(2,1)S(1)} all-to-all(bf16[16,216,128]{2,1,0:T(8,128)(2,1)S(1)} %bitcast.12), channel_id=1, replica_groups={{0,32,64,96,224,192,160,128,256,288,320,352,480,448,416,384},{1,33,65,9..., dimensions={0} | all-to-all | bytes 1769472 | tf_op jit(solution)/shard_map/all_to_all | solution.py:461
  80.7 0.1 shard_map.127
  80.8 16.4 %all_to_all.26.received = bf16[16,32,128]{2,1,0:T(8,128)(2,1)S(1)} all-to-all(bf16[16,32,128]{2,1,0:T(8,128)(2,1)S(1)} %shard_map.127), channel_id=1, replica_groups={{0,2,4,6,8,10,12,14,16,18,20,22,24,26,28,30},{1,3,5,7,9,11,13,15,17,19,..., dimensions={0} | all-to-all | bytes 262144 | tf_op jit(solution)/shard_map/all_to_all | solution.py:473
  97.2 16.7 %all_to_all.27.pieces = bf16[16,16,128]{2,1,0:T(8,128)(2,1)S(1)} all-to-all(bf16[16,16,128]{2,1,0:T(8,128)(2,1)S(1)} %shard_map.129), channel_id=1, replica_groups={{0,2,4,6,8,10,12,14,16,18,20,22,24,26,28,30},{1,3,5,7,9,11,13,15,17,19,..., dimensions={0} | all-to-all | bytes 131072 | tf_op jit(solution)/shard_map/all_to_all | solution.py:473
  113.9 0.1 shard_map.130
  114.1 15.5 %all_to_all.28 = bf16[16,216,128]{2,1,0:T(8,128)(2,1)S(1)} all-to-all(bf16[16,216,128]{2,1,0:T(8,128)(2,1)S(1)} %shard_map.130), channel_id=1, replica_groups={{0,32,64,96,224,192,160,128,256,288,320,352,480,448,416,384},{1,33,65,9..., dimensions={0} | all-to-all | bytes 1769472 | tf_op jit(solution)/shard_map/all_to_all | solution.py:461
  129.5 6.4 %collective-permute-start.5 = (bf16[3456,128]{1,0:T(8,128)(2,1)S(1)}, bf16[3456,128]{1,0:T(8,128)(2,1)S(1)}, u32[]{:S(2)}, u32[]{:S(2)}) collective-permute-start(bf16[3456,128]{1,0:T(8,128)(2,1)S(1)} %bitcast.10), channel_id=1, source_target_pairs={{0,1},{1,0},{2,3},{3,2},{4,5},{5,4},{6,7},{7,6},{8,9},{9,8},{10,11... | collective-permute-start | bytes 2654216 | tf_op jit(solution)/shard_map/ppermute | solution.py:453
  136.0 0.2 shard_map.128
  136.2 0.7 reshape.45
  136.8 1.1 collective-permute-done.5.other
  138.0 1.4 %shard_map.131 = (bf16[1152,128]{1,0:T(8,128)(2,1)}, bf16[384,128]{1,0:T(8,128)(2,1)}, bf16[1152,256]{1,0:T(8,128)(2,1)}, bf16[768,256]{1,0:T(8,128)(2,1)}, bf16[768,256]{1,0:T(8,128)(2,1)}) custom-call(s32[1]{0:T(128)} %bitcast.core, bf16[3456,128]{1,0:T(8,128)(2,1)S(1)} %bitcast.11, bf16[3456,128]{1,0:T(8,128)(2,1)S(1)} %collective-permute-done.5.other), custom_call_target="tpu_custom_call" | custom-call | flops 1000 | bytes 8000000 | tf_op jit(solution)/shard_map/pallas_call | solution.py:56
  (4 shorter events, 0.0 us)
Async XLA Ops:
  0.6 9.8 %collective-permute-start = (bf16[1024,128]{1,0:T(8,128)(2,1)}, bf16[1024,128]{1,0:T(8,128)(2,1)S(1)}, u32[]{:S(2)}, u32[]{:S(2)}) collective-permute-start(bf16[1024,128]{1,0:T(8,128)(2,1)} %bitcast.13), channel_id=1, source_target_pairs={{0,1},{1,2},{2,3},{3,4},{4,5},{5,6},{6,7},{7,8},{8,9},{9,10},{10,1... | collective-permute-start | bytes 786440 | tf_op jit(solution)/shard_map/ppermute | solution.py:448
  10.4 31.9 %all-to-all-start = ((bf16[32,16,128]{2,1,0:T(8,128)(2,1)}), bf16[32,16,128]{2,1,0:T(8,128)(2,1)S(1)}, u32[]{:S(2)}, u32[]{:S(2)}) async-start(bf16[32,16,128]{2,1,0:T(8,128)(2,1)} %shard_map.118), calls=%async_computation | async-start | bytes 262144 | tf_op jit(solution)/shard_map/all_to_all | solution.py:467
  29.3 13.2 %collective-permute-start.1 = (bf16[2,128,256]{2,1,0:T(8,128)(2,1)S(1)}, bf16[2,128,256]{2,1,0:T(8,128)(2,1)S(1)}, u32[]{:S(2)}, u32[]{:S(2)}) collective-permute-start(bf16[2,128,256]{2,1,0:T(8,128)(2,1)S(1)} %get-tuple-element.37.own), channel_id=1, source_target_pairs={{0,1},{1,2},{2,3},{3,4},{4,5},{5,6},{6,7},{7,8},{8,9},{9,10},{10,1... | collective-permute-start | bytes 393224 | tf_op jit(solution)/shard_map/ppermute | solution.py:448
  42.7 6.3 %collective-permute-start.3 = (bf16[256,256]{1,0:T(8,128)(2,1)S(1)}, bf16[256,256]{1,0:T(8,128)(2,1)S(1)}, u32[]{:S(2)}, u32[]{:S(2)}) collective-permute-start(bf16[256,256]{1,0:T(8,128)(2,1)S(1)} %get-tuple-element.42.sent), channel_id=1, source_target_pairs={{2,0},{3,1},{4,2},{5,3},{6,4},{7,5},{8,6},{9,7},{10,8},{11,9},{12,... | collective-permute-start | bytes 393224 | tf_op jit(solution)/shard_map/ppermute | solution.py:448
  44.0 8.4 %collective-permute-start.2 = (bf16[256,256]{1,0:T(8,128)(2,1)S(1)}, bf16[256,256]{1,0:T(8,128)(2,1)S(1)}, u32[]{:S(2)}, u32[]{:S(2)}) collective-permute-start(bf16[256,256]{1,0:T(8,128)(2,1)S(1)} %get-tuple-element.42.sent), channel_id=1, source_target_pairs={{1,0},{2,1},{3,2},{4,3},{5,4},{6,5},{7,6},{8,7},{9,8},{10,9},{11,1... | collective-permute-start | bytes 393224 | tf_op jit(solution)/shard_map/ppermute | solution.py:448
  55.6 4.4 %collective-permute-start.4 = (bf16[3584,128]{1,0:T(8,128)(2,1)S(1)}, bf16[3584,128]{1,0:T(8,128)(2,1)S(1)}, u32[]{:S(2)}, u32[]{:S(2)}) collective-permute-start(bf16[3584,128]{1,0:T(8,128)(2,1)S(1)} %get-tuple-element.52), channel_id=1, source_target_pairs={{0,1},{1,0},{2,3},{3,2},{4,5},{5,4},{6,7},{7,6},{8,9},{9,8},{10,11... | collective-permute-start | bytes 2752520 | tf_op jit(solution)/shard_map/ppermute | solution.py:453
  97.2 38.8 %copy-start = (bf16[3,256,256]{2,1,0:T(8,128)(2,1)S(1)}, bf16[3,256,256]{2,1,0:T(8,128)(2,1)}, u32[]{:S(2)}) copy-start(bf16[3,256,256]{2,1,0:T(8,128)(2,1)} %last_time.1) | copy-start | bytes 1179652
  129.5 8.4 %collective-permute-start.5 = (bf16[3456,128]{1,0:T(8,128)(2,1)S(1)}, bf16[3456,128]{1,0:T(8,128)(2,1)S(1)}, u32[]{:S(2)}, u32[]{:S(2)}) collective-permute-start(bf16[3456,128]{1,0:T(8,128)(2,1)S(1)} %bitcast.10), channel_id=1, source_target_pairs={{0,1},{1,0},{2,3},{3,2},{4,5},{5,4},{6,7},{7,6},{8,9},{9,8},{10,11... | collective-permute-start | bytes 2654216 | tf_op jit(solution)/shard_map/ppermute | solution.py:453

commit v13 on v12

--- a/solution.py
+++ b/solution.py
@@ -456,8 +456,7 @@
 def exchange_clip(blocks):
     count = lax.axis_size("clip")
     side = round(count**0.5)
-    rows = [list(range(first, first + side)) for first in range(0, count, side)]
-    path = [clip for at, row in enumerate(rows) for clip in (row if at % 2 == 0 else row[::-1])]
+    path = [row * side + (row + shift) % side for shift in range(side) for row in range(side)]
     return lax.all_to_all(
         blocks, "clip", split_axis=0, concat_axis=0, axis_index_groups=[path], tiled=True
     )

time: 140 us -> 140 us (level)
  no operation moved by 1% of the time
where the time goes in v13:
time: 140 us; the launch traced here: 139 us
  blocking collectives  68.9 us (49%)
  starting transfers between devices  37.7 us (27%)
  waiting for transfers between devices  16.4 us (12%)
  Pallas kernels  13.8 us (10%)
  local copies, waits for them, and re-layouts  1.53 us (1%)
    all_to_all x2, blocking collectives, exchange_clip(): lax.all_to_all(blocks, 'clip', split_axis=0, concat_axis=0, axis_index_gr...  35.4 us
    all_to_all x2, blocking collectives, exchange_chips(): lax.all_to_all(blocks, 'seq', split_axis=0, concat_axis=0, axis_index_gro...  33.5 us
    all_to_all x1, starting transfers between devices, exchange_seq(): lax.all_to_all(blocks, 'seq', split_axis=0, concat_axis=0, tiled=True)  16.1 us
    pallas_call x14, Pallas kernels, call(): pl.pallas_call(body, out_shape=[placed_output(*out) for out in outs], in_...  13.8 us
    ppermute x4, starting transfers between devices, from_behind(): return lax.ppermute(block, 'seq', route)  13.3 us
    all_to_all x1, waiting for transfers between devices, exchange_seq(): lax.all_to_all(blocks, 'seq', split_axis=0, concat_axis=0, tiled=True)  9.5 us
    ppermute x2, starting transfers between devices, swap_cores(): return lax.ppermute(block, 'seq', [(i, i ^ 1) for i in range(count)])  8.36 us
    ppermute x2, waiting for transfers between devices, swap_cores(): return lax.ppermute(block, 'seq', [(i, i ^ 1) for i in range(count)])  3.58 us
  transfers between devices with their start and end apart: 7, of which 4 were waited for; matrix products, arithmetic and copies ran while one was open for 1% of the time, Pallas kernels for 6%

profile of v13, /device:TPU:1, one launch (start us, length us, event | category | flops | bytes accessed | tf_op | source)
XLA Modules:
  0.0 139.2 jit_solution(6654031211224019320)
XLA Ops:
  0.6 4.9 %collective-permute-start = (bf16[1024,128]{1,0:T(8,128)(2,1)}, bf16[1024,128]{1,0:T(8,128)(2,1)S(1)}, u32[]{:S(2)}, u32[]{:S(2)}) collective-permute-start(bf16[1024,128]{1,0:T(8,128)(2,1)} %bitcast.13), channel_id=1, source_target_pairs={{0,1},{1,2},{2,3},{3,4},{4,5},{5,6},{6,7},{7,8},{8,9},{9,10},{10,1... | collective-permute-start | bytes 786440 | tf_op jit(solution)/shard_map/ppermute | solution.py:448
  5.6 2.0 %shard_map.119 = (bf16[4,2,256,128]{3,2,1,0:T(8,128)(2,1)S(1)}, f32[2,2,256,128]{3,2,1,0:T(8,128)S(1)}, bf16[1536,256]{1,0:T(8,128)(2,1)S(1)}) custom-call(bf16[1024,128]{1,0:T(8,128)(2,1)} %bitcast.14, bf16[3,3,128,128]{3,2,1,0:T(8,128)(2,1)} %plane_far.3), custom_call_target="tpu_custom_call" | custom-call | flops 1000 | bytes 8000000 | tf_op jit(solution)/shard_map/pallas_call | solution.py:56
  7.6 0.9 reshape_squeeze.3.rows
  8.5 2.0 %shard_map.118 = bf16[32,16,128]{2,1,0:T(8,128)(2,1)} custom-call(bf16[32,8,128]{2,1,0:T(8,128)(2,1)S(1)} %reshape_squeeze.3.rows, bf16[3,256,256]{2,1,0:T(8,128)(2,1)} %last_time.1), custom_call_target="tpu_custom_call" | custom-call | flops 1000 | bytes 8000000 | tf_op jit(solution)/shard_map/pallas_call | solution.py:56
  10.4 0.0 collective-permute-done.prior
  10.4 16.1 %all-to-all-start = ((bf16[32,16,128]{2,1,0:T(8,128)(2,1)}), bf16[32,16,128]{2,1,0:T(8,128)(2,1)S(1)}, u32[]{:S(2)}, u32[]{:S(2)}) async-start(bf16[32,16,128]{2,1,0:T(8,128)(2,1)} %shard_map.118), calls=%async_computation | async-start | bytes 262144 | tf_op jit(solution)/shard_map/all_to_all | solution.py:466
  26.5 0.8 shard_map.120.acts
  27.4 1.9 %shard_map.121 = (bf16[2560,128]{1,0:T(8,128)(2,1)S(1)}, bf16[2,128,256]{2,1,0:T(8,128)(2,1)S(1)}, bf16[3,256,256]{2,1,0:T(8,128)(2,1)S(1)}) custom-call(bf16[6,2,256,128]{3,2,1,0:T(8,128)(2,1)S(1)} %shard_map.120.acts, bf16[3,128,128]{2,1,0:T(8,128)(2,1)} %time_far.3, bf16[3,3,128,256]{3,2,1,0:T(8,128)(2,1)} %plane_far.5, bf16[3,256,256]{2,1,0:T(8,128)(2,1)} %down_far.3), custom_call_target="tpu_custom_call" | custom-call | flops 1000 | bytes 8000000 | tf_op jit(solution)/shard_map/pallas_call | solution.py:56
  29.3 3.5 %collective-permute-start.1 = (bf16[2,128,256]{2,1,0:T(8,128)(2,1)S(1)}, bf16[2,128,256]{2,1,0:T(8,128)(2,1)S(1)}, u32[]{:S(2)}, u32[]{:S(2)}) collective-permute-start(bf16[2,128,256]{2,1,0:T(8,128)(2,1)S(1)} %get-tuple-element.37.own), channel_id=1, source_target_pairs={{0,1},{1,2},{2,3},{3,4},{4,5},{5,6},{6,7},{7,8},{8,9},{9,10},{10,1... | collective-permute-start | bytes 393224 | tf_op jit(solution)/shard_map/ppermute | solution.py:448
  32.9 9.5 %all-to-all-done.received = bf16[32,16,128]{2,1,0:T(8,128)(2,1)S(1)} async-done(((bf16[32,16,128]{2,1,0:T(8,128)(2,1)}), bf16[32,16,128]{2,1,0:T(8,128)(2,1)S(1)}, u32[]{:S(2)}, u32[]{:S(2)}) %all-to-all-start) | async-done | bytes 131104 | tf_op jit(solution)/shard_map/all_to_all | solution.py:466
  42.4 0.1 shard_map.122
  42.5 0.3 shard_map.123
  42.7 1.3 collective-permute-start.3
  44.0 3.5 %collective-permute-start.2 = (bf16[256,256]{1,0:T(8,128)(2,1)S(1)}, bf16[256,256]{1,0:T(8,128)(2,1)S(1)}, u32[]{:S(2)}, u32[]{:S(2)}) collective-permute-start(bf16[256,256]{1,0:T(8,128)(2,1)S(1)} %get-tuple-element.42.sent), channel_id=1, source_target_pairs={{1,0},{2,1},{3,2},{4,3},{5,4},{6,5},{7,6},{8,7},{9,8},{10,9},{11,1... | collective-permute-start | bytes 393224 | tf_op jit(solution)/shard_map/ppermute | solution.py:448
  47.6 1.5 %shard_map.124 = (bf16[3,256,256]{2,1,0:T(8,128)(2,1)S(1)}, bf16[512,1024]{1,0:T(8,128)(2,1)S(1)}, f32[2560,128]{1,0:T(8,128)S(1)}, bf16[512,1536]{1,0:T(8,128)(2,1)S(1)}, f32[2,2,256,128]{3,2,1,0:T(8,128)S(1)}) custom-call(bf16[256,256]{1,0:T(8,128)(2,1)S(1)} %get-tuple-element.42.sent, bf16[128,256]{1,0:T(8,128)(2,1)S(1)} %get-tuple-element.43.lowered, ...), custom_call_target="tpu_custom_call" | custom-call | flops 1000 | bytes 8000000 | tf_op jit(solution)/shard_map/pallas_call | solution.py:56
  49.1 0.0 collective-permute-done.3.further
  49.1 3.4 %collective-permute-done.2.ahead = bf16[256,256]{1,0:T(8,128)(2,1)S(1)} collective-permute-done((bf16[256,256]{1,0:T(8,128)(2,1)S(1)}, bf16[256,256]{1,0:T(8,128)(2,1)S(1)}, u32[]{:S(2)}, u32[]{:S(2)}) %collective-permute-start.2) | collective-permute-done | bytes 131104 | tf_op jit(solution)/shard_map/ppermute | solution.py:448
  52.5 3.1 %shard_map.125 = (f32[3584,128]{1,0:T(8,128)S(1)}, bf16[3584,128]{1,0:T(8,128)(2,1)S(1)}) custom-call(s32[1]{0:T(128)} %bitcast.core, bf16[256,256]{1,0:T(8,128)(2,1)S(1)} %collective-permute-done.2.ahead, bf16[256,256]{1,0:T(8,128)(2,1)S(1)} %collective-permute-done.3.further, f32[2560,128]{1,0:T(8,128)S(1)} %get-tuple-element.46.grads, ...), custom_call_target="tpu_custom_call" | custom-call | flops 600000000 | bytes 2000000 | tf_op jit(solution)/shard_map/pallas_call | solution.py:56
  55.6 1.9 %collective-permute-start.4 = (bf16[3584,128]{1,0:T(8,128)(2,1)S(1)}, bf16[3584,128]{1,0:T(8,128)(2,1)S(1)}, u32[]{:S(2)}, u32[]{:S(2)}) collective-permute-start(bf16[3584,128]{1,0:T(8,128)(2,1)S(1)} %get-tuple-element.52), channel_id=1, source_target_pairs={{0,1},{1,0},{2,3},{3,2},{4,5},{5,4},{6,7},{7,6},{8,9},{9,8},{10,11... | collective-permute-start | bytes 2752520 | tf_op jit(solution)/shard_map/ppermute | solution.py:453
  57.5 2.4 %collective-permute-done.4.other = bf16[3584,128]{1,0:T(8,128)(2,1)S(1)} collective-permute-done((bf16[3584,128]{1,0:T(8,128)(2,1)S(1)}, bf16[3584,128]{1,0:T(8,128)(2,1)S(1)}, u32[]{:S(2)}, u32[]{:S(2)}) %collective-permute-start.4) | collective-permute-done | bytes 917536 | tf_op jit(solution)/shard_map/ppermute | solution.py:453
  59.9 0.2 shard_map.126
  60.1 21.3 %all_to_all.25.blocks = bf16[16,216,128]{2,1,0:T(8,128)(2,1)S(1)} all-to-all(bf16[16,216,128]{2,1,0:T(8,128)(2,1)S(1)} %bitcast.12), channel_id=1, replica_groups={{0,160,320,480,32,192,352,384,64,224,256,416,96,128,288,448},{1,161,321..., dimensions={0} | all-to-all | bytes 1769472 | tf_op jit(solution)/shard_map/all_to_all | solution.py:460
  81.4 0.1 shard_map.127
  81.5 16.3 %all_to_all.26.received = bf16[16,32,128]{2,1,0:T(8,128)(2,1)S(1)} all-to-all(bf16[16,32,128]{2,1,0:T(8,128)(2,1)S(1)} %shard_map.127), channel_id=1, replica_groups={{0,2,4,6,8,10,12,14,16,18,20,22,24,26,28,30},{1,3,5,7,9,11,13,15,17,19,..., dimensions={0} | all-to-all | bytes 262144 | tf_op jit(solution)/shard_map/all_to_all | solution.py:472
  97.9 17.2 %all_to_all.27.pieces = bf16[16,16,128]{2,1,0:T(8,128)(2,1)S(1)} all-to-all(bf16[16,16,128]{2,1,0:T(8,128)(2,1)S(1)} %shard_map.129), channel_id=1, replica_groups={{0,2,4,6,8,10,12,14,16,18,20,22,24,26,28,30},{1,3,5,7,9,11,13,15,17,19,..., dimensions={0} | all-to-all | bytes 131072 | tf_op jit(solution)/shard_map/all_to_all | solution.py:472
  115.1 0.1 shard_map.130
  115.2 14.1 %all_to_all.28 = bf16[16,216,128]{2,1,0:T(8,128)(2,1)S(1)} all-to-all(bf16[16,216,128]{2,1,0:T(8,128)(2,1)S(1)} %shard_map.130), channel_id=1, replica_groups={{0,160,320,480,32,192,352,384,64,224,256,416,96,128,288,448},{1,161,321..., dimensions={0} | all-to-all | bytes 1769472 | tf_op jit(solution)/shard_map/all_to_all | solution.py:460
  129.3 6.4 %collective-permute-start.5 = (bf16[3456,128]{1,0:T(8,128)(2,1)S(1)}, bf16[3456,128]{1,0:T(8,128)(2,1)S(1)}, u32[]{:S(2)}, u32[]{:S(2)}) collective-permute-start(bf16[3456,128]{1,0:T(8,128)(2,1)S(1)} %bitcast.10), channel_id=1, source_target_pairs={{0,1},{1,0},{2,3},{3,2},{4,5},{5,4},{6,7},{7,6},{8,9},{9,8},{10,11... | collective-permute-start | bytes 2654216 | tf_op jit(solution)/shard_map/ppermute | solution.py:453
  135.7 0.2 shard_map.128
  136.0 0.7 reshape.45
  136.6 1.1 collective-permute-done.5.other
  137.7 1.4 %shard_map.131 = (bf16[1152,128]{1,0:T(8,128)(2,1)}, bf16[384,128]{1,0:T(8,128)(2,1)}, bf16[1152,256]{1,0:T(8,128)(2,1)}, bf16[768,256]{1,0:T(8,128)(2,1)}, bf16[768,256]{1,0:T(8,128)(2,1)}) custom-call(s32[1]{0:T(128)} %bitcast.core, bf16[3456,128]{1,0:T(8,128)(2,1)S(1)} %bitcast.11, bf16[3456,128]{1,0:T(8,128)(2,1)S(1)} %collective-permute-done.5.other), custom_call_target="tpu_custom_call" | custom-call | flops 1000 | bytes 8000000 | tf_op jit(solution)/shard_map/pallas_call | solution.py:56
  (4 shorter events, 0.0 us)
Async XLA Ops:
  0.6 9.8 %collective-permute-start = (bf16[1024,128]{1,0:T(8,128)(2,1)}, bf16[1024,128]{1,0:T(8,128)(2,1)S(1)}, u32[]{:S(2)}, u32[]{:S(2)}) collective-permute-start(bf16[1024,128]{1,0:T(8,128)(2,1)} %bitcast.13), channel_id=1, source_target_pairs={{0,1},{1,2},{2,3},{3,4},{4,5},{5,6},{6,7},{7,8},{8,9},{9,10},{10,1... | collective-permute-start | bytes 786440 | tf_op jit(solution)/shard_map/ppermute | solution.py:448
  10.4 31.9 %all-to-all-start = ((bf16[32,16,128]{2,1,0:T(8,128)(2,1)}), bf16[32,16,128]{2,1,0:T(8,128)(2,1)S(1)}, u32[]{:S(2)}, u32[]{:S(2)}) async-start(bf16[32,16,128]{2,1,0:T(8,128)(2,1)} %shard_map.118), calls=%async_computation | async-start | bytes 262144 | tf_op jit(solution)/shard_map/all_to_all | solution.py:466
  29.3 13.2 %collective-permute-start.1 = (bf16[2,128,256]{2,1,0:T(8,128)(2,1)S(1)}, bf16[2,128,256]{2,1,0:T(8,128)(2,1)S(1)}, u32[]{:S(2)}, u32[]{:S(2)}) collective-permute-start(bf16[2,128,256]{2,1,0:T(8,128)(2,1)S(1)} %get-tuple-element.37.own), channel_id=1, source_target_pairs={{0,1},{1,2},{2,3},{3,4},{4,5},{5,6},{6,7},{7,8},{8,9},{9,10},{10,1... | collective-permute-start | bytes 393224 | tf_op jit(solution)/shard_map/ppermute | solution.py:448
  42.7 6.3 %collective-permute-start.3 = (bf16[256,256]{1,0:T(8,128)(2,1)S(1)}, bf16[256,256]{1,0:T(8,128)(2,1)S(1)}, u32[]{:S(2)}, u32[]{:S(2)}) collective-permute-start(bf16[256,256]{1,0:T(8,128)(2,1)S(1)} %get-tuple-element.42.sent), channel_id=1, source_target_pairs={{2,0},{3,1},{4,2},{5,3},{6,4},{7,5},{8,6},{9,7},{10,8},{11,9},{12,... | collective-permute-start | bytes 393224 | tf_op jit(solution)/shard_map/ppermute | solution.py:448
  44.0 8.4 %collective-permute-start.2 = (bf16[256,256]{1,0:T(8,128)(2,1)S(1)}, bf16[256,256]{1,0:T(8,128)(2,1)S(1)}, u32[]{:S(2)}, u32[]{:S(2)}) collective-permute-start(bf16[256,256]{1,0:T(8,128)(2,1)S(1)} %get-tuple-element.42.sent), channel_id=1, source_target_pairs={{1,0},{2,1},{3,2},{4,3},{5,4},{6,5},{7,6},{8,7},{9,8},{10,9},{11,1... | collective-permute-start | bytes 393224 | tf_op jit(solution)/shard_map/ppermute | solution.py:448
  55.6 4.4 %collective-permute-start.4 = (bf16[3584,128]{1,0:T(8,128)(2,1)S(1)}, bf16[3584,128]{1,0:T(8,128)(2,1)S(1)}, u32[]{:S(2)}, u32[]{:S(2)}) collective-permute-start(bf16[3584,128]{1,0:T(8,128)(2,1)S(1)} %get-tuple-element.52), channel_id=1, source_target_pairs={{0,1},{1,0},{2,3},{3,2},{4,5},{5,4},{6,7},{7,6},{8,9},{9,8},{10,11... | collective-permute-start | bytes 2752520 | tf_op jit(solution)/shard_map/ppermute | solution.py:453
  97.9 37.8 %copy-start = (bf16[3,256,256]{2,1,0:T(8,128)(2,1)S(1)}, bf16[3,256,256]{2,1,0:T(8,128)(2,1)}, u32[]{:S(2)}) copy-start(bf16[3,256,256]{2,1,0:T(8,128)(2,1)} %last_time.1) | copy-start | bytes 1179652
  129.3 8.5 %collective-permute-start.5 = (bf16[3456,128]{1,0:T(8,128)(2,1)S(1)}, bf16[3456,128]{1,0:T(8,128)(2,1)S(1)}, u32[]{:S(2)}, u32[]{:S(2)}) collective-permute-start(bf16[3456,128]{1,0:T(8,128)(2,1)S(1)} %bitcast.10), channel_id=1, source_target_pairs={{0,1},{1,0},{2,3},{3,2},{4,5},{5,4},{6,7},{7,6},{8,9},{9,8},{10,11... | collective-permute-start | bytes 2654216 | tf_op jit(solution)/shard_map/ppermute | solution.py:453
